TPU v7x, 32 devices: a whole 2x2x4 slice. The times are simulated.
32 devices in a mesh: fsdp: 4 (over y, x), tok: 8 (over z, core).
Axes of the slice: x: 2, y: 2, z: 4, core: 2. Of those that a mesh axis runs over, the one named last changes fastest.
Arguments:
- tokens: bfloat16 [8192, 8192], P(('fsdp', 'tok')), may hold values from -6 to 6
- frozen_value_weight: bfloat16 [8192, 1024], P(None, 'fsdp'), may hold values from -0.0625 to 0.0625
- adapter_down_maps: bfloat16 [8192, 4096], P('tok', 'fsdp'), may hold values from -0.0625 to 0.0625
- adapter_up_maps: bfloat16 [1024, 4096], P('tok', 'fsdp'), may hold values from -1.5 to 1.5
- cotangent: bfloat16 [8192, 1024], P(('fsdp', 'tok')), may hold values from -6 to 6
- packing_block_tenant: int32 [64], replicated, may hold values from 0 to 255
- packing_block_fill: int32 [64], replicated, may hold values from 1 to 128
Outputs:
- values: bfloat16 [8192, 1024], P(('fsdp', 'tok'))
- token_gradient: bfloat16 [8192, 8192], P(('fsdp', 'tok'))
- grad_down: float32 [8192, 4096], P('tok', 'fsdp')
- grad_up: float32 [1024, 4096], P('tok', 'fsdp')
All inputs are finite; a program needn't handle non-finite values.
Results may differ from a plain program's by a relative error of at most 0.0055.
Values may be sent and summed in bfloat16 or wider, within the bound.
No kernel may reach another device: no remote copies, remote signals or barrier semaphores. Data moves between devices by JAX's collectives and lax.ppermute only.
A program may use at most 128 MiB of HBM per device.

v0:
```python
import jax
import jax.numpy as jnp
from jax import lax
from jax.sharding import PartitionSpec as P

ADAPTER_RANK = 16
TENANT_COUNT = 256
BLOCK = 128


ADAPTER_SCALE = 2.0


def pick_columns(panel, tenants):
    grouped = panel.reshape(panel.shape[0], TENANT_COUNT, ADAPTER_RANK)
    return jnp.take(grouped, tenants, axis=1)


def local(
    tokens,
    frozen_value_weight,
    adapter_down_maps,
    adapter_up_maps,
    cotangent,
    packing_block_tenant,
    packing_block_fill,
):
    tok_rows = tokens.shape[0]
    dev_blocks = tok_rows // BLOCK
    tok_count = lax.axis_size("tok")
    group_blocks = dev_blocks * tok_count
    tenant_group_rows = group_blocks * BLOCK
    fsdp_here = lax.axis_index("fsdp")
    tok_here = lax.axis_index("tok")
    first_block = (fsdp_here * tok_count + tok_here) * dev_blocks
    my_fill = lax.dynamic_slice_in_dim(packing_block_fill, first_block, dev_blocks)
    used_rows = (jnp.arange(BLOCK, dtype=jnp.int32)[None, :] < my_fill[:, None]).reshape(
        tok_rows, 1
    )
    masked_token_rows = used_rows.astype(jnp.float32)
    grad_out = cotangent * used_rows.astype(jnp.bfloat16)
    group_tenants = lax.dynamic_slice_in_dim(
        packing_block_tenant, fsdp_here * group_blocks, group_blocks
    )
    one_hot = (group_tenants[:, None] == jnp.arange(TENANT_COUNT, dtype=jnp.int32)[None, :]).astype(
        jnp.float32
    )
    weight_full, down_full, up_full = (
        lax.all_gather(frozen_value_weight, "fsdp", axis=1, tiled=True),
        lax.all_gather(adapter_down_maps, "fsdp", axis=1, tiled=True),
        lax.all_gather(adapter_up_maps, "fsdp", axis=1, tiled=True),
    )
    frozen_output = jnp.dot(tokens, weight_full, preferred_element_type=jnp.float32)
    feat_cols, grad_cols = (
        lax.all_to_all(tokens, "tok", split_axis=1, concat_axis=0, tiled=True),
        lax.all_to_all(grad_out, "tok", split_axis=1, concat_axis=0, tiled=True),
    )
    feature_blocks = feat_cols.reshape(group_blocks, BLOCK, feat_cols.shape[1])
    gradient_blocks = grad_cols.reshape(group_blocks, BLOCK, grad_cols.shape[1])
    selected_down_map = pick_columns(down_full, group_tenants)
    up_sel = pick_columns(up_full, group_tenants)
    rank_part = jnp.einsum(
        "vxi,ivf->fvx", feature_blocks, selected_down_map, preferred_element_type=jnp.float32
    )
    back_part = jnp.einsum(
        "bkc,cbr->rbk", gradient_blocks, up_sel, preferred_element_type=jnp.float32
    )
    rank_total, back_total = lax.psum((rank_part, back_part), "tok")
    rank_space_input = rank_total.astype(jnp.bfloat16)
    rank_space_gradient = (ADAPTER_SCALE * back_total).astype(jnp.bfloat16)
    adapter_column_slice = (
        ADAPTER_SCALE
        * jnp.einsum("rbk,cbr->bkc", rank_space_input, up_sel, preferred_element_type=jnp.float32)
    ).astype(jnp.bfloat16)
    back_cols = jnp.einsum(
        "new,ien->ewi", rank_space_gradient, selected_down_map, preferred_element_type=jnp.float32
    ).astype(jnp.bfloat16)
    adapter_token_rows, backward_token_rows = (
        lax.all_to_all(
            adapter_column_slice.reshape(tenant_group_rows, -1),
            "tok",
            split_axis=0,
            concat_axis=1,
            tiled=True,
        ),
        lax.all_to_all(
            back_cols.reshape(tenant_group_rows, -1), "tok", split_axis=0, concat_axis=1, tiled=True
        ),
    )
    down_terms = jnp.einsum(
        "oum,eou->oem", feature_blocks, rank_space_gradient, preferred_element_type=jnp.float32
    )
    up_terms = ADAPTER_SCALE * jnp.einsum(
        "bkc,rbk->brc", gradient_blocks, rank_space_input, preferred_element_type=jnp.float32
    )
    down_part = jnp.einsum(
        "bg,brd->dgr", one_hot, down_terms, precision=lax.Precision.HIGHEST
    ).reshape(down_terms.shape[2], TENANT_COUNT * ADAPTER_RANK)
    up_part = jnp.einsum("bg,brc->cgr", one_hot, up_terms, precision=lax.Precision.HIGHEST).reshape(
        up_terms.shape[2], TENANT_COUNT * ADAPTER_RANK
    )
    down_sum, up_sum = (
        lax.psum_scatter(down_part, "fsdp", scatter_dimension=1, tiled=True),
        lax.psum_scatter(up_part, "fsdp", scatter_dimension=1, tiled=True),
    )
    values = (masked_token_rows * (frozen_output + adapter_token_rows.astype(jnp.float32))).astype(
        jnp.bfloat16
    )
    frozen_backward = lax.dot_general(
        grad_out, weight_full, (((1,), (1,)), ((), ())), preferred_element_type=jnp.float32
    )
    token_gradient = (frozen_backward + backward_token_rows.astype(jnp.float32)).astype(
        jnp.bfloat16
    )
    tenant_match = (
        packing_block_tenant[:, None] == jnp.arange(TENANT_COUNT, dtype=jnp.int32)[None, :]
    )
    counts = jnp.sum(
        jnp.where(tenant_match, packing_block_fill[:, None].astype(jnp.float32), 0.0), axis=0
    )
    denominator = jnp.repeat(jnp.maximum(counts, 1.0), ADAPTER_RANK)
    cols_here = down_sum.shape[1]
    denom_here = lax.dynamic_slice_in_dim(denominator, fsdp_here * cols_here, cols_here)
    return (values, token_gradient, down_sum / denom_here, up_sum / denom_here)


def solution(mesh):
    placed = (
        P(("fsdp", "tok"), None),
        P(None, "fsdp"),
        P("tok", "fsdp"),
        P("tok", "fsdp"),
        P(("fsdp", "tok"), None),
        P(),
        P(),
    )
    return jax.shard_map(
        local,
        mesh=mesh,
        in_specs=placed,
        out_specs=(
            P(("fsdp", "tok"), None),
            P(("fsdp", "tok"), None),
            P("tok", "fsdp"),
            P("tok", "fsdp"),
        ),
        check_vma=False,
    )
```

profile of v0, /device:TPU:0, one launch (start us, length us, event | category | flops | bytes accessed | tf_op | source)
XLA Modules:
  0.0 557.8 jit_solution(10438618737021198863)
XLA Ops:
  7.2 1.8 copy.39
  9.1 3.9 copy.37
  14.3 6.3 %all-to-all-start.2 = ((bf16[256,8,128]{2,0,1:T(8,128)(2,1)}), bf16[256,8,128]{2,0,1:T(8,128)(2,1)S(1)}, u32[]{:S(2)}, u32[]{:S(2)}) async-start(bf16[256,8,128]{2,0,1:T(8,128)(2,1)} %copy_bitcast_fusion.1), calls=%async_computation.2 | async-start | bytes 1048576 | tf_op jit(solution)/shard_map/all_to_all | solution.py:56
  20.6 4.9 copy.60
  25.5 10.5 %all-to-all-done.2 = bf16[256,8,128]{2,0,1:T(8,128)(2,1)S(1)} async-done(((bf16[256,8,128]{2,0,1:T(8,128)(2,1)}), bf16[256,8,128]{2,0,1:T(8,128)(2,1)S(1)}, u32[]{:S(2)}, u32[]{:S(2)}) %all-to-all-start.2) | async-done | bytes 524320 | tf_op jit(solution)/shard_map/all_to_all | solution.py:56
  35.9 4.7 all-to-all-start
  40.8 1.8 gather_fusion.1
  42.6 1.1 convolution_bitcast_fusion.2
  43.8 86.1 %all-gather.6.cloned.1.call-done = bf16[1024,4096]{0,1:T(8,128)(2,1)} async-done(((bf16[1024,1024]{0,1:T(8,128)(2,1)}), bf16[1024,4096]{0,1:T(8,128)(2,1)}) %all-gather.6.cloned.1.call-update) | async-done | bytes 8388624 | tf_op jit(solution)/shard_map/all_gather | solution.py:50
  129.9 4.0 gather_fusion
  134.6 3.4 convolution_bitcast_fusion.3
  138.1 29.2 %all-reduce.4 = bf16[16,16,128]{2,0,1:T(8,128)(2,1)S(1)} all-reduce(f32[16,16,128]{2,0,1:T(8,128)S(1)} %convolution_bitcast_fusion.3), channel_id=1, replica_groups=mesh['fsdp'=4,'tok'=8] {'tok'}, use_global_device_ids=true, to_apply=%region_0.1 | all-reduce | flops 32768 | bytes 196608 | tf_op jit(solution)/shard_map/psum | solution.py:68
  168.6 2.0 copy.46
  171.4 15.9 %all-reduce.3.cloned.1.call-done = f32[16,16,128]{2,0,1:T(8,128)} async-done(((f32[16,16,128]{2,0,1:T(8,128)}), f32[16,16,128]{2,0,1:T(8,128)}) %all-reduce.3.cloned.1.call-update) | async-done | bytes 131088 | tf_op jit(solution)/shard_map/psum | solution.py:68
  187.3 2.9 fusion.15
  190.2 10.9 %convolution_bitcast_fusion = f32[1024,256,16]{0,1,2:T(8,128)S(1)} fusion(f32[16,16,1024]{2,1,0:T(8,128)S(1)} %fusion.15, s32[16]{0:T(128)S(1)} %get-tuple-element.17), kind=kOutput, calls=%fused_computation.4 | convolution fusion | flops 805310464 | bytes 17825856 | tf_op jit(solution)/shard_map/bg,brd->dgr/dot_general | solution.py:96
  201.1 20.2 %copy.44 = f32[1024,256,16]{0,2,1:T(8,128)} copy(f32[1024,256,16]{0,1,2:T(8,128)S(1)} %convolution_bitcast_fusion) | data formatting | bytes 33554432 | tf_op jit(solution)/shard_map/bg,brd->dgr/transpose | solution.py:96
  222.2 3.3 convolution_convert_fusion
  225.6 4.5 all-to-all-start.3
  230.2 1.2 fusion.2
  231.4 92.7 %all-to-all-done.3 = bf16[8,256,1024]{2,1,0:T(8,128)(2,1)} async-done(((bf16[8,256,1024]{2,1,0:T(8,128)(2,1)}), bf16[8,256,1024]{2,1,0:T(8,128)(2,1)}, u32[]{:S(2)}, u32[]{:S(2)}) %all-to-all-start.3) | async-done | bytes 4194336 | tf_op jit(solution)/shard_map/all_to_all | solution.py:86
  324.1 3.8 all-to-all-start.1
  328.1 1.2 broadcast_divide_fusion.1
  330.4 3.2 convert_bitcast_fusion
  333.6 4.1 copy.52
  337.7 5.2 all-to-all-done.1
  342.9 41.2 %all-gather.4.cloned.1.call-done = bf16[8192,1024]{1,0:T(8,128)(2,1)} async-done(((bf16[8192,256]{1,0:T(8,128)(2,1)}), bf16[8192,1024]{1,0:T(8,128)(2,1)}) %all-gather.4.cloned.1.call-update) | async-done | bytes 16777232 | tf_op jit(solution)/shard_map/all_gather | solution.py:49
  384.1 12.3 %fusion.3 = bf16[256,1024]{1,0:T(8,128)(2,1)} fusion(bf16[256,8192]{1,0:T(8,128)(2,1)} %param.7, bf16[8192,1024]{1,0:T(8,128)(2,1)} %all-gather.4.cloned.1.call-done, f32[256]{0:T(256)S(1)} %get-tuple-element.19, bf16[8,256,128]{2,1,0:T(8,128)(2,1)S(1)} %all-to-all-done.1), kind=kOutput, calls=%fused_computation.14 | convolution fusion | flops 4296015872 | bytes 22021120 | tf_op jit(solution)/shard_map/dot_general | solution.py:53
  396.5 13.2 %fusion = bf16[256,8192]{1,0:T(8,128)(2,1)} fusion(f32[256,8192]{1,0:T(8,128)} %bitcast.67, bf16[8192,1024]{1,0:T(8,128)(2,1)} %all-gather.4.cloned.1.call-done, bf16[256,1024]{1,0:T(8,128)(2,1)S(1)} %copy-done, bf16[256]{0:T(256)(128)(2,1)S(1)} %get-tuple-element.18), kind=kOutput, calls=%fused_computation.3 | convolution fusion | flops 4299423744 | bytes 29884928 | tf_op jit(solution)/shard_map/dot_general | solution.py:109
  409.6 131.3 %reduce-scatter.3.cloned.1.call-done = f32[1024,1024]{0,1:T(8,128)} async-done(((f32[1024,4096]{0,1:T(8,128)}), f32[1024,1024]{0,1:T(8,128)}) %reduce-scatter.3.cloned.1.call-update) | async-done | bytes 4194320 | tf_op jit(solution)/shard_map/reduce_scatter | solution.py:103
  540.9 4.7 broadcast_divide_fusion
  545.6 5.3 copy.47
  (38 shorter events, 6.6 us)
Async XLA Ops:
  7.2 6.0 %copy-start.3 = (s32[64]{0:T(128)S(1)}, s32[64]{0:T(128)}, u32[]{:S(2)}) copy-start(s32[64]{0:T(128)} %param.13) | copy-start | bytes 772
  7.2 6.1 %copy-start = (bf16[256,1024]{1,0:T(8,128)(2,1)S(1)}, bf16[256,1024]{1,0:T(8,128)(2,1)}, u32[]{:S(2)}) copy-start(bf16[256,1024]{1,0:T(8,128)(2,1)} %param.11) | copy-start | bytes 1572868
  7.2 33.6 %all-gather.8.cloned.1.call-start = ((), (), s32[]{:S(2)}) async-start(), calls=%async_computation.8 | async-start | bytes 1310720 | tf_op jit(solution)/shard_map/all_gather | solution.py:51
  9.1 120.8 %all-gather.6.cloned.1.call-start = ((), (), s32[]{:S(2)}) async-start(), calls=%async_computation.7 | async-start | bytes 10485760 | tf_op jit(solution)/shard_map/all_gather | solution.py:50
  14.3 21.7 %all-to-all-start.2 = ((bf16[256,8,128]{2,0,1:T(8,128)(2,1)}), bf16[256,8,128]{2,0,1:T(8,128)(2,1)S(1)}, u32[]{:S(2)}, u32[]{:S(2)}) async-start(bf16[256,8,128]{2,0,1:T(8,128)(2,1)} %copy_bitcast_fusion.1), calls=%async_computation.2 | async-start | bytes 1048576 | tf_op jit(solution)/shard_map/all_to_all | solution.py:56
  35.9 4.8 copy-start.2
  35.9 98.7 %all-to-all-start = ((bf16[256,8,1024]{2,0,1:T(8,128)(2,1)}), bf16[256,8,1024]{2,0,1:T(8,128)(2,1)}, u32[]{:S(2)}, u32[]{:S(2)}) async-start(bf16[256,8,1024]{2,0,1:T(8,128)(2,1)} %bitcast.68), calls=%async_computation | async-start | bytes 8388608 | tf_op jit(solution)/shard_map/all_to_all | solution.py:55
  40.6 146.6 %all-reduce.3.cloned.1.call-start = ((), (), s32[]{:S(2)}) async-start(), calls=%async_computation.9 | async-start | bytes 262144 | tf_op jit(solution)/shard_map/psum | solution.py:68
  43.7 284.4 %reduce-scatter.5.cloned.1.call-start = ((), (), s32[]{:S(2)}) async-start(), calls=%async_computation.11 | async-start | bytes 2621440 | tf_op jit(solution)/shard_map/reduce_scatter | solution.py:104
  170.5 213.6 %all-gather.4.cloned.1.call-start = ((), (), s32[]{:S(2)}) async-start(), calls=%async_computation.6 | async-start | bytes 20971520 | tf_op jit(solution)/shard_map/all_gather | solution.py:49
  171.1 369.8 %reduce-scatter.3.cloned.1.call-start = ((), (), s32[]{:S(2)}) async-start(), calls=%async_computation.10 | async-start | bytes 20971520 | tf_op jit(solution)/shard_map/reduce_scatter | solution.py:103
  221.3 0.9 copy-start.1
  225.6 98.6 %all-to-all-start.3 = ((bf16[8,256,1024]{2,1,0:T(8,128)(2,1)}), bf16[8,256,1024]{2,1,0:T(8,128)(2,1)}, u32[]{:S(2)}, u32[]{:S(2)}) async-start(bf16[8,256,1024]{2,1,0:T(8,128)(2,1)} %bitcast.69), calls=%async_computation.3 | async-start | bytes 8388608 | tf_op jit(solution)/shard_map/all_to_all | solution.py:86
  324.1 18.8 %all-to-all-start.1 = ((bf16[8,256,128]{2,1,0:T(8,128)(2,1)}), bf16[8,256,128]{2,1,0:T(8,128)(2,1)S(1)}, u32[]{:S(2)}, u32[]{:S(2)}) async-start(bf16[8,256,128]{2,1,0:T(8,128)(2,1)} %bitcast.8), calls=%async_computation.1 | async-start | bytes 1048576 | tf_op jit(solution)/shard_map/all_to_all | solution.py:79
Sparse Core Ops, SparseCore 0:
  10.4 29.3 all-gather.7
  42.2 87.5 all-gather.5
  132.7 54.4 all-reduce.2
  190.9 34.1 reduce-scatter.4
  226.8 157.2 all-gather.3
  387.0 153.8 reduce-scatter.2
where the time goes:
time: 559 us; the launch traced here: 558 us
  waiting for transfers between devices  384 us (69%)
  local copies, waits for them, and re-layouts  50.2 us (9%)
  matrix products  49.7 us (9%)
  blocking collectives  29.2 us (5%)
  starting transfers between devices  19.7 us (4%)
  between operations  14.3 us (3%)
  other arithmetic  10.4 us (2%)
    reduce_scatter x1, waiting for transfers between devices, local(): lax.psum_scatter(down_part, 'fsdp', scatter_dimension=1, tiled=True)  131 us
    all_to_all x1, waiting for transfers between devices, local(): lax.all_to_all(back_cols.reshape(tenant_group_rows, -1), 'tok', split_axi...  92.7 us
    all_gather x1, waiting for transfers between devices, local(): lax.all_gather(adapter_down_maps, 'fsdp', axis=1, tiled=True)  86.1 us
    all_gather x1, waiting for transfers between devices, local(): lax.all_gather(frozen_value_weight, 'fsdp', axis=1, tiled=True)  41.2 us
    psum x1, blocking collectives, local(): rank_total, back_total = lax.psum((rank_part, back_part), 'tok')  29.2 us
    transpose x1, local copies, waits for them, and re-layouts, local(): jnp.einsum('bg,brd->dgr', one_hot, down_terms, precision=lax.Precision.HI...  20.2 us
    psum x1, waiting for transfers between devices, local(): rank_total, back_total = lax.psum((rank_part, back_part), 'tok')  15.9 us
    dot_general x1, matrix products, local(): lax.dot_general(grad_out, weight_full, (((1,), (1,)), ((), ())), preferre...  13.2 us
  transfers between devices with their start and end apart: 10, of which 8 were waited for; matrix products, arithmetic and copies ran while one was open for 17% of the time, Pallas kernels for 0%

commit v1 on v0

v1 whole, which is shorter than its diff:
```python
import functools

import jax
import jax.numpy as jnp
from jax import lax
from jax.experimental import pallas as pl
from jax.experimental.pallas import tpu as pltpu
from jax.sharding import PartitionSpec as P

ADAPTER_RANK = 16
TENANT_COUNT = 256
BLOCK = 128
ADAPTER_SCALE = 2.0
CHUNKS = 4
VMEM_LIMIT = 48 * 1024 * 1024

F32 = jnp.float32
BF16 = jnp.bfloat16
NT = (((1,), (1,)), ((), ()))
TN = (((0,), (0,)), ((), ()))
SMEM = pl.BlockSpec(memory_space=pltpu.SMEM)
VMEM = pl.BlockSpec(memory_space=pltpu.VMEM)


def dot(a, b, dims=(((1,), (0,)), ((), ()))):
    return lax.dot_general(a, b, dims, preferred_element_type=F32)


def block_rows(tenant_ref, block, shard, columns):
    base = tenant_ref[block] * ADAPTER_RANK - shard * columns
    lane = lax.broadcasted_iota(jnp.int32, (ADAPTER_RANK, columns), 1)
    row = lax.broadcasted_iota(jnp.int32, (ADAPTER_RANK, columns), 0)
    return jnp.where(lane - row == base, 1.0, 0.0)


def fill_pick(tenant_ref, pick_ref, row, first_block, count, shard):
    columns = pick_ref.shape[1]

    @pl.loop(0, count)
    def _(n):
        start = pl.multiple_of(row + n * ADAPTER_RANK, ADAPTER_RANK)
        rows = block_rows(tenant_ref, first_block + n, shard, columns)
        pick_ref[pl.ds(start, ADAPTER_RANK), :] = rows.astype(BF16)


def picked(pick_ref, down_ref, up_ref, out_ref):
    cut = down_ref.shape[0]
    out_ref[:, :cut] = dot(pick_ref[...], down_ref[...], NT).astype(BF16)
    out_ref[:, cut:] = dot(pick_ref[...], up_ref[...], NT).astype(BF16)


def send_select_kernel(group, where_ref, tenant_ref, down_ref, up_ref, x_ref, y_ref, pick_ref):
    here = where_ref[0]
    half = group // 2
    rows = half * ADAPTER_RANK
    for out_ref, part, others in ((x_ref, 0, (1, 3)), (y_ref, half, (2, 3))):
        for place, other in enumerate(others):
            first = (here ^ other) * group + part
            fill_pick(tenant_ref, pick_ref, place * rows, first, half, here)
        picked(pick_ref, down_ref, up_ref, out_ref)


def keep_select_kernel(
    group, where_ref, tenant_ref, down_ref, up_ref, x_ref, y_ref, keep_ref, on_y_ref, on_x_ref, pick_ref, part_ref
):
    here = where_ref[0]
    half = group // 2
    rows = half * ADAPTER_RANK
    for n, (came_ref, part, others, on_ref) in enumerate(
        ((x_ref, 0, (0, 2), on_y_ref), (y_ref, half, (0, 1), on_x_ref))
    ):
        for place, other in enumerate(others):
            first = (here ^ other) * group + part
            fill_pick(tenant_ref, pick_ref, place * rows, first, half, here)
        picked(pick_ref, down_ref, up_ref, part_ref)
        keep_ref[n * rows : (n + 1) * rows, :] = part_ref[:rows, :] + came_ref[:rows, :]
        on_ref[...] = part_ref[rows:, :] + came_ref[rows:, :]


def rank_kernel(
    where_ref, fill_ref, tokens_ref, cot_ref, maps_ref, grad_ref, at_ref, rg_ref, lora_ref, terms_ref, up_ref
):
    rows, width = cot_ref.shape
    shards, rank, both = maps_ref.shape
    cut = tokens_ref.shape[1] // shards
    blocks = rows // BLOCK
    first = where_ref[2]
    for n in range(blocks):
        row = lax.broadcasted_iota(jnp.int32, (BLOCK, width), 0)
        part = cot_ref[n * BLOCK : (n + 1) * BLOCK, :]
        grad_ref[n * BLOCK : (n + 1) * BLOCK, :] = jnp.where(
            row < fill_ref[first + n], part, jnp.zeros_like(part)
        )
    for s in range(shards):
        up_ref[:, s * (both - cut) : (s + 1) * (both - cut)] = maps_ref[s, :, cut:]
        at_ref[:, s * cut : (s + 1) * cut] = maps_ref[s, :, :cut]
    own = (
        lax.broadcasted_iota(jnp.int32, (rows, rank), 0) // BLOCK
        == lax.broadcasted_iota(jnp.int32, (rows, rank), 1) // ADAPTER_RANK
    )
    grad = grad_ref[...]
    rank_grad = jnp.where(own, ADAPTER_SCALE * dot(grad, up_ref[...], NT), 0.0).astype(BF16)
    rg_ref[...] = rank_grad
    rank_in = jnp.where(own, dot(tokens_ref[...], at_ref[...], NT), 0.0).astype(BF16)
    lora_ref[...] = (ADAPTER_SCALE * dot(rank_in, up_ref[...])).astype(BF16).astype(F32)
    up_terms = (ADAPTER_SCALE * dot(rank_in, grad, TN)).astype(BF16)
    for s in range(shards):
        terms_ref[s, :, :cut] = dot(rank_grad, tokens_ref[:, s * cut : (s + 1) * cut], TN).astype(BF16)
        terms_ref[s, :, cut:] = up_terms[:, s * (both - cut) : (s + 1) * (both - cut)]


def chunk_kernel(
    steps, final, where_ref, fill_ref, tokens_ref, own_ref, near_ref, far_ref, mine_ref, theirs_ref,
    at_ref, grad_ref, rg_ref, sum_ref, *refs
):
    out_ref, total_ref = refs[-3:-1] if final else refs[-2:]
    acc_ref = refs[-1]
    i = pl.program_id(0)
    here, core = where_ref[0], where_ref[1]
    wide = own_ref.shape[1]

    @pl.when(i == 0)
    def _():
        acc_ref[...] = sum_ref[...]

    last = jnp.where(i < steps // 2, mine_ref[...], theirs_ref[...])
    tokens = tokens_ref[...]
    back = dot(rg_ref[...], at_ref[...]).astype(BF16).astype(F32)
    for other, weight in (
        (here, own_ref[...]),
        (here ^ (1 + core), near_ref[...]),
        (here ^ (2 - core), far_ref[...]),
        (here ^ 3, last),
    ):
        place = pl.ds(pl.multiple_of(other * wide, wide), wide)
        back += dot(grad_ref[:, place], weight, NT)
        acc_ref[:, place] += dot(tokens, weight)
    out_ref[...] = back.astype(BF16)

    if final:
        first = where_ref[2]

        @pl.when(i == steps - 1)
        def _():
            for n in range(total_ref.shape[0] // BLOCK):
                part = acc_ref[n * BLOCK : (n + 1) * BLOCK, :]
                row = lax.broadcasted_iota(jnp.int32, part.shape, 0)
                total_ref[n * BLOCK : (n + 1) * BLOCK, :] = jnp.where(
                    row < fill_ref[first + n], part, 0.0
                ).astype(BF16)


def expand_kernel(
    group, where_ref, tenant_ref, fill_ref, r0_ref, r1_ref, r2_ref, r3a_ref, r3b_ref,
    down_ref, up_ref, pick_ref, scale_ref
):
    here = where_ref[0]
    columns = down_ref.shape[1]
    rows = group * ADAPTER_RANK
    scale_ref[...] = jnp.zeros_like(scale_ref)
    for place in range(4):
        first = (here ^ place) * group

        @pl.loop(0, group)
        def _(n):
            start = pl.multiple_of(place * rows + n * ADAPTER_RANK, ADAPTER_RANK)
            part = block_rows(tenant_ref, first + n, here, columns)
            pick_ref[pl.ds(start, ADAPTER_RANK), :] = part.astype(BF16)
            scale_ref[...] += part * fill_ref[first + n].astype(F32)

    scale = 1.0 / jnp.maximum(jnp.sum(scale_ref[...], axis=0, keepdims=True), 1.0)
    cut = down_ref.shape[0]
    both = r0_ref.shape[1]

    def sums(lo, hi):
        total = dot(r0_ref[:, lo:hi], pick_ref[:rows, :], TN)
        total += dot(r1_ref[:, lo:hi], pick_ref[rows : 2 * rows, :], TN)
        total += dot(r2_ref[:, lo:hi], pick_ref[2 * rows : 3 * rows, :], TN)
        total += dot(r3a_ref[:, lo:hi], pick_ref[3 * rows : 3 * rows + rows // 2, :], TN)
        total += dot(r3b_ref[:, lo:hi], pick_ref[3 * rows + rows // 2 :, :], TN)
        return total * scale

    step = min(cut, 256)
    for lo in range(0, cut, step):
        down_ref[lo : lo + step, :] = sums(lo, lo + step)
    up_ref[...] = sums(cut, both)


def params(**extra):
    return pltpu.CompilerParams(vmem_limit_bytes=VMEM_LIMIT, **extra)


def shape(*dims, dtype=BF16):
    return jax.ShapeDtypeStruct(dims, dtype)


def local(tokens, weight, down_maps, up_maps, cotangent, tenants, fills):
    shards = lax.axis_size("tok")
    groups = lax.axis_size("fsdp")
    rows, model = tokens.shape
    value = cotangent.shape[1]
    wide = weight.shape[1]
    cut, columns = down_maps.shape
    both = cut + up_maps.shape[0]
    dev_blocks = rows // BLOCK
    group = dev_blocks * shards
    rank = dev_blocks * ADAPTER_RANK
    group_rank = group * ADAPTER_RANK
    here = lax.axis_index("fsdp")
    tok_here = lax.axis_index("tok")
    core = tok_here % 2
    where = jnp.stack([here, core, (here * shards + tok_here) * dev_blocks]).astype(jnp.int32)

    def over(axis, flip):
        return lambda a: lax.ppermute(a, axis, [(i, i ^ flip) for i in range(lax.axis_size(axis))])

    on_x, on_y, on_core = over("fsdp", 1), over("fsdp", 2), over("tok", 1)

    def split(first, second):
        pairs = [
            (f * shards + t, (f ^ (second if t % 2 else first)) * shards + t)
            for f in range(groups)
            for t in range(shards)
        ]
        return lambda a: lax.ppermute(a, ("fsdp", "tok"), pairs)

    to_x, to_y = pl.pallas_call(
        functools.partial(send_select_kernel, group),
        out_shape=[shape(group_rank, both)] * 2,
        in_specs=[SMEM, SMEM, VMEM, VMEM],
        out_specs=[VMEM, VMEM],
        scratch_shapes=[pltpu.VMEM((group_rank, columns), BF16)],
        compiler_params=params(),
        name="select_sent",
    )(where, tenants, down_maps, up_maps)
    came_x, came_y = on_x(to_x), on_y(to_y)
    keep, on_y_next, on_x_next = pl.pallas_call(
        functools.partial(keep_select_kernel, group),
        out_shape=[shape(group_rank, both)] + [shape(group_rank // 2, both)] * 2,
        in_specs=[SMEM, SMEM, VMEM, VMEM, VMEM, VMEM],
        out_specs=[VMEM] * 3,
        scratch_shapes=[pltpu.VMEM((group_rank, columns), BF16), pltpu.VMEM((group_rank, both), BF16)],
        compiler_params=params(),
        name="select_kept",
    )(where, tenants, down_maps, up_maps, came_x, came_y)
    maps = keep + jnp.concatenate([on_y(on_y_next), on_x(on_x_next)], axis=0)
    maps = lax.all_to_all(maps.reshape(shards, rank, both), "tok", split_axis=0, concat_axis=0)

    chunk_rows = model // CHUNKS
    arrived = []
    for k in range(CHUNKS):
        own = lax.slice_in_dim(weight, k * chunk_rows, (k + 1) * chunk_rows, axis=0)
        near = split(1, 2)(own)
        far = on_core(near)
        half = chunk_rows // 2
        mine = split(2, 1)(lax.dynamic_slice_in_dim(near, core * half, half, axis=0))
        arrived.append((near, far, mine, on_core(mine)))

    grad, at, rank_grad, lora, terms = pl.pallas_call(
        rank_kernel,
        out_shape=[
            shape(rows, value),
            shape(rank, model),
            shape(rows, rank),
            shape(rows, value, dtype=F32),
            shape(shards, rank, both),
        ],
        in_specs=[SMEM, SMEM, VMEM, VMEM, VMEM],
        out_specs=[VMEM] * 5,
        scratch_shapes=[pltpu.VMEM((rank, value), BF16)],
        compiler_params=params(),
        name="rank_space",
    )(where, fills, tokens, cotangent, maps)

    r0 = lax.all_to_all(terms, "tok", split_axis=0, concat_axis=0).reshape(group_rank, both)
    r1, r2 = on_x(r0), on_y(r0)
    r3a, r3b = on_y(r1[: group_rank // 2]), on_x(r2[group_rank // 2 :])

    tile = 512
    steps = chunk_rows // tile
    total, token_gradient = lora, None
    for k, (near, far, mine, theirs) in enumerate(arrived):
        final = k == CHUNKS - 1

        def turned(i, where_ref):
            return (i + where_ref[1] * (steps // 2)) % steps

        def spot(i, w, f, k=k):
            return k * steps + turned(i, w)

        whole = lambda i, w, f: (0, 0)
        in_specs = [
            pl.BlockSpec((rows, tile), lambda i, w, f, spot=spot: (0, spot(i, w, f))),
            pl.BlockSpec((tile, wide), lambda i, w, f, spot=spot: (spot(i, w, f), 0)),
            pl.BlockSpec((tile, wide), lambda i, w, f: (turned(i, w), 0)),
            pl.BlockSpec((tile, wide), lambda i, w, f: (turned(i, w), 0)),
            pl.BlockSpec((tile, wide), lambda i, w, f: (jnp.minimum(i, steps // 2 - 1), 0)),
            pl.BlockSpec((tile, wide), lambda i, w, f: (jnp.maximum(i - steps // 2, 0), 0)),
            pl.BlockSpec((rank, tile), lambda i, w, f, spot=spot: (0, spot(i, w, f))),
            pl.BlockSpec((rows, value), whole),
            pl.BlockSpec((rows, rank), whole),
            pl.BlockSpec((rows, value), whole),
        ]
        operands = [where, fills, tokens, weight, near, far, mine, theirs, at, grad, rank_grad, total]
        aliases = {}
        if token_gradient is not None:
            in_specs.append(pl.BlockSpec(memory_space=pl.ANY))
            aliases = {len(operands): 0}
            operands.append(token_gradient)
        token_gradient, total = pl.pallas_call(
            functools.partial(chunk_kernel, steps, final),
            out_shape=[shape(rows, model), shape(rows, value, dtype=BF16 if final else F32)],
            grid_spec=pltpu.PrefetchScalarGridSpec(
                num_scalar_prefetch=2,
                grid=(steps,),
                in_specs=in_specs,
                out_specs=[
                    pl.BlockSpec((rows, tile), lambda i, w, f, spot=spot: (0, spot(i, w, f))),
                    pl.BlockSpec((rows, value), whole),
                ],
                scratch_shapes=[pltpu.VMEM((rows, value), F32)] if final else [],
            ),
            input_output_aliases=aliases,
            compiler_params=params(dimension_semantics=("arbitrary",)),
            cost_estimate=pl.CostEstimate(
                flops=4 * rows * chunk_rows * value,
                bytes_accessed=2 * chunk_rows * (2 * rows + value) + 8 * rows * value,
                transcendentals=0,
            ),
            name="base_chunk",
        )(*operands)

    grad_down, grad_up = pl.pallas_call(
        functools.partial(expand_kernel, group),
        out_shape=[shape(cut, columns, dtype=F32), shape(both - cut, columns, dtype=F32)],
        in_specs=[SMEM, SMEM, SMEM] + [VMEM] * 5,
        out_specs=[VMEM, VMEM],
        scratch_shapes=[
            pltpu.VMEM((groups * group_rank, columns), BF16),
            pltpu.VMEM((ADAPTER_RANK, columns), F32),
        ],
        compiler_params=params(),
        name="expand",
    )(where, tenants, fills, r0, r1, r2, r3a, r3b)
    return total, token_gradient, grad_down, grad_up


def solution(mesh):
    placed = (
        P(("fsdp", "tok"), None),
        P(None, "fsdp"),
        P("tok", "fsdp"),
        P("tok", "fsdp"),
        P(("fsdp", "tok"), None),
        P(),
        P(),
    )
    return jax.shard_map(
        local,
        mesh=mesh,
        in_specs=placed,
        out_specs=(
            P(("fsdp", "tok"), None),
            P(("fsdp", "tok"), None),
            P("tok", "fsdp"),
            P("tok", "fsdp"),
        ),
        check_vma=False,
    )
```

time: 559 us -> 167 us (0.30)
  waiting for transfers between devices: 384 us -> 70.3 us
  matrix products: 49.7 us -> 0 us
  Pallas kernels: 0 us -> 46 us
  local copies, waits for them, and re-layouts: 50.2 us -> 18.6 us
  blocking collectives: 29.2 us -> 0 us
  between operations: 14.3 us -> 0.78 us
  starting transfers between devices: 19.7 us -> 29.1 us
  other arithmetic: 10.4 us -> 1.06 us
    reduce_scatter x2 -> x0, waiting for transfers between devices: 131 us -> none  [the longest x1 131 us: local(): lax.psum_scatter(down_part, 'fsdp', scatter_dimension=1, tiled=True)]
    all_gather x3 -> x0, waiting for transfers between devices: 127 us -> none  [the longest x1 86.1 us: local(): lax.all_gather(adapter_down_maps, 'fsdp', axis=1, tiled=True)]
    all_to_all x4 -> x2, waiting for transfers between devices: 109 us -> 0.01 us  [the longest x1 0.01 us: local(): lax.all_to_all(maps.reshape(shards, rank, both), 'tok', split_axis=0, con...]
    ppermute x0 -> x24, waiting for transfers between devices: none -> 70.3 us  [the longest x8 42.8 us: split(): return lambda a: lax.ppermute(a, ('fsdp', 'tok'), pairs)]
    dot_general x10 -> x0, matrix products: 49.7 us -> none  [the longest x1 13.2 us: local(): lax.dot_general(grad_out, weight_full, (((1,), (1,)), ((), ())), preferre...]
    pallas_call x0 -> x8, Pallas kernels: none -> 46 us  [the longest x4 26.5 us: local(): pl.pallas_call(functools.partial(chunk_kernel, steps, final), out_shape=[...]
    psum x1 -> x0, blocking collectives: 29.2 us -> none  [local(): rank_total, back_total = lax.psum((rank_part, back_part), 'tok')]
    transpose x2 -> x0, local copies, waits for them, and re-layouts: 22.2 us -> none  [the longest x1 20.2 us: local(): jnp.einsum('bg,brd->dgr', one_hot, down_terms, precision=lax.Precision.HI...]
  transfers between devices with their start and end apart: 10 -> 26, of which waited for: 8 -> 9; matrix products, arithmetic and copies ran while one was open for 17% -> 5% of each run, Pallas kernels for 0% -> 20%
where the time goes in v1:
time: 167 us; the launch traced here: 166 us
  waiting for transfers between devices  70.3 us (42%)
  Pallas kernels  46 us (28%)
  starting transfers between devices  29.1 us (17%)
  local copies, waits for them, and re-layouts  18.6 us (11%)
    ppermute x8, waiting for transfers between devices, split(): return lambda a: lax.ppermute(a, ('fsdp', 'tok'), pairs)  42.8 us
    ppermute x16, waiting for transfers between devices, over(): lax.ppermute(a, axis, [(i, i ^ flip) for i in range(lax.axis_size(axis))])  27.5 us
    pallas_call x4, Pallas kernels, local(): pl.pallas_call(functools.partial(chunk_kernel, steps, final), out_shape=[...  26.5 us
    ppermute x16, starting transfers between devices, over(): lax.ppermute(a, axis, [(i, i ^ flip) for i in range(lax.axis_size(axis))])  13 us
    unnamed x36, local copies, waits for them, and re-layouts  11.5 us
    pallas_call x1, Pallas kernels, local(): pl.pallas_call(functools.partial(expand_kernel, group), out_shape=[shape(...  7.48 us
    ppermute x8, starting transfers between devices, split(): return lambda a: lax.ppermute(a, ('fsdp', 'tok'), pairs)  6.27 us
    pallas_call x1, Pallas kernels, local(): pl.pallas_call(rank_kernel, out_shape=[shape(rows, value), shape(rank, mo...  5.93 us
  transfers between devices with their start and end apart: 26, of which 9 were waited for; matrix products, arithmetic and copies ran while one was open for 5% of the time, Pallas kernels for 20%

profile of v1, /device:TPU:0, one launch (start us, length us, event | category | flops | bytes accessed | tf_op | source)
XLA Modules:
  0.0 165.8 jit_solution(4444341135680530058)
XLA Ops:
  0.7 1.6 copy-done
  3.9 3.0 %select_sent.1 = (bf16[256,1152]{1,0:T(8,128)(2,1)S(1)}, bf16[256,1152]{1,0:T(8,128)(2,1)S(1)}) custom-call(s32[3]{0:T(128)S(1)} %pad_add_fusion.where_ref, s32[64]{0:T(128)S(1)} %copy-done.15, bf16[1024,1024]{1,0:T(8,128)(2,1)S(1)} %copy-done, bf16[128,1024]{1,0:T(8,128)(2,1)S(1)} %copy-done.5), custom_call_target="tpu_custom_call" | custom-call | tf_op jit(solution)/shard_map/select_sent/pallas_call | solution.py:227
  6.9 3.0 %collective-permute-start.4 = (bf16[256,1152]{1,0:T(8,128)(2,1)S(1)}, bf16[256,1152]{1,0:T(8,128)(2,1)S(1)}, u32[]{:S(2)}, u32[]{:S(2)}) collective-permute-start(bf16[256,1152]{1,0:T(8,128)(2,1)S(1)} %get-tuple-element.24), channel_id=1, source_target_pairs={{0,8},{8,0},{16,24},{24,16},{1,9},{9,1},{17,25},{25,17},{2,10},{10... | collective-permute-start | bytes 1769480 | tf_op jit(solution)/shard_map/ppermute | solution.py:215
  9.9 1.5 collective-permute-start.5
  11.4 11.8 %collective-permute-done.4.x_ref = bf16[256,1152]{1,0:T(8,128)(2,1)S(1)} collective-permute-done((bf16[256,1152]{1,0:T(8,128)(2,1)S(1)}, bf16[256,1152]{1,0:T(8,128)(2,1)S(1)}, u32[]{:S(2)}, u32[]{:S(2)}) %collective-permute-start.4) | collective-permute-done | bytes 589856 | tf_op jit(solution)/shard_map/ppermute | solution.py:215
  23.2 1.5 collective-permute-done.5.y_ref
  26.3 3.0 %select_kept.1 = (bf16[256,1152]{1,0:T(8,128)(2,1)S(1)}, bf16[128,1152]{1,0:T(8,128)(2,1)S(1)}, bf16[128,1152]{1,0:T(8,128)(2,1)S(1)}) custom-call(s32[3]{0:T(128)S(1)} %pad_add_fusion.where_ref, s32[64]{0:T(128)S(1)} %copy-done.16, bf16[1024,1024]{1,0:T(8,128)(2,1)S(1)} %copy-done, bf16[128,1024]{1,0:T(8,128)(2,1)S(1)} %copy-done.6, ...), custom_call_target="tpu_custom_call" | custom-call | tf_op jit(solution)/shard_map/select_kept/pallas_call | solution.py:237
  29.3 1.6 collective-permute-start.6
  31.5 4.2 %fusion = (bf16[2048,256]{1,0:T(8,128)(2,1)}, bf16[2048,256]{1,0:T(8,128)(2,1)}, bf16[2048,256]{1,0:T(8,128)(2,1)}, bf16[2048,256]{1,0:T(8,128)(2,1)}) fusion(bf16[8192,256]{1,0:T(8,128)(2,1)} %own_ref.7), kind=kLoop, calls=%fused_computation.6 | loop fusion | bytes 8388608 | tf_op jit(solution)/shard_map/slice | solution.py:252
  35.7 1.5 collective-permute-start.16
  39.2 4.9 %all-to-all-start = ((bf16[8,32,1152]{2,1,0:T(8,128)(2,1)}), bf16[8,32,1152]{2,1,0:T(8,128)(2,1)}, u32[]{:S(2)}, u32[]{:S(2)}) async-start(bf16[8,32,1152]{2,1,0:T(8,128)(2,1)} %bitcast.3), calls=%async_computation | async-start | bytes 1179648 | tf_op jit(solution)/shard_map/all_to_all | solution.py:247
  44.1 1.0 collective-permute-start.8
  45.1 1.0 collective-permute-start
  46.1 4.7 %collective-permute-done.16.near_ref = bf16[2048,256]{1,0:T(8,128)(2,1)} collective-permute-done((bf16[2048,256]{1,0:T(8,128)(2,1)}, bf16[2048,256]{1,0:T(8,128)(2,1)}, u32[]{:S(2)}, u32[]{:S(2)}) %collective-permute-start.16) | collective-permute-done | bytes 1048608 | tf_op jit(solution)/shard_map/ppermute | solution.py:225
  50.8 1.9 %constant_dynamic-slice_fusion = bf16[1024,256]{1,0:T(8,128)(2,1)} fusion(bf16[2048,256]{1,0:T(8,128)(2,1)} %collective-permute-done.16.near_ref, s32[]{:T(128)S(6)} %select_n.14), kind=kLoop, calls=%fused_computation.1 | loop fusion | bytes 1048580 | tf_op jit(solution)/shard_map/dynamic_slice | solution.py:256
  53.0 15.7 %collective-permute-done.12.near_ref = bf16[2048,256]{1,0:T(8,128)(2,1)S(1)} collective-permute-done((bf16[2048,256]{1,0:T(8,128)(2,1)}, bf16[2048,256]{1,0:T(8,128)(2,1)S(1)}, u32[]{:S(2)}, u32[]{:S(2)}) %collective-permute-start.12) | collective-permute-done | bytes 1048608 | tf_op jit(solution)/shard_map/ppermute | solution.py:225
  69.9 1.0 copy-done.9
  70.9 5.9 %rank_space.1 = (bf16[256,1024]{1,0:T(8,128)(2,1)S(1)}, bf16[32,8192]{1,0:T(8,128)(2,1)S(1)}, bf16[256,32]{1,0:T(8,128)(2,1)S(1)}, f32[256,1024]{1,0:T(8,128)S(1)}, bf16[8,32,1152]{2,1,0:T(8,128)(2,1)S(1)}) custom-call(s32[3]{0:T(128)S(1)} %pad_add_fusion.where_ref, s32[64]{0:T(128)S(1)} %copy-done.14, bf16[256,8192]{1,0:T(8,128)(2,1)} %tokens_ref.9, ...), custom_call_target="tpu_custom_call" | custom-call | tf_op jit(solution)/shard_map/rank_space/pallas_call | solution.py:259
  78.6 4.9 %all-to-all-start.1 = ((bf16[8,32,1152]{2,1,0:T(8,128)(2,1)}), bf16[8,32,1152]{2,1,0:T(8,128)(2,1)}, u32[]{:S(2)}, u32[]{:S(2)}) async-start(bf16[8,32,1152]{2,1,0:T(8,128)(2,1)} %copy-done.8), calls=%async_computation.1 | async-start | bytes 1179648 | tf_op jit(solution)/shard_map/all_to_all | solution.py:275
  84.4 1.5 collective-permute-start.10
  85.9 15.3 %collective-permute-done.near_ref = bf16[2048,256]{1,0:T(8,128)(2,1)S(1)} collective-permute-done((bf16[2048,256]{1,0:T(8,128)(2,1)}, bf16[2048,256]{1,0:T(8,128)(2,1)S(1)}, u32[]{:S(2)}, u32[]{:S(2)}) %collective-permute-start) | collective-permute-done | bytes 1048608 | tf_op jit(solution)/shard_map/ppermute | solution.py:225
  101.7 1.4 collective-permute-start.19
  103.9 6.8 %collective-permute-done.2.mine_ref = bf16[1024,256]{1,0:T(8,128)(2,1)} collective-permute-done((bf16[1024,256]{1,0:T(8,128)(2,1)S(1)}, bf16[1024,256]{1,0:T(8,128)(2,1)}, u32[]{:S(2)}, u32[]{:S(2)}) %collective-permute-start.2) | collective-permute-done | bytes 524320 | tf_op jit(solution)/shard_map/ppermute | solution.py:225
  112.1 1.6 collective-permute-start.20
  113.7 13.7 %collective-permute-done.21.r2_ref = bf16[256,1152]{1,0:T(8,128)(2,1)S(1)} collective-permute-done((bf16[256,1152]{1,0:T(8,128)(2,1)}, bf16[256,1152]{1,0:T(8,128)(2,1)S(1)}, u32[]{:S(2)}, u32[]{:S(2)}) %collective-permute-start.21) | collective-permute-done | bytes 589856 | tf_op jit(solution)/shard_map/ppermute | solution.py:215
  127.4 1.0 copy-done.13
  128.5 6.8 %base_chunk.4 = (bf16[256,8192]{1,0:T(8,128)(2,1)}, f32[256,1024]{1,0:T(8,128)S(1)}) custom-call(s32[3]{0:T(128)S(1)} %pad_add_fusion.where_ref, s32[64]{0:T(128)S(1)} %copy-done.14, bf16[256,8192]{1,0:T(8,128)(2,1)} %tokens_ref.9, bf16[8192,256]{1,0:T(8,128)(2,1)} %own_ref.7, bf16[2048,256]{1,0:T(8,128)(2,1)} %collective-permute-done.16.near_ref, ...), custom_call_target="tpu_custom_call" | custom-call | flops 2147483648 | bytes 8388608 | tf_op jit(solution)/shard_map/base_chunk/pallas_call | solution.py:310
  136.3 6.8 %base_chunk.5 = (bf16[256,8192]{1,0:T(8,128)(2,1)}, f32[256,1024]{1,0:T(8,128)S(1)}) custom-call(s32[3]{0:T(128)S(1)} %pad_add_fusion.where_ref, s32[64]{0:T(128)S(1)} %copy-done.14, bf16[256,8192]{1,0:T(8,128)(2,1)} %tokens_ref.9, bf16[8192,256]{1,0:T(8,128)(2,1)} %own_ref.7, bf16[2048,256]{1,0:T(8,128)(2,1)S(1)} %copy-done.2, ...), custom_call_target="tpu_custom_call", output_to_operand_aliasing={{0}: (12, {})} | custom-call | flops 2147483648 | bytes 8388608 | tf_op jit(solution)/shard_map/base_chunk/pallas_call | solution.py:310
  143.2 1.6 collective-permute-start.23
  145.4 6.5 %base_chunk.6 = (bf16[256,8192]{1,0:T(8,128)(2,1)}, f32[256,1024]{1,0:T(8,128)S(1)}) custom-call(s32[3]{0:T(128)S(1)} %pad_add_fusion.where_ref, s32[64]{0:T(128)S(1)} %copy-done.14, bf16[256,8192]{1,0:T(8,128)(2,1)} %tokens_ref.9, bf16[8192,256]{1,0:T(8,128)(2,1)} %own_ref.7, ...), custom_call_target="tpu_custom_call", output_to_operand_aliasing={{0}: (12, {})} | custom-call | flops 2147483648 | bytes 8388608 | tf_op jit(solution)/shard_map/base_chunk/pallas_call | solution.py:310
  151.9 6.3 %base_chunk.7 = (bf16[256,8192]{1,0:T(8,128)(2,1)}, bf16[256,1024]{1,0:T(8,128)(2,1)}) custom-call(s32[3]{0:T(128)S(1)} %pad_add_fusion.where_ref, s32[64]{0:T(128)S(1)} %copy-done.14, bf16[256,8192]{1,0:T(8,128)(2,1)} %tokens_ref.9, bf16[8192,256]{1,0:T(8,128)(2,1)} %own_ref.7, ...), custom_call_target="tpu_custom_call", output_to_operand_aliasing={{0}: (12, {})} | custom-call | flops 2147483648 | bytes 8388608 | tf_op jit(solution)/shard_map/base_chunk/pallas_call | solution.py:310
  158.3 7.5 %expand.1 = (f32[1024,1024]{1,0:T(8,128)}, f32[128,1024]{1,0:T(8,128)}) custom-call(s32[3]{0:T(128)S(1)} %pad_add_fusion.where_ref, s32[64]{0:T(128)S(1)} %copy-done.17, s32[64]{0:T(128)S(1)} %copy-done.14, bf16[256,1152]{1,0:T(8,128)(2,1)} %bitcast.4.r0_ref, bf16[256,1152]{1,0:T(8,128)(2,1)S(1)} %collective-permute-done.20.r1_ref, ...), custom_call_target="tpu_custom_call" | custom-call | tf_op jit(solution)/shard_map/expand/pallas_call | solution.py:333
  (73 shorter events, 14.2 us)
Async XLA Ops:
  0.7 1.6 copy-start
  6.9 16.3 %collective-permute-start.4 = (bf16[256,1152]{1,0:T(8,128)(2,1)S(1)}, bf16[256,1152]{1,0:T(8,128)(2,1)S(1)}, u32[]{:S(2)}, u32[]{:S(2)}) collective-permute-start(bf16[256,1152]{1,0:T(8,128)(2,1)S(1)} %get-tuple-element.24), channel_id=1, source_target_pairs={{0,8},{8,0},{16,24},{24,16},{1,9},{9,1},{17,25},{25,17},{2,10},{10... | collective-permute-start | bytes 1769480 | tf_op jit(solution)/shard_map/ppermute | solution.py:215
  9.9 14.8 %collective-permute-start.5 = (bf16[256,1152]{1,0:T(8,128)(2,1)S(1)}, bf16[256,1152]{1,0:T(8,128)(2,1)S(1)}, u32[]{:S(2)}, u32[]{:S(2)}) collective-permute-start(bf16[256,1152]{1,0:T(8,128)(2,1)S(1)} %get-tuple-element.25), channel_id=1, source_target_pairs={{0,16},{8,24},{16,0},{24,8},{1,17},{9,25},{17,1},{25,9},{2,18},{10... | collective-permute-start | bytes 1769480 | tf_op jit(solution)/shard_map/ppermute | solution.py:215
  29.3 8.4 %collective-permute-start.6 = (bf16[128,1152]{1,0:T(8,128)(2,1)S(1)}, bf16[128,1152]{1,0:T(8,128)(2,1)S(1)}, u32[]{:S(2)}, u32[]{:S(2)}) collective-permute-start(bf16[128,1152]{1,0:T(8,128)(2,1)S(1)} %get-tuple-element.27), channel_id=1, source_target_pairs={{0,16},{8,24},{16,0},{24,8},{1,17},{9,25},{17,1},{25,9},{2,18},{10... | collective-permute-start | bytes 884744 | tf_op jit(solution)/shard_map/ppermute | solution.py:215
  30.9 7.3 %collective-permute-start.7 = (bf16[128,1152]{1,0:T(8,128)(2,1)S(1)}, bf16[128,1152]{1,0:T(8,128)(2,1)S(1)}, u32[]{:S(2)}, u32[]{:S(2)}) collective-permute-start(bf16[128,1152]{1,0:T(8,128)(2,1)S(1)} %get-tuple-element.28), channel_id=1, source_target_pairs={{0,8},{8,0},{16,24},{24,16},{1,9},{9,1},{17,25},{25,17},{2,10},{10... | collective-permute-start | bytes 884744 | tf_op jit(solution)/shard_map/ppermute | solution.py:215
  35.7 34.2 %copy-start.14 = (s32[64]{0:T(128)S(1)}, s32[64]{0:T(128)}, u32[]{:S(2)}) copy-start(s32[64]{0:T(128)} %fill_ref.11) | copy-start | bytes 772
  35.7 15.1 %collective-permute-start.16 = (bf16[2048,256]{1,0:T(8,128)(2,1)}, bf16[2048,256]{1,0:T(8,128)(2,1)}, u32[]{:S(2)}, u32[]{:S(2)}) collective-permute-start(bf16[2048,256]{1,0:T(8,128)(2,1)} %get-tuple-element.44), channel_id=1, source_target_pairs={{0,8},{1,17},{2,10},{3,19},{4,12},{5,21},{6,14},{7,23},{8,0},{9,25... | collective-permute-start | bytes 3145736 | tf_op jit(solution)/shard_map/ppermute | solution.py:225
  37.2 31.5 %collective-permute-start.12 = (bf16[2048,256]{1,0:T(8,128)(2,1)}, bf16[2048,256]{1,0:T(8,128)(2,1)S(1)}, u32[]{:S(2)}, u32[]{:S(2)}) collective-permute-start(bf16[2048,256]{1,0:T(8,128)(2,1)} %get-tuple-element.45), channel_id=1, source_target_pairs={{0,8},{1,17},{2,10},{3,19},{4,12},{5,21},{6,14},{7,23},{8,0},{9,25... | collective-permute-start | bytes 3145736 | tf_op jit(solution)/shard_map/ppermute | solution.py:225
  39.2 30.7 %all-to-all-start = ((bf16[8,32,1152]{2,1,0:T(8,128)(2,1)}), bf16[8,32,1152]{2,1,0:T(8,128)(2,1)}, u32[]{:S(2)}, u32[]{:S(2)}) async-start(bf16[8,32,1152]{2,1,0:T(8,128)(2,1)} %bitcast.3), calls=%async_computation | async-start | bytes 1179648 | tf_op jit(solution)/shard_map/all_to_all | solution.py:247
  44.1 40.3 %collective-permute-start.8 = (bf16[2048,256]{1,0:T(8,128)(2,1)}, bf16[2048,256]{1,0:T(8,128)(2,1)S(1)}, u32[]{:S(2)}, u32[]{:S(2)}) collective-permute-start(bf16[2048,256]{1,0:T(8,128)(2,1)} %get-tuple-element.46), channel_id=1, source_target_pairs={{0,8},{1,17},{2,10},{3,19},{4,12},{5,21},{6,14},{7,23},{8,0},{9,25... | collective-permute-start | bytes 3145736 | tf_op jit(solution)/shard_map/ppermute | solution.py:225
  45.1 56.2 %collective-permute-start = (bf16[2048,256]{1,0:T(8,128)(2,1)}, bf16[2048,256]{1,0:T(8,128)(2,1)S(1)}, u32[]{:S(2)}, u32[]{:S(2)}) collective-permute-start(bf16[2048,256]{1,0:T(8,128)(2,1)} %get-tuple-element.47), channel_id=1, source_target_pairs={{0,8},{1,17},{2,10},{3,19},{4,12},{5,21},{6,14},{7,23},{8,0},{9,25... | collective-permute-start | bytes 3145736 | tf_op jit(solution)/shard_map/ppermute | solution.py:225
  52.7 48.6 %collective-permute-start.18 = (bf16[1024,256]{1,0:T(8,128)(2,1)}, bf16[1024,256]{1,0:T(8,128)(2,1)}, u32[]{:S(2)}, u32[]{:S(2)}) collective-permute-start(bf16[1024,256]{1,0:T(8,128)(2,1)} %constant_dynamic-slice_fusion), channel_id=1, source_target_pairs={{0,16},{1,9},{2,18},{3,11},{4,20},{5,13},{6,22},{7,15},{8,24},{9,1... | collective-permute-start | bytes 1572872 | tf_op jit(solution)/shard_map/ppermute | solution.py:225
  69.6 32.1 %collective-permute-start.14 = (bf16[1024,256]{1,0:T(8,128)(2,1)}, bf16[1024,256]{1,0:T(8,128)(2,1)}, u32[]{:S(2)}, u32[]{:S(2)}) collective-permute-start(bf16[1024,256]{1,0:T(8,128)(2,1)} %constant_dynamic-slice_fusion.1), channel_id=1, source_target_pairs={{0,16},{1,9},{2,18},{3,11},{4,20},{5,13},{6,22},{7,15},{8,24},{9,1... | collective-permute-start | bytes 1572872 | tf_op jit(solution)/shard_map/ppermute | solution.py:225
  78.6 32.8 %all-to-all-start.1 = ((bf16[8,32,1152]{2,1,0:T(8,128)(2,1)}), bf16[8,32,1152]{2,1,0:T(8,128)(2,1)}, u32[]{:S(2)}, u32[]{:S(2)}) async-start(bf16[8,32,1152]{2,1,0:T(8,128)(2,1)} %copy-done.8), calls=%async_computation.1 | async-start | bytes 1179648 | tf_op jit(solution)/shard_map/all_to_all | solution.py:275
  83.6 28.2 %collective-permute-start.17 = (bf16[2048,256]{1,0:T(8,128)(2,1)}, bf16[2048,256]{1,0:T(8,128)(2,1)}, u32[]{:S(2)}, u32[]{:S(2)}) collective-permute-start(bf16[2048,256]{1,0:T(8,128)(2,1)} %collective-permute-done.16.near_ref), channel_id=1, source_target_pairs={{0,1},{1,0},{2,3},{3,2},{4,5},{5,4},{6,7},{7,6},{8,9},{9,8},{10,11... | collective-permute-start | bytes 3145736 | tf_op jit(solution)/shard_map/ppermute | solution.py:215
  84.4 18.7 %collective-permute-start.10 = (bf16[1024,256]{1,0:T(8,128)(2,1)S(1)}, bf16[1024,256]{1,0:T(8,128)(2,1)S(1)}, u32[]{:S(2)}, u32[]{:S(2)}) collective-permute-start(bf16[1024,256]{1,0:T(8,128)(2,1)S(1)} %constant_dynamic-slice_fusion.2), channel_id=1, source_target_pairs={{0,16},{1,9},{2,18},{3,11},{4,20},{5,13},{6,22},{7,15},{8,24},{9,1... | collective-permute-start | bytes 1572872 | tf_op jit(solution)/shard_map/ppermute | solution.py:225
  101.3 12.4 %collective-permute-start.13 = (bf16[2048,256]{1,0:T(8,128)(2,1)}, bf16[2048,256]{1,0:T(8,128)(2,1)}, u32[]{:S(2)}, u32[]{:S(2)}) collective-permute-start(bf16[2048,256]{1,0:T(8,128)(2,1)} %copy-done.1), channel_id=1, source_target_pairs={{0,1},{1,0},{2,3},{3,2},{4,5},{5,4},{6,7},{7,6},{8,9},{9,8},{10,11... | collective-permute-start | bytes 3145736 | tf_op jit(solution)/shard_map/ppermute | solution.py:215
  101.3 9.4 %collective-permute-start.2 = (bf16[1024,256]{1,0:T(8,128)(2,1)S(1)}, bf16[1024,256]{1,0:T(8,128)(2,1)}, u32[]{:S(2)}, u32[]{:S(2)}) collective-permute-start(bf16[1024,256]{1,0:T(8,128)(2,1)S(1)} %constant_dynamic-slice_fusion.3), channel_id=1, source_target_pairs={{0,16},{1,9},{2,18},{3,11},{4,20},{5,13},{6,22},{7,15},{8,24},{9,1... | collective-permute-start | bytes 1572872 | tf_op jit(solution)/shard_map/ppermute | solution.py:225
  101.7 9.0 %collective-permute-start.19 = (bf16[1024,256]{1,0:T(8,128)(2,1)}, bf16[1024,256]{1,0:T(8,128)(2,1)S(1)}, u32[]{:S(2)}, u32[]{:S(2)}) collective-permute-start(bf16[1024,256]{1,0:T(8,128)(2,1)} %collective-permute-done.18.mine_ref), channel_id=1, source_target_pairs={{0,1},{1,0},{2,3},{3,2},{4,5},{5,4},{6,7},{7,6},{8,9},{9,8},{10,11... | collective-permute-start | bytes 1572872 | tf_op jit(solution)/shard_map/ppermute | solution.py:215
  103.1 8.9 %collective-permute-start.15 = (bf16[1024,256]{1,0:T(8,128)(2,1)}, bf16[1024,256]{1,0:T(8,128)(2,1)}, u32[]{:S(2)}, u32[]{:S(2)}) collective-permute-start(bf16[1024,256]{1,0:T(8,128)(2,1)} %collective-permute-done.14.mine_ref), channel_id=1, source_target_pairs={{0,1},{1,0},{2,3},{3,2},{4,5},{5,4},{6,7},{7,6},{8,9},{9,8},{10,11... | collective-permute-start | bytes 1572872 | tf_op jit(solution)/shard_map/ppermute | solution.py:215
  110.7 34.7 %collective-permute-start.9 = (bf16[2048,256]{1,0:T(8,128)(2,1)S(1)}, bf16[2048,256]{1,0:T(8,128)(2,1)}, u32[]{:S(2)}, u32[]{:S(2)}) collective-permute-start(bf16[2048,256]{1,0:T(8,128)(2,1)S(1)} %collective-permute-done.8.near_ref), channel_id=1, source_target_pairs={{0,1},{1,0},{2,3},{3,2},{4,5},{5,4},{6,7},{7,6},{8,9},{9,8},{10,11... | collective-permute-start | bytes 3145736 | tf_op jit(solution)/shard_map/ppermute | solution.py:215
  111.5 16.0 %collective-permute-start.21 = (bf16[256,1152]{1,0:T(8,128)(2,1)}, bf16[256,1152]{1,0:T(8,128)(2,1)S(1)}, u32[]{:S(2)}, u32[]{:S(2)}) collective-permute-start(bf16[256,1152]{1,0:T(8,128)(2,1)} %bitcast.4.r0_ref), channel_id=1, source_target_pairs={{0,16},{8,24},{16,0},{24,8},{1,17},{9,25},{17,1},{25,9},{2,18},{10... | collective-permute-start | bytes 1769480 | tf_op jit(solution)/shard_map/ppermute | solution.py:215
  111.8 40.1 %collective-permute-start.1 = (bf16[2048,256]{1,0:T(8,128)(2,1)S(1)}, bf16[2048,256]{1,0:T(8,128)(2,1)S(1)}, u32[]{:S(2)}, u32[]{:S(2)}) collective-permute-start(bf16[2048,256]{1,0:T(8,128)(2,1)S(1)} %collective-permute-done.near_ref), channel_id=1, source_target_pairs={{0,1},{1,0},{2,3},{3,2},{4,5},{5,4},{6,7},{7,6},{8,9},{9,8},{10,11... | collective-permute-start | bytes 3145736 | tf_op jit(solution)/shard_map/ppermute | solution.py:215
  112.1 31.1 %collective-permute-start.20 = (bf16[256,1152]{1,0:T(8,128)(2,1)}, bf16[256,1152]{1,0:T(8,128)(2,1)S(1)}, u32[]{:S(2)}, u32[]{:S(2)}) collective-permute-start(bf16[256,1152]{1,0:T(8,128)(2,1)} %bitcast.4.r0_ref), channel_id=1, source_target_pairs={{0,8},{8,0},{16,24},{24,16},{1,9},{9,1},{17,25},{25,17},{2,10},{10... | collective-permute-start | bytes 1769480 | tf_op jit(solution)/shard_map/ppermute | solution.py:215
  113.7 31.1 %collective-permute-start.11 = (bf16[1024,256]{1,0:T(8,128)(2,1)}, bf16[1024,256]{1,0:T(8,128)(2,1)S(1)}, u32[]{:S(2)}, u32[]{:S(2)}) collective-permute-start(bf16[1024,256]{1,0:T(8,128)(2,1)} %copy-done.10), channel_id=1, source_target_pairs={{0,1},{1,0},{2,3},{3,2},{4,5},{5,4},{6,7},{7,6},{8,9},{9,8},{10,11... | collective-permute-start | bytes 1572872 | tf_op jit(solution)/shard_map/ppermute | solution.py:215
  127.4 24.5 %collective-permute-start.3 = (bf16[1024,256]{1,0:T(8,128)(2,1)}, bf16[1024,256]{1,0:T(8,128)(2,1)S(1)}, u32[]{:S(2)}, u32[]{:S(2)}) collective-permute-start(bf16[1024,256]{1,0:T(8,128)(2,1)} %collective-permute-done.2.mine_ref), channel_id=1, source_target_pairs={{0,1},{1,0},{2,3},{3,2},{4,5},{5,4},{6,7},{7,6},{8,9},{9,8},{10,11... | collective-permute-start | bytes 1572872 | tf_op jit(solution)/shard_map/ppermute | solution.py:215
  128.5 7.8 %copy-start.2 = (bf16[2048,256]{1,0:T(8,128)(2,1)S(1)}, bf16[2048,256]{1,0:T(8,128)(2,1)}, u32[]{:S(2)}) copy-start(bf16[2048,256]{1,0:T(8,128)(2,1)} %copy-done.1) | copy-start | bytes 3145732
  136.3 9.1 %copy-start.11 = (bf16[1024,256]{1,0:T(8,128)(2,1)S(1)}, bf16[1024,256]{1,0:T(8,128)(2,1)}, u32[]{:S(2)}) copy-start(bf16[1024,256]{1,0:T(8,128)(2,1)} %copy-done.10) | copy-start | bytes 1572868
  143.1 2.2 %copy-start.3 = (f32[256,1024]{1,0:T(8,128)}, f32[256,1024]{1,0:T(8,128)S(1)}, u32[]{:S(2)}) copy-start(f32[256,1024]{1,0:T(8,128)S(1)} %get-tuple-element.35.sum_ref) | copy-start | bytes 3145732
  143.2 15.1 %collective-permute-start.23 = (bf16[128,1152]{1,0:T(8,128)(2,1)S(1)}, bf16[128,1152]{1,0:T(8,128)(2,1)S(1)}, u32[]{:S(2)}, u32[]{:S(2)}) collective-permute-start(bf16[128,1152]{1,0:T(8,128)(2,1)S(1)} %slice.25), channel_id=1, source_target_pairs={{0,8},{8,0},{16,24},{24,16},{1,9},{9,1},{17,25},{25,17},{2,10},{10... | collective-permute-start | bytes 884744 | tf_op jit(solution)/shard_map/ppermute | solution.py:215
  144.8 13.5 %collective-permute-start.22 = (bf16[128,1152]{1,0:T(8,128)(2,1)S(1)}, bf16[128,1152]{1,0:T(8,128)(2,1)S(1)}, u32[]{:S(2)}, u32[]{:S(2)}) collective-permute-start(bf16[128,1152]{1,0:T(8,128)(2,1)S(1)} %slice.24), channel_id=1, source_target_pairs={{0,16},{8,24},{16,0},{24,8},{1,17},{9,25},{17,1},{25,9},{2,18},{10... | collective-permute-start | bytes 884744 | tf_op jit(solution)/shard_map/ppermute | solution.py:215
  151.9 6.4 %copy-start.17 = (s32[64]{0:T(128)S(1)}, s32[64]{0:T(128)}, u32[]{:S(2)}) copy-start(s32[64]{0:T(128)} %tenant_ref.5) | copy-start | bytes 772
  (12 other events, 10.8 us)

commit v2 on v1

--- a/solution.py
+++ b/solution.py
@@ -11,7 +11,7 @@
 TENANT_COUNT = 256
 BLOCK = 128
 ADAPTER_SCALE = 2.0
-CHUNKS = 4
+CHUNKS = (2, 2, 2, 2)
 VMEM_LIMIT = 48 * 1024 * 1024
 
 F32 = jnp.float32
@@ -20,6 +20,7 @@
 TN = (((0,), (0,)), ((), ()))
 SMEM = pl.BlockSpec(memory_space=pltpu.SMEM)
 VMEM = pl.BlockSpec(memory_space=pltpu.VMEM)
+ANY = pl.BlockSpec(memory_space=pl.ANY)
 
 
 def dot(a, b, dims=(((1,), (0,)), ((), ()))):
@@ -49,32 +50,37 @@
     out_ref[:, cut:] = dot(pick_ref[...], up_ref[...], NT).astype(BF16)
 
 
-def send_select_kernel(group, where_ref, tenant_ref, down_ref, up_ref, x_ref, y_ref, pick_ref):
-    here = where_ref[0]
-    half = group // 2
-    rows = half * ADAPTER_RANK
-    for out_ref, part, others in ((x_ref, 0, (1, 3)), (y_ref, half, (2, 3))):
-        for place, other in enumerate(others):
-            first = (here ^ other) * group + part
-            fill_pick(tenant_ref, pick_ref, place * rows, first, half, here)
-        picked(pick_ref, down_ref, up_ref, out_ref)
-
-
-def keep_select_kernel(
-    group, where_ref, tenant_ref, down_ref, up_ref, x_ref, y_ref, keep_ref, on_y_ref, on_x_ref, pick_ref, part_ref
-):
-    here = where_ref[0]
-    half = group // 2
-    rows = half * ADAPTER_RANK
-    for n, (came_ref, part, others, on_ref) in enumerate(
-        ((x_ref, 0, (0, 2), on_y_ref), (y_ref, half, (0, 1), on_x_ref))
-    ):
-        for place, other in enumerate(others):
-            first = (here ^ other) * group + part
-            fill_pick(tenant_ref, pick_ref, place * rows, first, half, here)
-        picked(pick_ref, down_ref, up_ref, part_ref)
-        keep_ref[n * rows : (n + 1) * rows, :] = part_ref[:rows, :] + came_ref[:rows, :]
-        on_ref[...] = part_ref[rows:, :] + came_ref[rows:, :]
+def pick_two(group, tenant_ref, pick_ref, here, others):
+    for place, other in enumerate(others):
+        fill_pick(tenant_ref, pick_ref, place * group * ADAPTER_RANK, (here ^ other) * group, group, here)
+
+
+def send_select_kernel(group, size, where_ref, tenant_ref, weight_ref, down_ref, up_ref, out_ref, piece_ref, pick_ref, sem):
+    copy = pltpu.make_async_copy(weight_ref.at[pl.ds(0, size), :], piece_ref, sem)
+    copy.start()
+    here, core = where_ref[0], where_ref[1]
+    pick_two(group, tenant_ref, pick_ref, here, (1 + core, 3))
+    picked(pick_ref, down_ref, up_ref, out_ref)
+    copy.wait()
+
+
+def keep_select_kernel(group, where_ref, tenant_ref, down_ref, up_ref, out_ref, pick_ref):
+    here, core = where_ref[0], where_ref[1]
+    pick_two(group, tenant_ref, pick_ref, here, (0, 2 - core))
+    picked(pick_ref, down_ref, up_ref, out_ref)
+
+
+def cut_kernel(start, where_ref, near_ref, weight_ref, half_ref, piece_ref, sems):
+    half = half_ref.shape[0]
+    at = pl.multiple_of(where_ref[1] * half, half)
+    copies = [
+        pltpu.make_async_copy(near_ref.at[pl.ds(at, half), :], half_ref, sems.at[0]),
+        pltpu.make_async_copy(weight_ref.at[pl.ds(start, piece_ref.shape[0]), :], piece_ref, sems.at[1]),
+    ]
+    for copy in copies:
+        copy.start()
+    for copy in copies:
+        copy.wait()
 
 
 def rank_kernel(
@@ -151,15 +157,14 @@
 
 
 def expand_kernel(
-    group, where_ref, tenant_ref, fill_ref, r0_ref, r1_ref, r2_ref, r3a_ref, r3b_ref,
-    down_ref, up_ref, pick_ref, scale_ref
+    group, where_ref, tenant_ref, fill_ref, r0_ref, r1_ref, r2_ref, r3_ref, _, down_ref, up_ref, pick_ref, scale_ref
 ):
-    here = where_ref[0]
+    here, core = where_ref[0], where_ref[1]
     columns = down_ref.shape[1]
     rows = group * ADAPTER_RANK
     scale_ref[...] = jnp.zeros_like(scale_ref)
-    for place in range(4):
-        first = (here ^ place) * group
+    for place, other in enumerate((0, 1 + core, 2 - core, 3)):
+        first = (here ^ other) * group
 
         @pl.loop(0, group)
         def _(n):
@@ -174,10 +179,8 @@
 
     def sums(lo, hi):
         total = dot(r0_ref[:, lo:hi], pick_ref[:rows, :], TN)
-        total += dot(r1_ref[:, lo:hi], pick_ref[rows : 2 * rows, :], TN)
-        total += dot(r2_ref[:, lo:hi], pick_ref[2 * rows : 3 * rows, :], TN)
-        total += dot(r3a_ref[:, lo:hi], pick_ref[3 * rows : 3 * rows + rows // 2, :], TN)
-        total += dot(r3b_ref[:, lo:hi], pick_ref[3 * rows + rows // 2 :, :], TN)
+        for n, ref in enumerate((r1_ref, r2_ref, r3_ref)):
+            total += dot(ref[:, lo:hi], pick_ref[(n + 1) * rows : (n + 2) * rows, :], TN)
         return total * scale
 
     step = min(cut, 256)
@@ -211,10 +214,8 @@
     core = tok_here % 2
     where = jnp.stack([here, core, (here * shards + tok_here) * dev_blocks]).astype(jnp.int32)
 
-    def over(axis, flip):
-        return lambda a: lax.ppermute(a, axis, [(i, i ^ flip) for i in range(lax.axis_size(axis))])
-
-    on_x, on_y, on_core = over("fsdp", 1), over("fsdp", 2), over("tok", 1)
+    def on_core(a):
+        return lax.ppermute(a, "tok", [(t, t ^ 1) for t in range(shards)])
 
     def split(first, second):
         pairs = [
@@ -224,36 +225,51 @@
         ]
         return lambda a: lax.ppermute(a, ("fsdp", "tok"), pairs)
 
-    to_x, to_y = pl.pallas_call(
-        functools.partial(send_select_kernel, group),
-        out_shape=[shape(group_rank, both)] * 2,
-        in_specs=[SMEM, SMEM, VMEM, VMEM],
-        out_specs=[VMEM, VMEM],
-        scratch_shapes=[pltpu.VMEM((group_rank, columns), BF16)],
+    first_way, second_way = split(1, 2), split(2, 1)
+
+    parts = [(model // 8 * sum(CHUNKS[:k]), model // 8 * size) for k, size in enumerate(CHUNKS)]
+    sent, piece = pl.pallas_call(
+        functools.partial(send_select_kernel, group, parts[0][1]),
+        out_shape=[shape(2 * group_rank, both), shape(parts[0][1], wide)],
+        in_specs=[SMEM, SMEM, ANY, VMEM, VMEM],
+        out_specs=[VMEM, ANY],
+        scratch_shapes=[pltpu.VMEM((2 * group_rank, columns), BF16), pltpu.SemaphoreType.DMA],
         compiler_params=params(),
         name="select_sent",
-    )(where, tenants, down_maps, up_maps)
-    came_x, came_y = on_x(to_x), on_y(to_y)
-    keep, on_y_next, on_x_next = pl.pallas_call(
+    )(where, tenants, weight, down_maps, up_maps)
+    came = first_way(sent)
+    kept = pl.pallas_call(
         functools.partial(keep_select_kernel, group),
-        out_shape=[shape(group_rank, both)] + [shape(group_rank // 2, both)] * 2,
-        in_specs=[SMEM, SMEM, VMEM, VMEM, VMEM, VMEM],
-        out_specs=[VMEM] * 3,
-        scratch_shapes=[pltpu.VMEM((group_rank, columns), BF16), pltpu.VMEM((group_rank, both), BF16)],
+        out_shape=shape(2 * group_rank, both),
+        in_specs=[SMEM, SMEM, VMEM, VMEM],
+        out_specs=VMEM,
+        scratch_shapes=[pltpu.VMEM((2 * group_rank, columns), BF16)],
         compiler_params=params(),
         name="select_kept",
-    )(where, tenants, down_maps, up_maps, came_x, came_y)
-    maps = keep + jnp.concatenate([on_y(on_y_next), on_x(on_x_next)], axis=0)
+    )(where, tenants, down_maps, up_maps)
+    sent = kept[group_rank:] + came[group_rank:]
+    maps = kept[:group_rank] + came[:group_rank] + second_way(sent)
     maps = lax.all_to_all(maps.reshape(shards, rank, both), "tok", split_axis=0, concat_axis=0)
 
-    chunk_rows = model // CHUNKS
     arrived = []
-    for k in range(CHUNKS):
-        own = lax.slice_in_dim(weight, k * chunk_rows, (k + 1) * chunk_rows, axis=0)
-        near = split(1, 2)(own)
+    for k, (_, size) in enumerate(parts):
+        near = first_way(piece)
         far = on_core(near)
-        half = chunk_rows // 2
-        mine = split(2, 1)(lax.dynamic_slice_in_dim(near, core * half, half, axis=0))
+        half = size // 2
+        if k + 1 < len(parts):
+            after, after_size = parts[k + 1]
+            part, piece = pl.pallas_call(
+                functools.partial(cut_kernel, after),
+                out_shape=[shape(half, wide), shape(after_size, wide)],
+                in_specs=[SMEM, ANY, ANY],
+                out_specs=[ANY, ANY],
+                scratch_shapes=[pltpu.SemaphoreType.DMA((2,))],
+                compiler_params=params(),
+                name="cut_chunk",
+            )(where, near, weight)
+        else:
+            part = lax.dynamic_slice_in_dim(near, core * half, half, axis=0)
+        mine = second_way(part)
         arrived.append((near, far, mine, on_core(mine)))
 
     grad, at, rank_grad, lora, terms = pl.pallas_call(
@@ -273,29 +289,31 @@
     )(where, fills, tokens, cotangent, maps)
 
     r0 = lax.all_to_all(terms, "tok", split_axis=0, concat_axis=0).reshape(group_rank, both)
-    r1, r2 = on_x(r0), on_y(r0)
-    r3a, r3b = on_y(r1[: group_rank // 2]), on_x(r2[group_rank // 2 :])
+    r1, r2 = first_way(r0), second_way(r0)
+    r3 = second_way(r1)
 
     tile = 512
-    steps = chunk_rows // tile
     total, token_gradient = lora, None
+    totals = []
     for k, (near, far, mine, theirs) in enumerate(arrived):
-        final = k == CHUNKS - 1
-
-        def turned(i, where_ref):
+        final = k == len(parts) - 1
+        start, chunk_rows = parts[k]
+        steps = chunk_rows // tile
+
+        def turned(i, where_ref, steps=steps):
             return (i + where_ref[1] * (steps // 2)) % steps
 
-        def spot(i, w, f, k=k):
-            return k * steps + turned(i, w)
+        def spot(i, w, f, start=start // tile, turned=turned):
+            return start + turned(i, w)
 
         whole = lambda i, w, f: (0, 0)
         in_specs = [
             pl.BlockSpec((rows, tile), lambda i, w, f, spot=spot: (0, spot(i, w, f))),
             pl.BlockSpec((tile, wide), lambda i, w, f, spot=spot: (spot(i, w, f), 0)),
-            pl.BlockSpec((tile, wide), lambda i, w, f: (turned(i, w), 0)),
-            pl.BlockSpec((tile, wide), lambda i, w, f: (turned(i, w), 0)),
-            pl.BlockSpec((tile, wide), lambda i, w, f: (jnp.minimum(i, steps // 2 - 1), 0)),
-            pl.BlockSpec((tile, wide), lambda i, w, f: (jnp.maximum(i - steps // 2, 0), 0)),
+            pl.BlockSpec((tile, wide), lambda i, w, f, turned=turned: (turned(i, w), 0)),
+            pl.BlockSpec((tile, wide), lambda i, w, f, turned=turned: (turned(i, w), 0)),
+            pl.BlockSpec((tile, wide), lambda i, w, f, half=steps // 2: (jnp.minimum(i, half - 1), 0)),
+            pl.BlockSpec((tile, wide), lambda i, w, f, half=steps // 2: (jnp.maximum(i - half, 0), 0)),
             pl.BlockSpec((rank, tile), lambda i, w, f, spot=spot: (0, spot(i, w, f))),
             pl.BlockSpec((rows, value), whole),
             pl.BlockSpec((rows, rank), whole),
@@ -329,11 +347,12 @@
             ),
             name="base_chunk",
         )(*operands)
+        totals.append(total)
 
     grad_down, grad_up = pl.pallas_call(
         functools.partial(expand_kernel, group),
         out_shape=[shape(cut, columns, dtype=F32), shape(both - cut, columns, dtype=F32)],
-        in_specs=[SMEM, SMEM, SMEM] + [VMEM] * 5,
+        in_specs=[SMEM, SMEM, SMEM] + [VMEM] * 4 + [ANY],
         out_specs=[VMEM, VMEM],
         scratch_shapes=[
             pltpu.VMEM((groups * group_rank, columns), BF16),
@@ -341,7 +360,7 @@
         ],
         compiler_params=params(),
         name="expand",
-    )(where, tenants, fills, r0, r1, r2, r3a, r3b)
+    )(where, tenants, fills, r0, r1, r2, r3, totals[-2])
     return total, token_gradient, grad_down, grad_up
 
 

time: 167 us -> 234 us (1.40)
  Pallas kernels: 46 us -> 114 us
  local copies, waits for them, and re-layouts: 18.6 us -> 11.7 us
  waiting for transfers between devices: 70.3 us -> 77.1 us
    pallas_call x2 -> x5, Pallas kernels: 6 us -> 73.9 us  [the longest x3 68.9 us: local(): pl.pallas_call(functools.partial(cut_kernel, after), out_shape=[shape(hal...]
    ppermute x8 -> x13, waiting for transfers between devices: 42.8 us -> 75.9 us  [split(): return lambda a: lax.ppermute(a, ('fsdp', 'tok'), pairs)]
    ppermute x16 -> x8, waiting for transfers between devices: 27.5 us -> 0.02 us  [on_core(): return lax.ppermute(a, 'tok', [(t, t ^ 1) for t in range(shards)])]
    ppermute x16 -> x8, starting transfers between devices: 13 us -> 3.3 us  [on_core(): return lax.ppermute(a, 'tok', [(t, t ^ 1) for t in range(shards)])]
    ppermute x8 -> x13, starting transfers between devices: 6.27 us -> 15.2 us  [split(): return lambda a: lax.ppermute(a, ('fsdp', 'tok'), pairs)]
    slice x3 -> x0, local copies, waits for them, and re-layouts: 4.28 us -> none  [the longest x1 4.24 us: local(): own = lax.slice_in_dim(weight, k * chunk_rows, (k + 1) * chunk_rows, axis=0)]
    unnamed x36 -> x28, local copies, waits for them, and re-layouts: 11.5 us -> 10.7 us
  transfers between devices with their start and end apart: 26 -> 23, of which waited for: 9 -> 7; matrix products, arithmetic and copies ran while one was open for 5% -> 1% of each run, Pallas kernels for 20% -> 45%
where the time goes in v2:
time: 234 us; the launch traced here: 233 us
  Pallas kernels  114 us (49%)
  waiting for transfers between devices  77.1 us (33%)
  starting transfers between devices  28.3 us (12%)
  local copies, waits for them, and re-layouts  11.7 us (5%)
    ppermute x13, waiting for transfers between devices, split(): return lambda a: lax.ppermute(a, ('fsdp', 'tok'), pairs)  75.9 us
    pallas_call x3, Pallas kernels, local(): pl.pallas_call(functools.partial(cut_kernel, after), out_shape=[shape(hal...  68.9 us
    pallas_call x4, Pallas kernels, local(): pl.pallas_call(functools.partial(chunk_kernel, steps, final), out_shape=[...  27.1 us
    ppermute x13, starting transfers between devices, split(): return lambda a: lax.ppermute(a, ('fsdp', 'tok'), pairs)  15.2 us
    unnamed x28, local copies, waits for them, and re-layouts  10.7 us
    pallas_call x1, Pallas kernels, local(): pl.pallas_call(functools.partial(expand_kernel, group), out_shape=[shape(...  6.89 us
    pallas_call x1, Pallas kernels, local(): pl.pallas_call(rank_kernel, out_shape=[shape(rows, value), shape(rank, mo...  5.8 us
    all_to_all x1, starting transfers between devices, local(): lax.all_to_all(terms, 'tok', split_axis=0, concat_axis=0)  4.93 us
  transfers between devices with their start and end apart: 23, of which 7 were waited for; matrix products, arithmetic and copies ran while one was open for 1% of the time, Pallas kernels for 45%

profile of v2, /device:TPU:0, one launch (start us, length us, event | category | flops | bytes accessed | tf_op | source)
XLA Modules:
  0.0 232.7 jit_solution(2477630598139892115)
XLA Ops:
  0.7 1.6 copy-done
  3.9 2.5 %select_sent.1 = (bf16[512,1152]{1,0:T(8,128)(2,1)S(1)}, bf16[2048,256]{1,0:T(8,128)(2,1)S(1)}) custom-call(s32[3]{0:T(128)S(1)} %pad_add_fusion.where_ref, s32[64]{0:T(128)S(1)} %copy-done.10, bf16[8192,256]{1,0:T(8,128)(2,1)} %own_ref.7, bf16[1024,1024]{1,0:T(8,128)(2,1)S(1)} %copy-done, bf16[128,1024]{1,0:T(8,128)(2,1)S(1)} %copy-done.5), custom_call_target="tpu_custom_call" | custom-call | tf_op jit(solution)/shard_map/select_sent/pallas_call | solution.py:231
  6.4 3.0 %collective-permute-start.7 = (bf16[512,1152]{1,0:T(8,128)(2,1)S(1)}, bf16[512,1152]{1,0:T(8,128)(2,1)S(1)}, u32[]{:S(2)}, u32[]{:S(2)}) collective-permute-start(bf16[512,1152]{1,0:T(8,128)(2,1)S(1)} %get-tuple-element.31), channel_id=1, source_target_pairs={{0,8},{1,17},{2,10},{3,19},{4,12},{5,21},{6,14},{7,23},{8,0},{9,25... | collective-permute-start | bytes 3538952 | tf_op jit(solution)/shard_map/ppermute | solution.py:226
  9.5 2.5 %select_kept.1 = bf16[512,1152]{1,0:T(8,128)(2,1)S(1)} custom-call(s32[3]{0:T(128)S(1)} %pad_add_fusion.where_ref, s32[64]{0:T(128)S(1)} %copy-done.10, bf16[1024,1024]{1,0:T(8,128)(2,1)S(1)} %copy-done, bf16[128,1024]{1,0:T(8,128)(2,1)S(1)} %copy-done.5), custom_call_target="tpu_custom_call" | custom-call | tf_op jit(solution)/shard_map/select_kept/pallas_call | solution.py:241
  12.0 22.9 %collective-permute-done.near_ref = bf16[2048,256]{1,0:T(8,128)(2,1)} collective-permute-done((bf16[2048,256]{1,0:T(8,128)(2,1)S(1)}, bf16[2048,256]{1,0:T(8,128)(2,1)}, u32[]{:S(2)}, u32[]{:S(2)}) %collective-permute-start) | collective-permute-done | bytes 1048608 | tf_op jit(solution)/shard_map/ppermute | solution.py:226
  35.0 1.9 cut_chunk.3
  36.9 2.1 collective-permute-start.1
  39.1 1.6 collective-permute-start.8
  40.7 17.4 %collective-permute-done.1.near_ref = bf16[2048,256]{1,0:T(8,128)(2,1)S(1)} collective-permute-done((bf16[2048,256]{1,0:T(8,128)(2,1)S(1)}, bf16[2048,256]{1,0:T(8,128)(2,1)S(1)}, u32[]{:S(2)}, u32[]{:S(2)}) %collective-permute-start.1) | collective-permute-done | bytes 1048608 | tf_op jit(solution)/shard_map/ppermute | solution.py:226
  58.0 33.5 %cut_chunk.4 = (bf16[1024,256]{1,0:T(8,128)(2,1)S(1)}, bf16[2048,256]{1,0:T(8,128)(2,1)}) custom-call(s32[3]{0:T(128)S(1)} %pad_add_fusion.where_ref, bf16[2048,256]{1,0:T(8,128)(2,1)S(1)} %collective-permute-done.1.near_ref, bf16[8192,256]{1,0:T(8,128)(2,1)} %own_ref.7), custom_call_target="tpu_custom_call" | custom-call | tf_op jit(solution)/shard_map/cut_chunk/pallas_call | solution.py:261
  91.5 1.6 collective-permute-start.2
  94.0 4.9 %all-to-all-start = ((bf16[8,32,1152]{2,1,0:T(8,128)(2,1)}), bf16[8,32,1152]{2,1,0:T(8,128)(2,1)S(1)}, u32[]{:S(2)}, u32[]{:S(2)}) async-start(bf16[8,32,1152]{2,1,0:T(8,128)(2,1)} %bitcast.5), calls=%async_computation | async-start | bytes 1179648 | tf_op jit(solution)/shard_map/all_to_all | solution.py:252
  99.4 10.4 %collective-permute-done.16.mine_ref = bf16[1024,256]{1,0:T(8,128)(2,1)} collective-permute-done((bf16[1024,256]{1,0:T(8,128)(2,1)S(1)}, bf16[1024,256]{1,0:T(8,128)(2,1)}, u32[]{:S(2)}, u32[]{:S(2)}) %collective-permute-start.16) | collective-permute-done | bytes 524320 | tf_op jit(solution)/shard_map/ppermute | solution.py:226
  109.9 2.3 collective-permute-start.17
  112.1 33.5 %cut_chunk.5 = (bf16[1024,256]{1,0:T(8,128)(2,1)S(1)}, bf16[2048,256]{1,0:T(8,128)(2,1)}) custom-call(s32[3]{0:T(128)S(1)} %pad_add_fusion.where_ref, bf16[2048,256]{1,0:T(8,128)(2,1)S(1)} %collective-permute-done.2.near_ref, bf16[8192,256]{1,0:T(8,128)(2,1)} %own_ref.7), custom_call_target="tpu_custom_call" | custom-call | tf_op jit(solution)/shard_map/cut_chunk/pallas_call | solution.py:261
  146.4 1.6 collective-permute-start.3
  148.8 1.1 copy-done.2
  149.9 1.0 copy-done.8
  150.9 5.8 %rank_space.1 = (bf16[256,1024]{1,0:T(8,128)(2,1)S(1)}, bf16[32,8192]{1,0:T(8,128)(2,1)S(1)}, bf16[256,32]{1,0:T(8,128)(2,1)S(1)}, f32[256,1024]{1,0:T(8,128)S(1)}, bf16[8,32,1152]{2,1,0:T(8,128)(2,1)S(1)}) custom-call(s32[3]{0:T(128)S(1)} %pad_add_fusion.where_ref, s32[64]{0:T(128)S(1)} %copy-done.9, bf16[256,8192]{1,0:T(8,128)(2,1)} %tokens_ref.9, ...), custom_call_target="tpu_custom_call" | custom-call | tf_op jit(solution)/shard_map/rank_space/pallas_call | solution.py:275
  158.5 4.9 %all-to-all-start.1 = ((bf16[8,32,1152]{2,1,0:T(8,128)(2,1)}), bf16[8,32,1152]{2,1,0:T(8,128)(2,1)}, u32[]{:S(2)}, u32[]{:S(2)}) async-start(bf16[8,32,1152]{2,1,0:T(8,128)(2,1)} %copy-done.7), calls=%async_computation.1 | async-start | bytes 1179648 | tf_op jit(solution)/shard_map/all_to_all | solution.py:291
  164.5 1.5 collective-permute-start.10
  166.0 7.5 %collective-permute-done.13.mine_ref = bf16[1024,256]{1,0:T(8,128)(2,1)} collective-permute-done((bf16[1024,256]{1,0:T(8,128)(2,1)}, bf16[1024,256]{1,0:T(8,128)(2,1)}, u32[]{:S(2)}, u32[]{:S(2)}) %collective-permute-start.13) | collective-permute-done | bytes 524320 | tf_op jit(solution)/shard_map/ppermute | solution.py:226
  174.0 5.1 %collective-permute-done.10.mine_ref = bf16[1024,256]{1,0:T(8,128)(2,1)} collective-permute-done((bf16[1024,256]{1,0:T(8,128)(2,1)}, bf16[1024,256]{1,0:T(8,128)(2,1)}, u32[]{:S(2)}, u32[]{:S(2)}) %collective-permute-start.10) | collective-permute-done | bytes 524320 | tf_op jit(solution)/shard_map/ppermute | solution.py:226
  179.1 1.2 all-to-all-done.1
  180.9 1.1 constant_dynamic-slice_fusion
  182.0 1.4 collective-permute-start.5
  184.2 12.6 %collective-permute-done.18.r1_ref = bf16[256,1152]{1,0:T(8,128)(2,1)S(1)} collective-permute-done((bf16[256,1152]{1,0:T(8,128)(2,1)}, bf16[256,1152]{1,0:T(8,128)(2,1)S(1)}, u32[]{:S(2)}, u32[]{:S(2)}) %collective-permute-start.18) | collective-permute-done | bytes 589856 | tf_op jit(solution)/shard_map/ppermute | solution.py:226
  196.8 7.0 %base_chunk.4 = (bf16[256,8192]{1,0:T(8,128)(2,1)}, f32[256,1024]{1,0:T(8,128)S(1)}) custom-call(s32[3]{0:T(128)S(1)} %pad_add_fusion.where_ref, s32[64]{0:T(128)S(1)} %copy-done.9, bf16[256,8192]{1,0:T(8,128)(2,1)} %tokens_ref.9, bf16[8192,256]{1,0:T(8,128)(2,1)} %own_ref.7, bf16[2048,256]{1,0:T(8,128)(2,1)} %collective-permute-done.near_ref, ...), custom_call_target="tpu_custom_call" | custom-call | flops 2147483648 | bytes 8388608 | tf_op jit(solution)/shard_map/base_chunk/pallas_call | solution.py:328
  204.8 6.8 %base_chunk.5 = (bf16[256,8192]{1,0:T(8,128)(2,1)}, f32[256,1024]{1,0:T(8,128)S(1)}) custom-call(s32[3]{0:T(128)S(1)} %pad_add_fusion.where_ref, s32[64]{0:T(128)S(1)} %copy-done.9, bf16[256,8192]{1,0:T(8,128)(2,1)} %tokens_ref.9, bf16[8192,256]{1,0:T(8,128)(2,1)} %own_ref.7, ...), custom_call_target="tpu_custom_call", output_to_operand_aliasing={{0}: (12, {})} | custom-call | flops 2147483648 | bytes 8388608 | tf_op jit(solution)/shard_map/base_chunk/pallas_call | solution.py:328
  212.6 6.8 %base_chunk.6 = (bf16[256,8192]{1,0:T(8,128)(2,1)}, f32[256,1024]{1,0:T(8,128)S(1)}) custom-call(s32[3]{0:T(128)S(1)} %pad_add_fusion.where_ref, s32[64]{0:T(128)S(1)} %copy-done.9, bf16[256,8192]{1,0:T(8,128)(2,1)} %tokens_ref.9, bf16[8192,256]{1,0:T(8,128)(2,1)} %own_ref.7, ...), custom_call_target="tpu_custom_call", output_to_operand_aliasing={{0}: (12, {})} | custom-call | flops 2147483648 | bytes 8388608 | tf_op jit(solution)/shard_map/base_chunk/pallas_call | solution.py:328
  219.4 6.9 %expand.1 = (f32[1024,1024]{1,0:T(8,128)}, f32[128,1024]{1,0:T(8,128)}) custom-call(s32[3]{0:T(128)S(1)} %pad_add_fusion.where_ref, s32[64]{0:T(128)S(1)} %copy-done.11, s32[64]{0:T(128)S(1)} %copy-done.9, bf16[256,1152]{1,0:T(8,128)(2,1)} %bitcast.4.r0_ref, bf16[256,1152]{1,0:T(8,128)(2,1)S(1)} %collective-permute-done.18.r1_ref, ...), custom_call_target="tpu_custom_call" | custom-call | tf_op jit(solution)/shard_map/expand/pallas_call | solution.py:352
  226.3 6.4 %base_chunk.7 = (bf16[256,8192]{1,0:T(8,128)(2,1)}, bf16[256,1024]{1,0:T(8,128)(2,1)}) custom-call(s32[3]{0:T(128)S(1)} %pad_add_fusion.where_ref, s32[64]{0:T(128)S(1)} %copy-done.9, bf16[256,8192]{1,0:T(8,128)(2,1)} %tokens_ref.9, bf16[8192,256]{1,0:T(8,128)(2,1)} %own_ref.7, ...), custom_call_target="tpu_custom_call", output_to_operand_aliasing={{0}: (12, {})} | custom-call | flops 2147483648 | bytes 8388608 | tf_op jit(solution)/shard_map/base_chunk/pallas_call | solution.py:328
  (57 shorter events, 11.6 us)
Async XLA Ops:
  0.7 1.6 copy-start
  6.4 32.6 %collective-permute-start.7 = (bf16[512,1152]{1,0:T(8,128)(2,1)S(1)}, bf16[512,1152]{1,0:T(8,128)(2,1)S(1)}, u32[]{:S(2)}, u32[]{:S(2)}) collective-permute-start(bf16[512,1152]{1,0:T(8,128)(2,1)S(1)} %get-tuple-element.31), channel_id=1, source_target_pairs={{0,8},{1,17},{2,10},{3,19},{4,12},{5,21},{6,14},{7,23},{8,0},{9,25... | collective-permute-start | bytes 3538952 | tf_op jit(solution)/shard_map/ppermute | solution.py:226
  9.5 25.5 %collective-permute-start = (bf16[2048,256]{1,0:T(8,128)(2,1)S(1)}, bf16[2048,256]{1,0:T(8,128)(2,1)}, u32[]{:S(2)}, u32[]{:S(2)}) collective-permute-start(bf16[2048,256]{1,0:T(8,128)(2,1)S(1)} %get-tuple-element.27), channel_id=1, source_target_pairs={{0,8},{1,17},{2,10},{3,19},{4,12},{5,21},{6,14},{7,23},{8,0},{9,25... | collective-permute-start | bytes 3145736 | tf_op jit(solution)/shard_map/ppermute | solution.py:226
  36.9 21.1 %collective-permute-start.1 = (bf16[2048,256]{1,0:T(8,128)(2,1)S(1)}, bf16[2048,256]{1,0:T(8,128)(2,1)S(1)}, u32[]{:S(2)}, u32[]{:S(2)}) collective-permute-start(bf16[2048,256]{1,0:T(8,128)(2,1)S(1)} %get-tuple-element.28), channel_id=1, source_target_pairs={{0,8},{1,17},{2,10},{3,19},{4,12},{5,21},{6,14},{7,23},{8,0},{9,25... | collective-permute-start | bytes 3145736 | tf_op jit(solution)/shard_map/ppermute | solution.py:226
  39.1 54.0 %collective-permute-start.8 = (bf16[256,1152]{1,0:T(8,128)(2,1)S(1)}, bf16[256,1152]{1,0:T(8,128)(2,1)S(1)}, u32[]{:S(2)}, u32[]{:S(2)}) collective-permute-start(bf16[256,1152]{1,0:T(8,128)(2,1)S(1)} %slice_add_fusion), channel_id=1, source_target_pairs={{0,16},{1,9},{2,18},{3,11},{4,20},{5,13},{6,22},{7,15},{8,24},{9,1... | collective-permute-start | bytes 1769480 | tf_op jit(solution)/shard_map/ppermute | solution.py:226
  91.5 2.5 %copy-start.12 = (bf16[1024,256]{1,0:T(8,128)(2,1)}, bf16[1024,256]{1,0:T(8,128)(2,1)S(1)}, u32[]{:S(2)}) copy-start(bf16[1024,256]{1,0:T(8,128)(2,1)S(1)} %get-tuple-element.36) | copy-start | bytes 1572868
  91.5 20.6 %collective-permute-start.2 = (bf16[2048,256]{1,0:T(8,128)(2,1)}, bf16[2048,256]{1,0:T(8,128)(2,1)S(1)}, u32[]{:S(2)}, u32[]{:S(2)}) collective-permute-start(bf16[2048,256]{1,0:T(8,128)(2,1)} %get-tuple-element.29), channel_id=1, source_target_pairs={{0,8},{1,17},{2,10},{3,19},{4,12},{5,21},{6,14},{7,23},{8,0},{9,25... | collective-permute-start | bytes 3145736 | tf_op jit(solution)/shard_map/ppermute | solution.py:226
  94.0 54.0 %all-to-all-start = ((bf16[8,32,1152]{2,1,0:T(8,128)(2,1)}), bf16[8,32,1152]{2,1,0:T(8,128)(2,1)S(1)}, u32[]{:S(2)}, u32[]{:S(2)}) async-start(bf16[8,32,1152]{2,1,0:T(8,128)(2,1)} %bitcast.5), calls=%async_computation | async-start | bytes 1179648 | tf_op jit(solution)/shard_map/all_to_all | solution.py:252
  98.9 49.9 %copy-start.9 = (s32[64]{0:T(128)S(1)}, s32[64]{0:T(128)}, u32[]{:S(2)}) copy-start(s32[64]{0:T(128)} %fill_ref.11) | copy-start | bytes 772
  98.9 11.0 %collective-permute-start.16 = (bf16[1024,256]{1,0:T(8,128)(2,1)S(1)}, bf16[1024,256]{1,0:T(8,128)(2,1)}, u32[]{:S(2)}, u32[]{:S(2)}) collective-permute-start(bf16[1024,256]{1,0:T(8,128)(2,1)S(1)} %get-tuple-element.37), channel_id=1, source_target_pairs={{0,16},{1,9},{2,18},{3,11},{4,20},{5,13},{6,22},{7,15},{8,24},{9,1... | collective-permute-start | bytes 1572872 | tf_op jit(solution)/shard_map/ppermute | solution.py:226
  109.9 54.6 %collective-permute-start.17 = (bf16[1024,256]{1,0:T(8,128)(2,1)}, bf16[1024,256]{1,0:T(8,128)(2,1)}, u32[]{:S(2)}, u32[]{:S(2)}) collective-permute-start(bf16[1024,256]{1,0:T(8,128)(2,1)} %collective-permute-done.16.mine_ref), channel_id=1, source_target_pairs={{0,1},{1,0},{2,3},{3,2},{4,5},{5,4},{6,7},{7,6},{8,9},{9,8},{10,11... | collective-permute-start | bytes 1572872 | tf_op jit(solution)/shard_map/ppermute | solution.py:218
  112.1 61.3 %collective-permute-start.15 = (bf16[2048,256]{1,0:T(8,128)(2,1)}, bf16[2048,256]{1,0:T(8,128)(2,1)}, u32[]{:S(2)}, u32[]{:S(2)}) collective-permute-start(bf16[2048,256]{1,0:T(8,128)(2,1)} %collective-permute-done.near_ref), channel_id=1, source_target_pairs={{0,1},{1,0},{2,3},{3,2},{4,5},{5,4},{6,7},{7,6},{8,9},{9,8},{10,11... | collective-permute-start | bytes 3145736 | tf_op jit(solution)/shard_map/ppermute | solution.py:218
  146.4 33.9 %collective-permute-start.3 = (bf16[2048,256]{1,0:T(8,128)(2,1)}, bf16[2048,256]{1,0:T(8,128)(2,1)}, u32[]{:S(2)}, u32[]{:S(2)}) collective-permute-start(bf16[2048,256]{1,0:T(8,128)(2,1)} %get-tuple-element.30), channel_id=1, source_target_pairs={{0,8},{1,17},{2,10},{3,19},{4,12},{5,21},{6,14},{7,23},{8,0},{9,25... | collective-permute-start | bytes 3145736 | tf_op jit(solution)/shard_map/ppermute | solution.py:226
  148.8 1.1 copy-start.2
  149.9 1.0 copy-start.8
  156.7 1.0 copy-start.6
  158.5 21.8 %all-to-all-start.1 = ((bf16[8,32,1152]{2,1,0:T(8,128)(2,1)}), bf16[8,32,1152]{2,1,0:T(8,128)(2,1)}, u32[]{:S(2)}, u32[]{:S(2)}) async-start(bf16[8,32,1152]{2,1,0:T(8,128)(2,1)} %copy-done.7), calls=%async_computation.1 | async-start | bytes 1179648 | tf_op jit(solution)/shard_map/all_to_all | solution.py:291
  163.5 18.5 %collective-permute-start.12 = (bf16[2048,256]{1,0:T(8,128)(2,1)S(1)}, bf16[2048,256]{1,0:T(8,128)(2,1)}, u32[]{:S(2)}, u32[]{:S(2)}) collective-permute-start(bf16[2048,256]{1,0:T(8,128)(2,1)S(1)} %collective-permute-done.1.near_ref), channel_id=1, source_target_pairs={{0,1},{1,0},{2,3},{3,2},{4,5},{5,4},{6,7},{7,6},{8,9},{9,8},{10,11... | collective-permute-start | bytes 3145736 | tf_op jit(solution)/shard_map/ppermute | solution.py:218
  164.0 9.5 %collective-permute-start.13 = (bf16[1024,256]{1,0:T(8,128)(2,1)}, bf16[1024,256]{1,0:T(8,128)(2,1)}, u32[]{:S(2)}, u32[]{:S(2)}) collective-permute-start(bf16[1024,256]{1,0:T(8,128)(2,1)} %copy-done.12), channel_id=1, source_target_pairs={{0,16},{1,9},{2,18},{3,11},{4,20},{5,13},{6,22},{7,15},{8,24},{9,1... | collective-permute-start | bytes 1572872 | tf_op jit(solution)/shard_map/ppermute | solution.py:226
  164.5 14.6 %collective-permute-start.10 = (bf16[1024,256]{1,0:T(8,128)(2,1)}, bf16[1024,256]{1,0:T(8,128)(2,1)}, u32[]{:S(2)}, u32[]{:S(2)}) collective-permute-start(bf16[1024,256]{1,0:T(8,128)(2,1)} %copy-done.13), channel_id=1, source_target_pairs={{0,16},{1,9},{2,18},{3,11},{4,20},{5,13},{6,22},{7,15},{8,24},{9,1... | collective-permute-start | bytes 1572872 | tf_op jit(solution)/shard_map/ppermute | solution.py:226
  173.5 9.9 %collective-permute-start.14 = (bf16[1024,256]{1,0:T(8,128)(2,1)}, bf16[1024,256]{1,0:T(8,128)(2,1)}, u32[]{:S(2)}, u32[]{:S(2)}) collective-permute-start(bf16[1024,256]{1,0:T(8,128)(2,1)} %collective-permute-done.13.mine_ref), channel_id=1, source_target_pairs={{0,1},{1,0},{2,3},{3,2},{4,5},{5,4},{6,7},{7,6},{8,9},{9,8},{10,11... | collective-permute-start | bytes 1572872 | tf_op jit(solution)/shard_map/ppermute | solution.py:218
  173.5 39.1 %collective-permute-start.9 = (bf16[2048,256]{1,0:T(8,128)(2,1)S(1)}, bf16[2048,256]{1,0:T(8,128)(2,1)}, u32[]{:S(2)}, u32[]{:S(2)}) collective-permute-start(bf16[2048,256]{1,0:T(8,128)(2,1)S(1)} %collective-permute-done.2.near_ref), channel_id=1, source_target_pairs={{0,1},{1,0},{2,3},{3,2},{4,5},{5,4},{6,7},{7,6},{8,9},{9,8},{10,11... | collective-permute-start | bytes 3145736 | tf_op jit(solution)/shard_map/ppermute | solution.py:218
  179.1 4.3 %collective-permute-start.11 = (bf16[1024,256]{1,0:T(8,128)(2,1)}, bf16[1024,256]{1,0:T(8,128)(2,1)}, u32[]{:S(2)}, u32[]{:S(2)}) collective-permute-start(bf16[1024,256]{1,0:T(8,128)(2,1)} %collective-permute-done.10.mine_ref), channel_id=1, source_target_pairs={{0,1},{1,0},{2,3},{3,2},{4,5},{5,4},{6,7},{7,6},{8,9},{9,8},{10,11... | collective-permute-start | bytes 1572872 | tf_op jit(solution)/shard_map/ppermute | solution.py:218
  180.3 16.4 %collective-permute-start.18 = (bf16[256,1152]{1,0:T(8,128)(2,1)}, bf16[256,1152]{1,0:T(8,128)(2,1)S(1)}, u32[]{:S(2)}, u32[]{:S(2)}) collective-permute-start(bf16[256,1152]{1,0:T(8,128)(2,1)} %bitcast.4.r0_ref), channel_id=1, source_target_pairs={{0,8},{1,17},{2,10},{3,19},{4,12},{5,21},{6,14},{7,23},{8,0},{9,25... | collective-permute-start | bytes 1769480 | tf_op jit(solution)/shard_map/ppermute | solution.py:226
  182.0 14.8 %collective-permute-start.5 = (bf16[1024,256]{1,0:T(8,128)(2,1)S(1)}, bf16[1024,256]{1,0:T(8,128)(2,1)S(1)}, u32[]{:S(2)}, u32[]{:S(2)}) collective-permute-start(bf16[1024,256]{1,0:T(8,128)(2,1)S(1)} %constant_dynamic-slice_fusion), channel_id=1, source_target_pairs={{0,16},{1,9},{2,18},{3,11},{4,20},{5,13},{6,22},{7,15},{8,24},{9,1... | collective-permute-start | bytes 1572872 | tf_op jit(solution)/shard_map/ppermute | solution.py:226
  183.4 42.9 %collective-permute-start.4 = (bf16[2048,256]{1,0:T(8,128)(2,1)}, bf16[2048,256]{1,0:T(8,128)(2,1)S(1)}, u32[]{:S(2)}, u32[]{:S(2)}) collective-permute-start(bf16[2048,256]{1,0:T(8,128)(2,1)} %collective-permute-done.3.near_ref), channel_id=1, source_target_pairs={{0,1},{1,0},{2,3},{3,2},{4,5},{5,4},{6,7},{7,6},{8,9},{9,8},{10,11... | collective-permute-start | bytes 3145736 | tf_op jit(solution)/shard_map/ppermute | solution.py:218
  183.4 36.0 %collective-permute-start.19 = (bf16[256,1152]{1,0:T(8,128)(2,1)}, bf16[256,1152]{1,0:T(8,128)(2,1)S(1)}, u32[]{:S(2)}, u32[]{:S(2)}) collective-permute-start(bf16[256,1152]{1,0:T(8,128)(2,1)} %bitcast.4.r0_ref), channel_id=1, source_target_pairs={{0,16},{1,9},{2,18},{3,11},{4,20},{5,13},{6,22},{7,15},{8,24},{9,1... | collective-permute-start | bytes 1769480 | tf_op jit(solution)/shard_map/ppermute | solution.py:226
  196.8 22.6 %collective-permute-start.20 = (bf16[256,1152]{1,0:T(8,128)(2,1)S(1)}, bf16[256,1152]{1,0:T(8,128)(2,1)S(1)}, u32[]{:S(2)}, u32[]{:S(2)}) collective-permute-start(bf16[256,1152]{1,0:T(8,128)(2,1)S(1)} %collective-permute-done.18.r1_ref), channel_id=1, source_target_pairs={{0,16},{1,9},{2,18},{3,11},{4,20},{5,13},{6,22},{7,15},{8,24},{9,1... | collective-permute-start | bytes 1769480 | tf_op jit(solution)/shard_map/ppermute | solution.py:226
  196.8 29.5 %collective-permute-start.6 = (bf16[1024,256]{1,0:T(8,128)(2,1)S(1)}, bf16[1024,256]{1,0:T(8,128)(2,1)S(1)}, u32[]{:S(2)}, u32[]{:S(2)}) collective-permute-start(bf16[1024,256]{1,0:T(8,128)(2,1)S(1)} %collective-permute-done.5.mine_ref), channel_id=1, source_target_pairs={{0,1},{1,0},{2,3},{3,2},{4,5},{5,4},{6,7},{7,6},{8,9},{9,8},{10,11... | collective-permute-start | bytes 1572872 | tf_op jit(solution)/shard_map/ppermute | solution.py:218
  203.8 1.0 copy-start.4
  211.6 1.0 copy-start.3
  212.5 6.9 %copy-start.11 = (s32[64]{0:T(128)S(1)}, s32[64]{0:T(128)}, u32[]{:S(2)}) copy-start(s32[64]{0:T(128)} %tenant_ref.5) | copy-start | bytes 772
  (5 other events, 4.0 us)

commit v3 on v2

--- a/solution.py
+++ b/solution.py
@@ -232,7 +232,7 @@
         functools.partial(send_select_kernel, group, parts[0][1]),
         out_shape=[shape(2 * group_rank, both), shape(parts[0][1], wide)],
         in_specs=[SMEM, SMEM, ANY, VMEM, VMEM],
-        out_specs=[VMEM, ANY],
+        out_specs=[VMEM, VMEM],
         scratch_shapes=[pltpu.VMEM((2 * group_rank, columns), BF16), pltpu.SemaphoreType.DMA],
         compiler_params=params(),
         name="select_sent",
@@ -262,7 +262,7 @@
                 functools.partial(cut_kernel, after),
                 out_shape=[shape(half, wide), shape(after_size, wide)],
                 in_specs=[SMEM, ANY, ANY],
-                out_specs=[ANY, ANY],
+                out_specs=[VMEM, VMEM],
                 scratch_shapes=[pltpu.SemaphoreType.DMA((2,))],
                 compiler_params=params(),
                 name="cut_chunk",

time: 234 us -> 172 us (0.74)
  Pallas kernels: 114 us -> 52.3 us
    pallas_call x3, Pallas kernels: 68.9 us -> 7.53 us  [local(): pl.pallas_call(functools.partial(cut_kernel, after), out_shape=[shape(hal...]
  transfers between devices with their start and end apart: 23 -> 23, of which waited for: 7 -> 7; matrix products, arithmetic and copies ran while one was open for 1% -> 1% of each run, Pallas kernels for 45% -> 25%
where the time goes in v3:
time: 172 us; the launch traced here: 171 us
  waiting for transfers between devices  77.1 us (45%)
  Pallas kernels  52.3 us (30%)
  starting transfers between devices  28.3 us (16%)
  local copies, waits for them, and re-layouts  11.7 us (7%)
    ppermute x13, waiting for transfers between devices, split(): return lambda a: lax.ppermute(a, ('fsdp', 'tok'), pairs)  75.9 us
    pallas_call x4, Pallas kernels, local(): pl.pallas_call(functools.partial(chunk_kernel, steps, final), out_shape=[...  27.1 us
    ppermute x13, starting transfers between devices, split(): return lambda a: lax.ppermute(a, ('fsdp', 'tok'), pairs)  15.2 us
    unnamed x28, local copies, waits for them, and re-layouts  10.7 us
    pallas_call x3, Pallas kernels, local(): pl.pallas_call(functools.partial(cut_kernel, after), out_shape=[shape(hal...  7.53 us
    pallas_call x1, Pallas kernels, local(): pl.pallas_call(functools.partial(expand_kernel, group), out_shape=[shape(...  6.89 us
    pallas_call x1, Pallas kernels, local(): pl.pallas_call(rank_kernel, out_shape=[shape(rows, value), shape(rank, mo...  5.8 us
    all_to_all x1, starting transfers between devices, local(): lax.all_to_all(terms, 'tok', split_axis=0, concat_axis=0)  4.93 us
  transfers between devices with their start and end apart: 23, of which 7 were waited for; matrix products, arithmetic and copies ran while one was open for 1% of the time, Pallas kernels for 25%

profile of v3, /device:TPU:0, one launch (start us, length us, event | category | flops | bytes accessed | tf_op | source)
XLA Modules:
  0.0 171.4 jit_solution(13714894951837506961)
XLA Ops:
  0.7 1.6 copy-done
  3.9 2.5 %select_sent.1 = (bf16[512,1152]{1,0:T(8,128)(2,1)S(1)}, bf16[2048,256]{1,0:T(8,128)(2,1)S(1)}) custom-call(s32[3]{0:T(128)S(1)} %pad_add_fusion.where_ref, s32[64]{0:T(128)S(1)} %copy-done.10, bf16[8192,256]{1,0:T(8,128)(2,1)} %own_ref.7, bf16[1024,1024]{1,0:T(8,128)(2,1)S(1)} %copy-done, bf16[128,1024]{1,0:T(8,128)(2,1)S(1)} %copy-done.5), custom_call_target="tpu_custom_call" | custom-call | tf_op jit(solution)/shard_map/select_sent/pallas_call | solution.py:231
  6.4 3.0 %collective-permute-start.7 = (bf16[512,1152]{1,0:T(8,128)(2,1)S(1)}, bf16[512,1152]{1,0:T(8,128)(2,1)S(1)}, u32[]{:S(2)}, u32[]{:S(2)}) collective-permute-start(bf16[512,1152]{1,0:T(8,128)(2,1)S(1)} %get-tuple-element.31), channel_id=1, source_target_pairs={{0,8},{1,17},{2,10},{3,19},{4,12},{5,21},{6,14},{7,23},{8,0},{9,25... | collective-permute-start | bytes 3538952 | tf_op jit(solution)/shard_map/ppermute | solution.py:226
  9.5 2.5 %select_kept.1 = bf16[512,1152]{1,0:T(8,128)(2,1)S(1)} custom-call(s32[3]{0:T(128)S(1)} %pad_add_fusion.where_ref, s32[64]{0:T(128)S(1)} %copy-done.10, bf16[1024,1024]{1,0:T(8,128)(2,1)S(1)} %copy-done, bf16[128,1024]{1,0:T(8,128)(2,1)S(1)} %copy-done.5), custom_call_target="tpu_custom_call" | custom-call | tf_op jit(solution)/shard_map/select_kept/pallas_call | solution.py:241
  12.0 22.9 %collective-permute-done.near_ref = bf16[2048,256]{1,0:T(8,128)(2,1)} collective-permute-done((bf16[2048,256]{1,0:T(8,128)(2,1)S(1)}, bf16[2048,256]{1,0:T(8,128)(2,1)}, u32[]{:S(2)}, u32[]{:S(2)}) %collective-permute-start) | collective-permute-done | bytes 1048608 | tf_op jit(solution)/shard_map/ppermute | solution.py:226
  35.0 1.9 %cut_chunk.3 = (bf16[1024,256]{1,0:T(8,128)(2,1)S(1)}, bf16[2048,256]{1,0:T(8,128)(2,1)S(1)}) custom-call(s32[3]{0:T(128)S(1)} %pad_add_fusion.where_ref, bf16[2048,256]{1,0:T(8,128)(2,1)} %collective-permute-done.near_ref, bf16[8192,256]{1,0:T(8,128)(2,1)} %own_ref.7), custom_call_target="tpu_custom_call" | custom-call | tf_op jit(solution)/shard_map/cut_chunk/pallas_call | solution.py:261
  36.9 2.1 %collective-permute-start.1 = (bf16[2048,256]{1,0:T(8,128)(2,1)S(1)}, bf16[2048,256]{1,0:T(8,128)(2,1)S(1)}, u32[]{:S(2)}, u32[]{:S(2)}) collective-permute-start(bf16[2048,256]{1,0:T(8,128)(2,1)S(1)} %get-tuple-element.28), channel_id=1, source_target_pairs={{0,8},{1,17},{2,10},{3,19},{4,12},{5,21},{6,14},{7,23},{8,0},{9,25... | collective-permute-start | bytes 3145736 | tf_op jit(solution)/shard_map/ppermute | solution.py:226
  39.1 1.6 collective-permute-start.8
  40.7 17.4 %collective-permute-done.1.near_ref = bf16[2048,256]{1,0:T(8,128)(2,1)S(1)} collective-permute-done((bf16[2048,256]{1,0:T(8,128)(2,1)S(1)}, bf16[2048,256]{1,0:T(8,128)(2,1)S(1)}, u32[]{:S(2)}, u32[]{:S(2)}) %collective-permute-start.1) | collective-permute-done | bytes 1048608 | tf_op jit(solution)/shard_map/ppermute | solution.py:226
  58.0 2.8 %cut_chunk.4 = (bf16[1024,256]{1,0:T(8,128)(2,1)S(1)}, bf16[2048,256]{1,0:T(8,128)(2,1)}) custom-call(s32[3]{0:T(128)S(1)} %pad_add_fusion.where_ref, bf16[2048,256]{1,0:T(8,128)(2,1)S(1)} %collective-permute-done.1.near_ref, bf16[8192,256]{1,0:T(8,128)(2,1)} %own_ref.7), custom_call_target="tpu_custom_call" | custom-call | tf_op jit(solution)/shard_map/cut_chunk/pallas_call | solution.py:261
  60.9 1.6 collective-permute-start.2
  63.3 4.9 %all-to-all-start = ((bf16[8,32,1152]{2,1,0:T(8,128)(2,1)}), bf16[8,32,1152]{2,1,0:T(8,128)(2,1)S(1)}, u32[]{:S(2)}, u32[]{:S(2)}) async-start(bf16[8,32,1152]{2,1,0:T(8,128)(2,1)} %bitcast.5), calls=%async_computation | async-start | bytes 1179648 | tf_op jit(solution)/shard_map/all_to_all | solution.py:252
  68.8 10.4 %collective-permute-done.16.mine_ref = bf16[1024,256]{1,0:T(8,128)(2,1)} collective-permute-done((bf16[1024,256]{1,0:T(8,128)(2,1)S(1)}, bf16[1024,256]{1,0:T(8,128)(2,1)}, u32[]{:S(2)}, u32[]{:S(2)}) %collective-permute-start.16) | collective-permute-done | bytes 524320 | tf_op jit(solution)/shard_map/ppermute | solution.py:226
  79.2 2.3 %collective-permute-start.17 = (bf16[1024,256]{1,0:T(8,128)(2,1)}, bf16[1024,256]{1,0:T(8,128)(2,1)}, u32[]{:S(2)}, u32[]{:S(2)}) collective-permute-start(bf16[1024,256]{1,0:T(8,128)(2,1)} %collective-permute-done.16.mine_ref), channel_id=1, source_target_pairs={{0,1},{1,0},{2,3},{3,2},{4,5},{5,4},{6,7},{7,6},{8,9},{9,8},{10,11... | collective-permute-start | bytes 1572872 | tf_op jit(solution)/shard_map/ppermute | solution.py:218
  81.5 2.8 %cut_chunk.5 = (bf16[1024,256]{1,0:T(8,128)(2,1)S(1)}, bf16[2048,256]{1,0:T(8,128)(2,1)}) custom-call(s32[3]{0:T(128)S(1)} %pad_add_fusion.where_ref, bf16[2048,256]{1,0:T(8,128)(2,1)S(1)} %collective-permute-done.2.near_ref, bf16[8192,256]{1,0:T(8,128)(2,1)} %own_ref.7), custom_call_target="tpu_custom_call" | custom-call | tf_op jit(solution)/shard_map/cut_chunk/pallas_call | solution.py:261
  85.1 1.6 collective-permute-start.3
  87.5 1.1 copy-done.2
  88.5 1.0 copy-done.8
  89.6 5.8 %rank_space.1 = (bf16[256,1024]{1,0:T(8,128)(2,1)S(1)}, bf16[32,8192]{1,0:T(8,128)(2,1)S(1)}, bf16[256,32]{1,0:T(8,128)(2,1)S(1)}, f32[256,1024]{1,0:T(8,128)S(1)}, bf16[8,32,1152]{2,1,0:T(8,128)(2,1)S(1)}) custom-call(s32[3]{0:T(128)S(1)} %pad_add_fusion.where_ref, s32[64]{0:T(128)S(1)} %copy-done.9, bf16[256,8192]{1,0:T(8,128)(2,1)} %tokens_ref.9, ...), custom_call_target="tpu_custom_call" | custom-call | tf_op jit(solution)/shard_map/rank_space/pallas_call | solution.py:275
  97.2 4.9 %all-to-all-start.1 = ((bf16[8,32,1152]{2,1,0:T(8,128)(2,1)}), bf16[8,32,1152]{2,1,0:T(8,128)(2,1)}, u32[]{:S(2)}, u32[]{:S(2)}) async-start(bf16[8,32,1152]{2,1,0:T(8,128)(2,1)} %copy-done.7), calls=%async_computation.1 | async-start | bytes 1179648 | tf_op jit(solution)/shard_map/all_to_all | solution.py:291
  103.2 1.5 collective-permute-start.10
  104.7 7.5 %collective-permute-done.13.mine_ref = bf16[1024,256]{1,0:T(8,128)(2,1)} collective-permute-done((bf16[1024,256]{1,0:T(8,128)(2,1)}, bf16[1024,256]{1,0:T(8,128)(2,1)}, u32[]{:S(2)}, u32[]{:S(2)}) %collective-permute-start.13) | collective-permute-done | bytes 524320 | tf_op jit(solution)/shard_map/ppermute | solution.py:226
  112.7 5.1 %collective-permute-done.10.mine_ref = bf16[1024,256]{1,0:T(8,128)(2,1)} collective-permute-done((bf16[1024,256]{1,0:T(8,128)(2,1)}, bf16[1024,256]{1,0:T(8,128)(2,1)}, u32[]{:S(2)}, u32[]{:S(2)}) %collective-permute-start.10) | collective-permute-done | bytes 524320 | tf_op jit(solution)/shard_map/ppermute | solution.py:226
  117.8 1.2 all-to-all-done.1
  119.6 1.1 constant_dynamic-slice_fusion
  120.7 1.3 collective-permute-start.5
  122.8 12.6 %collective-permute-done.18.r1_ref = bf16[256,1152]{1,0:T(8,128)(2,1)S(1)} collective-permute-done((bf16[256,1152]{1,0:T(8,128)(2,1)}, bf16[256,1152]{1,0:T(8,128)(2,1)S(1)}, u32[]{:S(2)}, u32[]{:S(2)}) %collective-permute-start.18) | collective-permute-done | bytes 589856 | tf_op jit(solution)/shard_map/ppermute | solution.py:226
  135.4 7.0 %base_chunk.4 = (bf16[256,8192]{1,0:T(8,128)(2,1)}, f32[256,1024]{1,0:T(8,128)S(1)}) custom-call(s32[3]{0:T(128)S(1)} %pad_add_fusion.where_ref, s32[64]{0:T(128)S(1)} %copy-done.9, bf16[256,8192]{1,0:T(8,128)(2,1)} %tokens_ref.9, bf16[8192,256]{1,0:T(8,128)(2,1)} %own_ref.7, bf16[2048,256]{1,0:T(8,128)(2,1)} %collective-permute-done.near_ref, ...), custom_call_target="tpu_custom_call" | custom-call | flops 2147483648 | bytes 8388608 | tf_op jit(solution)/shard_map/base_chunk/pallas_call | solution.py:328
  143.4 6.8 %base_chunk.5 = (bf16[256,8192]{1,0:T(8,128)(2,1)}, f32[256,1024]{1,0:T(8,128)S(1)}) custom-call(s32[3]{0:T(128)S(1)} %pad_add_fusion.where_ref, s32[64]{0:T(128)S(1)} %copy-done.9, bf16[256,8192]{1,0:T(8,128)(2,1)} %tokens_ref.9, bf16[8192,256]{1,0:T(8,128)(2,1)} %own_ref.7, ...), custom_call_target="tpu_custom_call", output_to_operand_aliasing={{0}: (12, {})} | custom-call | flops 2147483648 | bytes 8388608 | tf_op jit(solution)/shard_map/base_chunk/pallas_call | solution.py:328
  151.2 6.8 %base_chunk.6 = (bf16[256,8192]{1,0:T(8,128)(2,1)}, f32[256,1024]{1,0:T(8,128)S(1)}) custom-call(s32[3]{0:T(128)S(1)} %pad_add_fusion.where_ref, s32[64]{0:T(128)S(1)} %copy-done.9, bf16[256,8192]{1,0:T(8,128)(2,1)} %tokens_ref.9, bf16[8192,256]{1,0:T(8,128)(2,1)} %own_ref.7, ...), custom_call_target="tpu_custom_call", output_to_operand_aliasing={{0}: (12, {})} | custom-call | flops 2147483648 | bytes 8388608 | tf_op jit(solution)/shard_map/base_chunk/pallas_call | solution.py:328
  158.1 6.9 %expand.1 = (f32[1024,1024]{1,0:T(8,128)}, f32[128,1024]{1,0:T(8,128)}) custom-call(s32[3]{0:T(128)S(1)} %pad_add_fusion.where_ref, s32[64]{0:T(128)S(1)} %copy-done.11, s32[64]{0:T(128)S(1)} %copy-done.9, bf16[256,1152]{1,0:T(8,128)(2,1)} %bitcast.4.r0_ref, bf16[256,1152]{1,0:T(8,128)(2,1)S(1)} %collective-permute-done.18.r1_ref, ...), custom_call_target="tpu_custom_call" | custom-call | tf_op jit(solution)/shard_map/expand/pallas_call | solution.py:352
  165.0 6.4 %base_chunk.7 = (bf16[256,8192]{1,0:T(8,128)(2,1)}, bf16[256,1024]{1,0:T(8,128)(2,1)}) custom-call(s32[3]{0:T(128)S(1)} %pad_add_fusion.where_ref, s32[64]{0:T(128)S(1)} %copy-done.9, bf16[256,8192]{1,0:T(8,128)(2,1)} %tokens_ref.9, bf16[8192,256]{1,0:T(8,128)(2,1)} %own_ref.7, ...), custom_call_target="tpu_custom_call", output_to_operand_aliasing={{0}: (12, {})} | custom-call | flops 2147483648 | bytes 8388608 | tf_op jit(solution)/shard_map/base_chunk/pallas_call | solution.py:328
  (57 shorter events, 11.6 us)
Async XLA Ops:
  0.7 1.6 copy-start
  6.4 32.6 %collective-permute-start.7 = (bf16[512,1152]{1,0:T(8,128)(2,1)S(1)}, bf16[512,1152]{1,0:T(8,128)(2,1)S(1)}, u32[]{:S(2)}, u32[]{:S(2)}) collective-permute-start(bf16[512,1152]{1,0:T(8,128)(2,1)S(1)} %get-tuple-element.31), channel_id=1, source_target_pairs={{0,8},{1,17},{2,10},{3,19},{4,12},{5,21},{6,14},{7,23},{8,0},{9,25... | collective-permute-start | bytes 3538952 | tf_op jit(solution)/shard_map/ppermute | solution.py:226
  9.5 25.5 %collective-permute-start = (bf16[2048,256]{1,0:T(8,128)(2,1)S(1)}, bf16[2048,256]{1,0:T(8,128)(2,1)}, u32[]{:S(2)}, u32[]{:S(2)}) collective-permute-start(bf16[2048,256]{1,0:T(8,128)(2,1)S(1)} %get-tuple-element.27), channel_id=1, source_target_pairs={{0,8},{1,17},{2,10},{3,19},{4,12},{5,21},{6,14},{7,23},{8,0},{9,25... | collective-permute-start | bytes 3145736 | tf_op jit(solution)/shard_map/ppermute | solution.py:226
  36.9 21.1 %collective-permute-start.1 = (bf16[2048,256]{1,0:T(8,128)(2,1)S(1)}, bf16[2048,256]{1,0:T(8,128)(2,1)S(1)}, u32[]{:S(2)}, u32[]{:S(2)}) collective-permute-start(bf16[2048,256]{1,0:T(8,128)(2,1)S(1)} %get-tuple-element.28), channel_id=1, source_target_pairs={{0,8},{1,17},{2,10},{3,19},{4,12},{5,21},{6,14},{7,23},{8,0},{9,25... | collective-permute-start | bytes 3145736 | tf_op jit(solution)/shard_map/ppermute | solution.py:226
  39.1 23.3 %collective-permute-start.8 = (bf16[256,1152]{1,0:T(8,128)(2,1)S(1)}, bf16[256,1152]{1,0:T(8,128)(2,1)S(1)}, u32[]{:S(2)}, u32[]{:S(2)}) collective-permute-start(bf16[256,1152]{1,0:T(8,128)(2,1)S(1)} %slice_add_fusion), channel_id=1, source_target_pairs={{0,16},{1,9},{2,18},{3,11},{4,20},{5,13},{6,22},{7,15},{8,24},{9,1... | collective-permute-start | bytes 1769480 | tf_op jit(solution)/shard_map/ppermute | solution.py:226
  60.8 2.5 %copy-start.12 = (bf16[1024,256]{1,0:T(8,128)(2,1)}, bf16[1024,256]{1,0:T(8,128)(2,1)S(1)}, u32[]{:S(2)}) copy-start(bf16[1024,256]{1,0:T(8,128)(2,1)S(1)} %get-tuple-element.36) | copy-start | bytes 1572868
  60.9 20.6 %collective-permute-start.2 = (bf16[2048,256]{1,0:T(8,128)(2,1)}, bf16[2048,256]{1,0:T(8,128)(2,1)S(1)}, u32[]{:S(2)}, u32[]{:S(2)}) collective-permute-start(bf16[2048,256]{1,0:T(8,128)(2,1)} %get-tuple-element.29), channel_id=1, source_target_pairs={{0,8},{1,17},{2,10},{3,19},{4,12},{5,21},{6,14},{7,23},{8,0},{9,25... | collective-permute-start | bytes 3145736 | tf_op jit(solution)/shard_map/ppermute | solution.py:226
  63.3 23.3 %all-to-all-start = ((bf16[8,32,1152]{2,1,0:T(8,128)(2,1)}), bf16[8,32,1152]{2,1,0:T(8,128)(2,1)S(1)}, u32[]{:S(2)}, u32[]{:S(2)}) async-start(bf16[8,32,1152]{2,1,0:T(8,128)(2,1)} %bitcast.5), calls=%async_computation | async-start | bytes 1179648 | tf_op jit(solution)/shard_map/all_to_all | solution.py:252
  68.2 19.3 %copy-start.9 = (s32[64]{0:T(128)S(1)}, s32[64]{0:T(128)}, u32[]{:S(2)}) copy-start(s32[64]{0:T(128)} %fill_ref.11) | copy-start | bytes 772
  68.2 11.0 %collective-permute-start.16 = (bf16[1024,256]{1,0:T(8,128)(2,1)S(1)}, bf16[1024,256]{1,0:T(8,128)(2,1)}, u32[]{:S(2)}, u32[]{:S(2)}) collective-permute-start(bf16[1024,256]{1,0:T(8,128)(2,1)S(1)} %get-tuple-element.37), channel_id=1, source_target_pairs={{0,16},{1,9},{2,18},{3,11},{4,20},{5,13},{6,22},{7,15},{8,24},{9,1... | collective-permute-start | bytes 1572872 | tf_op jit(solution)/shard_map/ppermute | solution.py:226
  79.2 24.0 %collective-permute-start.17 = (bf16[1024,256]{1,0:T(8,128)(2,1)}, bf16[1024,256]{1,0:T(8,128)(2,1)}, u32[]{:S(2)}, u32[]{:S(2)}) collective-permute-start(bf16[1024,256]{1,0:T(8,128)(2,1)} %collective-permute-done.16.mine_ref), channel_id=1, source_target_pairs={{0,1},{1,0},{2,3},{3,2},{4,5},{5,4},{6,7},{7,6},{8,9},{9,8},{10,11... | collective-permute-start | bytes 1572872 | tf_op jit(solution)/shard_map/ppermute | solution.py:218
  81.5 30.7 %collective-permute-start.15 = (bf16[2048,256]{1,0:T(8,128)(2,1)}, bf16[2048,256]{1,0:T(8,128)(2,1)}, u32[]{:S(2)}, u32[]{:S(2)}) collective-permute-start(bf16[2048,256]{1,0:T(8,128)(2,1)} %collective-permute-done.near_ref), channel_id=1, source_target_pairs={{0,1},{1,0},{2,3},{3,2},{4,5},{5,4},{6,7},{7,6},{8,9},{9,8},{10,11... | collective-permute-start | bytes 3145736 | tf_op jit(solution)/shard_map/ppermute | solution.py:218
  85.1 33.9 %collective-permute-start.3 = (bf16[2048,256]{1,0:T(8,128)(2,1)}, bf16[2048,256]{1,0:T(8,128)(2,1)}, u32[]{:S(2)}, u32[]{:S(2)}) collective-permute-start(bf16[2048,256]{1,0:T(8,128)(2,1)} %get-tuple-element.30), channel_id=1, source_target_pairs={{0,8},{1,17},{2,10},{3,19},{4,12},{5,21},{6,14},{7,23},{8,0},{9,25... | collective-permute-start | bytes 3145736 | tf_op jit(solution)/shard_map/ppermute | solution.py:226
  87.5 1.1 copy-start.2
  88.5 1.0 copy-start.8
  95.4 1.0 copy-start.6
  97.2 21.8 %all-to-all-start.1 = ((bf16[8,32,1152]{2,1,0:T(8,128)(2,1)}), bf16[8,32,1152]{2,1,0:T(8,128)(2,1)}, u32[]{:S(2)}, u32[]{:S(2)}) async-start(bf16[8,32,1152]{2,1,0:T(8,128)(2,1)} %copy-done.7), calls=%async_computation.1 | async-start | bytes 1179648 | tf_op jit(solution)/shard_map/all_to_all | solution.py:291
  102.1 18.5 %collective-permute-start.12 = (bf16[2048,256]{1,0:T(8,128)(2,1)S(1)}, bf16[2048,256]{1,0:T(8,128)(2,1)}, u32[]{:S(2)}, u32[]{:S(2)}) collective-permute-start(bf16[2048,256]{1,0:T(8,128)(2,1)S(1)} %collective-permute-done.1.near_ref), channel_id=1, source_target_pairs={{0,1},{1,0},{2,3},{3,2},{4,5},{5,4},{6,7},{7,6},{8,9},{9,8},{10,11... | collective-permute-start | bytes 3145736 | tf_op jit(solution)/shard_map/ppermute | solution.py:218
  102.6 9.5 %collective-permute-start.13 = (bf16[1024,256]{1,0:T(8,128)(2,1)}, bf16[1024,256]{1,0:T(8,128)(2,1)}, u32[]{:S(2)}, u32[]{:S(2)}) collective-permute-start(bf16[1024,256]{1,0:T(8,128)(2,1)} %copy-done.12), channel_id=1, source_target_pairs={{0,16},{1,9},{2,18},{3,11},{4,20},{5,13},{6,22},{7,15},{8,24},{9,1... | collective-permute-start | bytes 1572872 | tf_op jit(solution)/shard_map/ppermute | solution.py:226
  103.2 14.6 %collective-permute-start.10 = (bf16[1024,256]{1,0:T(8,128)(2,1)}, bf16[1024,256]{1,0:T(8,128)(2,1)}, u32[]{:S(2)}, u32[]{:S(2)}) collective-permute-start(bf16[1024,256]{1,0:T(8,128)(2,1)} %copy-done.13), channel_id=1, source_target_pairs={{0,16},{1,9},{2,18},{3,11},{4,20},{5,13},{6,22},{7,15},{8,24},{9,1... | collective-permute-start | bytes 1572872 | tf_op jit(solution)/shard_map/ppermute | solution.py:226
  112.1 9.9 %collective-permute-start.14 = (bf16[1024,256]{1,0:T(8,128)(2,1)}, bf16[1024,256]{1,0:T(8,128)(2,1)}, u32[]{:S(2)}, u32[]{:S(2)}) collective-permute-start(bf16[1024,256]{1,0:T(8,128)(2,1)} %collective-permute-done.13.mine_ref), channel_id=1, source_target_pairs={{0,1},{1,0},{2,3},{3,2},{4,5},{5,4},{6,7},{7,6},{8,9},{9,8},{10,11... | collective-permute-start | bytes 1572872 | tf_op jit(solution)/shard_map/ppermute | solution.py:218
  112.1 39.1 %collective-permute-start.9 = (bf16[2048,256]{1,0:T(8,128)(2,1)S(1)}, bf16[2048,256]{1,0:T(8,128)(2,1)}, u32[]{:S(2)}, u32[]{:S(2)}) collective-permute-start(bf16[2048,256]{1,0:T(8,128)(2,1)S(1)} %collective-permute-done.2.near_ref), channel_id=1, source_target_pairs={{0,1},{1,0},{2,3},{3,2},{4,5},{5,4},{6,7},{7,6},{8,9},{9,8},{10,11... | collective-permute-start | bytes 3145736 | tf_op jit(solution)/shard_map/ppermute | solution.py:218
  117.8 4.3 %collective-permute-start.11 = (bf16[1024,256]{1,0:T(8,128)(2,1)}, bf16[1024,256]{1,0:T(8,128)(2,1)}, u32[]{:S(2)}, u32[]{:S(2)}) collective-permute-start(bf16[1024,256]{1,0:T(8,128)(2,1)} %collective-permute-done.10.mine_ref), channel_id=1, source_target_pairs={{0,1},{1,0},{2,3},{3,2},{4,5},{5,4},{6,7},{7,6},{8,9},{9,8},{10,11... | collective-permute-start | bytes 1572872 | tf_op jit(solution)/shard_map/ppermute | solution.py:218
  119.0 16.4 %collective-permute-start.18 = (bf16[256,1152]{1,0:T(8,128)(2,1)}, bf16[256,1152]{1,0:T(8,128)(2,1)S(1)}, u32[]{:S(2)}, u32[]{:S(2)}) collective-permute-start(bf16[256,1152]{1,0:T(8,128)(2,1)} %bitcast.4.r0_ref), channel_id=1, source_target_pairs={{0,8},{1,17},{2,10},{3,19},{4,12},{5,21},{6,14},{7,23},{8,0},{9,25... | collective-permute-start | bytes 1769480 | tf_op jit(solution)/shard_map/ppermute | solution.py:226
  120.7 14.8 %collective-permute-start.5 = (bf16[1024,256]{1,0:T(8,128)(2,1)S(1)}, bf16[1024,256]{1,0:T(8,128)(2,1)S(1)}, u32[]{:S(2)}, u32[]{:S(2)}) collective-permute-start(bf16[1024,256]{1,0:T(8,128)(2,1)S(1)} %constant_dynamic-slice_fusion), channel_id=1, source_target_pairs={{0,16},{1,9},{2,18},{3,11},{4,20},{5,13},{6,22},{7,15},{8,24},{9,1... | collective-permute-start | bytes 1572872 | tf_op jit(solution)/shard_map/ppermute | solution.py:226
  122.0 43.0 %collective-permute-start.4 = (bf16[2048,256]{1,0:T(8,128)(2,1)}, bf16[2048,256]{1,0:T(8,128)(2,1)S(1)}, u32[]{:S(2)}, u32[]{:S(2)}) collective-permute-start(bf16[2048,256]{1,0:T(8,128)(2,1)} %collective-permute-done.3.near_ref), channel_id=1, source_target_pairs={{0,1},{1,0},{2,3},{3,2},{4,5},{5,4},{6,7},{7,6},{8,9},{9,8},{10,11... | collective-permute-start | bytes 3145736 | tf_op jit(solution)/shard_map/ppermute | solution.py:218
  122.0 36.0 %collective-permute-start.19 = (bf16[256,1152]{1,0:T(8,128)(2,1)}, bf16[256,1152]{1,0:T(8,128)(2,1)S(1)}, u32[]{:S(2)}, u32[]{:S(2)}) collective-permute-start(bf16[256,1152]{1,0:T(8,128)(2,1)} %bitcast.4.r0_ref), channel_id=1, source_target_pairs={{0,16},{1,9},{2,18},{3,11},{4,20},{5,13},{6,22},{7,15},{8,24},{9,1... | collective-permute-start | bytes 1769480 | tf_op jit(solution)/shard_map/ppermute | solution.py:226
  135.4 22.7 %collective-permute-start.20 = (bf16[256,1152]{1,0:T(8,128)(2,1)S(1)}, bf16[256,1152]{1,0:T(8,128)(2,1)S(1)}, u32[]{:S(2)}, u32[]{:S(2)}) collective-permute-start(bf16[256,1152]{1,0:T(8,128)(2,1)S(1)} %collective-permute-done.18.r1_ref), channel_id=1, source_target_pairs={{0,16},{1,9},{2,18},{3,11},{4,20},{5,13},{6,22},{7,15},{8,24},{9,1... | collective-permute-start | bytes 1769480 | tf_op jit(solution)/shard_map/ppermute | solution.py:226
  135.4 29.6 %collective-permute-start.6 = (bf16[1024,256]{1,0:T(8,128)(2,1)S(1)}, bf16[1024,256]{1,0:T(8,128)(2,1)S(1)}, u32[]{:S(2)}, u32[]{:S(2)}) collective-permute-start(bf16[1024,256]{1,0:T(8,128)(2,1)S(1)} %collective-permute-done.5.mine_ref), channel_id=1, source_target_pairs={{0,1},{1,0},{2,3},{3,2},{4,5},{5,4},{6,7},{7,6},{8,9},{9,8},{10,11... | collective-permute-start | bytes 1572872 | tf_op jit(solution)/shard_map/ppermute | solution.py:218
  142.5 1.0 copy-start.4
  150.3 1.0 copy-start.3
  151.2 6.9 %copy-start.11 = (s32[64]{0:T(128)S(1)}, s32[64]{0:T(128)}, u32[]{:S(2)}) copy-start(s32[64]{0:T(128)} %tenant_ref.5) | copy-start | bytes 772
  (5 other events, 4.0 us)

commit v4 on v3

--- a/solution.py
+++ b/solution.py
@@ -11,7 +11,7 @@
 TENANT_COUNT = 256
 BLOCK = 128
 ADAPTER_SCALE = 2.0
-CHUNKS = (2, 2, 2, 2)
+SPREAD = 4
 VMEM_LIMIT = 48 * 1024 * 1024
 
 F32 = jnp.float32
@@ -55,8 +55,10 @@
         fill_pick(tenant_ref, pick_ref, place * group * ADAPTER_RANK, (here ^ other) * group, group, here)
 
 
-def send_select_kernel(group, size, where_ref, tenant_ref, weight_ref, down_ref, up_ref, out_ref, piece_ref, pick_ref, sem):
-    copy = pltpu.make_async_copy(weight_ref.at[pl.ds(0, size), :], piece_ref, sem)
+def send_select_kernel(group, where_ref, tenant_ref, weight_ref, down_ref, up_ref, out_ref, piece_ref, pick_ref, sem):
+    size = piece_ref.shape[0]
+    start = pl.multiple_of(where_ref[3] * size, size)
+    copy = pltpu.make_async_copy(weight_ref.at[pl.ds(start, size), :], piece_ref, sem)
     copy.start()
     here, core = where_ref[0], where_ref[1]
     pick_two(group, tenant_ref, pick_ref, here, (1 + core, 3))
@@ -70,17 +72,11 @@
     picked(pick_ref, down_ref, up_ref, out_ref)
 
 
-def cut_kernel(start, where_ref, near_ref, weight_ref, half_ref, piece_ref, sems):
-    half = half_ref.shape[0]
-    at = pl.multiple_of(where_ref[1] * half, half)
-    copies = [
-        pltpu.make_async_copy(near_ref.at[pl.ds(at, half), :], half_ref, sems.at[0]),
-        pltpu.make_async_copy(weight_ref.at[pl.ds(start, piece_ref.shape[0]), :], piece_ref, sems.at[1]),
-    ]
-    for copy in copies:
-        copy.start()
-    for copy in copies:
-        copy.wait()
+def sum_kernel(start, keep_ref, came_ref, weight_ref, out_ref, piece_ref, sem):
+    copy = pltpu.make_async_copy(weight_ref.at[pl.ds(start, piece_ref.shape[0]), :], piece_ref, sem)
+    copy.start()
+    out_ref[...] = keep_ref[...] + came_ref[...]
+    copy.wait()
 
 
 def rank_kernel(
@@ -115,45 +111,60 @@
         terms_ref[s, :, cut:] = up_terms[:, s * (both - cut) : (s + 1) * (both - cut)]
 
 
-def chunk_kernel(
-    steps, final, where_ref, fill_ref, tokens_ref, own_ref, near_ref, far_ref, mine_ref, theirs_ref,
-    at_ref, grad_ref, rg_ref, sum_ref, *refs
-):
-    out_ref, total_ref = refs[-3:-1] if final else refs[-2:]
-    acc_ref = refs[-1]
-    i = pl.program_id(0)
-    here, core = where_ref[0], where_ref[1]
-    wide = own_ref.shape[1]
-
-    @pl.when(i == 0)
-    def _():
-        acc_ref[...] = sum_ref[...]
-
-    last = jnp.where(i < steps // 2, mine_ref[...], theirs_ref[...])
-    tokens = tokens_ref[...]
+def base_tile(tokens, pieces, at_ref, grad_ref, rg_ref, out_ref, acc_ref):
     back = dot(rg_ref[...], at_ref[...]).astype(BF16).astype(F32)
-    for other, weight in (
-        (here, own_ref[...]),
-        (here ^ (1 + core), near_ref[...]),
-        (here ^ (2 - core), far_ref[...]),
-        (here ^ 3, last),
-    ):
+    wide = pieces[0][1].shape[1]
+    for other, weight in pieces:
         place = pl.ds(pl.multiple_of(other * wide, wide), wide)
         back += dot(grad_ref[:, place], weight, NT)
         acc_ref[:, place] += dot(tokens, weight)
     out_ref[...] = back.astype(BF16)
 
-    if final:
-        first = where_ref[2]
-
-        @pl.when(i == steps - 1)
-        def _():
-            for n in range(total_ref.shape[0] // BLOCK):
-                part = acc_ref[n * BLOCK : (n + 1) * BLOCK, :]
-                row = lax.broadcasted_iota(jnp.int32, part.shape, 0)
-                total_ref[n * BLOCK : (n + 1) * BLOCK, :] = jnp.where(
-                    row < fill_ref[first + n], part, 0.0
-                ).astype(BF16)
+
+def spread_kernel(
+    where_ref, tokens_ref, own_ref, others_ref, at_ref, grad_ref, rg_ref, sum_ref, out_ref, total_ref
+):
+    i = pl.program_id(0)
+    here, core = where_ref[0], i % 2
+
+    @pl.when(i == 0)
+    def _():
+        total_ref[...] = sum_ref[...]
+
+    pieces = (
+        (here, own_ref[...]),
+        (here ^ (1 + core), others_ref[0, 0]),
+        (here ^ (2 - core), others_ref[0, 1]),
+        (here ^ 3, others_ref[0, 2]),
+    )
+    base_tile(tokens_ref[...], pieces, at_ref, grad_ref, rg_ref, out_ref, total_ref)
+
+
+def swap_kernel(
+    steps, where_ref, fill_ref, tokens_ref, own_ref, near_ref, far_ref, mine_ref, theirs_ref,
+    at_ref, grad_ref, rg_ref, sum_ref, _, out_ref, total_ref, acc_ref
+):
+    i = pl.program_id(0)
+    here, core, first = where_ref[0], where_ref[1], where_ref[2]
+
+    @pl.when(i == 0)
+    def _():
+        acc_ref[...] = sum_ref[...]
+
+    pieces = (
+        (here, own_ref[...]),
+        (here ^ (1 + core), near_ref[...]),
+        (here ^ (2 - core), far_ref[...]),
+        (here ^ 3, jnp.where(i < steps // 2, mine_ref[...], theirs_ref[...])),
+    )
+    base_tile(tokens_ref[...], pieces, at_ref, grad_ref, rg_ref, out_ref, acc_ref)
+
+    @pl.when(i == steps - 1)
+    def _():
+        for n in range(total_ref.shape[0] // BLOCK):
+            part = acc_ref[n * BLOCK : (n + 1) * BLOCK, :]
+            row = lax.broadcasted_iota(jnp.int32, part.shape, 0)
+            total_ref[n * BLOCK : (n + 1) * BLOCK, :] = jnp.where(row < fill_ref[first + n], part, 0.0).astype(BF16)
 
 
 def expand_kernel(
@@ -212,7 +223,7 @@
     here = lax.axis_index("fsdp")
     tok_here = lax.axis_index("tok")
     core = tok_here % 2
-    where = jnp.stack([here, core, (here * shards + tok_here) * dev_blocks]).astype(jnp.int32)
+    where = jnp.stack([here, core, (here * shards + tok_here) * dev_blocks, tok_here]).astype(jnp.int32)
 
     def on_core(a):
         return lax.ppermute(a, "tok", [(t, t ^ 1) for t in range(shards)])
@@ -227,10 +238,11 @@
 
     first_way, second_way = split(1, 2), split(2, 1)
 
-    parts = [(model // 8 * sum(CHUNKS[:k]), model // 8 * size) for k, size in enumerate(CHUNKS)]
+    spread = model // 8 * SPREAD
+    swapped = model - spread
     sent, piece = pl.pallas_call(
-        functools.partial(send_select_kernel, group, parts[0][1]),
-        out_shape=[shape(2 * group_rank, both), shape(parts[0][1], wide)],
+        functools.partial(send_select_kernel, group),
+        out_shape=[shape(2 * group_rank, both), shape(spread // shards, wide)],
         in_specs=[SMEM, SMEM, ANY, VMEM, VMEM],
         out_specs=[VMEM, VMEM],
         scratch_shapes=[pltpu.VMEM((2 * group_rank, columns), BF16), pltpu.SemaphoreType.DMA],
@@ -248,29 +260,26 @@
         name="select_kept",
     )(where, tenants, down_maps, up_maps)
     sent = kept[group_rank:] + came[group_rank:]
-    maps = kept[:group_rank] + came[:group_rank] + second_way(sent)
+    keep = kept[:group_rank] + came[:group_rank]
+
+    first = first_way(piece)
+    others = lax.all_gather(jnp.stack([first, second_way(piece), second_way(first)]), "tok")
+
+    maps, piece = pl.pallas_call(
+        functools.partial(sum_kernel, spread),
+        out_shape=[shape(group_rank, both), shape(swapped, wide)],
+        in_specs=[VMEM, VMEM, ANY],
+        out_specs=[VMEM, VMEM],
+        scratch_shapes=[pltpu.SemaphoreType.DMA],
+        compiler_params=params(),
+        name="sum_and_cut",
+    )(keep, second_way(sent), weight)
     maps = lax.all_to_all(maps.reshape(shards, rank, both), "tok", split_axis=0, concat_axis=0)
 
-    arrived = []
-    for k, (_, size) in enumerate(parts):
-        near = first_way(piece)
-        far = on_core(near)
-        half = size // 2
-        if k + 1 < len(parts):
-            after, after_size = parts[k + 1]
-            part, piece = pl.pallas_call(
-                functools.partial(cut_kernel, after),
-                out_shape=[shape(half, wide), shape(after_size, wide)],
-                in_specs=[SMEM, ANY, ANY],
-                out_specs=[VMEM, VMEM],
-                scratch_shapes=[pltpu.SemaphoreType.DMA((2,))],
-                compiler_params=params(),
-                name="cut_chunk",
-            )(where, near, weight)
-        else:
-            part = lax.dynamic_slice_in_dim(near, core * half, half, axis=0)
-        mine = second_way(part)
-        arrived.append((near, far, mine, on_core(mine)))
+    near = first_way(piece)
+    far = on_core(near)
+    mine = second_way(lax.dynamic_slice_in_dim(near, core * (swapped // 2), swapped // 2, axis=0))
+    theirs = on_core(mine)
 
     grad, at, rank_grad, lora, terms = pl.pallas_call(
         rank_kernel,
@@ -292,62 +301,71 @@
     r1, r2 = first_way(r0), second_way(r0)
     r3 = second_way(r1)
 
+    whole = lambda i, *refs: (0, 0)
+    along = lambda spot: pl.BlockSpec((rows, tile), lambda i, *refs: (0, spot(i, *refs)))
+    down = lambda spot: pl.BlockSpec((tile, wide), lambda i, *refs: (spot(i, *refs), 0))
+
+    def cost(count):
+        return pl.CostEstimate(
+            flops=4 * rows * count * value,
+            bytes_accessed=2 * count * (2 * rows + value) + 8 * rows * value,
+            transcendentals=0,
+        )
+
+    tile = spread // shards
+    token_gradient, total = pl.pallas_call(
+        spread_kernel,
+        out_shape=[shape(rows, model), shape(rows, value, dtype=F32)],
+        grid_spec=pltpu.PrefetchScalarGridSpec(
+            num_scalar_prefetch=1,
+            grid=(shards,),
+            in_specs=[
+                along(lambda i, w: i),
+                down(lambda i, w: i),
+                pl.BlockSpec((1, 3, tile, wide), lambda i, w: (i, 0, 0, 0)),
+                pl.BlockSpec((rank, tile), lambda i, w: (0, i)),
+                pl.BlockSpec((rows, value), whole),
+                pl.BlockSpec((rows, rank), whole),
+                pl.BlockSpec((rows, value), whole),
+            ],
+            out_specs=[along(lambda i, w: i), pl.BlockSpec((rows, value), whole)],
+        ),
+        compiler_params=params(dimension_semantics=("arbitrary",)),
+        cost_estimate=cost(spread),
+        name="base_spread",
+    )(where, tokens, weight, others, at, grad, rank_grad, lora)
+
     tile = 512
-    total, token_gradient = lora, None
-    totals = []
-    for k, (near, far, mine, theirs) in enumerate(arrived):
-        final = k == len(parts) - 1
-        start, chunk_rows = parts[k]
-        steps = chunk_rows // tile
-
-        def turned(i, where_ref, steps=steps):
-            return (i + where_ref[1] * (steps // 2)) % steps
-
-        def spot(i, w, f, start=start // tile, turned=turned):
-            return start + turned(i, w)
-
-        whole = lambda i, w, f: (0, 0)
-        in_specs = [
-            pl.BlockSpec((rows, tile), lambda i, w, f, spot=spot: (0, spot(i, w, f))),
-            pl.BlockSpec((tile, wide), lambda i, w, f, spot=spot: (spot(i, w, f), 0)),
-            pl.BlockSpec((tile, wide), lambda i, w, f, turned=turned: (turned(i, w), 0)),
-            pl.BlockSpec((tile, wide), lambda i, w, f, turned=turned: (turned(i, w), 0)),
-            pl.BlockSpec((tile, wide), lambda i, w, f, half=steps // 2: (jnp.minimum(i, half - 1), 0)),
-            pl.BlockSpec((tile, wide), lambda i, w, f, half=steps // 2: (jnp.maximum(i - half, 0), 0)),
-            pl.BlockSpec((rank, tile), lambda i, w, f, spot=spot: (0, spot(i, w, f))),
-            pl.BlockSpec((rows, value), whole),
-            pl.BlockSpec((rows, rank), whole),
-            pl.BlockSpec((rows, value), whole),
-        ]
-        operands = [where, fills, tokens, weight, near, far, mine, theirs, at, grad, rank_grad, total]
-        aliases = {}
-        if token_gradient is not None:
-            in_specs.append(pl.BlockSpec(memory_space=pl.ANY))
-            aliases = {len(operands): 0}
-            operands.append(token_gradient)
-        token_gradient, total = pl.pallas_call(
-            functools.partial(chunk_kernel, steps, final),
-            out_shape=[shape(rows, model), shape(rows, value, dtype=BF16 if final else F32)],
-            grid_spec=pltpu.PrefetchScalarGridSpec(
-                num_scalar_prefetch=2,
-                grid=(steps,),
-                in_specs=in_specs,
-                out_specs=[
-                    pl.BlockSpec((rows, tile), lambda i, w, f, spot=spot: (0, spot(i, w, f))),
-                    pl.BlockSpec((rows, value), whole),
-                ],
-                scratch_shapes=[pltpu.VMEM((rows, value), F32)] if final else [],
-            ),
-            input_output_aliases=aliases,
-            compiler_params=params(dimension_semantics=("arbitrary",)),
-            cost_estimate=pl.CostEstimate(
-                flops=4 * rows * chunk_rows * value,
-                bytes_accessed=2 * chunk_rows * (2 * rows + value) + 8 * rows * value,
-                transcendentals=0,
-            ),
-            name="base_chunk",
-        )(*operands)
-        totals.append(total)
+    steps = swapped // tile
+    turned = lambda i, w, f: (i + w[1] * (steps // 2)) % steps
+    spot = lambda i, w, f: spread // tile + turned(i, w, f)
+    values, token_gradient = pl.pallas_call(
+        functools.partial(swap_kernel, steps),
+        out_shape=[shape(rows, model), shape(rows, value)],
+        grid_spec=pltpu.PrefetchScalarGridSpec(
+            num_scalar_prefetch=2,
+            grid=(steps,),
+            in_specs=[
+                along(spot),
+                down(spot),
+                down(turned),
+                down(turned),
+                down(lambda i, w, f: jnp.minimum(i, steps // 2 - 1)),
+                down(lambda i, w, f: jnp.maximum(i - steps // 2, 0)),
+                pl.BlockSpec((rank, tile), lambda i, w, f: (0, spot(i, w, f))),
+                pl.BlockSpec((rows, value), whole),
+                pl.BlockSpec((rows, rank), whole),
+                pl.BlockSpec((rows, value), whole),
+                ANY,
+            ],
+            out_specs=[along(spot), pl.BlockSpec((rows, value), whole)],
+            scratch_shapes=[pltpu.VMEM((rows, value), F32)],
+        ),
+        input_output_aliases={12: 0},
+        compiler_params=params(dimension_semantics=("arbitrary",)),
+        cost_estimate=cost(swapped),
+        name="base_swapped",
+    )(where, fills, tokens, weight, near, far, mine, theirs, at, grad, rank_grad, total, token_gradient)[::-1]
 
     grad_down, grad_up = pl.pallas_call(
         functools.partial(expand_kernel, group),
@@ -360,8 +378,8 @@
         ],
         compiler_params=params(),
         name="expand",
-    )(where, tenants, fills, r0, r1, r2, r3, totals[-2])
-    return total, token_gradient, grad_down, grad_up
+    )(where, tenants, fills, r0, r1, r2, r3, total)
+    return values, token_gradient, grad_down, grad_up
 
 
 def solution(mesh):

time: 172 us -> 181 us (1.052)
  waiting for transfers between devices: 77.1 us -> 92 us
  between operations: 0.79 us -> 14.1 us
  Pallas kernels: 52.3 us -> 44.2 us
  local copies, waits for them, and re-layouts: 11.7 us -> 5.49 us
  starting transfers between devices: 28.3 us -> 23.6 us
    all_to_all x1, waiting for transfers between devices: 0.01 us -> 32.1 us  [local(): lax.all_to_all(maps.reshape(shards, rank, both), 'tok', split_axis=0, con...]
    ppermute x13 -> x10, waiting for transfers between devices: 75.9 us -> 45.9 us  [split(): return lambda a: lax.ppermute(a, ('fsdp', 'tok'), pairs)]
    all_to_all x1, waiting for transfers between devices: 1.25 us -> 14 us  [local(): lax.all_to_all(terms, 'tok', split_axis=0, concat_axis=0)]
    pallas_call x8 -> x4, Pallas kernels: 37.1 us -> 28 us  [the longest x1 11.3 us: local(): pl.pallas_call(functools.partial(swap_kernel, steps), out_shape=[shape(ro...]
    unnamed x28 -> x16, local copies, waits for them, and re-layouts: 10.7 us -> 3.22 us
    ppermute x8 -> x2, starting transfers between devices: 3.3 us -> 0.5 us  [on_core(): return lax.ppermute(a, 'tok', [(t, t ^ 1) for t in range(shards)])]
    ppermute x13 -> x10, starting transfers between devices: 15.2 us -> 13.5 us  [split(): return lambda a: lax.ppermute(a, ('fsdp', 'tok'), pairs)]
  transfers between devices with their start and end apart: 23 -> 15, of which waited for: 7 -> 8; matrix products, arithmetic and copies ran while one was open for 1% -> 1% of each run, Pallas kernels for 25% -> 17%
where the time goes in v4:
time: 181 us
  waiting for transfers between devices  92 us (51%)
  Pallas kernels  44.2 us (24%)
  starting transfers between devices  23.6 us (13%)
  between operations  14.1 us (8%)
  local copies, waits for them, and re-layouts  5.49 us (3%)
    ppermute x10, waiting for transfers between devices, split(): return lambda a: lax.ppermute(a, ('fsdp', 'tok'), pairs)  45.9 us
    all_to_all x1, waiting for transfers between devices, local(): lax.all_to_all(maps.reshape(shards, rank, both), 'tok', split_axis=0, con...  32.1 us
    all_to_all x1, waiting for transfers between devices, local(): lax.all_to_all(terms, 'tok', split_axis=0, concat_axis=0)  14 us
    ppermute x10, starting transfers between devices, split(): return lambda a: lax.ppermute(a, ('fsdp', 'tok'), pairs)  13.5 us
    pallas_call x1, Pallas kernels, local(): pl.pallas_call(functools.partial(swap_kernel, steps), out_shape=[shape(ro...  11.3 us
    pallas_call x1, Pallas kernels, local(): pl.pallas_call(spread_kernel, out_shape=[shape(rows, model), shape(rows,...  11 us
    pallas_call x1, Pallas kernels, local(): pl.pallas_call(functools.partial(expand_kernel, group), out_shape=[shape(...  7.06 us
    pallas_call x1, Pallas kernels, local(): pl.pallas_call(rank_kernel, out_shape=[shape(rows, value), shape(rank, mo...  6.64 us
  transfers between devices with their start and end apart: 15, of which 8 were waited for; matrix products, arithmetic and copies ran while one was open for 1% of the time, Pallas kernels for 17%

profile of v4, /device:TPU:0, one launch (start us, length us, event | category | flops | bytes accessed | tf_op | source)
XLA Modules:
  0.0 180.6 jit_solution(5242480109317434937)
XLA Ops:
  7.2 0.1 pad_add_fusion.where_ref
  7.3 1.6 copy-done
  8.9 0.9 copy-done.2
  9.8 0.7 copy-done.5
  10.5 2.5 %select_sent.1 = (bf16[512,1152]{1,0:T(8,128)(2,1)S(1)}, bf16[512,256]{1,0:T(8,128)(2,1)S(1)}) custom-call(s32[4]{0:T(128)S(1)} %pad_add_fusion.where_ref, s32[64]{0:T(128)S(1)} %copy-done.5, bf16[8192,256]{1,0:T(8,128)(2,1)} %own_ref.3, bf16[1024,1024]{1,0:T(8,128)(2,1)S(1)} %copy-done, bf16[128,1024]{1,0:T(8,128)(2,1)S(1)} %copy-done.2), custom_call_target="tpu_custom_call" | custom-call | tf_op jit(solution)/shard_map/select_sent/pallas_call | solution.py:243
  13.1 3.0 %collective-permute-start.6 = (bf16[512,256]{1,0:T(8,128)(2,1)S(1)}, bf16[512,256]{1,0:T(8,128)(2,1)S(1)}, u32[]{:S(2)}, u32[]{:S(2)}) collective-permute-start(bf16[512,256]{1,0:T(8,128)(2,1)S(1)} %get-tuple-element.25), channel_id=1, source_target_pairs={{0,8},{1,17},{2,10},{3,19},{4,12},{5,21},{6,14},{7,23},{8,0},{9,25... | collective-permute-start | bytes 786440 | tf_op jit(solution)/shard_map/ppermute | solution.py:237
  16.1 1.5 collective-permute-start.7
  17.6 5.1 %collective-permute-done.6 = bf16[512,256]{1,0:T(8,128)(2,1)S(1)} collective-permute-done((bf16[512,256]{1,0:T(8,128)(2,1)S(1)}, bf16[512,256]{1,0:T(8,128)(2,1)S(1)}, u32[]{:S(2)}, u32[]{:S(2)}) %collective-permute-start.6) | collective-permute-done | bytes 262176 | tf_op jit(solution)/shard_map/ppermute | solution.py:237
  22.7 1.6 collective-permute-start.8
  24.2 4.8 %collective-permute-done.8 = bf16[512,256]{1,0:T(8,128)(2,1)S(1)} collective-permute-done((bf16[512,256]{1,0:T(8,128)(2,1)S(1)}, bf16[512,256]{1,0:T(8,128)(2,1)S(1)}, u32[]{:S(2)}, u32[]{:S(2)}) %collective-permute-start.8) | collective-permute-done | bytes 262176 | tf_op jit(solution)/shard_map/ppermute | solution.py:237
  29.0 1.0 pad_maximum_fusion
  30.0 2.5 %collective-permute-start = (bf16[512,1152]{1,0:T(8,128)(2,1)S(1)}, bf16[512,1152]{1,0:T(8,128)(2,1)S(1)}, u32[]{:S(2)}, u32[]{:S(2)}) collective-permute-start(bf16[512,1152]{1,0:T(8,128)(2,1)S(1)} %get-tuple-element.19), channel_id=1, source_target_pairs={{0,8},{1,17},{2,10},{3,19},{4,12},{5,21},{6,14},{7,23},{8,0},{9,25... | collective-permute-start | bytes 3538952 | tf_op jit(solution)/shard_map/ppermute | solution.py:237
  32.6 2.5 %select_kept.1 = bf16[512,1152]{1,0:T(8,128)(2,1)S(1)} custom-call(s32[4]{0:T(128)S(1)} %pad_add_fusion.where_ref, s32[64]{0:T(128)S(1)} %copy-done.6, bf16[1024,1024]{1,0:T(8,128)(2,1)S(1)} %copy-done.1, bf16[128,1024]{1,0:T(8,128)(2,1)S(1)} %copy-done.3), custom_call_target="tpu_custom_call" | custom-call | tf_op jit(solution)/shard_map/select_kept/pallas_call | solution.py:253
  35.1 12.4 %collective-permute-done = bf16[512,1152]{1,0:T(8,128)(2,1)S(1)} collective-permute-done((bf16[512,1152]{1,0:T(8,128)(2,1)S(1)}, bf16[512,1152]{1,0:T(8,128)(2,1)S(1)}, u32[]{:S(2)}, u32[]{:S(2)}) %collective-permute-start) | collective-permute-done | bytes 1179680 | tf_op jit(solution)/shard_map/ppermute | solution.py:237
  47.5 0.1 slice_add_fusion
  47.6 1.5 collective-permute-start.1
  49.1 8.4 %collective-permute-done.1.came_ref = bf16[256,1152]{1,0:T(8,128)(2,1)S(1)} collective-permute-done((bf16[256,1152]{1,0:T(8,128)(2,1)S(1)}, bf16[256,1152]{1,0:T(8,128)(2,1)S(1)}, u32[]{:S(2)}, u32[]{:S(2)}) %collective-permute-start.1) | collective-permute-done | bytes 589856 | tf_op jit(solution)/shard_map/ppermute | solution.py:237
  57.6 3.2 %sum_and_cut.1 = (bf16[256,1152]{1,0:T(8,128)(2,1)}, bf16[4096,256]{1,0:T(8,128)(2,1)}) custom-call(bf16[256,1152]{1,0:T(8,128)(2,1)S(1)} %get-tuple-element.35.keep_ref, bf16[256,1152]{1,0:T(8,128)(2,1)S(1)} %collective-permute-done.1.came_ref, bf16[8192,256]{1,0:T(8,128)(2,1)} %own_ref.3), custom_call_target="tpu_custom_call" | custom-call | tf_op jit(solution)/shard_map/sum_and_cut/pallas_call | solution.py:268
  60.8 2.5 %collective-permute-start.2 = (bf16[4096,256]{1,0:T(8,128)(2,1)}, bf16[4096,256]{1,0:T(8,128)(2,1)}, u32[]{:S(2)}, u32[]{:S(2)}) collective-permute-start(bf16[4096,256]{1,0:T(8,128)(2,1)} %get-tuple-element.20), channel_id=1, source_target_pairs={{0,8},{1,17},{2,10},{3,19},{4,12},{5,21},{6,14},{7,23},{8,0},{9,25... | collective-permute-start | bytes 6291464 | tf_op jit(solution)/shard_map/ppermute | solution.py:237
  63.3 5.2 %all-to-all-start = ((bf16[8,32,1152]{2,1,0:T(8,128)(2,1)}), bf16[8,32,1152]{2,1,0:T(8,128)(2,1)S(1)}, u32[]{:S(2)}, u32[]{:S(2)}) async-start(bf16[8,32,1152]{2,1,0:T(8,128)(2,1)} %bitcast.4), calls=%async_computation | async-start | bytes 1179648 | tf_op jit(solution)/shard_map/all_to_all | solution.py:277
  68.5 32.1 %all-to-all-done.maps_ref = bf16[8,32,1152]{2,1,0:T(8,128)(2,1)S(1)} async-done(((bf16[8,32,1152]{2,1,0:T(8,128)(2,1)}), bf16[8,32,1152]{2,1,0:T(8,128)(2,1)S(1)}, u32[]{:S(2)}, u32[]{:S(2)}) %all-to-all-start) | async-done | bytes 589856 | tf_op jit(solution)/shard_map/all_to_all | solution.py:277
  100.6 6.6 %rank_space.1 = (bf16[256,1024]{1,0:T(8,128)(2,1)S(1)}, bf16[32,8192]{1,0:T(8,128)(2,1)S(1)}, bf16[256,32]{1,0:T(8,128)(2,1)S(1)}, f32[256,1024]{1,0:T(8,128)S(1)}, bf16[8,32,1152]{2,1,0:T(8,128)(2,1)}) custom-call(s32[4]{0:T(128)S(1)} %pad_add_fusion.where_ref, s32[64]{0:T(128)S(1)} %copy-done.7, bf16[256,8192]{1,0:T(8,128)(2,1)} %tokens_ref.5, ...), custom_call_target="tpu_custom_call" | custom-call | tf_op jit(solution)/shard_map/rank_space/pallas_call | solution.py:284
  107.3 4.3 %all-to-all-start.1 = ((bf16[8,32,1152]{2,1,0:T(8,128)(2,1)}), bf16[8,32,1152]{2,1,0:T(8,128)(2,1)S(1)}, u32[]{:S(2)}, u32[]{:S(2)}) async-start(bf16[8,32,1152]{2,1,0:T(8,128)(2,1)} %get-tuple-element.31), calls=%async_computation.1 | async-start | bytes 1179648 | tf_op jit(solution)/shard_map/all_to_all | solution.py:300
  111.6 2.3 %constant_dynamic-slice_fusion = bf16[2048,256]{1,0:T(8,128)(2,1)} fusion(bf16[4096,256]{1,0:T(8,128)(2,1)} %collective-permute-done.2.near_ref, s32[]{:T(128)S(6)} %select_n.11), kind=kLoop, calls=%fused_computation.4 | loop fusion | bytes 2097156 | tf_op jit(solution)/shard_map/dynamic_slice | solution.py:281
  113.8 0.5 collective-permute-start.3
  114.3 14.0 %all-to-all-done.1 = bf16[8,32,1152]{2,1,0:T(8,128)(2,1)S(1)} async-done(((bf16[8,32,1152]{2,1,0:T(8,128)(2,1)}), bf16[8,32,1152]{2,1,0:T(8,128)(2,1)S(1)}, u32[]{:S(2)}, u32[]{:S(2)}) %all-to-all-start.1) | async-done | bytes 589856 | tf_op jit(solution)/shard_map/all_to_all | solution.py:300
  128.3 0.6 collective-permute-done.4.mine_ref
  129.0 0.8 collective-permute-start.10
  129.7 14.6 %collective-permute-done.9.r1_ref = bf16[256,1152]{1,0:T(8,128)(2,1)S(1)} collective-permute-done((bf16[256,1152]{1,0:T(8,128)(2,1)S(1)}, bf16[256,1152]{1,0:T(8,128)(2,1)S(1)}, u32[]{:S(2)}, u32[]{:S(2)}) %collective-permute-start.9) | collective-permute-done | bytes 589856 | tf_op jit(solution)/shard_map/ppermute | solution.py:237
  144.4 11.0 %base_spread.1 = (bf16[256,8192]{1,0:T(8,128)(2,1)}, f32[256,1024]{1,0:T(8,128)S(1)}) custom-call(s32[4]{0:T(128)S(1)} %pad_add_fusion.where_ref, bf16[256,8192]{1,0:T(8,128)(2,1)} %tokens_ref.5, bf16[8192,256]{1,0:T(8,128)(2,1)} %own_ref.3, bf16[8,3,512,256]{3,2,1,0:T(8,128)(2,1)} %bitcast.13, bf16[32,8192]{1,0:T(8,128)(2,1)S(1)} %get-tuple-element.22.at_ref, ...), custom_call_target="tpu_custom_call" | custom-call | flops 4294967296 | bytes 14680064 | tf_op jit(solution)/shard_map/base_spread/pallas_call | solution.py:316
  155.4 7.1 %expand.1 = (f32[1024,1024]{1,0:T(8,128)}, f32[128,1024]{1,0:T(8,128)}) custom-call(s32[4]{0:T(128)S(1)} %pad_add_fusion.where_ref, s32[64]{0:T(128)S(1)} %copy-done.6, s32[64]{0:T(128)S(1)} %copy-done.7, bf16[256,1152]{1,0:T(8,128)(2,1)S(1)} %bitcast.12, bf16[256,1152]{1,0:T(8,128)(2,1)S(1)} %collective-permute-done.9.r1_ref, ...), custom_call_target="tpu_custom_call" | custom-call | tf_op jit(solution)/shard_map/expand/pallas_call | solution.py:370
  162.4 11.3 %base_swapped.1 = (bf16[256,8192]{1,0:T(8,128)(2,1)}, bf16[256,1024]{1,0:T(8,128)(2,1)}) custom-call(s32[4]{0:T(128)S(1)} %pad_add_fusion.where_ref, s32[64]{0:T(128)S(1)} %copy-done.7, bf16[256,8192]{1,0:T(8,128)(2,1)} %tokens_ref.5, bf16[8192,256]{1,0:T(8,128)(2,1)} %own_ref.3, ...), custom_call_target="tpu_custom_call", output_to_operand_aliasing={{0}: (12, {})} | custom-call | flops 4294967296 | bytes 14680064 | tf_op jit(solution)/shard_map/base_swapped/pallas_call | solution.py:342
  (26 shorter events, 0.1 us)
Async XLA Ops:
  7.2 137.2 %all-gather.3.cloned.1.call-start = ((), (), s32[]{:S(2)}) async-start(), calls=%async_computation.2 | async-start | bytes 7077888 | tf_op jit(solution)/shard_map/all_gather | solution.py:266
  7.3 1.6 copy-start
  8.9 0.9 copy-start.2
  9.8 0.7 copy-start.5
  13.0 19.5 %copy-start.1 = (bf16[1024,1024]{1,0:T(8,128)(2,1)S(1)}, bf16[1024,1024]{1,0:T(8,128)(2,1)}, u32[]{:S(2)}) copy-start(bf16[1024,1024]{1,0:T(8,128)(2,1)} %down_ref.3) | copy-start | bytes 6291460
  13.0 19.5 %copy-start.3 = (bf16[128,1024]{1,0:T(8,128)(2,1)S(1)}, bf16[128,1024]{1,0:T(8,128)(2,1)}, u32[]{:S(2)}) copy-start(bf16[128,1024]{1,0:T(8,128)(2,1)} %up_ref.3) | copy-start | bytes 786436
  13.0 19.5 %copy-start.6 = (s32[64]{0:T(128)S(1)}, s32[64]{0:T(128)}, u32[]{:S(2)}) copy-start(s32[64]{0:T(128)} %tenant_ref.5) | copy-start | bytes 772
  13.1 9.6 %collective-permute-start.6 = (bf16[512,256]{1,0:T(8,128)(2,1)S(1)}, bf16[512,256]{1,0:T(8,128)(2,1)S(1)}, u32[]{:S(2)}, u32[]{:S(2)}) collective-permute-start(bf16[512,256]{1,0:T(8,128)(2,1)S(1)} %get-tuple-element.25), channel_id=1, source_target_pairs={{0,8},{1,17},{2,10},{3,19},{4,12},{5,21},{6,14},{7,23},{8,0},{9,25... | collective-permute-start | bytes 786440 | tf_op jit(solution)/shard_map/ppermute | solution.py:237
  16.1 8.2 %collective-permute-start.7 = (bf16[512,256]{1,0:T(8,128)(2,1)S(1)}, bf16[512,256]{1,0:T(8,128)(2,1)S(1)}, u32[]{:S(2)}, u32[]{:S(2)}) collective-permute-start(bf16[512,256]{1,0:T(8,128)(2,1)S(1)} %get-tuple-element.25), channel_id=1, source_target_pairs={{0,16},{1,9},{2,18},{3,11},{4,20},{5,13},{6,22},{7,15},{8,24},{9,1... | collective-permute-start | bytes 786440 | tf_op jit(solution)/shard_map/ppermute | solution.py:237
  22.7 6.4 %collective-permute-start.8 = (bf16[512,256]{1,0:T(8,128)(2,1)S(1)}, bf16[512,256]{1,0:T(8,128)(2,1)S(1)}, u32[]{:S(2)}, u32[]{:S(2)}) collective-permute-start(bf16[512,256]{1,0:T(8,128)(2,1)S(1)} %collective-permute-done.6), channel_id=1, source_target_pairs={{0,16},{1,9},{2,18},{3,11},{4,20},{5,13},{6,22},{7,15},{8,24},{9,1... | collective-permute-start | bytes 786440 | tf_op jit(solution)/shard_map/ppermute | solution.py:237
  30.0 17.5 %collective-permute-start = (bf16[512,1152]{1,0:T(8,128)(2,1)S(1)}, bf16[512,1152]{1,0:T(8,128)(2,1)S(1)}, u32[]{:S(2)}, u32[]{:S(2)}) collective-permute-start(bf16[512,1152]{1,0:T(8,128)(2,1)S(1)} %get-tuple-element.19), channel_id=1, source_target_pairs={{0,8},{1,17},{2,10},{3,19},{4,12},{5,21},{6,14},{7,23},{8,0},{9,25... | collective-permute-start | bytes 3538952 | tf_op jit(solution)/shard_map/ppermute | solution.py:237
  47.6 9.9 %collective-permute-start.1 = (bf16[256,1152]{1,0:T(8,128)(2,1)S(1)}, bf16[256,1152]{1,0:T(8,128)(2,1)S(1)}, u32[]{:S(2)}, u32[]{:S(2)}) collective-permute-start(bf16[256,1152]{1,0:T(8,128)(2,1)S(1)} %get-tuple-element.34), channel_id=1, source_target_pairs={{0,16},{1,9},{2,18},{3,11},{4,20},{5,13},{6,22},{7,15},{8,24},{9,1... | collective-permute-start | bytes 1769480 | tf_op jit(solution)/shard_map/ppermute | solution.py:237
  57.6 43.1 %copy-start.4 = (bf16[256,1024]{1,0:T(8,128)(2,1)S(1)}, bf16[256,1024]{1,0:T(8,128)(2,1)}, u32[]{:S(2)}) copy-start(bf16[256,1024]{1,0:T(8,128)(2,1)} %cot_ref.1) | copy-start | bytes 1572868
  57.6 43.1 %copy-start.7 = (s32[64]{0:T(128)S(1)}, s32[64]{0:T(128)}, u32[]{:S(2)}) copy-start(s32[64]{0:T(128)} %fill_ref.5) | copy-start | bytes 772
  60.8 50.8 %collective-permute-start.2 = (bf16[4096,256]{1,0:T(8,128)(2,1)}, bf16[4096,256]{1,0:T(8,128)(2,1)}, u32[]{:S(2)}, u32[]{:S(2)}) collective-permute-start(bf16[4096,256]{1,0:T(8,128)(2,1)} %get-tuple-element.20), channel_id=1, source_target_pairs={{0,8},{1,17},{2,10},{3,19},{4,12},{5,21},{6,14},{7,23},{8,0},{9,25... | collective-permute-start | bytes 6291464 | tf_op jit(solution)/shard_map/ppermute | solution.py:237
  63.3 37.3 %all-to-all-start = ((bf16[8,32,1152]{2,1,0:T(8,128)(2,1)}), bf16[8,32,1152]{2,1,0:T(8,128)(2,1)S(1)}, u32[]{:S(2)}, u32[]{:S(2)}) async-start(bf16[8,32,1152]{2,1,0:T(8,128)(2,1)} %bitcast.4), calls=%async_computation | async-start | bytes 1179648 | tf_op jit(solution)/shard_map/all_to_all | solution.py:277
  107.3 21.1 %all-to-all-start.1 = ((bf16[8,32,1152]{2,1,0:T(8,128)(2,1)}), bf16[8,32,1152]{2,1,0:T(8,128)(2,1)S(1)}, u32[]{:S(2)}, u32[]{:S(2)}) async-start(bf16[8,32,1152]{2,1,0:T(8,128)(2,1)} %get-tuple-element.31), calls=%async_computation.1 | async-start | bytes 1179648 | tf_op jit(solution)/shard_map/all_to_all | solution.py:300
  113.8 15.1 %collective-permute-start.4 = (bf16[2048,256]{1,0:T(8,128)(2,1)}, bf16[2048,256]{1,0:T(8,128)(2,1)}, u32[]{:S(2)}, u32[]{:S(2)}) collective-permute-start(bf16[2048,256]{1,0:T(8,128)(2,1)} %constant_dynamic-slice_fusion), channel_id=1, source_target_pairs={{0,16},{1,9},{2,18},{3,11},{4,20},{5,13},{6,22},{7,15},{8,24},{9,1... | collective-permute-start | bytes 3145736 | tf_op jit(solution)/shard_map/ppermute | solution.py:237
  113.8 48.6 %collective-permute-start.3 = (bf16[4096,256]{1,0:T(8,128)(2,1)}, bf16[4096,256]{1,0:T(8,128)(2,1)}, u32[]{:S(2)}, u32[]{:S(2)}) collective-permute-start(bf16[4096,256]{1,0:T(8,128)(2,1)} %collective-permute-done.2.near_ref), channel_id=1, source_target_pairs={{0,1},{1,0},{2,3},{3,2},{4,5},{5,4},{6,7},{7,6},{8,9},{9,8},{10,11... | collective-permute-start | bytes 6291464 | tf_op jit(solution)/shard_map/ppermute | solution.py:229
  128.3 16.0 %collective-permute-start.9 = (bf16[256,1152]{1,0:T(8,128)(2,1)S(1)}, bf16[256,1152]{1,0:T(8,128)(2,1)S(1)}, u32[]{:S(2)}, u32[]{:S(2)}) collective-permute-start(bf16[256,1152]{1,0:T(8,128)(2,1)S(1)} %bitcast.10), channel_id=1, source_target_pairs={{0,8},{1,17},{2,10},{3,19},{4,12},{5,21},{6,14},{7,23},{8,0},{9,25... | collective-permute-start | bytes 1769480 | tf_op jit(solution)/shard_map/ppermute | solution.py:237
  129.0 33.5 %collective-permute-start.5 = (bf16[2048,256]{1,0:T(8,128)(2,1)}, bf16[2048,256]{1,0:T(8,128)(2,1)}, u32[]{:S(2)}, u32[]{:S(2)}) collective-permute-start(bf16[2048,256]{1,0:T(8,128)(2,1)} %collective-permute-done.4.mine_ref), channel_id=1, source_target_pairs={{0,1},{1,0},{2,3},{3,2},{4,5},{5,4},{6,7},{7,6},{8,9},{9,8},{10,11... | collective-permute-start | bytes 3145736 | tf_op jit(solution)/shard_map/ppermute | solution.py:229
  129.0 26.4 %collective-permute-start.10 = (bf16[256,1152]{1,0:T(8,128)(2,1)S(1)}, bf16[256,1152]{1,0:T(8,128)(2,1)}, u32[]{:S(2)}, u32[]{:S(2)}) collective-permute-start(bf16[256,1152]{1,0:T(8,128)(2,1)S(1)} %bitcast.11), channel_id=1, source_target_pairs={{0,16},{1,9},{2,18},{3,11},{4,20},{5,13},{6,22},{7,15},{8,24},{9,1... | collective-permute-start | bytes 1769480 | tf_op jit(solution)/shard_map/ppermute | solution.py:237
  144.4 11.0 %collective-permute-start.11 = (bf16[256,1152]{1,0:T(8,128)(2,1)S(1)}, bf16[256,1152]{1,0:T(8,128)(2,1)}, u32[]{:S(2)}, u32[]{:S(2)}) collective-permute-start(bf16[256,1152]{1,0:T(8,128)(2,1)S(1)} %collective-permute-done.9.r1_ref), channel_id=1, source_target_pairs={{0,16},{1,9},{2,18},{3,11},{4,20},{5,13},{6,22},{7,15},{8,24},{9,1... | collective-permute-start | bytes 1769480 | tf_op jit(solution)/shard_map/ppermute | solution.py:237
Sparse Core Ops, SparseCore 0:
  30.1 78.6 all-gather.2

commit v5 on v4

v5 whole, which is shorter than its diff:
```python
import functools

import jax
import jax.numpy as jnp
from jax import lax
from jax.experimental import pallas as pl
from jax.experimental.pallas import tpu as pltpu
from jax.sharding import PartitionSpec as P

ADAPTER_RANK = 16
BLOCK = 128
ADAPTER_SCALE = 2.0
SPREAD = 3
VMEM_LIMIT = 48 * 1024 * 1024

F32 = jnp.float32
BF16 = jnp.bfloat16
NT = (((1,), (1,)), ((), ()))
TN = (((0,), (0,)), ((), ()))
SMEM = pl.BlockSpec(memory_space=pltpu.SMEM)
VMEM = pl.BlockSpec(memory_space=pltpu.VMEM)
ANY = pl.BlockSpec(memory_space=pl.ANY)


def dot(a, b, dims=(((1,), (0,)), ((), ()))):
    return lax.dot_general(a, b, dims, preferred_element_type=F32)


def block_rows(tenant_ref, block, shard, columns):
    base = tenant_ref[block] * ADAPTER_RANK - shard * columns
    lane = lax.broadcasted_iota(jnp.int32, (ADAPTER_RANK, columns), 1)
    row = lax.broadcasted_iota(jnp.int32, (ADAPTER_RANK, columns), 0)
    return jnp.where(lane - row == base, 1.0, 0.0)


def fill_pick(tenant_ref, pick_ref, row, first_block, count, shard):
    columns = pick_ref.shape[1]

    @pl.loop(0, count)
    def _(n):
        start = pl.multiple_of(row + n * ADAPTER_RANK, ADAPTER_RANK)
        rows = block_rows(tenant_ref, first_block + n, shard, columns)
        pick_ref[pl.ds(start, ADAPTER_RANK), :] = rows.astype(BF16)


def pick_two(group, tenant_ref, pick_ref, here, others):
    for place, other in enumerate(others):
        fill_pick(tenant_ref, pick_ref, place * group * ADAPTER_RANK, (here ^ other) * group, group, here)


def up_select_kernel(where_ref, tenant_ref, up_ref, out_ref, pick_ref):
    fill_pick(tenant_ref, pick_ref, 0, 0, tenant_ref.shape[0], where_ref[0])
    out_ref[...] = dot(pick_ref[...], up_ref[...], NT).astype(BF16)


def send_select_kernel(group, where_ref, tenant_ref, weight_ref, down_ref, out_ref, piece_ref, pick_ref, sem):
    size = piece_ref.shape[0]
    start = pl.multiple_of(where_ref[3] * size, size)
    copy = pltpu.make_async_copy(weight_ref.at[pl.ds(start, size), :], piece_ref, sem)
    copy.start()
    here, core = where_ref[0], where_ref[1]
    pick_two(group, tenant_ref, pick_ref, here, (1 + core, 3))
    out_ref[...] = dot(pick_ref[...], down_ref[...], NT).astype(BF16)
    copy.wait()


def keep_select_kernel(group, where_ref, tenant_ref, down_ref, out_ref, pick_ref):
    here, core = where_ref[0], where_ref[1]
    pick_two(group, tenant_ref, pick_ref, here, (0, 2 - core))
    out_ref[...] = dot(pick_ref[...], down_ref[...], NT).astype(BF16)


def sum_kernel(start, keep_ref, came_ref, weight_ref, keep_out_ref, send_out_ref, piece_ref, sem):
    copy = pltpu.make_async_copy(weight_ref.at[pl.ds(start, piece_ref.shape[0]), :], piece_ref, sem)
    copy.start()
    rows = keep_out_ref.shape[0]
    send_out_ref[...] = keep_ref[rows:, :] + came_ref[rows:, :]
    keep_out_ref[...] = keep_ref[:rows, :] + came_ref[:rows, :]
    copy.wait()


def block_diagonal(a):
    own = (
        lax.broadcasted_iota(jnp.int32, a.shape, 0) // BLOCK
        == lax.broadcasted_iota(jnp.int32, a.shape, 1) // ADAPTER_RANK
    )
    return jnp.where(own, a, 0.0).astype(BF16)


def down_terms_kernel(
    where_ref, fill_ref, tokens_ref, cot_ref, maps_ref, grad_ref, rg_ref, up_ref, terms_ref, full_ref
):
    rows, value = cot_ref.shape
    devices, _, width = maps_ref.shape
    shards = value // width
    here, first = where_ref[0], where_ref[2]
    wide = value * shards // devices
    for s in range(shards):
        total = maps_ref[s]
        for f in range(1, devices // shards):
            total += maps_ref[f * shards + s]
        full_ref[:, s * width : (s + 1) * width] = total
    for n in range(rows // BLOCK):
        span = slice(n * BLOCK, (n + 1) * BLOCK)
        row = lax.broadcasted_iota(jnp.int32, (BLOCK, wide), 0)
        for other in range(value // wide):
            part = cot_ref[span, pl.ds(pl.multiple_of((here ^ other) * wide, wide), wide)]
            grad_ref[span, other * wide : (other + 1) * wide] = jnp.where(
                row < fill_ref[first + n], part, jnp.zeros_like(part)
            )
    for other in range(value // wide):
        up_ref[:, other * wide : (other + 1) * wide] = full_ref[
            :, pl.ds(pl.multiple_of((here ^ other) * wide, wide), wide)
        ]
    rank_grad = block_diagonal(ADAPTER_SCALE * dot(grad_ref[...], up_ref[...], NT))
    rg_ref[...] = rank_grad
    cut = terms_ref.shape[2]
    for s in range(terms_ref.shape[0]):
        terms_ref[s] = dot(rank_grad, tokens_ref[:, s * cut : (s + 1) * cut], TN).astype(BF16)


def up_terms_kernel(where_ref, tokens_ref, maps_ref, grad_ref, up_ref, at_ref, lora_ref, terms_ref, full_ref):
    shards, _, cut = maps_ref.shape
    devices, _, width = terms_ref.shape
    value = grad_ref.shape[1]
    wide = value * shards // devices
    here = where_ref[0]
    for s in range(shards):
        at_ref[:, s * cut : (s + 1) * cut] = maps_ref[s]
    rank_in = block_diagonal(dot(tokens_ref[...], at_ref[...], NT))
    lora_ref[...] = (ADAPTER_SCALE * dot(rank_in, up_ref[...])).astype(BF16).astype(F32)
    terms = (ADAPTER_SCALE * dot(rank_in, grad_ref[...], TN)).astype(BF16)
    for other in range(value // wide):
        full_ref[:, pl.ds(pl.multiple_of((here ^ other) * wide, wide), wide)] = terms[
            :, other * wide : (other + 1) * wide
        ]
    for d in range(devices):
        s = d % shards
        terms_ref[d] = full_ref[:, s * width : (s + 1) * width]


def base_tile(core, tokens_ref, own, near, far, last, at_ref, grad_ref, rg_ref, out_ref, acc_ref):
    one, two = jnp.where(core == 0, near, far), jnp.where(core == 0, far, near)
    weight = jnp.concatenate([own, one, two, last], axis=1)
    back = dot(rg_ref[...], at_ref[...]).astype(BF16).astype(F32)
    out_ref[...] = (back + dot(grad_ref[...], weight, NT)).astype(BF16)
    acc_ref[...] += dot(tokens_ref[...], weight)


def spread_kernel(tokens_ref, own_ref, others_ref, at_ref, grad_ref, rg_ref, sum_ref, out_ref, total_ref):
    i = pl.program_id(0)

    @pl.when(i == 0)
    def _():
        total_ref[...] = sum_ref[...]

    base_tile(
        i % 2, tokens_ref, own_ref[...], others_ref[0, 0], others_ref[0, 1], others_ref[0, 2],
        at_ref, grad_ref, rg_ref, out_ref, total_ref,
    )


def swap_kernel(
    steps, where_ref, fill_ref, tokens_ref, own_ref, near_ref, far_ref, mine_ref, theirs_ref,
    at_ref, grad_ref, rg_ref, sum_ref, _, out_ref, total_ref, acc_ref
):
    i = pl.program_id(0)
    here, core, first = where_ref[0], where_ref[1], where_ref[2]

    @pl.when(i == 0)
    def _():
        acc_ref[...] = sum_ref[...]

    last = jnp.where(i < steps // 2, mine_ref[...], theirs_ref[...])
    base_tile(
        core, tokens_ref, own_ref[...], near_ref[...], far_ref[...], last,
        at_ref, grad_ref, rg_ref, out_ref, acc_ref,
    )

    @pl.when(i == steps - 1)
    def _():
        wide = own_ref.shape[1]
        for n in range(total_ref.shape[0] // BLOCK):
            span = slice(n * BLOCK, (n + 1) * BLOCK)
            for other in range(total_ref.shape[1] // wide):
                part = acc_ref[span, other * wide : (other + 1) * wide]
                row = lax.broadcasted_iota(jnp.int32, part.shape, 0)
                total_ref[span, pl.ds(pl.multiple_of((here ^ other) * wide, wide), wide)] = jnp.where(
                    row < fill_ref[first + n], part, 0.0
                ).astype(BF16)


def fill_expand(tenant_ref, fill_ref, pick_ref, scale_ref, row, first, count, shard):
    columns = pick_ref.shape[1]

    @pl.loop(0, count)
    def _(n):
        start = pl.multiple_of(row + n * ADAPTER_RANK, ADAPTER_RANK)
        part = block_rows(tenant_ref, first + n, shard, columns)
        pick_ref[pl.ds(start, ADAPTER_RANK), :] = part.astype(BF16)
        scale_ref[...] += part * fill_ref[first + n].astype(F32)


def tenant_scale(scale_ref):
    return 1.0 / jnp.maximum(jnp.sum(scale_ref[...], axis=0, keepdims=True), 1.0)


def expand_down_kernel(
    group, where_ref, tenant_ref, fill_ref, r0_ref, r1_ref, r2_ref, r3_ref, down_ref, pick_ref, scale_ref
):
    here, core = where_ref[0], where_ref[1]
    rows = group * ADAPTER_RANK
    scale_ref[...] = jnp.zeros_like(scale_ref)
    for place, other in enumerate((0, 1 + core, 2 - core, 3)):
        fill_expand(
            tenant_ref, fill_ref, pick_ref, scale_ref, place * rows, (here ^ other) * group, group, here
        )
    scale = tenant_scale(scale_ref)
    cut = down_ref.shape[0]
    step = min(cut, 256)
    for lo in range(0, cut, step):
        terms = jnp.concatenate([ref[:, lo : lo + step] for ref in (r0_ref, r1_ref, r2_ref, r3_ref)], axis=0)
        down_ref[lo : lo + step, :] = dot(terms, pick_ref[...], TN) * scale


def expand_up_kernel(where_ref, tenant_ref, fill_ref, terms_ref, up_ref, pick_ref, scale_ref):
    scale_ref[...] = jnp.zeros_like(scale_ref)
    fill_expand(tenant_ref, fill_ref, pick_ref, scale_ref, 0, 0, tenant_ref.shape[0], where_ref[0])
    up_ref[...] = dot(terms_ref[...], pick_ref[...], TN) * tenant_scale(scale_ref)


def params(**extra):
    return pltpu.CompilerParams(vmem_limit_bytes=VMEM_LIMIT, **extra)


def shape(*dims, dtype=BF16):
    return jax.ShapeDtypeStruct(dims, dtype)


def local(tokens, weight, down_maps, up_maps, cotangent, tenants, fills):
    shards = lax.axis_size("tok")
    groups = lax.axis_size("fsdp")
    devices = groups * shards
    rows, model = tokens.shape
    value = cotangent.shape[1]
    wide = weight.shape[1]
    cut, columns = down_maps.shape
    width = up_maps.shape[0]
    dev_blocks = rows // BLOCK
    group = dev_blocks * shards
    rank = dev_blocks * ADAPTER_RANK
    group_rank = group * ADAPTER_RANK
    here = lax.axis_index("fsdp")
    tok_here = lax.axis_index("tok")
    core = tok_here % 2
    where = jnp.stack([here, core, (here * shards + tok_here) * dev_blocks, tok_here]).astype(jnp.int32)

    def on_core(a):
        return lax.ppermute(a, "tok", [(t, t ^ 1) for t in range(shards)])

    def split(first, second):
        pairs = [
            (f * shards + t, (f ^ (second if t % 2 else first)) * shards + t)
            for f in range(groups)
            for t in range(shards)
        ]
        return lambda a: lax.ppermute(a, ("fsdp", "tok"), pairs)

    first_way, second_way = split(1, 2), split(2, 1)

    def everywhere(a):
        return lax.all_to_all(a, ("fsdp", "tok"), split_axis=0, concat_axis=0)

    def along_tok(a):
        return lax.all_to_all(a, "tok", split_axis=0, concat_axis=0)

    def call(body, out_shape, in_specs, name, scratch=(), out_specs=None, **extra):
        return pl.pallas_call(
            body,
            out_shape=out_shape,
            in_specs=in_specs,
            out_specs=out_specs or jax.tree.map(lambda _: VMEM, out_shape),
            scratch_shapes=list(scratch),
            compiler_params=params(),
            name=name,
            **extra,
        )

    up_sent = call(
        up_select_kernel,
        shape(devices * rank, width),
        [SMEM, SMEM, VMEM],
        "select_up",
        [pltpu.VMEM((devices * rank, columns), BF16)],
    )(where, tenants, up_maps)
    up_came = everywhere(up_sent.reshape(devices, rank, width))

    spread = max(model // 8 * SPREAD, BLOCK * shards)
    swapped = model - spread
    pick = pltpu.VMEM((2 * group_rank, columns), BF16)
    sent, share = call(
        functools.partial(send_select_kernel, group),
        [shape(2 * group_rank, cut), shape(spread // shards, wide)],
        [SMEM, SMEM, ANY, VMEM],
        "select_sent",
        [pick, pltpu.SemaphoreType.DMA],
    )(where, tenants, weight, down_maps)
    came = first_way(sent)
    kept = call(
        functools.partial(keep_select_kernel, group),
        shape(2 * group_rank, cut),
        [SMEM, SMEM, VMEM],
        "select_kept",
        [pick],
    )(where, tenants, down_maps)
    keep, sent, piece = call(
        functools.partial(sum_kernel, spread),
        [shape(group_rank, cut), shape(group_rank, cut), shape(swapped, wide)],
        [VMEM, VMEM, ANY],
        "sum_and_cut",
        [pltpu.SemaphoreType.DMA],
    )(kept, came, weight)
    down_came = along_tok((keep + second_way(sent)).reshape(shards, rank, cut))

    grad, rank_grad, up, down_terms = call(
        down_terms_kernel,
        [shape(rows, value), shape(rows, rank), shape(rank, value), shape(shards, rank, cut)],
        [SMEM, SMEM, VMEM, VMEM, VMEM],
        "down_terms",
        [pltpu.VMEM((rank, value), BF16)],
    )(where, fills, tokens, cotangent, up_came)
    r0 = along_tok(down_terms).reshape(group_rank, cut)
    r1, r2 = first_way(r0), second_way(r0)
    r3 = second_way(r1)

    at, lora, up_terms = call(
        up_terms_kernel,
        [shape(rank, model), shape(rows, value, dtype=F32), shape(devices, rank, width)],
        [SMEM, VMEM, VMEM, VMEM, VMEM],
        "up_terms",
        [pltpu.VMEM((rank, value), BF16)],
    )(where, tokens, down_came, grad, up)
    r_up = everywhere(up_terms).reshape(devices * rank, width)

    first = first_way(share)
    others = lax.all_gather(jnp.stack([first, second_way(share), second_way(first)]), "tok")

    near = first_way(piece)
    far = on_core(near)
    mine = second_way(lax.dynamic_slice_in_dim(near, core * (swapped // 2), swapped // 2, axis=0))
    theirs = on_core(mine)

    expand_scratch = [
        pltpu.VMEM((devices * rank, columns), BF16),
        pltpu.VMEM((ADAPTER_RANK, columns), F32),
    ]
    grad_down = call(
        functools.partial(expand_down_kernel, group),
        shape(cut, columns, dtype=F32),
        [SMEM, SMEM, SMEM] + [VMEM] * 4,
        "expand_down",
        expand_scratch,
    )(where, tenants, fills, r0, r1, r2, r3)
    grad_up = call(
        expand_up_kernel,
        shape(width, columns, dtype=F32),
        [SMEM, SMEM, SMEM, VMEM],
        "expand_up",
        expand_scratch,
    )(where, tenants, fills, r_up)

    whole = lambda i, *refs: (0, 0)
    along = lambda spot, tile: pl.BlockSpec((rows, tile), lambda i, *refs: (0, spot(i, *refs)))
    down = lambda spot, tile: pl.BlockSpec((tile, wide), lambda i, *refs: (spot(i, *refs), 0))
    resident = [
        pl.BlockSpec((rows, value), whole),
        pl.BlockSpec((rows, rank), whole),
        pl.BlockSpec((rows, value), whole),
    ]

    def cost(count):
        return pl.CostEstimate(
            flops=4 * rows * count * value,
            bytes_accessed=2 * count * (2 * rows + value) + 8 * rows * value,
            transcendentals=0,
        )

    tile = spread // shards
    same = lambda i: i
    token_gradient, total = pl.pallas_call(
        spread_kernel,
        out_shape=[shape(rows, model), shape(rows, value, dtype=F32)],
        grid=(shards,),
        in_specs=[
            along(same, tile),
            down(same, tile),
            pl.BlockSpec((1, 3, tile, wide), lambda i: (i, 0, 0, 0)),
            pl.BlockSpec((rank, tile), lambda i: (0, i)),
        ]
        + resident,
        out_specs=[along(same, tile), pl.BlockSpec((rows, value), whole)],
        compiler_params=params(dimension_semantics=("arbitrary",)),
        cost_estimate=cost(spread),
        name="base_spread",
    )(tokens, weight, others, at, grad, rank_grad, lora)

    tile = 512
    steps = swapped // tile
    half = steps // 2
    turned = lambda i, w, f: (i + w[1] * half) % steps
    spot = lambda i, w, f: spread // tile + turned(i, w, f)
    token_gradient, values = pl.pallas_call(
        functools.partial(swap_kernel, steps),
        out_shape=[shape(rows, model), shape(rows, value)],
        grid_spec=pltpu.PrefetchScalarGridSpec(
            num_scalar_prefetch=2,
            grid=(steps,),
            in_specs=[
                along(spot, tile),
                down(spot, tile),
                down(turned, tile),
                down(turned, tile),
                down(lambda i, w, f: jnp.minimum(i, half - 1), tile),
                down(lambda i, w, f: jnp.maximum(i - half, 0), tile),
                pl.BlockSpec((rank, tile), lambda i, w, f: (0, spot(i, w, f))),
            ]
            + resident
            + [ANY],
            out_specs=[along(spot, tile), pl.BlockSpec((rows, value), whole)],
            scratch_shapes=[pltpu.VMEM((rows, value), F32)],
        ),
        input_output_aliases={12: 0},
        compiler_params=params(dimension_semantics=("arbitrary",)),
        cost_estimate=cost(swapped),
        name="base_swapped",
    )(where, fills, tokens, weight, near, far, mine, theirs, at, grad, rank_grad, total, token_gradient)
    return values, token_gradient, grad_down, grad_up


def solution(mesh):
    placed = (
        P(("fsdp", "tok"), None),
        P(None, "fsdp"),
        P("tok", "fsdp"),
        P("tok", "fsdp"),
        P(("fsdp", "tok"), None),
        P(),
        P(),
    )
    return jax.shard_map(
        local,
        mesh=mesh,
        in_specs=placed,
        out_specs=(
            P(("fsdp", "tok"), None),
            P(("fsdp", "tok"), None),
            P("tok", "fsdp"),
            P("tok", "fsdp"),
        ),
        check_vma=False,
    )
```

time: 181 us -> 195 us (1.077)
  starting transfers between devices: 23.6 us -> 37.3 us
  waiting for transfers between devices: 92 us -> 80.1 us
  Pallas kernels: 44.2 us -> 50.8 us
  local copies, waits for them, and re-layouts: 5.49 us -> 9.82 us
    all_to_all x2 -> x4, waiting for transfers between devices: 46.1 us -> 29.6 us  [the longest x2 29.6 us: everywhere(): return lax.all_to_all(a, ('fsdp', 'tok'), split_axis=0, concat_axis=0)]
    all_to_all x2 -> x4, starting transfers between devices: 9.55 us -> 19.9 us  [the longest x2 10.1 us: along_tok(): return lax.all_to_all(a, 'tok', split_axis=0, concat_axis=0)]
    pallas_call x5 -> x8, Pallas kernels: 21.9 us -> 27.5 us  [the longest x1 7.04 us: local(): call(functools.partial(expand_down_kernel, group), shape(cut, columns, dt...]
    ppermute x10, waiting for transfers between devices: 45.9 us -> 50.5 us  [split(): return lambda a: lax.ppermute(a, ('fsdp', 'tok'), pairs)]
    unnamed x16 -> x22, local copies, waits for them, and re-layouts: 3.22 us -> 7.35 us
    ppermute x10, starting transfers between devices: 13.5 us -> 16.9 us  [split(): return lambda a: lax.ppermute(a, ('fsdp', 'tok'), pairs)]
    pallas_call x1, Pallas kernels: 11.3 us -> 13.4 us  [local(): pl.pallas_call(functools.partial(swap_kernel, steps), out_shape=[shape(ro...]
  transfers between devices with their start and end apart: 15 -> 17, of which waited for: 8 -> 7; matrix products, arithmetic and copies ran while one was open for 1% -> 2% of each run, Pallas kernels for 17% -> 18%
where the time goes in v5:
time: 195 us; the launch traced here: 194 us
  waiting for transfers between devices  80.1 us (41%)
  Pallas kernels  50.8 us (26%)
  starting transfers between devices  37.3 us (19%)
  between operations  14.2 us (7%)
  local copies, waits for them, and re-layouts  9.82 us (5%)
  other arithmetic  1.95 us (1%)
    ppermute x10, waiting for transfers between devices, split(): return lambda a: lax.ppermute(a, ('fsdp', 'tok'), pairs)  50.5 us
    all_to_all x2, waiting for transfers between devices, everywhere(): return lax.all_to_all(a, ('fsdp', 'tok'), split_axis=0, concat_axis=0)  29.6 us
    ppermute x10, starting transfers between devices, split(): return lambda a: lax.ppermute(a, ('fsdp', 'tok'), pairs)  16.9 us
    pallas_call x1, Pallas kernels, local(): pl.pallas_call(functools.partial(swap_kernel, steps), out_shape=[shape(ro...  13.4 us
    all_to_all x2, starting transfers between devices, along_tok(): return lax.all_to_all(a, 'tok', split_axis=0, concat_axis=0)  10.1 us
    pallas_call x1, Pallas kernels, local(): pl.pallas_call(spread_kernel, out_shape=[shape(rows, model), shape(rows,...  9.96 us
    all_to_all x2, starting transfers between devices, everywhere(): return lax.all_to_all(a, ('fsdp', 'tok'), split_axis=0, concat_axis=0)  9.82 us
    unnamed x22, local copies, waits for them, and re-layouts  7.35 us
  transfers between devices with their start and end apart: 17, of which 7 were waited for; matrix products, arithmetic and copies ran while one was open for 2% of the time, Pallas kernels for 18%

profile of v5, /device:TPU:0, one launch (start us, length us, event | category | flops | bytes accessed | tf_op | source)
XLA Modules:
  0.0 194.2 jit_solution(16144414178739034638)
XLA Ops:
  7.3 1.6 copy-done.1
  9.6 2.2 %select_sent.1 = (bf16[512,1024]{1,0:T(8,128)(2,1)S(1)}, bf16[384,256]{1,0:T(8,128)(2,1)S(1)}) custom-call(s32[4]{0:T(128)S(1)} %pad_add_fusion.where_ref, s32[64]{0:T(128)S(1)} %copy-done.8, bf16[8192,256]{1,0:T(8,128)(2,1)} %own_ref.3, bf16[1024,1024]{1,0:T(8,128)(2,1)S(1)} %copy-done.1), custom_call_target="tpu_custom_call" | custom-call | tf_op jit(solution)/shard_map/select_sent/pallas_call | solution.py:301
  11.8 3.0 %collective-permute-start.6 = (bf16[384,256]{1,0:T(8,128)(2,1)S(1)}, bf16[384,256]{1,0:T(8,128)(2,1)S(1)}, u32[]{:S(2)}, u32[]{:S(2)}) collective-permute-start(bf16[384,256]{1,0:T(8,128)(2,1)S(1)} %get-tuple-element.28), channel_id=1, source_target_pairs={{0,8},{1,17},{2,10},{3,19},{4,12},{5,21},{6,14},{7,23},{8,0},{9,25... | collective-permute-start | bytes 589832 | tf_op jit(solution)/shard_map/ppermute | solution.py:267
  14.8 1.5 collective-permute-start.7
  16.3 3.7 %collective-permute-done.6 = bf16[384,256]{1,0:T(8,128)(2,1)S(1)} collective-permute-done((bf16[384,256]{1,0:T(8,128)(2,1)S(1)}, bf16[384,256]{1,0:T(8,128)(2,1)S(1)}, u32[]{:S(2)}, u32[]{:S(2)}) %collective-permute-start.6) | collective-permute-done | bytes 196640 | tf_op jit(solution)/shard_map/ppermute | solution.py:267
  20.0 1.6 collective-permute-start.8
  21.6 4.1 %collective-permute-done.8 = bf16[384,256]{1,0:T(8,128)(2,1)S(1)} collective-permute-done((bf16[384,256]{1,0:T(8,128)(2,1)S(1)}, bf16[384,256]{1,0:T(8,128)(2,1)S(1)}, u32[]{:S(2)}, u32[]{:S(2)}) %collective-permute-start.8) | collective-permute-done | bytes 196640 | tf_op jit(solution)/shard_map/ppermute | solution.py:267
  26.6 2.5 %collective-permute-start = (bf16[512,1024]{1,0:T(8,128)(2,1)S(1)}, bf16[512,1024]{1,0:T(8,128)(2,1)S(1)}, u32[]{:S(2)}, u32[]{:S(2)}) collective-permute-start(bf16[512,1024]{1,0:T(8,128)(2,1)S(1)} %get-tuple-element.20), channel_id=1, source_target_pairs={{0,8},{1,17},{2,10},{3,19},{4,12},{5,21},{6,14},{7,23},{8,0},{9,25... | collective-permute-start | bytes 3145736 | tf_op jit(solution)/shard_map/ppermute | solution.py:267
  29.1 2.2 %select_kept.1.keep_ref = bf16[512,1024]{1,0:T(8,128)(2,1)S(1)} custom-call(s32[4]{0:T(128)S(1)} %pad_add_fusion.where_ref, s32[64]{0:T(128)S(1)} %copy-done.8, bf16[1024,1024]{1,0:T(8,128)(2,1)S(1)} %copy-done.2), custom_call_target="tpu_custom_call" | custom-call | tf_op jit(solution)/shard_map/select_kept/pallas_call | solution.py:309
  31.4 10.5 %collective-permute-done.came_ref = bf16[512,1024]{1,0:T(8,128)(2,1)S(1)} collective-permute-done((bf16[512,1024]{1,0:T(8,128)(2,1)S(1)}, bf16[512,1024]{1,0:T(8,128)(2,1)S(1)}, u32[]{:S(2)}, u32[]{:S(2)}) %collective-permute-start) | collective-permute-done | bytes 1048608 | tf_op jit(solution)/shard_map/ppermute | solution.py:267
  41.9 3.3 %sum_and_cut.1 = (bf16[256,1024]{1,0:T(8,128)(2,1)S(1)}, bf16[256,1024]{1,0:T(8,128)(2,1)S(1)}, bf16[5120,256]{1,0:T(8,128)(2,1)}) custom-call(bf16[512,1024]{1,0:T(8,128)(2,1)S(1)} %select_kept.1.keep_ref, bf16[512,1024]{1,0:T(8,128)(2,1)S(1)} %collective-permute-done.came_ref, bf16[8192,256]{1,0:T(8,128)(2,1)} %own_ref.3), custom_call_target="tpu_custom_call" | custom-call | tf_op jit(solution)/shard_map/sum_and_cut/pallas_call | solution.py:316
  45.2 2.1 %collective-permute-start.1 = (bf16[5120,256]{1,0:T(8,128)(2,1)}, bf16[5120,256]{1,0:T(8,128)(2,1)}, u32[]{:S(2)}, u32[]{:S(2)}) collective-permute-start(bf16[5120,256]{1,0:T(8,128)(2,1)} %get-tuple-element.21), channel_id=1, source_target_pairs={{0,8},{1,17},{2,10},{3,19},{4,12},{5,21},{6,14},{7,23},{8,0},{9,25... | collective-permute-start | bytes 7864328 | tf_op jit(solution)/shard_map/ppermute | solution.py:267
  47.2 2.8 %select_up.1 = bf16[1024,128]{1,0:T(8,128)(2,1)} custom-call(s32[4]{0:T(128)S(1)} %pad_add_fusion.where_ref, s32[64]{0:T(128)S(1)} %copy-done.8, bf16[128,1024]{1,0:T(8,128)(2,1)S(1)} %copy-done.6), custom_call_target="tpu_custom_call" | custom-call | tf_op jit(solution)/shard_map/select_up/pallas_call | solution.py:289
  50.0 4.1 %all-to-all-start.1 = ((bf16[32,32,128]{2,1,0:T(8,128)(2,1)}), bf16[32,32,128]{2,1,0:T(8,128)(2,1)S(1)}, u32[]{:S(2)}, u32[]{:S(2)}) async-start(bf16[32,32,128]{2,1,0:T(8,128)(2,1)} %bitcast.5), calls=%async_computation.1 | async-start | bytes 524288 | tf_op jit(solution)/shard_map/all_to_all | solution.py:272
  54.2 26.3 %all-to-all-done.1.maps_ref = bf16[32,32,128]{2,1,0:T(8,128)(2,1)S(1)} async-done(((bf16[32,32,128]{2,1,0:T(8,128)(2,1)}), bf16[32,32,128]{2,1,0:T(8,128)(2,1)S(1)}, u32[]{:S(2)}, u32[]{:S(2)}) %all-to-all-start.1) | async-done | bytes 262176 | tf_op jit(solution)/shard_map/all_to_all | solution.py:272
  80.5 2.2 %copy-done = bf16[256,8192]{1,0:T(8,128)(2,1)S(1)} copy-done((bf16[256,8192]{1,0:T(8,128)(2,1)S(1)}, bf16[256,8192]{1,0:T(8,128)(2,1)}, u32[]{:S(2)}) %copy-start) | copy-done | bytes 4194328
  82.7 2.7 %down_terms.1 = (bf16[256,1024]{1,0:T(8,128)(2,1)S(1)}, bf16[256,32]{1,0:T(8,128)(2,1)S(1)}, bf16[32,1024]{1,0:T(8,128)(2,1)S(1)}, bf16[8,32,1024]{2,1,0:T(8,128)(2,1)}) custom-call(s32[4]{0:T(128)S(1)} %pad_add_fusion.where_ref, s32[64]{0:T(128)S(1)} %copy-done.10, bf16[256,8192]{1,0:T(8,128)(2,1)S(1)} %copy-done, bf16[256,1024]{1,0:T(8,128)(2,1)S(1)} %copy-done.5, ...), custom_call_target="tpu_custom_call" | custom-call | tf_op jit(solution)/shard_map/down_terms/pallas_call | solution.py:325
  85.4 5.0 %all-to-all-start.2 = ((bf16[8,32,1024]{2,1,0:T(8,128)(2,1)}), bf16[8,32,1024]{2,1,0:T(8,128)(2,1)S(1)}, u32[]{:S(2)}, u32[]{:S(2)}) async-start(bf16[8,32,1024]{2,1,0:T(8,128)(2,1)} %get-tuple-element.34), calls=%async_computation.2 | async-start | bytes 1048576 | tf_op jit(solution)/shard_map/all_to_all | solution.py:275
  90.4 2.5 %constant_dynamic-slice_fusion = bf16[2560,256]{1,0:T(8,128)(2,1)} fusion(bf16[5120,256]{1,0:T(8,128)(2,1)} %collective-permute-done.1.near_ref, s32[]{:T(128)S(6)} %select_n.11), kind=kLoop, calls=%fused_computation.2 | loop fusion | bytes 2621444 | tf_op jit(solution)/shard_map/dynamic_slice | solution.py:350
  92.9 1.3 collective-permute-start.3
  95.6 20.7 %collective-permute-done.5 = bf16[256,1024]{1,0:T(8,128)(2,1)S(1)} collective-permute-done((bf16[256,1024]{1,0:T(8,128)(2,1)S(1)}, bf16[256,1024]{1,0:T(8,128)(2,1)S(1)}, u32[]{:S(2)}, u32[]{:S(2)}) %collective-permute-start.5) | collective-permute-done | bytes 524320 | tf_op jit(solution)/shard_map/ppermute | solution.py:267
  117.3 5.1 %all-to-all-start = ((bf16[8,32,1024]{2,1,0:T(8,128)(2,1)}), bf16[8,32,1024]{2,1,0:T(8,128)(2,1)S(1)}, u32[]{:S(2)}, u32[]{:S(2)}) async-start(bf16[8,32,1024]{2,1,0:T(8,128)(2,1)} %bitcast.17), calls=%async_computation | async-start | bytes 1048576 | tf_op jit(solution)/shard_map/all_to_all | solution.py:275
  122.4 1.3 collective-permute-start.9
  124.9 11.5 %collective-permute-done.9.r1_ref = bf16[256,1024]{1,0:T(8,128)(2,1)} collective-permute-done((bf16[256,1024]{1,0:T(8,128)(2,1)S(1)}, bf16[256,1024]{1,0:T(8,128)(2,1)}, u32[]{:S(2)}, u32[]{:S(2)}) %collective-permute-start.9) | collective-permute-done | bytes 524320 | tf_op jit(solution)/shard_map/ppermute | solution.py:267
  136.4 1.3 collective-permute-start.11
  137.8 4.1 %up_terms.1 = (bf16[32,8192]{1,0:T(8,128)(2,1)S(1)}, f32[256,1024]{1,0:T(8,128)S(1)}, bf16[32,32,128]{2,1,0:T(8,128)(2,1)S(1)}) custom-call(s32[4]{0:T(128)S(1)} %pad_add_fusion.where_ref, bf16[256,8192]{1,0:T(8,128)(2,1)} %tokens_ref.7, bf16[8,32,1024]{2,1,0:T(8,128)(2,1)S(1)} %all-to-all-done.maps_ref, bf16[256,1024]{1,0:T(8,128)(2,1)S(1)} %get-tuple-element.24.grad_ref, ...), custom_call_target="tpu_custom_call" | custom-call | tf_op jit(solution)/shard_map/up_terms/pallas_call | solution.py:336
  143.6 5.7 %all-to-all-start.3 = ((bf16[32,32,128]{2,1,0:T(8,128)(2,1)}), bf16[32,32,128]{2,1,0:T(8,128)(2,1)S(1)}, u32[]{:S(2)}, u32[]{:S(2)}) async-start(bf16[32,32,128]{2,1,0:T(8,128)(2,1)} %copy-done.7), calls=%async_computation.3 | async-start | bytes 524288 | tf_op jit(solution)/shard_map/all_to_all | solution.py:272
  149.3 7.0 %expand_down.1 = f32[1024,1024]{1,0:T(8,128)} custom-call(s32[4]{0:T(128)S(1)} %pad_add_fusion.where_ref, s32[64]{0:T(128)S(1)} %copy-done.9, s32[64]{0:T(128)S(1)} %copy-done.10, bf16[256,1024]{1,0:T(8,128)(2,1)S(1)} %bitcast.14, bf16[256,1024]{1,0:T(8,128)(2,1)} %collective-permute-done.9.r1_ref, bf16[256,1024]{1,0:T(8,128)(2,1)} %collective-permute-done.10.r2_ref, ...), custom_call_target="tpu_custom_call" | custom-call | tf_op jit(solution)/shard_map/expand_down/pallas_call | solution.py:357
  156.3 3.3 %all-to-all-done.3 = bf16[32,32,128]{2,1,0:T(8,128)(2,1)S(1)} async-done(((bf16[32,32,128]{2,1,0:T(8,128)(2,1)}), bf16[32,32,128]{2,1,0:T(8,128)(2,1)S(1)}, u32[]{:S(2)}, u32[]{:S(2)}) %all-to-all-start.3) | async-done | bytes 262176 | tf_op jit(solution)/shard_map/all_to_all | solution.py:272
  159.6 3.1 %expand_up.1 = f32[128,1024]{1,0:T(8,128)} custom-call(s32[4]{0:T(128)S(1)} %pad_add_fusion.where_ref, s32[64]{0:T(128)S(1)} %copy-done.9, s32[64]{0:T(128)S(1)} %copy-done.10, bf16[1024,128]{1,0:T(8,128)(2,1)S(1)} %bitcast.15), custom_call_target="tpu_custom_call" | custom-call | tf_op jit(solution)/shard_map/expand_up/pallas_call | solution.py:364
  164.0 10.0 %base_spread.1 = (bf16[256,8192]{1,0:T(8,128)(2,1)}, f32[256,1024]{1,0:T(8,128)S(1)}) custom-call(bf16[256,8192]{1,0:T(8,128)(2,1)} %tokens_ref.7, bf16[8192,256]{1,0:T(8,128)(2,1)} %own_ref.3, bf16[8,3,384,256]{3,2,1,0:T(8,128)(2,1)} %bitcast.16, bf16[32,8192]{1,0:T(8,128)(2,1)S(1)} %get-tuple-element.26.at_ref, ...), custom_call_target="tpu_custom_call" | custom-call | flops 3221225472 | bytes 11534336 | tf_op jit(solution)/shard_map/base_spread/pallas_call | solution.py:390
  173.9 13.4 %base_swapped.1 = (bf16[256,8192]{1,0:T(8,128)(2,1)}, bf16[256,1024]{1,0:T(8,128)(2,1)}) custom-call(s32[4]{0:T(128)S(1)} %pad_add_fusion.where_ref, s32[64]{0:T(128)S(1)} %copy-done.10, bf16[256,8192]{1,0:T(8,128)(2,1)} %tokens_ref.7, bf16[8192,256]{1,0:T(8,128)(2,1)} %own_ref.3, ...), custom_call_target="tpu_custom_call", output_to_operand_aliasing={{0}: (12, {})} | custom-call | flops 5368709120 | bytes 17825792 | tf_op jit(solution)/shard_map/base_swapped/pallas_call | solution.py:412
  (39 shorter events, 8.3 us)
Async XLA Ops:
  7.2 155.6 %all-gather.3.cloned.1.call-start = ((), (), s32[]{:S(2)}) async-start(), calls=%async_computation.4 | async-start | bytes 5308416 | tf_op jit(solution)/shard_map/all_gather | solution.py:346
  7.3 1.6 copy-start.1
  8.9 0.7 copy-start.8
  9.5 19.6 %copy-start.2 = (bf16[1024,1024]{1,0:T(8,128)(2,1)S(1)}, bf16[1024,1024]{1,0:T(8,128)(2,1)}, u32[]{:S(2)}) copy-start(bf16[1024,1024]{1,0:T(8,128)(2,1)} %down_ref.3) | copy-start | bytes 6291460
  11.8 8.2 %collective-permute-start.6 = (bf16[384,256]{1,0:T(8,128)(2,1)S(1)}, bf16[384,256]{1,0:T(8,128)(2,1)S(1)}, u32[]{:S(2)}, u32[]{:S(2)}) collective-permute-start(bf16[384,256]{1,0:T(8,128)(2,1)S(1)} %get-tuple-element.28), channel_id=1, source_target_pairs={{0,8},{1,17},{2,10},{3,19},{4,12},{5,21},{6,14},{7,23},{8,0},{9,25... | collective-permute-start | bytes 589832 | tf_op jit(solution)/shard_map/ppermute | solution.py:267
  14.8 6.8 %collective-permute-start.7 = (bf16[384,256]{1,0:T(8,128)(2,1)S(1)}, bf16[384,256]{1,0:T(8,128)(2,1)S(1)}, u32[]{:S(2)}, u32[]{:S(2)}) collective-permute-start(bf16[384,256]{1,0:T(8,128)(2,1)S(1)} %get-tuple-element.28), channel_id=1, source_target_pairs={{0,16},{1,9},{2,18},{3,11},{4,20},{5,13},{6,22},{7,15},{8,24},{9,1... | collective-permute-start | bytes 589832 | tf_op jit(solution)/shard_map/ppermute | solution.py:267
  20.0 5.7 %collective-permute-start.8 = (bf16[384,256]{1,0:T(8,128)(2,1)S(1)}, bf16[384,256]{1,0:T(8,128)(2,1)S(1)}, u32[]{:S(2)}, u32[]{:S(2)}) collective-permute-start(bf16[384,256]{1,0:T(8,128)(2,1)S(1)} %collective-permute-done.6), channel_id=1, source_target_pairs={{0,16},{1,9},{2,18},{3,11},{4,20},{5,13},{6,22},{7,15},{8,24},{9,1... | collective-permute-start | bytes 589832 | tf_op jit(solution)/shard_map/ppermute | solution.py:267
  26.6 15.3 %collective-permute-start = (bf16[512,1024]{1,0:T(8,128)(2,1)S(1)}, bf16[512,1024]{1,0:T(8,128)(2,1)S(1)}, u32[]{:S(2)}, u32[]{:S(2)}) collective-permute-start(bf16[512,1024]{1,0:T(8,128)(2,1)S(1)} %get-tuple-element.20), channel_id=1, source_target_pairs={{0,8},{1,17},{2,10},{3,19},{4,12},{5,21},{6,14},{7,23},{8,0},{9,25... | collective-permute-start | bytes 3145736 | tf_op jit(solution)/shard_map/ppermute | solution.py:267
  31.4 15.9 %copy-start.6 = (bf16[128,1024]{1,0:T(8,128)(2,1)S(1)}, bf16[128,1024]{1,0:T(8,128)(2,1)}, u32[]{:S(2)}) copy-start(bf16[128,1024]{1,0:T(8,128)(2,1)} %up_ref.1) | copy-start | bytes 786436
  31.4 49.1 %copy-start.5 = (bf16[256,1024]{1,0:T(8,128)(2,1)S(1)}, bf16[256,1024]{1,0:T(8,128)(2,1)}, u32[]{:S(2)}) copy-start(bf16[256,1024]{1,0:T(8,128)(2,1)} %cot_ref.1) | copy-start | bytes 1572868
  31.4 49.1 %copy-start.10 = (s32[64]{0:T(128)S(1)}, s32[64]{0:T(128)}, u32[]{:S(2)}) copy-start(s32[64]{0:T(128)} %fill_ref.7) | copy-start | bytes 772
  45.2 45.2 %collective-permute-start.1 = (bf16[5120,256]{1,0:T(8,128)(2,1)}, bf16[5120,256]{1,0:T(8,128)(2,1)}, u32[]{:S(2)}, u32[]{:S(2)}) collective-permute-start(bf16[5120,256]{1,0:T(8,128)(2,1)} %get-tuple-element.21), channel_id=1, source_target_pairs={{0,8},{1,17},{2,10},{3,19},{4,12},{5,21},{6,14},{7,23},{8,0},{9,25... | collective-permute-start | bytes 7864328 | tf_op jit(solution)/shard_map/ppermute | solution.py:267
  50.0 30.4 %all-to-all-start.1 = ((bf16[32,32,128]{2,1,0:T(8,128)(2,1)}), bf16[32,32,128]{2,1,0:T(8,128)(2,1)S(1)}, u32[]{:S(2)}, u32[]{:S(2)}) async-start(bf16[32,32,128]{2,1,0:T(8,128)(2,1)} %bitcast.5), calls=%async_computation.1 | async-start | bytes 524288 | tf_op jit(solution)/shard_map/all_to_all | solution.py:272
  80.5 2.2 %copy-start = (bf16[256,8192]{1,0:T(8,128)(2,1)S(1)}, bf16[256,8192]{1,0:T(8,128)(2,1)}, u32[]{:S(2)}) copy-start(bf16[256,8192]{1,0:T(8,128)(2,1)} %tokens_ref.7) | copy-start | bytes 12582916
  85.4 31.9 %all-to-all-start.2 = ((bf16[8,32,1024]{2,1,0:T(8,128)(2,1)}), bf16[8,32,1024]{2,1,0:T(8,128)(2,1)S(1)}, u32[]{:S(2)}, u32[]{:S(2)}) async-start(bf16[8,32,1024]{2,1,0:T(8,128)(2,1)} %get-tuple-element.34), calls=%async_computation.2 | async-start | bytes 1048576 | tf_op jit(solution)/shard_map/all_to_all | solution.py:275
  92.9 30.8 %collective-permute-start.3 = (bf16[2560,256]{1,0:T(8,128)(2,1)}, bf16[2560,256]{1,0:T(8,128)(2,1)S(1)}, u32[]{:S(2)}, u32[]{:S(2)}) collective-permute-start(bf16[2560,256]{1,0:T(8,128)(2,1)} %constant_dynamic-slice_fusion), channel_id=1, source_target_pairs={{0,16},{1,9},{2,18},{3,11},{4,20},{5,13},{6,22},{7,15},{8,24},{9,1... | collective-permute-start | bytes 3932168 | tf_op jit(solution)/shard_map/ppermute | solution.py:267
  94.1 79.8 %collective-permute-start.2 = (bf16[5120,256]{1,0:T(8,128)(2,1)}, bf16[5120,256]{1,0:T(8,128)(2,1)}, u32[]{:S(2)}, u32[]{:S(2)}) collective-permute-start(bf16[5120,256]{1,0:T(8,128)(2,1)} %collective-permute-done.1.near_ref), channel_id=1, source_target_pairs={{0,1},{1,0},{2,3},{3,2},{4,5},{5,4},{6,7},{7,6},{8,9},{9,8},{10,11... | collective-permute-start | bytes 7864328 | tf_op jit(solution)/shard_map/ppermute | solution.py:259
  94.4 21.9 %collective-permute-start.5 = (bf16[256,1024]{1,0:T(8,128)(2,1)S(1)}, bf16[256,1024]{1,0:T(8,128)(2,1)S(1)}, u32[]{:S(2)}, u32[]{:S(2)}) collective-permute-start(bf16[256,1024]{1,0:T(8,128)(2,1)S(1)} %get-tuple-element.23), channel_id=1, source_target_pairs={{0,16},{1,9},{2,18},{3,11},{4,20},{5,13},{6,22},{7,15},{8,24},{9,1... | collective-permute-start | bytes 1572872 | tf_op jit(solution)/shard_map/ppermute | solution.py:267
  117.3 20.5 %all-to-all-start = ((bf16[8,32,1024]{2,1,0:T(8,128)(2,1)}), bf16[8,32,1024]{2,1,0:T(8,128)(2,1)S(1)}, u32[]{:S(2)}, u32[]{:S(2)}) async-start(bf16[8,32,1024]{2,1,0:T(8,128)(2,1)} %bitcast.17), calls=%async_computation | async-start | bytes 1048576 | tf_op jit(solution)/shard_map/all_to_all | solution.py:275
  122.4 14.1 %collective-permute-start.9 = (bf16[256,1024]{1,0:T(8,128)(2,1)S(1)}, bf16[256,1024]{1,0:T(8,128)(2,1)}, u32[]{:S(2)}, u32[]{:S(2)}) collective-permute-start(bf16[256,1024]{1,0:T(8,128)(2,1)S(1)} %bitcast.12), channel_id=1, source_target_pairs={{0,8},{1,17},{2,10},{3,19},{4,12},{5,21},{6,14},{7,23},{8,0},{9,25... | collective-permute-start | bytes 1572872 | tf_op jit(solution)/shard_map/ppermute | solution.py:267
  123.7 50.2 %collective-permute-start.4 = (bf16[2560,256]{1,0:T(8,128)(2,1)S(1)}, bf16[2560,256]{1,0:T(8,128)(2,1)}, u32[]{:S(2)}, u32[]{:S(2)}) collective-permute-start(bf16[2560,256]{1,0:T(8,128)(2,1)S(1)} %collective-permute-done.3.mine_ref), channel_id=1, source_target_pairs={{0,1},{1,0},{2,3},{3,2},{4,5},{5,4},{6,7},{7,6},{8,9},{9,8},{10,11... | collective-permute-start | bytes 3932168 | tf_op jit(solution)/shard_map/ppermute | solution.py:259
  123.9 25.4 %collective-permute-start.10 = (bf16[256,1024]{1,0:T(8,128)(2,1)S(1)}, bf16[256,1024]{1,0:T(8,128)(2,1)}, u32[]{:S(2)}, u32[]{:S(2)}) collective-permute-start(bf16[256,1024]{1,0:T(8,128)(2,1)S(1)} %bitcast.13), channel_id=1, source_target_pairs={{0,16},{1,9},{2,18},{3,11},{4,20},{5,13},{6,22},{7,15},{8,24},{9,1... | collective-permute-start | bytes 1572872 | tf_op jit(solution)/shard_map/ppermute | solution.py:267
  136.4 12.8 %collective-permute-start.11 = (bf16[256,1024]{1,0:T(8,128)(2,1)}, bf16[256,1024]{1,0:T(8,128)(2,1)}, u32[]{:S(2)}, u32[]{:S(2)}) collective-permute-start(bf16[256,1024]{1,0:T(8,128)(2,1)} %collective-permute-done.9.r1_ref), channel_id=1, source_target_pairs={{0,16},{1,9},{2,18},{3,11},{4,20},{5,13},{6,22},{7,15},{8,24},{9,1... | collective-permute-start | bytes 1572872 | tf_op jit(solution)/shard_map/ppermute | solution.py:267
  137.8 11.5 %copy-start.9 = (s32[64]{0:T(128)S(1)}, s32[64]{0:T(128)}, u32[]{:S(2)}) copy-start(s32[64]{0:T(128)} %tenant_ref.9) | copy-start | bytes 772
  141.9 1.0 copy-start.3
  142.9 0.7 copy-start.7
  143.6 16.1 %all-to-all-start.3 = ((bf16[32,32,128]{2,1,0:T(8,128)(2,1)}), bf16[32,32,128]{2,1,0:T(8,128)(2,1)S(1)}, u32[]{:S(2)}, u32[]{:S(2)}) async-start(bf16[32,32,128]{2,1,0:T(8,128)(2,1)} %copy-done.7), calls=%async_computation.3 | async-start | bytes 524288 | tf_op jit(solution)/shard_map/all_to_all | solution.py:272
  162.7 1.2 copy-start.4
Sparse Core Ops, SparseCore 0:
  26.7 58.6 all-gather.2

commit v6 on v5

v6 whole, which is shorter than its diff:
```python
import functools

import jax
import jax.numpy as jnp
from jax import lax
from jax.experimental import pallas as pl
from jax.experimental.pallas import tpu as pltpu
from jax.sharding import PartitionSpec as P

ADAPTER_RANK = 16
BLOCK = 128
ADAPTER_SCALE = 2.0
CHUNKS = (3, 3, 2)
VMEM_LIMIT = 48 * 1024 * 1024

F32 = jnp.float32
BF16 = jnp.bfloat16
NT = (((1,), (1,)), ((), ()))
TN = (((0,), (0,)), ((), ()))
SMEM = pl.BlockSpec(memory_space=pltpu.SMEM)
VMEM = pl.BlockSpec(memory_space=pltpu.VMEM)
ANY = pl.BlockSpec(memory_space=pl.ANY)


def dot(a, b, dims=(((1,), (0,)), ((), ()))):
    return lax.dot_general(a, b, dims, preferred_element_type=F32)


def block_rows(tenant_ref, block, shard, columns):
    base = tenant_ref[block] * ADAPTER_RANK - shard * columns
    lane = lax.broadcasted_iota(jnp.int32, (ADAPTER_RANK, columns), 1)
    row = lax.broadcasted_iota(jnp.int32, (ADAPTER_RANK, columns), 0)
    return jnp.where(lane - row == base, 1.0, 0.0)


def fill_pick(tenant_ref, pick_ref, row, first_block, count, shard):
    columns = pick_ref.shape[1]

    @pl.loop(0, count)
    def _(n):
        start = pl.multiple_of(row + n * ADAPTER_RANK, ADAPTER_RANK)
        rows = block_rows(tenant_ref, first_block + n, shard, columns)
        pick_ref[pl.ds(start, ADAPTER_RANK), :] = rows.astype(BF16)


def pick_two(group, tenant_ref, pick_ref, here, others):
    for place, other in enumerate(others):
        fill_pick(tenant_ref, pick_ref, place * group * ADAPTER_RANK, (here ^ other) * group, group, here)


def picked(pick_ref, down_ref, up_ref, out_ref):
    cut = down_ref.shape[0]
    out_ref[:, :cut] = dot(pick_ref[...], down_ref[...], NT).astype(BF16)
    out_ref[:, cut:] = dot(pick_ref[...], up_ref[...], NT).astype(BF16)


def send_select_kernel(group, where_ref, tenant_ref, down_ref, up_ref, out_ref, pick_ref):
    here, core = where_ref[0], where_ref[1]
    pick_two(group, tenant_ref, pick_ref, here, (1 + core, 3))
    picked(pick_ref, down_ref, up_ref, out_ref)


def keep_select_kernel(group, where_ref, tenant_ref, down_ref, up_ref, out_ref, pick_ref):
    here, core = where_ref[0], where_ref[1]
    pick_two(group, tenant_ref, pick_ref, here, (0, 2 - core))
    picked(pick_ref, down_ref, up_ref, out_ref)


def sum_kernel(start, keep_ref, came_ref, weight_ref, keep_out_ref, send_out_ref, piece_ref, sem):
    copy = pltpu.make_async_copy(weight_ref.at[pl.ds(start, piece_ref.shape[0]), :], piece_ref, sem)
    copy.start()
    rows = keep_out_ref.shape[0]
    send_out_ref[...] = keep_ref[rows:, :] + came_ref[rows:, :]
    keep_out_ref[...] = keep_ref[:rows, :] + came_ref[:rows, :]
    copy.wait()


def cut_kernel(start, where_ref, near_ref, weight_ref, half_ref, *refs):
    *piece_refs, sems = refs
    half = half_ref.shape[0]
    at = pl.multiple_of(where_ref[1] * half, half)
    copies = [pltpu.make_async_copy(near_ref.at[pl.ds(at, half), :], half_ref, sems.at[0])]
    for piece_ref in piece_refs:
        copies.append(
            pltpu.make_async_copy(weight_ref.at[pl.ds(start, piece_ref.shape[0]), :], piece_ref, sems.at[1])
        )
    for copy in copies:
        copy.start()
    for copy in copies:
        copy.wait()


def block_diagonal(a):
    own = (
        lax.broadcasted_iota(jnp.int32, a.shape, 0) // BLOCK
        == lax.broadcasted_iota(jnp.int32, a.shape, 1) // ADAPTER_RANK
    )
    return jnp.where(own, a, 0.0).astype(BF16)


def rank_kernel(
    where_ref, fill_ref, tokens_ref, cot_ref, maps_ref,
    grad_ref, rg_ref, at_ref, lora_ref, terms_ref, full_ref, up_ref
):
    rows, value = cot_ref.shape
    shards, _, both = maps_ref.shape
    cut = at_ref.shape[1] // shards
    width = both - cut
    wide = value // 4
    here, first = where_ref[0], where_ref[2]
    turned = [pl.ds(pl.multiple_of((here ^ n) * wide, wide), wide) for n in range(4)]
    for s in range(shards):
        full_ref[:, s * width : (s + 1) * width] = maps_ref[s, :, cut:]
        at_ref[:, s * cut : (s + 1) * cut] = maps_ref[s, :, :cut]
    for n, place in enumerate(turned):
        up_ref[:, n * wide : (n + 1) * wide] = full_ref[:, place]
        for block in range(rows // BLOCK):
            span = slice(block * BLOCK, (block + 1) * BLOCK)
            part = cot_ref[span, place]
            row = lax.broadcasted_iota(jnp.int32, part.shape, 0)
            grad_ref[span, n * wide : (n + 1) * wide] = jnp.where(
                row < fill_ref[first + block], part, jnp.zeros_like(part)
            )
    rank_grad = block_diagonal(ADAPTER_SCALE * dot(grad_ref[...], up_ref[...], NT))
    rg_ref[...] = rank_grad
    rank_in = block_diagonal(dot(tokens_ref[...], at_ref[...], NT))
    lora_ref[...] = (ADAPTER_SCALE * dot(rank_in, up_ref[...])).astype(BF16)
    up_terms = (ADAPTER_SCALE * dot(rank_in, grad_ref[...], TN)).astype(BF16)
    for n, place in enumerate(turned):
        full_ref[:, place] = up_terms[:, n * wide : (n + 1) * wide]
    for s in range(shards):
        terms_ref[s, :, :cut] = dot(rank_grad, tokens_ref[:, s * cut : (s + 1) * cut], TN).astype(BF16)
        terms_ref[s, :, cut:] = full_ref[:, s * width : (s + 1) * width]


def base_tile(core, tokens_ref, own, near, far, last, at_ref, grad_ref, rg_ref, out_ref, acc_ref):
    one, two = jnp.where(core == 0, near, far), jnp.where(core == 0, far, near)
    weight = jnp.concatenate([own, one, two, last], axis=1)
    back = dot(rg_ref[...], at_ref[...]).astype(BF16).astype(F32)
    out_ref[...] = (back + dot(grad_ref[...], weight, NT)).astype(BF16)
    acc_ref[...] += dot(tokens_ref[...], weight)


def base_kernel(
    steps, final, where_ref, fill_ref, tokens_ref, own_ref, near_ref, far_ref, mine_ref, theirs_ref,
    at_ref, grad_ref, rg_ref, sum_ref, *refs
):
    out_ref, total_ref = refs[-3:-1] if final else refs[-2:]
    acc_ref = refs[-1]
    i = pl.program_id(0)
    here, core, first = where_ref[0], where_ref[1], where_ref[2]

    @pl.when(i == 0)
    def _():
        acc_ref[...] = sum_ref[...].astype(F32)

    last = jnp.where(i < steps // 2, mine_ref[...], theirs_ref[...])
    base_tile(
        core, tokens_ref, own_ref[...], near_ref[...], far_ref[...], last,
        at_ref, grad_ref, rg_ref, out_ref, acc_ref,
    )

    if final:

        @pl.when(i == steps - 1)
        def _():
            wide = own_ref.shape[1]
            for n in range(total_ref.shape[0] // BLOCK):
                span = slice(n * BLOCK, (n + 1) * BLOCK)
                for other in range(total_ref.shape[1] // wide):
                    part = acc_ref[span, other * wide : (other + 1) * wide]
                    row = lax.broadcasted_iota(jnp.int32, part.shape, 0)
                    total_ref[span, pl.ds(pl.multiple_of((here ^ other) * wide, wide), wide)] = jnp.where(
                        row < fill_ref[first + n], part, 0.0
                    ).astype(BF16)


def fill_expand(tenant_ref, fill_ref, pick_ref, scale_ref, row, first, count, shard):
    columns = pick_ref.shape[1]

    @pl.loop(0, count)
    def _(n):
        start = pl.multiple_of(row + n * ADAPTER_RANK, ADAPTER_RANK)
        part = block_rows(tenant_ref, first + n, shard, columns)
        pick_ref[pl.ds(start, ADAPTER_RANK), :] = part.astype(BF16)
        scale_ref[...] += part * fill_ref[first + n].astype(F32)


def tenant_scale(scale_ref):
    return 1.0 / jnp.maximum(jnp.sum(scale_ref[...], axis=0, keepdims=True), 1.0)


def expand_kernel(
    group, where_ref, tenant_ref, fill_ref, r0_ref, r1_ref, r2_ref, r3_ref, down_ref, up_ref, pick_ref, scale_ref
):
    here, core = where_ref[0], where_ref[1]
    rows = group * ADAPTER_RANK
    scale_ref[...] = jnp.zeros_like(scale_ref)
    for place, other in enumerate((0, 1 + core, 2 - core, 3)):
        fill_expand(
            tenant_ref, fill_ref, pick_ref, scale_ref, place * rows, (here ^ other) * group, group, here
        )
    scale = tenant_scale(scale_ref)
    cut, both = down_ref.shape[0], r0_ref.shape[1]

    def means(lo, hi):
        terms = jnp.concatenate([ref[:, lo:hi] for ref in (r0_ref, r1_ref, r2_ref, r3_ref)], axis=0)
        return dot(terms, pick_ref[...], TN) * scale

    step = min(cut, 256)
    for lo in range(0, cut, step):
        down_ref[lo : lo + step, :] = means(lo, lo + step)
    up_ref[...] = means(cut, both)


def after(body, place, *tokens):
    return lambda *refs: body(*refs[:place], *refs[place + len(tokens) :])


def params(**extra):
    return pltpu.CompilerParams(vmem_limit_bytes=VMEM_LIMIT, **extra)


def shape(*dims, dtype=BF16):
    return jax.ShapeDtypeStruct(dims, dtype)


def local(tokens, weight, down_maps, up_maps, cotangent, tenants, fills):
    shards = lax.axis_size("tok")
    groups = lax.axis_size("fsdp")
    devices = groups * shards
    rows, model = tokens.shape
    value = cotangent.shape[1]
    wide = weight.shape[1]
    cut, columns = down_maps.shape
    width = up_maps.shape[0]
    dev_blocks = rows // BLOCK
    group = dev_blocks * shards
    rank = dev_blocks * ADAPTER_RANK
    group_rank = group * ADAPTER_RANK
    here = lax.axis_index("fsdp")
    tok_here = lax.axis_index("tok")
    core = tok_here % 2
    where = jnp.stack([here, core, (here * shards + tok_here) * dev_blocks, tok_here]).astype(jnp.int32)

    def on_core(a):
        return lax.ppermute(a, "tok", [(t, t ^ 1) for t in range(shards)])

    def split(first, second):
        pairs = [
            (f * shards + t, (f ^ (second if t % 2 else first)) * shards + t)
            for f in range(groups)
            for t in range(shards)
        ]
        return lambda a: lax.ppermute(a, ("fsdp", "tok"), pairs)

    first_way, second_way = split(1, 2), split(2, 1)

    def along_tok(a):
        return lax.all_to_all(a, "tok", split_axis=0, concat_axis=0)

    def call(body, out_shape, in_specs, name, scratch=(), out_specs=None, **extra):
        return pl.pallas_call(
            body,
            out_shape=out_shape,
            in_specs=in_specs,
            out_specs=out_specs or jax.tree.map(lambda _: VMEM, out_shape),
            scratch_shapes=list(scratch),
            compiler_params=params(),
            name=name,
            **extra,
        )

    parts = [(model // 8 * sum(CHUNKS[:k]), model // 8 * size) for k, size in enumerate(CHUNKS)]
    both = cut + width
    pick = pltpu.VMEM((2 * group_rank, columns), BF16)
    sent = call(
        functools.partial(send_select_kernel, group),
        shape(2 * group_rank, both),
        [SMEM, SMEM, VMEM, VMEM],
        "select_sent",
        [pick],
    )(where, tenants, down_maps, up_maps)
    came = first_way(sent)
    kept = call(
        after(functools.partial(keep_select_kernel, group), 4, sent),
        shape(2 * group_rank, both),
        [SMEM, SMEM, VMEM, VMEM, ANY],
        "select_kept",
        [pick],
    )(where, tenants, down_maps, up_maps, sent)
    keep, sent, piece = call(
        functools.partial(sum_kernel, parts[0][0]),
        [shape(group_rank, both), shape(group_rank, both), shape(parts[0][1], wide)],
        [VMEM, VMEM, ANY],
        "sum_and_cut",
        [pltpu.SemaphoreType.DMA],
    )(kept, came, weight)
    maps = along_tok((keep + second_way(sent)).reshape(shards, rank, both))

    arrived, pieces = [], []
    for k, (_, size) in enumerate(parts):
        near = first_way(piece)
        far = on_core(near)
        nexts = parts[k + 1 : k + 2]
        part, *cuts = call(
            functools.partial(cut_kernel, nexts[0][0] if nexts else 0),
            [shape(size // 2, wide)] + [shape(n, wide) for _, n in nexts],
            [SMEM, ANY, ANY],
            "cut_chunk",
            [pltpu.SemaphoreType.DMA((2,))],
        )(where, near, weight)
        mine = second_way(part)
        arrived.append((near, far, mine, on_core(mine)))
        pieces.append(part)
        if cuts:
            piece = cuts[0]

    grad, rank_grad, at, lora, terms = call(
        after(rank_kernel, 5, pieces[0]),
        [
            shape(rows, value),
            shape(rows, rank),
            shape(rank, model),
            shape(rows, value),
            shape(shards, rank, both),
        ],
        [SMEM, SMEM, VMEM, VMEM, VMEM, ANY],
        "rank_space",
        [pltpu.VMEM((rank, value), BF16)] * 2,
    )(where, fills, tokens, cotangent, maps, pieces[0])
    r0 = along_tok(terms).reshape(group_rank, both)
    r1, r2 = first_way(r0), second_way(r0)
    r3 = second_way(r1)

    whole = lambda i, *refs: (0, 0)
    along = lambda spot, tile: pl.BlockSpec((rows, tile), lambda i, *refs: (0, spot(i, *refs)))
    down = lambda spot, tile: pl.BlockSpec((tile, wide), lambda i, *refs: (spot(i, *refs), 0))
    resident = [
        pl.BlockSpec((rows, value), whole),
        pl.BlockSpec((rows, rank), whole),
        pl.BlockSpec((rows, value), whole),
    ]

    def cost(count):
        return pl.CostEstimate(
            flops=4 * rows * count * value,
            bytes_accessed=2 * count * (2 * rows + value) + 8 * rows * value,
            transcendentals=0,
        )

    tile = 512
    total, token_gradient, grad_down = lora, None, None
    for k, ((start, size), (near, far, mine, theirs)) in enumerate(zip(parts, arrived)):
        final = k == len(parts) - 1
        steps = size // tile
        half = steps // 2
        if final:
            grad_down, grad_up = call(
                after(functools.partial(expand_kernel, group), 7, total),
                [shape(cut, columns, dtype=F32), shape(width, columns, dtype=F32)],
                [SMEM, SMEM, SMEM] + [VMEM] * 4 + [ANY],
                "expand",
                [pltpu.VMEM((devices * rank, columns), BF16), pltpu.VMEM((ADAPTER_RANK, columns), F32)],
            )(where, tenants, fills, r0, r1, r2, r3, total)
        turned = lambda i, w, f, half=half, steps=steps: (i + w[1] * half) % steps
        spot = lambda i, w, f, start=start, turned=turned: start // tile + turned(i, w, f)
        extra = [a for a in (token_gradient, grad_down, pieces[1] if k == 0 else None) if a is not None]
        token_gradient, total = pl.pallas_call(
            functools.partial(base_kernel, steps, final),
            out_shape=[shape(rows, model), shape(rows, value, dtype=BF16 if final else F32)],
            grid_spec=pltpu.PrefetchScalarGridSpec(
                num_scalar_prefetch=2,
                grid=(steps,),
                in_specs=[
                    along(spot, tile),
                    down(spot, tile),
                    down(turned, tile),
                    down(turned, tile),
                    down(lambda i, w, f, half=half: jnp.minimum(i, half - 1), tile),
                    down(lambda i, w, f, half=half: jnp.maximum(i - half, 0), tile),
                    pl.BlockSpec((rank, tile), lambda i, w, f, spot=spot: (0, spot(i, w, f))),
                ]
                + resident
                + [ANY] * len(extra),
                out_specs=[along(spot, tile), pl.BlockSpec((rows, value), whole)],
                scratch_shapes=[pltpu.VMEM((rows, value), F32)] if final else [],
            ),
            input_output_aliases={12: 0} if k else {},
            compiler_params=params(dimension_semantics=("arbitrary",)),
            cost_estimate=cost(size),
            name="base_chunk",
        )(where, fills, tokens, weight, near, far, mine, theirs, at, grad, rank_grad, total, *extra)
    return total, token_gradient, grad_down, grad_up


def solution(mesh):
    placed = (
        P(("fsdp", "tok"), None),
        P(None, "fsdp"),
        P("tok", "fsdp"),
        P("tok", "fsdp"),
        P(("fsdp", "tok"), None),
        P(),
        P(),
    )
    return jax.shard_map(
        local,
        mesh=mesh,
        in_specs=placed,
        out_specs=(
            P(("fsdp", "tok"), None),
            P(("fsdp", "tok"), None),
            P("tok", "fsdp"),
            P("tok", "fsdp"),
        ),
        check_vma=False,
    )
```

time: 195 us -> 170 us (0.87)
  between operations: 14.2 us -> 0.8 us
  starting transfers between devices: 37.3 us -> 24.2 us
  local copies, waits for them, and re-layouts: 9.82 us -> 12.6 us
    all_to_all x2 -> x0, waiting for transfers between devices: 29.6 us -> none  [everywhere(): return lax.all_to_all(a, ('fsdp', 'tok'), split_axis=0, concat_axis=0)]
    ppermute x10 -> x11, waiting for transfers between devices: 50.5 us -> 75.4 us  [split(): return lambda a: lax.ppermute(a, ('fsdp', 'tok'), pairs)]
    all_to_all x2 -> x0, starting transfers between devices: 9.82 us -> none  [everywhere(): return lax.all_to_all(a, ('fsdp', 'tok'), split_axis=0, concat_axis=0)]
    unnamed x22 -> x40, local copies, waits for them, and re-layouts: 7.35 us -> 12.6 us
    all_to_all x2, waiting for transfers between devices: 0.01 us -> 4.56 us  [along_tok(): return lax.all_to_all(a, 'tok', split_axis=0, concat_axis=0)]
    ppermute x10 -> x11, starting transfers between devices: 16.9 us -> 13.8 us  [split(): return lambda a: lax.ppermute(a, ('fsdp', 'tok'), pairs)]
    dynamic_slice x1 -> x0, local copies, waits for them, and re-layouts: 2.46 us -> none  [local(): lax.dynamic_slice_in_dim(near, core * (swapped // 2), swapped // 2, axis=0)]
    pallas_call x10 -> x11, Pallas kernels: 50.8 us -> 50.6 us  [the longest x3 23.6 us: local(): pl.pallas_call(functools.partial(base_kernel, steps, final), out_shape=[s...]
  transfers between devices with their start and end apart: 17 -> 19, of which waited for: 7 -> 6; matrix products, arithmetic and copies ran while one was open for 2% -> 1% of each run, Pallas kernels for 18% -> 24%
where the time goes in v6:
time: 170 us; the launch traced here: 169 us
  waiting for transfers between devices  80 us (47%)
  Pallas kernels  50.6 us (30%)
  starting transfers between devices  24.2 us (14%)
  local copies, waits for them, and re-layouts  12.6 us (7%)
    ppermute x11, waiting for transfers between devices, split(): return lambda a: lax.ppermute(a, ('fsdp', 'tok'), pairs)  75.4 us
    pallas_call x3, Pallas kernels, local(): pl.pallas_call(functools.partial(base_kernel, steps, final), out_shape=[s...  23.6 us
    ppermute x11, starting transfers between devices, split(): return lambda a: lax.ppermute(a, ('fsdp', 'tok'), pairs)  13.8 us
    unnamed x40, local copies, waits for them, and re-layouts  12.6 us
    all_to_all x2, starting transfers between devices, along_tok(): return lax.all_to_all(a, 'tok', split_axis=0, concat_axis=0)  9.76 us
    pallas_call x3, Pallas kernels, local(): call(functools.partial(cut_kernel, nexts[0][0] if nexts else 0), [shape(s...  7.73 us
    pallas_call x1, Pallas kernels, local(): call(after(functools.partial(expand_kernel, group), 7, total), [shape(cut...  6.92 us
    pallas_call x1, Pallas kernels, local(): call(after(rank_kernel, 5, pieces[0]), [shape(rows, value), shape(rows, r...  5.91 us
  transfers between devices with their start and end apart: 19, of which 6 were waited for; matrix products, arithmetic and copies ran while one was open for 1% of the time, Pallas kernels for 24%

profile of v6, /device:TPU:0, one launch (start us, length us, event | category | flops | bytes accessed | tf_op | source)
XLA Modules:
  0.0 169.3 jit_solution(8287417560482748925)
XLA Ops:
  0.7 1.6 copy-done.1
  2.3 0.9 copy-done.8
  3.9 2.5 %select_sent.1.refs_4_ = bf16[512,1152]{1,0:T(8,128)(2,1)S(1)} custom-call(s32[4]{0:T(128)S(1)} %pad_add_fusion.where_ref.refs_0_, s32[64]{0:T(128)S(1)} %copy-done.18, bf16[1024,1024]{1,0:T(8,128)(2,1)S(1)} %copy-done.1, bf16[128,1024]{1,0:T(8,128)(2,1)S(1)} %copy-done.8), custom_call_target="tpu_custom_call" | custom-call | tf_op jit(solution)/shard_map/select_sent/pallas_call | solution.py:277
  6.4 3.0 %collective-permute-start = (bf16[512,1152]{1,0:T(8,128)(2,1)S(1)}, bf16[512,1152]{1,0:T(8,128)(2,1)S(1)}, u32[]{:S(2)}, u32[]{:S(2)}) collective-permute-start(bf16[512,1152]{1,0:T(8,128)(2,1)S(1)} %select_sent.1.refs_4_), channel_id=1, source_target_pairs={{0,8},{1,17},{2,10},{3,19},{4,12},{5,21},{6,14},{7,23},{8,0},{9,25... | collective-permute-start | bytes 3538952 | tf_op jit(solution)/shard_map/ppermute | solution.py:255
  9.4 2.5 %select_kept.1.keep_ref = bf16[512,1152]{1,0:T(8,128)(2,1)S(1)} custom-call(s32[4]{0:T(128)S(1)} %pad_add_fusion.where_ref.refs_0_, s32[64]{0:T(128)S(1)} %copy-done.19, bf16[1024,1024]{1,0:T(8,128)(2,1)S(1)} %copy-done.1, bf16[128,1024]{1,0:T(8,128)(2,1)S(1)} %copy-done.8, bf16[512,1152]{1,0:T(8,128)(2,1)S(1)} %select_sent.1.refs_4_), custom_call_target="tpu_custom_call" | custom-call | tf_op jit(solution)/shard_map/select_kept/pallas_call | solution.py:285
  11.9 11.7 %collective-permute-done.came_ref = bf16[512,1152]{1,0:T(8,128)(2,1)S(1)} collective-permute-done((bf16[512,1152]{1,0:T(8,128)(2,1)S(1)}, bf16[512,1152]{1,0:T(8,128)(2,1)S(1)}, u32[]{:S(2)}, u32[]{:S(2)}) %collective-permute-start) | collective-permute-done | bytes 1179680 | tf_op jit(solution)/shard_map/ppermute | solution.py:255
  23.6 1.4 sum_and_cut.1
  25.0 2.1 %collective-permute-start.1 = (bf16[3072,256]{1,0:T(8,128)(2,1)S(1)}, bf16[3072,256]{1,0:T(8,128)(2,1)S(1)}, u32[]{:S(2)}, u32[]{:S(2)}) collective-permute-start(bf16[3072,256]{1,0:T(8,128)(2,1)S(1)} %get-tuple-element.24), channel_id=1, source_target_pairs={{0,8},{1,17},{2,10},{3,19},{4,12},{5,21},{6,14},{7,23},{8,0},{9,25... | collective-permute-start | bytes 4718600 | tf_op jit(solution)/shard_map/ppermute | solution.py:255
  27.1 1.5 collective-permute-start.7
  28.6 23.0 %collective-permute-done.1.near_ref = bf16[3072,256]{1,0:T(8,128)(2,1)S(1)} collective-permute-done((bf16[3072,256]{1,0:T(8,128)(2,1)S(1)}, bf16[3072,256]{1,0:T(8,128)(2,1)S(1)}, u32[]{:S(2)}, u32[]{:S(2)}) %collective-permute-start.1) | collective-permute-done | bytes 1572896 | tf_op jit(solution)/shard_map/ppermute | solution.py:255
  51.6 3.2 %cut_chunk.3 = (bf16[1536,256]{1,0:T(8,128)(2,1)S(1)}, bf16[3072,256]{1,0:T(8,128)(2,1)}) custom-call(s32[4]{0:T(128)S(1)} %pad_add_fusion.where_ref.refs_0_, bf16[3072,256]{1,0:T(8,128)(2,1)S(1)} %collective-permute-done.1.near_ref, bf16[8192,256]{1,0:T(8,128)(2,1)} %own_ref.5), custom_call_target="tpu_custom_call" | custom-call | tf_op jit(solution)/shard_map/cut_chunk/pallas_call | solution.py:306
  55.7 1.5 collective-permute-start.2
  57.2 1.0 add.12
  58.2 4.9 %all-to-all-start = ((bf16[8,32,1152]{2,1,0:T(8,128)(2,1)}), bf16[8,32,1152]{2,1,0:T(8,128)(2,1)}, u32[]{:S(2)}, u32[]{:S(2)}) async-start(bf16[8,32,1152]{2,1,0:T(8,128)(2,1)} %bitcast.6), calls=%async_computation | async-start | bytes 1179648 | tf_op jit(solution)/shard_map/all_to_all | solution.py:260
  63.8 20.9 %collective-permute-done.2.near_ref = bf16[3072,256]{1,0:T(8,128)(2,1)S(1)} collective-permute-done((bf16[3072,256]{1,0:T(8,128)(2,1)}, bf16[3072,256]{1,0:T(8,128)(2,1)S(1)}, u32[]{:S(2)}, u32[]{:S(2)}) %collective-permute-start.2) | collective-permute-done | bytes 1572896 | tf_op jit(solution)/shard_map/ppermute | solution.py:255
  84.7 2.8 %cut_chunk.4 = (bf16[1536,256]{1,0:T(8,128)(2,1)S(1)}, bf16[2048,256]{1,0:T(8,128)(2,1)}) custom-call(s32[4]{0:T(128)S(1)} %pad_add_fusion.where_ref.refs_0_, bf16[3072,256]{1,0:T(8,128)(2,1)S(1)} %collective-permute-done.2.near_ref, bf16[8192,256]{1,0:T(8,128)(2,1)} %own_ref.5), custom_call_target="tpu_custom_call" | custom-call | tf_op jit(solution)/shard_map/cut_chunk/pallas_call | solution.py:306
  87.6 0.9 copy-done.9
  88.4 1.5 collective-permute-start.3
  89.9 1.1 copy-done.12
  91.1 1.0 copy-done.14
  92.1 5.9 %rank_space.1 = (bf16[256,1024]{1,0:T(8,128)(2,1)S(1)}, bf16[256,32]{1,0:T(8,128)(2,1)S(1)}, bf16[32,8192]{1,0:T(8,128)(2,1)S(1)}, bf16[256,1024]{1,0:T(8,128)(2,1)S(1)}, bf16[8,32,1152]{2,1,0:T(8,128)(2,1)S(1)}) custom-call(s32[4]{0:T(128)S(1)} %pad_add_fusion.where_ref.refs_0_, s32[64]{0:T(128)S(1)} %copy-done.17, bf16[256,8192]{1,0:T(8,128)(2,1)} %tokens_ref.5, ...), custom_call_target="tpu_custom_call" | custom-call | tf_op jit(solution)/shard_map/rank_space/pallas_call | solution.py:319
  101.3 4.9 %all-to-all-start.1 = ((bf16[8,32,1152]{2,1,0:T(8,128)(2,1)}), bf16[8,32,1152]{2,1,0:T(8,128)(2,1)}, u32[]{:S(2)}, u32[]{:S(2)}) async-start(bf16[8,32,1152]{2,1,0:T(8,128)(2,1)} %copy-done.13), calls=%async_computation.1 | async-start | bytes 1179648 | tf_op jit(solution)/shard_map/all_to_all | solution.py:260
  107.2 11.3 %collective-permute-done.9.mine_ref = bf16[1536,256]{1,0:T(8,128)(2,1)} collective-permute-done((bf16[1536,256]{1,0:T(8,128)(2,1)}, bf16[1536,256]{1,0:T(8,128)(2,1)}, u32[]{:S(2)}, u32[]{:S(2)}) %collective-permute-start.9) | collective-permute-done | bytes 786464 | tf_op jit(solution)/shard_map/ppermute | solution.py:255
  118.5 4.6 %all-to-all-done.1 = bf16[8,32,1152]{2,1,0:T(8,128)(2,1)} async-done(((bf16[8,32,1152]{2,1,0:T(8,128)(2,1)}), bf16[8,32,1152]{2,1,0:T(8,128)(2,1)}, u32[]{:S(2)}, u32[]{:S(2)}) %all-to-all-start.1) | async-done | bytes 589856 | tf_op jit(solution)/shard_map/all_to_all | solution.py:260
  123.5 2.2 %copy-done = bf16[8192,256]{1,0:T(8,128)(2,1)S(1)} copy-done((bf16[8192,256]{1,0:T(8,128)(2,1)S(1)}, bf16[8192,256]{1,0:T(8,128)(2,1)}, u32[]{:S(2)}) %copy-start) | copy-done | bytes 4194328
  125.7 1.8 %cut_chunk.5 = bf16[1024,256]{1,0:T(8,128)(2,1)S(1)} custom-call(s32[4]{0:T(128)S(1)} %pad_add_fusion.where_ref.refs_0_, bf16[2048,256]{1,0:T(8,128)(2,1)} %collective-permute-done.3.near_ref, bf16[8192,256]{1,0:T(8,128)(2,1)S(1)} %copy-done), custom_call_target="tpu_custom_call" | custom-call | tf_op jit(solution)/shard_map/cut_chunk/pallas_call | solution.py:306
  128.1 8.5 %collective-permute-done.14.refs_4_ = bf16[256,1152]{1,0:T(8,128)(2,1)S(1)} collective-permute-done((bf16[256,1152]{1,0:T(8,128)(2,1)}, bf16[256,1152]{1,0:T(8,128)(2,1)S(1)}, u32[]{:S(2)}, u32[]{:S(2)}) %collective-permute-start.14) | collective-permute-done | bytes 589856 | tf_op jit(solution)/shard_map/ppermute | solution.py:255
  136.6 2.0 %collective-permute-start.16 = (bf16[256,1152]{1,0:T(8,128)(2,1)S(1)}, bf16[256,1152]{1,0:T(8,128)(2,1)S(1)}, u32[]{:S(2)}, u32[]{:S(2)}) collective-permute-start(bf16[256,1152]{1,0:T(8,128)(2,1)S(1)} %collective-permute-done.14.refs_4_), channel_id=1, source_target_pairs={{0,16},{1,9},{2,18},{3,11},{4,20},{5,13},{6,22},{7,15},{8,24},{9,1... | collective-permute-start | bytes 1769480 | tf_op jit(solution)/shard_map/ppermute | solution.py:255
  138.7 8.6 %base_chunk.3 = (bf16[256,8192]{1,0:T(8,128)(2,1)}, f32[256,1024]{1,0:T(8,128)S(1)}) custom-call(s32[4]{0:T(128)S(1)} %pad_add_fusion.where_ref.refs_0_, s32[64]{0:T(128)S(1)} %copy-done.17, bf16[256,8192]{1,0:T(8,128)(2,1)} %tokens_ref.5, bf16[8192,256]{1,0:T(8,128)(2,1)} %own_ref.5, bf16[3072,256]{1,0:T(8,128)(2,1)} %copy-done.2, ...), custom_call_target="tpu_custom_call" | custom-call | flops 3221225472 | bytes 11534336 | tf_op jit(solution)/shard_map/base_chunk/pallas_call | solution.py:369
  147.3 8.5 %base_chunk.4 = (bf16[256,8192]{1,0:T(8,128)(2,1)}, f32[256,1024]{1,0:T(8,128)S(1)}) custom-call(s32[4]{0:T(128)S(1)} %pad_add_fusion.where_ref.refs_0_, s32[64]{0:T(128)S(1)} %copy-done.17, bf16[256,8192]{1,0:T(8,128)(2,1)} %tokens_ref.5, bf16[8192,256]{1,0:T(8,128)(2,1)} %own_ref.5, bf16[3072,256]{1,0:T(8,128)(2,1)} %copy-done.3, ...), custom_call_target="tpu_custom_call", output_to_operand_aliasing={{0}: (12, {})} | custom-call | flops 3221225472 | bytes 11534336 | tf_op jit(solution)/shard_map/base_chunk/pallas_call | solution.py:369
  155.9 6.9 %expand.1 = (f32[1024,1024]{1,0:T(8,128)}, f32[128,1024]{1,0:T(8,128)}) custom-call(s32[4]{0:T(128)S(1)} %pad_add_fusion.where_ref.refs_0_, s32[64]{0:T(128)S(1)} %copy-done.19, s32[64]{0:T(128)S(1)} %copy-done.17, bf16[256,1152]{1,0:T(8,128)(2,1)} %bitcast.5.refs_3_, bf16[256,1152]{1,0:T(8,128)(2,1)S(1)} %collective-permute-done.14.refs_4_, ...), custom_call_target="tpu_custom_call" | custom-call | tf_op jit(solution)/shard_map/expand/pallas_call | solution.py:359
  162.8 6.5 %base_chunk.5 = (bf16[256,8192]{1,0:T(8,128)(2,1)}, bf16[256,1024]{1,0:T(8,128)(2,1)}) custom-call(s32[4]{0:T(128)S(1)} %pad_add_fusion.where_ref.refs_0_, s32[64]{0:T(128)S(1)} %copy-done.17, bf16[256,8192]{1,0:T(8,128)(2,1)} %tokens_ref.5, bf16[8192,256]{1,0:T(8,128)(2,1)} %own_ref.5, ...), custom_call_target="tpu_custom_call", output_to_operand_aliasing={{0}: (12, {})} | custom-call | flops 2147483648 | bytes 8388608 | tf_op jit(solution)/shard_map/base_chunk/pallas_call | solution.py:369
  (59 shorter events, 7.8 us)
Async XLA Ops:
  0.7 1.6 copy-start.1
  2.3 0.9 copy-start.8
  3.9 5.5 %copy-start.19 = (s32[64]{0:T(128)S(1)}, s32[64]{0:T(128)}, u32[]{:S(2)}) copy-start(s32[64]{0:T(128)} %refs_1_.5) | copy-start | bytes 772
  6.4 17.2 %collective-permute-start = (bf16[512,1152]{1,0:T(8,128)(2,1)S(1)}, bf16[512,1152]{1,0:T(8,128)(2,1)S(1)}, u32[]{:S(2)}, u32[]{:S(2)}) collective-permute-start(bf16[512,1152]{1,0:T(8,128)(2,1)S(1)} %select_sent.1.refs_4_), channel_id=1, source_target_pairs={{0,8},{1,17},{2,10},{3,19},{4,12},{5,21},{6,14},{7,23},{8,0},{9,25... | collective-permute-start | bytes 3538952 | tf_op jit(solution)/shard_map/ppermute | solution.py:255
  25.0 26.6 %collective-permute-start.1 = (bf16[3072,256]{1,0:T(8,128)(2,1)S(1)}, bf16[3072,256]{1,0:T(8,128)(2,1)S(1)}, u32[]{:S(2)}, u32[]{:S(2)}) collective-permute-start(bf16[3072,256]{1,0:T(8,128)(2,1)S(1)} %get-tuple-element.24), channel_id=1, source_target_pairs={{0,8},{1,17},{2,10},{3,19},{4,12},{5,21},{6,14},{7,23},{8,0},{9,25... | collective-permute-start | bytes 4718600 | tf_op jit(solution)/shard_map/ppermute | solution.py:255
  27.1 30.0 %collective-permute-start.7 = (bf16[256,1152]{1,0:T(8,128)(2,1)S(1)}, bf16[256,1152]{1,0:T(8,128)(2,1)S(1)}, u32[]{:S(2)}, u32[]{:S(2)}) collective-permute-start(bf16[256,1152]{1,0:T(8,128)(2,1)S(1)} %get-tuple-element.28), channel_id=1, source_target_pairs={{0,16},{1,9},{2,18},{3,11},{4,20},{5,13},{6,22},{7,15},{8,24},{9,1... | collective-permute-start | bytes 1769480 | tf_op jit(solution)/shard_map/ppermute | solution.py:255
  51.6 12.0 %copy-start.2 = (bf16[3072,256]{1,0:T(8,128)(2,1)}, bf16[3072,256]{1,0:T(8,128)(2,1)S(1)}, u32[]{:S(2)}) copy-start(bf16[3072,256]{1,0:T(8,128)(2,1)S(1)} %collective-permute-done.1.near_ref) | copy-start | bytes 4718596
  55.7 29.1 %collective-permute-start.2 = (bf16[3072,256]{1,0:T(8,128)(2,1)}, bf16[3072,256]{1,0:T(8,128)(2,1)S(1)}, u32[]{:S(2)}, u32[]{:S(2)}) collective-permute-start(bf16[3072,256]{1,0:T(8,128)(2,1)} %get-tuple-element.25), channel_id=1, source_target_pairs={{0,8},{1,17},{2,10},{3,19},{4,12},{5,21},{6,14},{7,23},{8,0},{9,25... | collective-permute-start | bytes 4718600 | tf_op jit(solution)/shard_map/ppermute | solution.py:255
  58.2 31.8 %all-to-all-start = ((bf16[8,32,1152]{2,1,0:T(8,128)(2,1)}), bf16[8,32,1152]{2,1,0:T(8,128)(2,1)}, u32[]{:S(2)}, u32[]{:S(2)}) async-start(bf16[8,32,1152]{2,1,0:T(8,128)(2,1)} %bitcast.6), calls=%async_computation | async-start | bytes 1179648 | tf_op jit(solution)/shard_map/all_to_all | solution.py:260
  63.1 26.9 %copy-start.17 = (s32[64]{0:T(128)S(1)}, s32[64]{0:T(128)}, u32[]{:S(2)}) copy-start(s32[64]{0:T(128)} %fill_ref.5) | copy-start | bytes 772
  63.1 43.6 %collective-permute-start.12 = (bf16[1536,256]{1,0:T(8,128)(2,1)}, bf16[1536,256]{1,0:T(8,128)(2,1)}, u32[]{:S(2)}, u32[]{:S(2)}) collective-permute-start(bf16[1536,256]{1,0:T(8,128)(2,1)} %copy-done.11), channel_id=1, source_target_pairs={{0,16},{1,9},{2,18},{3,11},{4,20},{5,13},{6,22},{7,15},{8,24},{9,1... | collective-permute-start | bytes 2359304 | tf_op jit(solution)/shard_map/ppermute | solution.py:255
  63.6 64.5 %collective-permute-start.11 = (bf16[3072,256]{1,0:T(8,128)(2,1)S(1)}, bf16[3072,256]{1,0:T(8,128)(2,1)}, u32[]{:S(2)}, u32[]{:S(2)}) collective-permute-start(bf16[3072,256]{1,0:T(8,128)(2,1)S(1)} %collective-permute-done.1.near_ref), channel_id=1, source_target_pairs={{0,1},{1,0},{2,3},{3,2},{4,5},{5,4},{6,7},{7,6},{8,9},{9,8},{10,11... | collective-permute-start | bytes 4718600 | tf_op jit(solution)/shard_map/ppermute | solution.py:247
  84.7 22.2 %copy-start.3 = (bf16[3072,256]{1,0:T(8,128)(2,1)}, bf16[3072,256]{1,0:T(8,128)(2,1)S(1)}, u32[]{:S(2)}) copy-start(bf16[3072,256]{1,0:T(8,128)(2,1)S(1)} %collective-permute-done.2.near_ref) | copy-start | bytes 4718596
  88.4 34.6 %collective-permute-start.3 = (bf16[2048,256]{1,0:T(8,128)(2,1)}, bf16[2048,256]{1,0:T(8,128)(2,1)}, u32[]{:S(2)}, u32[]{:S(2)}) collective-permute-start(bf16[2048,256]{1,0:T(8,128)(2,1)} %get-tuple-element.26), channel_id=1, source_target_pairs={{0,8},{1,17},{2,10},{3,19},{4,12},{5,21},{6,14},{7,23},{8,0},{9,25... | collective-permute-start | bytes 3145736 | tf_op jit(solution)/shard_map/ppermute | solution.py:255
  89.9 1.1 copy-start.12
  91.1 1.0 copy-start.14
  101.3 21.8 %all-to-all-start.1 = ((bf16[8,32,1152]{2,1,0:T(8,128)(2,1)}), bf16[8,32,1152]{2,1,0:T(8,128)(2,1)}, u32[]{:S(2)}, u32[]{:S(2)}) async-start(bf16[8,32,1152]{2,1,0:T(8,128)(2,1)} %copy-done.13), calls=%async_computation.1 | async-start | bytes 1179648 | tf_op jit(solution)/shard_map/all_to_all | solution.py:260
  106.1 12.3 %collective-permute-start.9 = (bf16[1536,256]{1,0:T(8,128)(2,1)}, bf16[1536,256]{1,0:T(8,128)(2,1)}, u32[]{:S(2)}, u32[]{:S(2)}) collective-permute-start(bf16[1536,256]{1,0:T(8,128)(2,1)} %copy-done.9), channel_id=1, source_target_pairs={{0,16},{1,9},{2,18},{3,11},{4,20},{5,13},{6,22},{7,15},{8,24},{9,1... | collective-permute-start | bytes 2359304 | tf_op jit(solution)/shard_map/ppermute | solution.py:255
  106.7 20.9 %collective-permute-start.13 = (bf16[1536,256]{1,0:T(8,128)(2,1)}, bf16[1536,256]{1,0:T(8,128)(2,1)}, u32[]{:S(2)}, u32[]{:S(2)}) collective-permute-start(bf16[1536,256]{1,0:T(8,128)(2,1)} %collective-permute-done.12.mine_ref), channel_id=1, source_target_pairs={{0,1},{1,0},{2,3},{3,2},{4,5},{5,4},{6,7},{7,6},{8,9},{9,8},{10,11... | collective-permute-start | bytes 2359304 | tf_op jit(solution)/shard_map/ppermute | solution.py:247
  106.9 40.4 %collective-permute-start.8 = (bf16[3072,256]{1,0:T(8,128)(2,1)S(1)}, bf16[3072,256]{1,0:T(8,128)(2,1)}, u32[]{:S(2)}, u32[]{:S(2)}) collective-permute-start(bf16[3072,256]{1,0:T(8,128)(2,1)S(1)} %collective-permute-done.2.near_ref), channel_id=1, source_target_pairs={{0,1},{1,0},{2,3},{3,2},{4,5},{5,4},{6,7},{7,6},{8,9},{9,8},{10,11... | collective-permute-start | bytes 4718600 | tf_op jit(solution)/shard_map/ppermute | solution.py:247
  118.4 18.2 %collective-permute-start.10 = (bf16[1536,256]{1,0:T(8,128)(2,1)}, bf16[1536,256]{1,0:T(8,128)(2,1)}, u32[]{:S(2)}, u32[]{:S(2)}) collective-permute-start(bf16[1536,256]{1,0:T(8,128)(2,1)} %collective-permute-done.9.mine_ref), channel_id=1, source_target_pairs={{0,1},{1,0},{2,3},{3,2},{4,5},{5,4},{6,7},{7,6},{8,9},{9,8},{10,11... | collective-permute-start | bytes 2359304 | tf_op jit(solution)/shard_map/ppermute | solution.py:247
  123.0 13.6 %collective-permute-start.14 = (bf16[256,1152]{1,0:T(8,128)(2,1)}, bf16[256,1152]{1,0:T(8,128)(2,1)S(1)}, u32[]{:S(2)}, u32[]{:S(2)}) collective-permute-start(bf16[256,1152]{1,0:T(8,128)(2,1)} %bitcast.5.refs_3_), channel_id=1, source_target_pairs={{0,8},{1,17},{2,10},{3,19},{4,12},{5,21},{6,14},{7,23},{8,0},{9,25... | collective-permute-start | bytes 1769480 | tf_op jit(solution)/shard_map/ppermute | solution.py:255
  123.5 2.2 %copy-start = (bf16[8192,256]{1,0:T(8,128)(2,1)S(1)}, bf16[8192,256]{1,0:T(8,128)(2,1)}, u32[]{:S(2)}) copy-start(bf16[8192,256]{1,0:T(8,128)(2,1)} %own_ref.5) | copy-start | bytes 12582916
  125.7 12.9 %copy-start.5 = (bf16[256,1024]{1,0:T(8,128)(2,1)S(1)}, bf16[256,1024]{1,0:T(8,128)(2,1)}, u32[]{:S(2)}) copy-start(bf16[256,1024]{1,0:T(8,128)(2,1)} %copy-done.4) | copy-start | bytes 1572868
  125.7 12.9 %copy-start.7 = (bf16[32,8192]{1,0:T(8,128)(2,1)S(1)}, bf16[32,8192]{1,0:T(8,128)(2,1)}, u32[]{:S(2)}) copy-start(bf16[32,8192]{1,0:T(8,128)(2,1)} %copy-done.6) | copy-start | bytes 1572868
  125.7 13.0 %copy-start.10 = (bf16[1536,256]{1,0:T(8,128)(2,1)S(1)}, bf16[1536,256]{1,0:T(8,128)(2,1)}, u32[]{:S(2)}) copy-start(bf16[1536,256]{1,0:T(8,128)(2,1)} %copy-done.9) | copy-start | bytes 2359300
  125.7 13.0 %copy-start.16 = (bf16[256,1024]{1,0:T(8,128)(2,1)S(1)}, bf16[256,1024]{1,0:T(8,128)(2,1)}, u32[]{:S(2)}) copy-start(bf16[256,1024]{1,0:T(8,128)(2,1)} %copy-done.15) | copy-start | bytes 1572868
  127.5 11.2 %collective-permute-start.5 = (bf16[1024,256]{1,0:T(8,128)(2,1)S(1)}, bf16[1024,256]{1,0:T(8,128)(2,1)S(1)}, u32[]{:S(2)}, u32[]{:S(2)}) collective-permute-start(bf16[1024,256]{1,0:T(8,128)(2,1)S(1)} %cut_chunk.5), channel_id=1, source_target_pairs={{0,16},{1,9},{2,18},{3,11},{4,20},{5,13},{6,22},{7,15},{8,24},{9,1... | collective-permute-start | bytes 1572872 | tf_op jit(solution)/shard_map/ppermute | solution.py:255
  128.1 34.7 %collective-permute-start.4 = (bf16[2048,256]{1,0:T(8,128)(2,1)}, bf16[2048,256]{1,0:T(8,128)(2,1)S(1)}, u32[]{:S(2)}, u32[]{:S(2)}) collective-permute-start(bf16[2048,256]{1,0:T(8,128)(2,1)} %collective-permute-done.3.near_ref), channel_id=1, source_target_pairs={{0,1},{1,0},{2,3},{3,2},{4,5},{5,4},{6,7},{7,6},{8,9},{9,8},{10,11... | collective-permute-start | bytes 3145736 | tf_op jit(solution)/shard_map/ppermute | solution.py:247
  136.6 19.2 %collective-permute-start.15 = (bf16[256,1152]{1,0:T(8,128)(2,1)}, bf16[256,1152]{1,0:T(8,128)(2,1)S(1)}, u32[]{:S(2)}, u32[]{:S(2)}) collective-permute-start(bf16[256,1152]{1,0:T(8,128)(2,1)} %bitcast.5.refs_3_), channel_id=1, source_target_pairs={{0,16},{1,9},{2,18},{3,11},{4,20},{5,13},{6,22},{7,15},{8,24},{9,1... | collective-permute-start | bytes 1769480 | tf_op jit(solution)/shard_map/ppermute | solution.py:255
  136.6 19.2 %collective-permute-start.16 = (bf16[256,1152]{1,0:T(8,128)(2,1)S(1)}, bf16[256,1152]{1,0:T(8,128)(2,1)S(1)}, u32[]{:S(2)}, u32[]{:S(2)}) collective-permute-start(bf16[256,1152]{1,0:T(8,128)(2,1)S(1)} %collective-permute-done.14.refs_4_), channel_id=1, source_target_pairs={{0,16},{1,9},{2,18},{3,11},{4,20},{5,13},{6,22},{7,15},{8,24},{9,1... | collective-permute-start | bytes 1769480 | tf_op jit(solution)/shard_map/ppermute | solution.py:255
  138.7 24.1 %collective-permute-start.6 = (bf16[1024,256]{1,0:T(8,128)(2,1)S(1)}, bf16[1024,256]{1,0:T(8,128)(2,1)S(1)}, u32[]{:S(2)}, u32[]{:S(2)}) collective-permute-start(bf16[1024,256]{1,0:T(8,128)(2,1)S(1)} %collective-permute-done.5.mine_ref), channel_id=1, source_target_pairs={{0,1},{1,0},{2,3},{3,2},{4,5},{5,4},{6,7},{7,6},{8,9},{9,8},{10,11... | collective-permute-start | bytes 1572872 | tf_op jit(solution)/shard_map/ppermute | solution.py:247
  (7 other events, 5.7 us)

commit v7 on v6

--- a/solution.py
+++ b/solution.py
@@ -60,19 +60,23 @@
     picked(pick_ref, down_ref, up_ref, out_ref)
 
 
-def keep_select_kernel(group, where_ref, tenant_ref, down_ref, up_ref, out_ref, pick_ref):
+def keep_select_kernel(group, where_ref, tenant_ref, down_ref, up_ref, weight_ref, out_ref, piece_ref, pick_ref, sem):
+    copy = pltpu.make_async_copy(weight_ref.at[pl.ds(0, piece_ref.shape[0]), :], piece_ref, sem)
+    copy.start()
     here, core = where_ref[0], where_ref[1]
     pick_two(group, tenant_ref, pick_ref, here, (0, 2 - core))
     picked(pick_ref, down_ref, up_ref, out_ref)
-
-
-def sum_kernel(start, keep_ref, came_ref, weight_ref, keep_out_ref, send_out_ref, piece_ref, sem):
-    copy = pltpu.make_async_copy(weight_ref.at[pl.ds(start, piece_ref.shape[0]), :], piece_ref, sem)
-    copy.start()
-    rows = keep_out_ref.shape[0]
-    send_out_ref[...] = keep_ref[rows:, :] + came_ref[rows:, :]
-    keep_out_ref[...] = keep_ref[:rows, :] + came_ref[:rows, :]
     copy.wait()
+
+
+def sum_two_kernel(kept_ref, came_ref, keep_ref, send_ref):
+    rows = keep_ref.shape[0]
+    send_ref[...] = kept_ref[rows:, :] + came_ref[rows:, :]
+    keep_ref[...] = kept_ref[:rows, :] + came_ref[:rows, :]
+
+
+def sum_kernel(keep_ref, came_ref, out_ref):
+    out_ref[...] = keep_ref[...] + came_ref[...]
 
 
 def cut_kernel(start, where_ref, near_ref, weight_ref, half_ref, *refs):
@@ -282,42 +286,42 @@
         [pick],
     )(where, tenants, down_maps, up_maps)
     came = first_way(sent)
-    kept = call(
-        after(functools.partial(keep_select_kernel, group), 4, sent),
-        shape(2 * group_rank, both),
-        [SMEM, SMEM, VMEM, VMEM, ANY],
+    kept, piece = call(
+        after(functools.partial(keep_select_kernel, group), 5, sent),
+        [shape(2 * group_rank, both), shape(parts[0][1], wide)],
+        [SMEM, SMEM, VMEM, VMEM, ANY, ANY],
         "select_kept",
-        [pick],
-    )(where, tenants, down_maps, up_maps, sent)
-    keep, sent, piece = call(
-        functools.partial(sum_kernel, parts[0][0]),
-        [shape(group_rank, both), shape(group_rank, both), shape(parts[0][1], wide)],
-        [VMEM, VMEM, ANY],
-        "sum_and_cut",
-        [pltpu.SemaphoreType.DMA],
-    )(kept, came, weight)
-    maps = along_tok((keep + second_way(sent)).reshape(shards, rank, both))
-
-    arrived, pieces = [], []
-    for k, (_, size) in enumerate(parts):
-        near = first_way(piece)
-        far = on_core(near)
+        [pick, pltpu.SemaphoreType.DMA],
+    )(where, tenants, down_maps, up_maps, weight, sent)
+    keep, sent = call(sum_two_kernel, [shape(group_rank, both)] * 2, [VMEM] * 2, "sum_two")(kept, came)
+
+    arrived = []
+
+    def cut_chunk(*earlier):
+        k = len(arrived)
         nexts = parts[k + 1 : k + 2]
+        near = first_way(pieces[k])
         part, *cuts = call(
-            functools.partial(cut_kernel, nexts[0][0] if nexts else 0),
-            [shape(size // 2, wide)] + [shape(n, wide) for _, n in nexts],
-            [SMEM, ANY, ANY],
+            after(functools.partial(cut_kernel, nexts[0][0] if nexts else 0), 3, *earlier),
+            [shape(parts[k][1] // 2, wide)] + [shape(n, wide) for _, n in nexts],
+            [SMEM, ANY, ANY] + [ANY] * len(earlier),
             "cut_chunk",
             [pltpu.SemaphoreType.DMA((2,))],
-        )(where, near, weight)
+        )(where, near, weight, *earlier)
         mine = second_way(part)
-        arrived.append((near, far, mine, on_core(mine)))
-        pieces.append(part)
-        if cuts:
-            piece = cuts[0]
+        arrived.append((near, on_core(near), mine, on_core(mine)))
+        pieces.extend(cuts)
+        return part
+
+    pieces = [piece]
+    part = cut_chunk(sent)
+    maps = call(after(sum_kernel, 2, part), shape(group_rank, both), [VMEM, VMEM, ANY], "sum")(
+        keep, second_way(sent), part
+    )
+    maps = along_tok(maps.reshape(shards, rank, both))
 
     grad, rank_grad, at, lora, terms = call(
-        after(rank_kernel, 5, pieces[0]),
+        rank_kernel,
         [
             shape(rows, value),
             shape(rows, rank),
@@ -325,10 +329,10 @@
             shape(rows, value),
             shape(shards, rank, both),
         ],
-        [SMEM, SMEM, VMEM, VMEM, VMEM, ANY],
+        [SMEM, SMEM, VMEM, VMEM, VMEM],
         "rank_space",
         [pltpu.VMEM((rank, value), BF16)] * 2,
-    )(where, fills, tokens, cotangent, maps, pieces[0])
+    )(where, fills, tokens, cotangent, maps)
     r0 = along_tok(terms).reshape(group_rank, both)
     r1, r2 = first_way(r0), second_way(r0)
     r3 = second_way(r1)
@@ -350,22 +354,16 @@
         )
 
     tile = 512
-    total, token_gradient, grad_down = lora, None, None
-    for k, ((start, size), (near, far, mine, theirs)) in enumerate(zip(parts, arrived)):
+    total, token_gradient, early = lora, None, rank_grad
+    for k, (start, size) in enumerate(parts):
         final = k == len(parts) - 1
         steps = size // tile
         half = steps // 2
-        if final:
-            grad_down, grad_up = call(
-                after(functools.partial(expand_kernel, group), 7, total),
-                [shape(cut, columns, dtype=F32), shape(width, columns, dtype=F32)],
-                [SMEM, SMEM, SMEM] + [VMEM] * 4 + [ANY],
-                "expand",
-                [pltpu.VMEM((devices * rank, columns), BF16), pltpu.VMEM((ADAPTER_RANK, columns), F32)],
-            )(where, tenants, fills, r0, r1, r2, r3, total)
+        part = None if final else cut_chunk(early, arrived[k][1], arrived[k][3])
+        near, far, mine, theirs = arrived[k]
         turned = lambda i, w, f, half=half, steps=steps: (i + w[1] * half) % steps
         spot = lambda i, w, f, start=start, turned=turned: start // tile + turned(i, w, f)
-        extra = [a for a in (token_gradient, grad_down, pieces[1] if k == 0 else None) if a is not None]
+        extra = [a for a in (token_gradient, part, r0 if k == 0 else None) if a is not None]
         token_gradient, total = pl.pallas_call(
             functools.partial(base_kernel, steps, final),
             out_shape=[shape(rows, model), shape(rows, value, dtype=BF16 if final else F32)],
@@ -391,6 +389,15 @@
             cost_estimate=cost(size),
             name="base_chunk",
         )(where, fills, tokens, weight, near, far, mine, theirs, at, grad, rank_grad, total, *extra)
+        early = total
+
+    grad_down, grad_up = call(
+        after(functools.partial(expand_kernel, group), 7, total),
+        [shape(cut, columns, dtype=F32), shape(width, columns, dtype=F32)],
+        [SMEM, SMEM, SMEM] + [VMEM] * 4 + [ANY],
+        "expand",
+        [pltpu.VMEM((devices * rank, columns), BF16), pltpu.VMEM((ADAPTER_RANK, columns), F32)],
+    )(where, tenants, fills, r0, r1, r2, r3, total)
     return total, token_gradient, grad_down, grad_up
 
 

time: 170 us -> 170 us (level)
    ppermute x11, waiting for transfers between devices: 75.4 us -> 66 us  [split(): return lambda a: lax.ppermute(a, ('fsdp', 'tok'), pairs)]
    all_to_all x2, waiting for transfers between devices: 4.56 us -> 13.6 us  [along_tok(): return lax.all_to_all(a, 'tok', split_axis=0, concat_axis=0)]
    pallas_call x6 -> x7, Pallas kernels: 17.6 us -> 18.8 us  [the longest x3 9.09 us: cut_chunk(): call(after(functools.partial(cut_kernel, nexts[0][0] if nexts else 0), 3,...]
    unnamed x40 -> x42, local copies, waits for them, and re-layouts: 12.6 us -> 11.9 us
  transfers between devices with their start and end apart: 19 -> 19, of which waited for: 6 -> 7; matrix products, arithmetic and copies ran while one was open for 1% -> 0% of each run, Pallas kernels for 24% -> 21%
where the time goes in v7:
time: 170 us; the launch traced here: 169 us
  waiting for transfers between devices  79.7 us (47%)
  Pallas kernels  51.7 us (30%)
  starting transfers between devices  24.4 us (14%)
  local copies, waits for them, and re-layouts  11.9 us (7%)
    ppermute x11, waiting for transfers between devices, split(): return lambda a: lax.ppermute(a, ('fsdp', 'tok'), pairs)  66 us
    pallas_call x3, Pallas kernels, local(): pl.pallas_call(functools.partial(base_kernel, steps, final), out_shape=[s...  23.6 us
    ppermute x11, starting transfers between devices, split(): return lambda a: lax.ppermute(a, ('fsdp', 'tok'), pairs)  14.4 us
    all_to_all x2, waiting for transfers between devices, along_tok(): return lax.all_to_all(a, 'tok', split_axis=0, concat_axis=0)  13.6 us
    unnamed x42, local copies, waits for them, and re-layouts  11.9 us
    all_to_all x2, starting transfers between devices, along_tok(): return lax.all_to_all(a, 'tok', split_axis=0, concat_axis=0)  9.89 us
    pallas_call x3, Pallas kernels, cut_chunk(): call(after(functools.partial(cut_kernel, nexts[0][0] if nexts else 0), 3,...  9.09 us
    pallas_call x1, Pallas kernels, local(): call(after(functools.partial(expand_kernel, group), 7, total), [shape(cut...  6.88 us
  transfers between devices with their start and end apart: 19, of which 7 were waited for; matrix products, arithmetic and copies ran while one was open for 0% of the time, Pallas kernels for 21%

profile of v7, /device:TPU:0, one launch (start us, length us, event | category | flops | bytes accessed | tf_op | source)
XLA Modules:
  0.0 168.7 jit_solution(13577322540792799422)
XLA Ops:
  0.7 1.6 copy-done
  3.9 2.5 %select_sent.1.refs_5_ = bf16[512,1152]{1,0:T(8,128)(2,1)S(1)} custom-call(s32[4]{0:T(128)S(1)} %pad_add_fusion.where_ref.refs_0_, s32[64]{0:T(128)S(1)} %copy-done.18, bf16[1024,1024]{1,0:T(8,128)(2,1)S(1)} %copy-done, bf16[128,1024]{1,0:T(8,128)(2,1)S(1)} %copy-done.11), custom_call_target="tpu_custom_call" | custom-call | tf_op jit(solution)/shard_map/select_sent/pallas_call | solution.py:281
  6.4 3.6 %select_kept.1 = (bf16[512,1152]{1,0:T(8,128)(2,1)S(1)}, bf16[3072,256]{1,0:T(8,128)(2,1)S(1)}) custom-call(s32[4]{0:T(128)S(1)} %pad_add_fusion.where_ref.refs_0_, s32[64]{0:T(128)S(1)} %copy-done.19, bf16[1024,1024]{1,0:T(8,128)(2,1)} %refs_2_.5, bf16[128,1024]{1,0:T(8,128)(2,1)S(1)} %copy-done.11, bf16[8192,256]{1,0:T(8,128)(2,1)} %own_ref.5, ...), custom_call_target="tpu_custom_call" | custom-call | tf_op jit(solution)/shard_map/select_kept/pallas_call | solution.py:289
  10.0 3.0 %collective-permute-start = (bf16[3072,256]{1,0:T(8,128)(2,1)S(1)}, bf16[3072,256]{1,0:T(8,128)(2,1)}, u32[]{:S(2)}, u32[]{:S(2)}) collective-permute-start(bf16[3072,256]{1,0:T(8,128)(2,1)S(1)} %get-tuple-element.25), channel_id=1, source_target_pairs={{0,8},{1,17},{2,10},{3,19},{4,12},{5,21},{6,14},{7,23},{8,0},{9,25... | collective-permute-start | bytes 4718600 | tf_op jit(solution)/shard_map/ppermute | solution.py:259
  13.1 31.0 %collective-permute-done.1.came_ref = bf16[512,1152]{1,0:T(8,128)(2,1)S(1)} collective-permute-done((bf16[512,1152]{1,0:T(8,128)(2,1)S(1)}, bf16[512,1152]{1,0:T(8,128)(2,1)S(1)}, u32[]{:S(2)}, u32[]{:S(2)}) %collective-permute-start.1) | collective-permute-done | bytes 1179680 | tf_op jit(solution)/shard_map/ppermute | solution.py:259
  44.2 2.1 %collective-permute-start.3 = (bf16[256,1152]{1,0:T(8,128)(2,1)S(1)}, bf16[256,1152]{1,0:T(8,128)(2,1)S(1)}, u32[]{:S(2)}, u32[]{:S(2)}) collective-permute-start(bf16[256,1152]{1,0:T(8,128)(2,1)S(1)} %get-tuple-element.27.refs_3_), channel_id=1, source_target_pairs={{0,16},{1,9},{2,18},{3,11},{4,20},{5,13},{6,22},{7,15},{8,24},{9,1... | collective-permute-start | bytes 1769480 | tf_op jit(solution)/shard_map/ppermute | solution.py:259
  46.3 3.6 %cut_chunk.3 = (bf16[1536,256]{1,0:T(8,128)(2,1)}, bf16[3072,256]{1,0:T(8,128)(2,1)}) custom-call(s32[4]{0:T(128)S(1)} %pad_add_fusion.where_ref.refs_0_, bf16[3072,256]{1,0:T(8,128)(2,1)} %collective-permute-done.refs_1_.near_ref, bf16[8192,256]{1,0:T(8,128)(2,1)} %own_ref.5, bf16[256,1152]{1,0:T(8,128)(2,1)S(1)} %get-tuple-element.27.refs_3_), custom_call_target="tpu_custom_call" | custom-call | tf_op jit(solution)/shard_map/cut_chunk/pallas_call | solution.py:304
  50.0 2.0 %collective-permute-start.2 = (bf16[3072,256]{1,0:T(8,128)(2,1)}, bf16[3072,256]{1,0:T(8,128)(2,1)S(1)}, u32[]{:S(2)}, u32[]{:S(2)}) collective-permute-start(bf16[3072,256]{1,0:T(8,128)(2,1)} %get-tuple-element.28), channel_id=1, source_target_pairs={{0,8},{1,17},{2,10},{3,19},{4,12},{5,21},{6,14},{7,23},{8,0},{9,25... | collective-permute-start | bytes 4718600 | tf_op jit(solution)/shard_map/ppermute | solution.py:259
  52.0 4.7 %collective-permute-done.3.refs_1_ = bf16[256,1152]{1,0:T(8,128)(2,1)S(1)} collective-permute-done((bf16[256,1152]{1,0:T(8,128)(2,1)S(1)}, bf16[256,1152]{1,0:T(8,128)(2,1)S(1)}, u32[]{:S(2)}, u32[]{:S(2)}) %collective-permute-start.3) | collective-permute-done | bytes 589856 | tf_op jit(solution)/shard_map/ppermute | solution.py:259
  57.6 5.7 %all-to-all-start = ((bf16[8,32,1152]{2,1,0:T(8,128)(2,1)}), bf16[8,32,1152]{2,1,0:T(8,128)(2,1)}, u32[]{:S(2)}, u32[]{:S(2)}) async-start(bf16[8,32,1152]{2,1,0:T(8,128)(2,1)} %bitcast.6), calls=%async_computation | async-start | bytes 1179648 | tf_op jit(solution)/shard_map/all_to_all | solution.py:264
  63.3 10.4 %collective-permute-done.5.mine_ref = bf16[1536,256]{1,0:T(8,128)(2,1)} collective-permute-done((bf16[1536,256]{1,0:T(8,128)(2,1)}, bf16[1536,256]{1,0:T(8,128)(2,1)}, u32[]{:S(2)}, u32[]{:S(2)}) %collective-permute-start.5) | collective-permute-done | bytes 786464 | tf_op jit(solution)/shard_map/ppermute | solution.py:259
  73.7 6.5 %all-to-all-done.maps_ref = bf16[8,32,1152]{2,1,0:T(8,128)(2,1)} async-done(((bf16[8,32,1152]{2,1,0:T(8,128)(2,1)}), bf16[8,32,1152]{2,1,0:T(8,128)(2,1)}, u32[]{:S(2)}, u32[]{:S(2)}) %all-to-all-start) | async-done | bytes 589856 | tf_op jit(solution)/shard_map/all_to_all | solution.py:264
  80.2 1.0 copy-done.13
  81.2 5.9 %rank_space.1 = (bf16[256,1024]{1,0:T(8,128)(2,1)S(1)}, bf16[256,32]{1,0:T(8,128)(2,1)S(1)}, bf16[32,8192]{1,0:T(8,128)(2,1)S(1)}, bf16[256,1024]{1,0:T(8,128)(2,1)S(1)}, bf16[8,32,1152]{2,1,0:T(8,128)(2,1)S(1)}) custom-call(s32[4]{0:T(128)S(1)} %pad_add_fusion.where_ref.refs_0_, s32[64]{0:T(128)S(1)} %copy-done.17, bf16[256,8192]{1,0:T(8,128)(2,1)} %tokens_ref.7, ...), custom_call_target="tpu_custom_call" | custom-call | tf_op jit(solution)/shard_map/rank_space/pallas_call | solution.py:323
  88.9 3.6 %cut_chunk.4 = (bf16[1536,256]{1,0:T(8,128)(2,1)}, bf16[2048,256]{1,0:T(8,128)(2,1)S(1)}) custom-call(s32[4]{0:T(128)S(1)} %pad_add_fusion.where_ref.refs_0_, bf16[3072,256]{1,0:T(8,128)(2,1)S(1)} %collective-permute-done.2.refs_1_.near_ref, bf16[8192,256]{1,0:T(8,128)(2,1)} %own_ref.5, bf16[256,32]{1,0:T(8,128)(2,1)S(1)} %get-tuple-element.31.refs_3_.rg_ref, ...), custom_call_target="tpu_custom_call" | custom-call | tf_op jit(solution)/shard_map/cut_chunk/pallas_call | solution.py:304
  93.4 1.5 collective-permute-start.10
  95.0 4.2 %all-to-all-start.1 = ((bf16[8,32,1152]{2,1,0:T(8,128)(2,1)}), bf16[8,32,1152]{2,1,0:T(8,128)(2,1)}, u32[]{:S(2)}, u32[]{:S(2)}) async-start(bf16[8,32,1152]{2,1,0:T(8,128)(2,1)} %copy-done.12), calls=%async_computation.1 | async-start | bytes 1179648 | tf_op jit(solution)/shard_map/all_to_all | solution.py:264
  99.2 1.5 collective-permute-start.7
  100.7 8.1 %collective-permute-done.10.mine_ref = bf16[1536,256]{1,0:T(8,128)(2,1)} collective-permute-done((bf16[1536,256]{1,0:T(8,128)(2,1)}, bf16[1536,256]{1,0:T(8,128)(2,1)}, u32[]{:S(2)}, u32[]{:S(2)}) %collective-permute-start.10) | collective-permute-done | bytes 786464 | tf_op jit(solution)/shard_map/ppermute | solution.py:259
  108.8 7.1 %all-to-all-done.1 = bf16[8,32,1152]{2,1,0:T(8,128)(2,1)} async-done(((bf16[8,32,1152]{2,1,0:T(8,128)(2,1)}), bf16[8,32,1152]{2,1,0:T(8,128)(2,1)}, u32[]{:S(2)}, u32[]{:S(2)}) %all-to-all-start.1) | async-done | bytes 589856 | tf_op jit(solution)/shard_map/all_to_all | solution.py:264
  115.9 1.0 copy-done.5
  117.0 1.0 copy-done.8
  118.0 1.0 copy-done.15
  119.1 8.6 %base_chunk.3 = (bf16[256,8192]{1,0:T(8,128)(2,1)}, f32[256,1024]{1,0:T(8,128)S(1)}) custom-call(s32[4]{0:T(128)S(1)} %pad_add_fusion.where_ref.refs_0_, s32[64]{0:T(128)S(1)} %copy-done.17, bf16[256,8192]{1,0:T(8,128)(2,1)} %tokens_ref.7, bf16[8192,256]{1,0:T(8,128)(2,1)} %own_ref.5, bf16[3072,256]{1,0:T(8,128)(2,1)} %collective-permute-done.refs_1_.near_ref, ...), custom_call_target="tpu_custom_call" | custom-call | flops 3221225472 | bytes 11534336 | tf_op jit(solution)/shard_map/base_chunk/pallas_call | solution.py:367
  127.8 1.9 %cut_chunk.5.refs_1_ = bf16[1024,256]{1,0:T(8,128)(2,1)S(1)} custom-call(s32[4]{0:T(128)S(1)} %pad_add_fusion.where_ref.refs_0_, bf16[2048,256]{1,0:T(8,128)(2,1)} %collective-permute-done.7.refs_1_.near_ref, bf16[8192,256]{1,0:T(8,128)(2,1)} %own_ref.5, f32[256,1024]{1,0:T(8,128)S(1)} %get-tuple-element.38.refs_3_.sum_ref, ...), custom_call_target="tpu_custom_call" | custom-call | tf_op jit(solution)/shard_map/cut_chunk/pallas_call | solution.py:304
  130.6 1.2 collective-permute-start.14
  131.8 11.9 %collective-permute-done.12.mine_ref = bf16[1024,256]{1,0:T(8,128)(2,1)S(1)} collective-permute-done((bf16[1024,256]{1,0:T(8,128)(2,1)S(1)}, bf16[1024,256]{1,0:T(8,128)(2,1)S(1)}, u32[]{:S(2)}, u32[]{:S(2)}) %collective-permute-start.12) | collective-permute-done | bytes 524320 | tf_op jit(solution)/shard_map/ppermute | solution.py:259
  143.7 1.2 collective-permute-start.15
  145.7 8.5 %base_chunk.4 = (bf16[256,8192]{1,0:T(8,128)(2,1)}, f32[256,1024]{1,0:T(8,128)S(1)}) custom-call(s32[4]{0:T(128)S(1)} %pad_add_fusion.where_ref.refs_0_, s32[64]{0:T(128)S(1)} %copy-done.17, bf16[256,8192]{1,0:T(8,128)(2,1)} %tokens_ref.7, bf16[8192,256]{1,0:T(8,128)(2,1)} %own_ref.5, bf16[3072,256]{1,0:T(8,128)(2,1)} %copy-done.1, ...), custom_call_target="tpu_custom_call", output_to_operand_aliasing={{0}: (12, {})} | custom-call | flops 3221225472 | bytes 11534336 | tf_op jit(solution)/shard_map/base_chunk/pallas_call | solution.py:367
  154.2 6.5 %base_chunk.5 = (bf16[256,8192]{1,0:T(8,128)(2,1)}, bf16[256,1024]{1,0:T(8,128)(2,1)}) custom-call(s32[4]{0:T(128)S(1)} %pad_add_fusion.where_ref.refs_0_, s32[64]{0:T(128)S(1)} %copy-done.17, bf16[256,8192]{1,0:T(8,128)(2,1)} %tokens_ref.7, bf16[8192,256]{1,0:T(8,128)(2,1)} %own_ref.5, ...), custom_call_target="tpu_custom_call", output_to_operand_aliasing={{0}: (12, {})} | custom-call | flops 2147483648 | bytes 8388608 | tf_op jit(solution)/shard_map/base_chunk/pallas_call | solution.py:367
  160.7 1.0 copy-done.16
  161.8 6.9 %expand.1 = (f32[1024,1024]{1,0:T(8,128)}, f32[128,1024]{1,0:T(8,128)}) custom-call(s32[4]{0:T(128)S(1)} %pad_add_fusion.where_ref.refs_0_, s32[64]{0:T(128)S(1)} %copy-done.19, s32[64]{0:T(128)S(1)} %copy-done.17, bf16[256,1152]{1,0:T(8,128)(2,1)} %bitcast.5.refs_1_.refs_3_, bf16[256,1152]{1,0:T(8,128)(2,1)S(1)} %collective-permute-done.14.refs_4_, ...), custom_call_target="tpu_custom_call" | custom-call | tf_op jit(solution)/shard_map/expand/pallas_call | solution.py:394
  (61 shorter events, 7.4 us)
Async XLA Ops:
  0.7 1.6 copy-start
  3.9 2.5 %copy-start.19 = (s32[64]{0:T(128)S(1)}, s32[64]{0:T(128)}, u32[]{:S(2)}) copy-start(s32[64]{0:T(128)} %refs_1_.3) | copy-start | bytes 772
  10.0 36.3 %collective-permute-start = (bf16[3072,256]{1,0:T(8,128)(2,1)S(1)}, bf16[3072,256]{1,0:T(8,128)(2,1)}, u32[]{:S(2)}, u32[]{:S(2)}) collective-permute-start(bf16[3072,256]{1,0:T(8,128)(2,1)S(1)} %get-tuple-element.25), channel_id=1, source_target_pairs={{0,8},{1,17},{2,10},{3,19},{4,12},{5,21},{6,14},{7,23},{8,0},{9,25... | collective-permute-start | bytes 4718600 | tf_op jit(solution)/shard_map/ppermute | solution.py:259
  13.0 31.0 %collective-permute-start.1 = (bf16[512,1152]{1,0:T(8,128)(2,1)S(1)}, bf16[512,1152]{1,0:T(8,128)(2,1)S(1)}, u32[]{:S(2)}, u32[]{:S(2)}) collective-permute-start(bf16[512,1152]{1,0:T(8,128)(2,1)S(1)} %select_sent.1.refs_5_), channel_id=1, source_target_pairs={{0,8},{1,17},{2,10},{3,19},{4,12},{5,21},{6,14},{7,23},{8,0},{9,25... | collective-permute-start | bytes 3538952 | tf_op jit(solution)/shard_map/ppermute | solution.py:259
  44.2 12.5 %collective-permute-start.3 = (bf16[256,1152]{1,0:T(8,128)(2,1)S(1)}, bf16[256,1152]{1,0:T(8,128)(2,1)S(1)}, u32[]{:S(2)}, u32[]{:S(2)}) collective-permute-start(bf16[256,1152]{1,0:T(8,128)(2,1)S(1)} %get-tuple-element.27.refs_3_), channel_id=1, source_target_pairs={{0,16},{1,9},{2,18},{3,11},{4,20},{5,13},{6,22},{7,15},{8,24},{9,1... | collective-permute-start | bytes 1769480 | tf_op jit(solution)/shard_map/ppermute | solution.py:259
  49.9 23.7 %collective-permute-start.5 = (bf16[1536,256]{1,0:T(8,128)(2,1)}, bf16[1536,256]{1,0:T(8,128)(2,1)}, u32[]{:S(2)}, u32[]{:S(2)}) collective-permute-start(bf16[1536,256]{1,0:T(8,128)(2,1)} %get-tuple-element.30.refs_2_), channel_id=1, source_target_pairs={{0,16},{1,9},{2,18},{3,11},{4,20},{5,13},{6,22},{7,15},{8,24},{9,1... | collective-permute-start | bytes 2359304 | tf_op jit(solution)/shard_map/ppermute | solution.py:259
  50.0 38.8 %collective-permute-start.2 = (bf16[3072,256]{1,0:T(8,128)(2,1)}, bf16[3072,256]{1,0:T(8,128)(2,1)S(1)}, u32[]{:S(2)}, u32[]{:S(2)}) collective-permute-start(bf16[3072,256]{1,0:T(8,128)(2,1)} %get-tuple-element.28), channel_id=1, source_target_pairs={{0,8},{1,17},{2,10},{3,19},{4,12},{5,21},{6,14},{7,23},{8,0},{9,25... | collective-permute-start | bytes 4718600 | tf_op jit(solution)/shard_map/ppermute | solution.py:259
  52.0 36.8 %collective-permute-start.4 = (bf16[3072,256]{1,0:T(8,128)(2,1)}, bf16[3072,256]{1,0:T(8,128)(2,1)S(1)}, u32[]{:S(2)}, u32[]{:S(2)}) collective-permute-start(bf16[3072,256]{1,0:T(8,128)(2,1)} %collective-permute-done.refs_1_.near_ref), channel_id=1, source_target_pairs={{0,1},{1,0},{2,3},{3,2},{4,5},{5,4},{6,7},{7,6},{8,9},{9,8},{10,11... | collective-permute-start | bytes 4718600 | tf_op jit(solution)/shard_map/ppermute | solution.py:251
  56.7 23.5 %copy-start.17 = (s32[64]{0:T(128)S(1)}, s32[64]{0:T(128)}, u32[]{:S(2)}) copy-start(s32[64]{0:T(128)} %refs_2_.9) | copy-start | bytes 772
  57.6 22.6 %all-to-all-start = ((bf16[8,32,1152]{2,1,0:T(8,128)(2,1)}), bf16[8,32,1152]{2,1,0:T(8,128)(2,1)}, u32[]{:S(2)}, u32[]{:S(2)}) async-start(bf16[8,32,1152]{2,1,0:T(8,128)(2,1)} %bitcast.6), calls=%async_computation | async-start | bytes 1179648 | tf_op jit(solution)/shard_map/all_to_all | solution.py:264
  73.7 15.1 %collective-permute-start.6 = (bf16[1536,256]{1,0:T(8,128)(2,1)}, bf16[1536,256]{1,0:T(8,128)(2,1)}, u32[]{:S(2)}, u32[]{:S(2)}) collective-permute-start(bf16[1536,256]{1,0:T(8,128)(2,1)} %collective-permute-done.5.mine_ref), channel_id=1, source_target_pairs={{0,1},{1,0},{2,3},{3,2},{4,5},{5,4},{6,7},{7,6},{8,9},{9,8},{10,11... | collective-permute-start | bytes 2359304 | tf_op jit(solution)/shard_map/ppermute | solution.py:251
  80.2 1.0 copy-start.13
  88.8 3.6 %copy-start.4 = (bf16[256,1024]{1,0:T(8,128)(2,1)}, bf16[256,1024]{1,0:T(8,128)(2,1)S(1)}, u32[]{:S(2)}) copy-start(bf16[256,1024]{1,0:T(8,128)(2,1)S(1)} %get-tuple-element.34.grad_ref) | copy-start | bytes 1572868
  88.8 3.6 %copy-start.7 = (bf16[32,8192]{1,0:T(8,128)(2,1)}, bf16[32,8192]{1,0:T(8,128)(2,1)S(1)}, u32[]{:S(2)}) copy-start(bf16[32,8192]{1,0:T(8,128)(2,1)S(1)} %get-tuple-element.33.at_ref) | copy-start | bytes 1572868
  88.8 6.2 %copy-start.1 = (bf16[3072,256]{1,0:T(8,128)(2,1)}, bf16[3072,256]{1,0:T(8,128)(2,1)S(1)}, u32[]{:S(2)}) copy-start(bf16[3072,256]{1,0:T(8,128)(2,1)S(1)} %collective-permute-done.2.refs_1_.near_ref) | copy-start | bytes 4718596
  88.8 3.6 %copy-start.3 = (bf16[3072,256]{1,0:T(8,128)(2,1)}, bf16[3072,256]{1,0:T(8,128)(2,1)S(1)}, u32[]{:S(2)}) copy-start(bf16[3072,256]{1,0:T(8,128)(2,1)S(1)} %collective-permute-done.4.refs_4_.far_ref) | copy-start | bytes 4718596
  93.4 15.4 %collective-permute-start.10 = (bf16[1536,256]{1,0:T(8,128)(2,1)}, bf16[1536,256]{1,0:T(8,128)(2,1)}, u32[]{:S(2)}, u32[]{:S(2)}) collective-permute-start(bf16[1536,256]{1,0:T(8,128)(2,1)} %get-tuple-element.36.refs_0_), channel_id=1, source_target_pairs={{0,16},{1,9},{2,18},{3,11},{4,20},{5,13},{6,22},{7,15},{8,24},{9,1... | collective-permute-start | bytes 2359304 | tf_op jit(solution)/shard_map/ppermute | solution.py:259
  95.0 32.8 %collective-permute-start.9 = (bf16[3072,256]{1,0:T(8,128)(2,1)S(1)}, bf16[3072,256]{1,0:T(8,128)(2,1)S(1)}, u32[]{:S(2)}, u32[]{:S(2)}) collective-permute-start(bf16[3072,256]{1,0:T(8,128)(2,1)S(1)} %collective-permute-done.2.refs_1_.near_ref), channel_id=1, source_target_pairs={{0,1},{1,0},{2,3},{3,2},{4,5},{5,4},{6,7},{7,6},{8,9},{9,8},{10,11... | collective-permute-start | bytes 4718600 | tf_op jit(solution)/shard_map/ppermute | solution.py:251
  95.0 21.0 %all-to-all-start.1 = ((bf16[8,32,1152]{2,1,0:T(8,128)(2,1)}), bf16[8,32,1152]{2,1,0:T(8,128)(2,1)}, u32[]{:S(2)}, u32[]{:S(2)}) async-start(bf16[8,32,1152]{2,1,0:T(8,128)(2,1)} %copy-done.12), calls=%async_computation.1 | async-start | bytes 1179648 | tf_op jit(solution)/shard_map/all_to_all | solution.py:264
  99.2 28.5 %collective-permute-start.7 = (bf16[2048,256]{1,0:T(8,128)(2,1)}, bf16[2048,256]{1,0:T(8,128)(2,1)}, u32[]{:S(2)}, u32[]{:S(2)}) collective-permute-start(bf16[2048,256]{1,0:T(8,128)(2,1)} %copy-done.20), channel_id=1, source_target_pairs={{0,8},{1,17},{2,10},{3,19},{4,12},{5,21},{6,14},{7,23},{8,0},{9,25... | collective-permute-start | bytes 3145736 | tf_op jit(solution)/shard_map/ppermute | solution.py:259
  108.8 18.9 %collective-permute-start.11 = (bf16[1536,256]{1,0:T(8,128)(2,1)}, bf16[1536,256]{1,0:T(8,128)(2,1)}, u32[]{:S(2)}, u32[]{:S(2)}) collective-permute-start(bf16[1536,256]{1,0:T(8,128)(2,1)} %collective-permute-done.10.mine_ref), channel_id=1, source_target_pairs={{0,1},{1,0},{2,3},{3,2},{4,5},{5,4},{6,7},{7,6},{8,9},{9,8},{10,11... | collective-permute-start | bytes 2359304 | tf_op jit(solution)/shard_map/ppermute | solution.py:251
  115.9 1.0 copy-start.5
  127.7 26.6 %collective-permute-start.8 = (bf16[2048,256]{1,0:T(8,128)(2,1)}, bf16[2048,256]{1,0:T(8,128)(2,1)S(1)}, u32[]{:S(2)}, u32[]{:S(2)}) collective-permute-start(bf16[2048,256]{1,0:T(8,128)(2,1)} %collective-permute-done.7.refs_1_.near_ref), channel_id=1, source_target_pairs={{0,1},{1,0},{2,3},{3,2},{4,5},{5,4},{6,7},{7,6},{8,9},{9,8},{10,11... | collective-permute-start | bytes 3145736 | tf_op jit(solution)/shard_map/ppermute | solution.py:251
  127.7 2.0 %copy-start.2 = (bf16[3072,256]{1,0:T(8,128)(2,1)}, bf16[3072,256]{1,0:T(8,128)(2,1)S(1)}, u32[]{:S(2)}) copy-start(bf16[3072,256]{1,0:T(8,128)(2,1)S(1)} %collective-permute-done.9.refs_4_.far_ref) | copy-start | bytes 4718596
  127.8 18.0 %copy-start.6 = (bf16[256,1024]{1,0:T(8,128)(2,1)S(1)}, bf16[256,1024]{1,0:T(8,128)(2,1)}, u32[]{:S(2)}) copy-start(bf16[256,1024]{1,0:T(8,128)(2,1)} %copy-done.4) | copy-start | bytes 1572868
  127.8 17.9 %copy-start.9 = (bf16[32,8192]{1,0:T(8,128)(2,1)S(1)}, bf16[32,8192]{1,0:T(8,128)(2,1)}, u32[]{:S(2)}) copy-start(bf16[32,8192]{1,0:T(8,128)(2,1)} %copy-done.7) | copy-start | bytes 1572868
  129.7 14.0 %collective-permute-start.12 = (bf16[1024,256]{1,0:T(8,128)(2,1)S(1)}, bf16[1024,256]{1,0:T(8,128)(2,1)S(1)}, u32[]{:S(2)}, u32[]{:S(2)}) collective-permute-start(bf16[1024,256]{1,0:T(8,128)(2,1)S(1)} %cut_chunk.5.refs_1_), channel_id=1, source_target_pairs={{0,16},{1,9},{2,18},{3,11},{4,20},{5,13},{6,22},{7,15},{8,24},{9,1... | collective-permute-start | bytes 1572872 | tf_op jit(solution)/shard_map/ppermute | solution.py:259
  130.6 14.3 %collective-permute-start.14 = (bf16[256,1152]{1,0:T(8,128)(2,1)}, bf16[256,1152]{1,0:T(8,128)(2,1)S(1)}, u32[]{:S(2)}, u32[]{:S(2)}) collective-permute-start(bf16[256,1152]{1,0:T(8,128)(2,1)} %bitcast.5.refs_1_.refs_3_), channel_id=1, source_target_pairs={{0,8},{1,17},{2,10},{3,19},{4,12},{5,21},{6,14},{7,23},{8,0},{9,25... | collective-permute-start | bytes 1769480 | tf_op jit(solution)/shard_map/ppermute | solution.py:259
  143.7 10.5 %collective-permute-start.13 = (bf16[1024,256]{1,0:T(8,128)(2,1)S(1)}, bf16[1024,256]{1,0:T(8,128)(2,1)S(1)}, u32[]{:S(2)}, u32[]{:S(2)}) collective-permute-start(bf16[1024,256]{1,0:T(8,128)(2,1)S(1)} %collective-permute-done.12.mine_ref), channel_id=1, source_target_pairs={{0,1},{1,0},{2,3},{3,2},{4,5},{5,4},{6,7},{7,6},{8,9},{9,8},{10,11... | collective-permute-start | bytes 1572872 | tf_op jit(solution)/shard_map/ppermute | solution.py:251
  143.7 17.0 %collective-permute-start.15 = (bf16[256,1152]{1,0:T(8,128)(2,1)}, bf16[256,1152]{1,0:T(8,128)(2,1)S(1)}, u32[]{:S(2)}, u32[]{:S(2)}) collective-permute-start(bf16[256,1152]{1,0:T(8,128)(2,1)} %bitcast.5.refs_1_.refs_3_), channel_id=1, source_target_pairs={{0,16},{1,9},{2,18},{3,11},{4,20},{5,13},{6,22},{7,15},{8,24},{9,1... | collective-permute-start | bytes 1769480 | tf_op jit(solution)/shard_map/ppermute | solution.py:259
  144.9 15.8 %collective-permute-start.16 = (bf16[256,1152]{1,0:T(8,128)(2,1)S(1)}, bf16[256,1152]{1,0:T(8,128)(2,1)S(1)}, u32[]{:S(2)}, u32[]{:S(2)}) collective-permute-start(bf16[256,1152]{1,0:T(8,128)(2,1)S(1)} %collective-permute-done.14.refs_4_), channel_id=1, source_target_pairs={{0,16},{1,9},{2,18},{3,11},{4,20},{5,13},{6,22},{7,15},{8,24},{9,1... | collective-permute-start | bytes 1769480 | tf_op jit(solution)/shard_map/ppermute | solution.py:259
  160.7 1.0 copy-start.16
  (8 other events, 7.2 us)

commit v8 on v7

--- a/solution.py
+++ b/solution.py
@@ -10,7 +10,7 @@
 ADAPTER_RANK = 16
 BLOCK = 128
 ADAPTER_SCALE = 2.0
-CHUNKS = (3, 3, 2)
+SPREAD = 3
 VMEM_LIMIT = 48 * 1024 * 1024
 
 F32 = jnp.float32
@@ -61,7 +61,9 @@
 
 
 def keep_select_kernel(group, where_ref, tenant_ref, down_ref, up_ref, weight_ref, out_ref, piece_ref, pick_ref, sem):
-    copy = pltpu.make_async_copy(weight_ref.at[pl.ds(0, piece_ref.shape[0]), :], piece_ref, sem)
+    size = piece_ref.shape[0]
+    start = pl.multiple_of(where_ref[3] * size, size)
+    copy = pltpu.make_async_copy(weight_ref.at[pl.ds(start, size), :], piece_ref, sem)
     copy.start()
     here, core = where_ref[0], where_ref[1]
     pick_two(group, tenant_ref, pick_ref, here, (0, 2 - core))
@@ -75,23 +77,15 @@
     keep_ref[...] = kept_ref[:rows, :] + came_ref[:rows, :]
 
 
-def sum_kernel(keep_ref, came_ref, out_ref):
+def sum_kernel(start, keep_ref, came_ref, weight_ref, out_ref, piece_ref, sem):
+    copy = pltpu.make_async_copy(weight_ref.at[pl.ds(start, piece_ref.shape[0]), :], piece_ref, sem)
+    copy.start()
     out_ref[...] = keep_ref[...] + came_ref[...]
-
-
-def cut_kernel(start, where_ref, near_ref, weight_ref, half_ref, *refs):
-    *piece_refs, sems = refs
-    half = half_ref.shape[0]
-    at = pl.multiple_of(where_ref[1] * half, half)
-    copies = [pltpu.make_async_copy(near_ref.at[pl.ds(at, half), :], half_ref, sems.at[0])]
-    for piece_ref in piece_refs:
-        copies.append(
-            pltpu.make_async_copy(weight_ref.at[pl.ds(start, piece_ref.shape[0]), :], piece_ref, sems.at[1])
-        )
-    for copy in copies:
-        copy.start()
-    for copy in copies:
-        copy.wait()
+    copy.wait()
+
+
+def gate_kernel(in_ref, out_ref):
+    out_ref[...] = in_ref[...]
 
 
 def block_diagonal(a):
@@ -145,18 +139,29 @@
     acc_ref[...] += dot(tokens_ref[...], weight)
 
 
-def base_kernel(
-    steps, final, where_ref, fill_ref, tokens_ref, own_ref, near_ref, far_ref, mine_ref, theirs_ref,
-    at_ref, grad_ref, rg_ref, sum_ref, *refs
+def spread_kernel(tokens_ref, own_ref, others_ref, at_ref, grad_ref, rg_ref, sum_ref, out_ref, total_ref):
+    i = pl.program_id(0)
+
+    @pl.when(i == 0)
+    def _():
+        total_ref[...] = sum_ref[...].astype(F32)
+
+    base_tile(
+        i % 2, tokens_ref, own_ref[...], others_ref[0, 0], others_ref[0, 1], others_ref[0, 2],
+        at_ref, grad_ref, rg_ref, out_ref, total_ref,
+    )
+
+
+def swap_kernel(
+    steps, where_ref, fill_ref, tokens_ref, own_ref, near_ref, far_ref, mine_ref, theirs_ref,
+    at_ref, grad_ref, rg_ref, sum_ref, _, out_ref, total_ref, acc_ref
 ):
-    out_ref, total_ref = refs[-3:-1] if final else refs[-2:]
-    acc_ref = refs[-1]
     i = pl.program_id(0)
     here, core, first = where_ref[0], where_ref[1], where_ref[2]
 
     @pl.when(i == 0)
     def _():
-        acc_ref[...] = sum_ref[...].astype(F32)
+        acc_ref[...] = sum_ref[...]
 
     last = jnp.where(i < steps // 2, mine_ref[...], theirs_ref[...])
     base_tile(
@@ -164,19 +169,17 @@
         at_ref, grad_ref, rg_ref, out_ref, acc_ref,
     )
 
-    if final:
-
-        @pl.when(i == steps - 1)
-        def _():
-            wide = own_ref.shape[1]
-            for n in range(total_ref.shape[0] // BLOCK):
-                span = slice(n * BLOCK, (n + 1) * BLOCK)
-                for other in range(total_ref.shape[1] // wide):
-                    part = acc_ref[span, other * wide : (other + 1) * wide]
-                    row = lax.broadcasted_iota(jnp.int32, part.shape, 0)
-                    total_ref[span, pl.ds(pl.multiple_of((here ^ other) * wide, wide), wide)] = jnp.where(
-                        row < fill_ref[first + n], part, 0.0
-                    ).astype(BF16)
+    @pl.when(i == steps - 1)
+    def _():
+        wide = own_ref.shape[1]
+        for n in range(total_ref.shape[0] // BLOCK):
+            span = slice(n * BLOCK, (n + 1) * BLOCK)
+            for other in range(total_ref.shape[1] // wide):
+                part = acc_ref[span, other * wide : (other + 1) * wide]
+                row = lax.broadcasted_iota(jnp.int32, part.shape, 0)
+                total_ref[span, pl.ds(pl.multiple_of((here ^ other) * wide, wide), wide)] = jnp.where(
+                    row < fill_ref[first + n], part, 0.0
+                ).astype(BF16)
 
 
 def fill_expand(tenant_ref, fill_ref, pick_ref, scale_ref, row, first, count, shard):
@@ -275,7 +278,8 @@
             **extra,
         )
 
-    parts = [(model // 8 * sum(CHUNKS[:k]), model // 8 * size) for k, size in enumerate(CHUNKS)]
+    spread = max(model // 8 * SPREAD, BLOCK * shards)
+    swapped = model - spread
     both = cut + width
     pick = pltpu.VMEM((2 * group_rank, columns), BF16)
     sent = call(
@@ -286,39 +290,33 @@
         [pick],
     )(where, tenants, down_maps, up_maps)
     came = first_way(sent)
-    kept, piece = call(
+    kept, share = call(
         after(functools.partial(keep_select_kernel, group), 5, sent),
-        [shape(2 * group_rank, both), shape(parts[0][1], wide)],
+        [shape(2 * group_rank, both), shape(spread // shards, wide)],
         [SMEM, SMEM, VMEM, VMEM, ANY, ANY],
         "select_kept",
         [pick, pltpu.SemaphoreType.DMA],
     )(where, tenants, down_maps, up_maps, weight, sent)
-    keep, sent = call(sum_two_kernel, [shape(group_rank, both)] * 2, [VMEM] * 2, "sum_two")(kept, came)
-
-    arrived = []
-
-    def cut_chunk(*earlier):
-        k = len(arrived)
-        nexts = parts[k + 1 : k + 2]
-        near = first_way(pieces[k])
-        part, *cuts = call(
-            after(functools.partial(cut_kernel, nexts[0][0] if nexts else 0), 3, *earlier),
-            [shape(parts[k][1] // 2, wide)] + [shape(n, wide) for _, n in nexts],
-            [SMEM, ANY, ANY] + [ANY] * len(earlier),
-            "cut_chunk",
-            [pltpu.SemaphoreType.DMA((2,))],
-        )(where, near, weight, *earlier)
-        mine = second_way(part)
-        arrived.append((near, on_core(near), mine, on_core(mine)))
-        pieces.extend(cuts)
-        return part
-
-    pieces = [piece]
-    part = cut_chunk(sent)
-    maps = call(after(sum_kernel, 2, part), shape(group_rank, both), [VMEM, VMEM, ANY], "sum")(
-        keep, second_way(sent), part
-    )
+    first = first_way(share)
+    shares = jnp.stack([first, second_way(share), second_way(first)])
+    others = lax.all_gather(shares, "tok")
+
+    keep, sent = call(after(sum_two_kernel, 2, shares), [shape(group_rank, both)] * 2, [VMEM, VMEM, ANY], "sum_two")(
+        kept, came, shares
+    )
+    maps, piece = call(
+        functools.partial(sum_kernel, spread),
+        [shape(group_rank, both), shape(swapped, wide)],
+        [VMEM, VMEM, ANY],
+        "sum_and_cut",
+        [pltpu.SemaphoreType.DMA],
+    )(keep, second_way(sent), weight)
     maps = along_tok(maps.reshape(shards, rank, both))
+
+    near = first_way(piece)
+    far = on_core(near)
+    mine = second_way(lax.dynamic_slice_in_dim(near, core * (swapped // 2), swapped // 2, axis=0))
+    theirs = on_core(mine)
 
     grad, rank_grad, at, lora, terms = call(
         rank_kernel,
@@ -333,10 +331,6 @@
         "rank_space",
         [pltpu.VMEM((rank, value), BF16)] * 2,
     )(where, fills, tokens, cotangent, maps)
-    r0 = along_tok(terms).reshape(group_rank, both)
-    r1, r2 = first_way(r0), second_way(r0)
-    r3 = second_way(r1)
-
     whole = lambda i, *refs: (0, 0)
     along = lambda spot, tile: pl.BlockSpec((rows, tile), lambda i, *refs: (0, spot(i, *refs)))
     down = lambda spot, tile: pl.BlockSpec((tile, wide), lambda i, *refs: (spot(i, *refs), 0))
@@ -353,52 +347,68 @@
             transcendentals=0,
         )
 
+    tile = spread // shards
+    same = lambda i: i
+    token_gradient, total = pl.pallas_call(
+        spread_kernel,
+        out_shape=[shape(rows, model), shape(rows, value, dtype=F32)],
+        grid=(shards,),
+        in_specs=[
+            along(same, tile),
+            down(same, tile),
+            pl.BlockSpec((1, 3, tile, wide), lambda i: (i, 0, 0, 0)),
+            pl.BlockSpec((rank, tile), lambda i: (0, i)),
+        ]
+        + resident,
+        out_specs=[along(same, tile), pl.BlockSpec((rows, value), whole)],
+        compiler_params=params(dimension_semantics=("arbitrary",)),
+        cost_estimate=cost(spread),
+        name="base_spread",
+    )(tokens, weight, others, at, grad, rank_grad, lora)
+
+    r0 = along_tok(terms).reshape(group_rank, both)
+    r0 = call(after(gate_kernel, 1, total), shape(group_rank, both), [VMEM, ANY], "gate")(r0, total)
+    r1, r2 = first_way(r0), second_way(r0)
+    r3 = second_way(r1)
+
     tile = 512
-    total, token_gradient, early = lora, None, rank_grad
-    for k, (start, size) in enumerate(parts):
-        final = k == len(parts) - 1
-        steps = size // tile
-        half = steps // 2
-        part = None if final else cut_chunk(early, arrived[k][1], arrived[k][3])
-        near, far, mine, theirs = arrived[k]
-        turned = lambda i, w, f, half=half, steps=steps: (i + w[1] * half) % steps
-        spot = lambda i, w, f, start=start, turned=turned: start // tile + turned(i, w, f)
-        extra = [a for a in (token_gradient, part, r0 if k == 0 else None) if a is not None]
-        token_gradient, total = pl.pallas_call(
-            functools.partial(base_kernel, steps, final),
-            out_shape=[shape(rows, model), shape(rows, value, dtype=BF16 if final else F32)],
-            grid_spec=pltpu.PrefetchScalarGridSpec(
-                num_scalar_prefetch=2,
-                grid=(steps,),
-                in_specs=[
-                    along(spot, tile),
-                    down(spot, tile),
-                    down(turned, tile),
-                    down(turned, tile),
-                    down(lambda i, w, f, half=half: jnp.minimum(i, half - 1), tile),
-                    down(lambda i, w, f, half=half: jnp.maximum(i - half, 0), tile),
-                    pl.BlockSpec((rank, tile), lambda i, w, f, spot=spot: (0, spot(i, w, f))),
-                ]
-                + resident
-                + [ANY] * len(extra),
-                out_specs=[along(spot, tile), pl.BlockSpec((rows, value), whole)],
-                scratch_shapes=[pltpu.VMEM((rows, value), F32)] if final else [],
-            ),
-            input_output_aliases={12: 0} if k else {},
-            compiler_params=params(dimension_semantics=("arbitrary",)),
-            cost_estimate=cost(size),
-            name="base_chunk",
-        )(where, fills, tokens, weight, near, far, mine, theirs, at, grad, rank_grad, total, *extra)
-        early = total
-
+    steps = swapped // tile
+    half = steps // 2
+    turned = lambda i, w, f: (i + w[1] * half) % steps
+    spot = lambda i, w, f: spread // tile + turned(i, w, f)
+    token_gradient, values = pl.pallas_call(
+        functools.partial(swap_kernel, steps),
+        out_shape=[shape(rows, model), shape(rows, value)],
+        grid_spec=pltpu.PrefetchScalarGridSpec(
+            num_scalar_prefetch=2,
+            grid=(steps,),
+            in_specs=[
+                along(spot, tile),
+                down(spot, tile),
+                down(turned, tile),
+                down(turned, tile),
+                down(lambda i, w, f: jnp.minimum(i, half - 1), tile),
+                down(lambda i, w, f: jnp.maximum(i - half, 0), tile),
+                pl.BlockSpec((rank, tile), lambda i, w, f: (0, spot(i, w, f))),
+            ]
+            + resident
+            + [ANY],
+            out_specs=[along(spot, tile), pl.BlockSpec((rows, value), whole)],
+            scratch_shapes=[pltpu.VMEM((rows, value), F32)],
+        ),
+        input_output_aliases={12: 0},
+        compiler_params=params(dimension_semantics=("arbitrary",)),
+        cost_estimate=cost(swapped),
+        name="base_swapped",
+    )(where, fills, tokens, weight, near, far, mine, theirs, at, grad, rank_grad, total, token_gradient)
     grad_down, grad_up = call(
-        after(functools.partial(expand_kernel, group), 7, total),
+        after(functools.partial(expand_kernel, group), 7, values),
         [shape(cut, columns, dtype=F32), shape(width, columns, dtype=F32)],
         [SMEM, SMEM, SMEM] + [VMEM] * 4 + [ANY],
         "expand",
         [pltpu.VMEM((devices * rank, columns), BF16), pltpu.VMEM((ADAPTER_RANK, columns), F32)],
-    )(where, tenants, fills, r0, r1, r2, r3, total)
-    return total, token_gradient, grad_down, grad_up
+    )(where, tenants, fills, r0, r1, r2, r3, values)
+    return values, token_gradient, grad_down, grad_up
 
 
 def solution(mesh):

time: 170 us -> 172 us (1.012)
  between operations: 0.88 us -> 14.1 us
  Pallas kernels: 51.7 us -> 45.1 us
  waiting for transfers between devices: 79.7 us -> 75.4 us
  local copies, waits for them, and re-layouts: 11.9 us -> 7.77 us
  starting transfers between devices: 24.4 us -> 28.2 us
    all_to_all x2, waiting for transfers between devices: 13.6 us -> 2.65 us  [along_tok(): return lax.all_to_all(a, 'tok', split_axis=0, concat_axis=0)]
    ppermute x11 -> x10, waiting for transfers between devices: 66 us -> 72.7 us  [split(): return lambda a: lax.ppermute(a, ('fsdp', 'tok'), pairs)]
    unnamed x42 -> x16, local copies, waits for them, and re-layouts: 11.9 us -> 5.31 us
    pallas_call x9 -> x6, Pallas kernels: 39.7 us -> 33.4 us  [the longest x1 13.5 us: local(): pl.pallas_call(functools.partial(swap_kernel, steps), out_shape=[shape(ro...]
    ppermute x11 -> x10, starting transfers between devices: 14.4 us -> 16.9 us  [split(): return lambda a: lax.ppermute(a, ('fsdp', 'tok'), pairs)]
    dynamic_slice x0 -> x1, local copies, waits for them, and re-layouts: none -> 2.46 us  [local(): lax.dynamic_slice_in_dim(near, core * (swapped // 2), swapped // 2, axis=0)]
  transfers between devices with their start and end apart: 19 -> 15, of which waited for: 7 -> 8; matrix products, arithmetic and copies ran while one was open for 0% -> 1% of each run, Pallas kernels for 21% -> 20%
where the time goes in v8:
time: 172 us; the launch traced here: 171 us
  waiting for transfers between devices  75.4 us (44%)
  Pallas kernels  45.1 us (26%)
  starting transfers between devices  28.2 us (16%)
  between operations  14.1 us (8%)
  local copies, waits for them, and re-layouts  7.77 us (5%)
    ppermute x10, waiting for transfers between devices, split(): return lambda a: lax.ppermute(a, ('fsdp', 'tok'), pairs)  72.7 us
    ppermute x10, starting transfers between devices, split(): return lambda a: lax.ppermute(a, ('fsdp', 'tok'), pairs)  16.9 us
    pallas_call x1, Pallas kernels, local(): pl.pallas_call(functools.partial(swap_kernel, steps), out_shape=[shape(ro...  13.5 us
    all_to_all x2, starting transfers between devices, along_tok(): return lax.all_to_all(a, 'tok', split_axis=0, concat_axis=0)  11.2 us
    pallas_call x1, Pallas kernels, local(): pl.pallas_call(spread_kernel, out_shape=[shape(rows, model), shape(rows,...  9.9 us
    pallas_call x1, Pallas kernels, local(): call(rank_kernel, [shape(rows, value), shape(rows, rank), shape(rank, mod...  6.65 us
    pallas_call x1, Pallas kernels, local(): call(after(functools.partial(expand_kernel, group), 7, values), [shape(cu...  6.37 us
    unnamed x16, local copies, waits for them, and re-layouts  5.31 us
  transfers between devices with their start and end apart: 15, of which 8 were waited for; matrix products, arithmetic and copies ran while one was open for 1% of the time, Pallas kernels for 20%

profile of v8, /device:TPU:0, one launch (start us, length us, event | category | flops | bytes accessed | tf_op | source)
XLA Modules:
  0.0 171.5 jit_solution(8660215205275678394)
XLA Ops:
  7.3 1.6 copy-done
  8.9 0.9 copy-done.2
  10.5 2.5 %select_sent.1.refs_5_ = bf16[512,1152]{1,0:T(8,128)(2,1)S(1)} custom-call(s32[4]{0:T(128)S(1)} %pad_add_fusion.where_ref.refs_0_, s32[64]{0:T(128)S(1)} %copy-done.6, bf16[1024,1024]{1,0:T(8,128)(2,1)S(1)} %copy-done, bf16[128,1024]{1,0:T(8,128)(2,1)S(1)} %copy-done.2), custom_call_target="tpu_custom_call" | custom-call | tf_op jit(solution)/shard_map/select_sent/pallas_call | solution.py:285
  13.0 2.5 %select_kept.1 = (bf16[512,1152]{1,0:T(8,128)(2,1)S(1)}, bf16[384,256]{1,0:T(8,128)(2,1)S(1)}) custom-call(s32[4]{0:T(128)S(1)} %pad_add_fusion.where_ref.refs_0_, s32[64]{0:T(128)S(1)} %copy-done.6, bf16[1024,1024]{1,0:T(8,128)(2,1)S(1)} %copy-done, bf16[128,1024]{1,0:T(8,128)(2,1)S(1)} %copy-done.2, bf16[8192,256]{1,0:T(8,128)(2,1)} %own_ref.3, ...), custom_call_target="tpu_custom_call" | custom-call | tf_op jit(solution)/shard_map/select_kept/pallas_call | solution.py:293
  15.5 3.0 %collective-permute-start.1 = (bf16[384,256]{1,0:T(8,128)(2,1)S(1)}, bf16[384,256]{1,0:T(8,128)(2,1)S(1)}, u32[]{:S(2)}, u32[]{:S(2)}) collective-permute-start(bf16[384,256]{1,0:T(8,128)(2,1)S(1)} %get-tuple-element.22), channel_id=1, source_target_pairs={{0,8},{1,17},{2,10},{3,19},{4,12},{5,21},{6,14},{7,23},{8,0},{9,25... | collective-permute-start | bytes 589832 | tf_op jit(solution)/shard_map/ppermute | solution.py:262
  18.5 1.5 collective-permute-start.2
  20.1 3.7 %collective-permute-done.1 = bf16[384,256]{1,0:T(8,128)(2,1)S(1)} collective-permute-done((bf16[384,256]{1,0:T(8,128)(2,1)S(1)}, bf16[384,256]{1,0:T(8,128)(2,1)S(1)}, u32[]{:S(2)}, u32[]{:S(2)}) %collective-permute-start.1) | collective-permute-done | bytes 196640 | tf_op jit(solution)/shard_map/ppermute | solution.py:262
  23.7 1.6 collective-permute-start.3
  25.3 4.1 %collective-permute-done.3 = bf16[384,256]{1,0:T(8,128)(2,1)S(1)} collective-permute-done((bf16[384,256]{1,0:T(8,128)(2,1)S(1)}, bf16[384,256]{1,0:T(8,128)(2,1)S(1)}, u32[]{:S(2)}, u32[]{:S(2)}) %collective-permute-start.3) | collective-permute-done | bytes 196640 | tf_op jit(solution)/shard_map/ppermute | solution.py:262
  29.4 0.9 pad_maximum_fusion.refs_2_
  30.3 2.5 %collective-permute-start = (bf16[512,1152]{1,0:T(8,128)(2,1)S(1)}, bf16[512,1152]{1,0:T(8,128)(2,1)S(1)}, u32[]{:S(2)}, u32[]{:S(2)}) collective-permute-start(bf16[512,1152]{1,0:T(8,128)(2,1)S(1)} %select_sent.1.refs_5_), channel_id=1, source_target_pairs={{0,8},{1,17},{2,10},{3,19},{4,12},{5,21},{6,14},{7,23},{8,0},{9,25... | collective-permute-start | bytes 3538952 | tf_op jit(solution)/shard_map/ppermute | solution.py:262
  32.8 14.2 %collective-permute-done.refs_1_ = bf16[512,1152]{1,0:T(8,128)(2,1)S(1)} collective-permute-done((bf16[512,1152]{1,0:T(8,128)(2,1)S(1)}, bf16[512,1152]{1,0:T(8,128)(2,1)S(1)}, u32[]{:S(2)}, u32[]{:S(2)}) %collective-permute-start) | collective-permute-done | bytes 1179680 | tf_op jit(solution)/shard_map/ppermute | solution.py:262
  47.0 1.1 copy-done.1
  48.2 1.2 collective-permute-start.4
  49.4 8.8 %collective-permute-done.4.came_ref = bf16[256,1152]{1,0:T(8,128)(2,1)S(1)} collective-permute-done((bf16[256,1152]{1,0:T(8,128)(2,1)S(1)}, bf16[256,1152]{1,0:T(8,128)(2,1)S(1)}, u32[]{:S(2)}, u32[]{:S(2)}) %collective-permute-start.4) | collective-permute-done | bytes 589856 | tf_op jit(solution)/shard_map/ppermute | solution.py:262
  58.2 3.4 %sum_and_cut.1 = (bf16[256,1152]{1,0:T(8,128)(2,1)}, bf16[5120,256]{1,0:T(8,128)(2,1)}) custom-call(bf16[256,1152]{1,0:T(8,128)(2,1)S(1)} %get-tuple-element.23.keep_ref, bf16[256,1152]{1,0:T(8,128)(2,1)S(1)} %collective-permute-done.4.came_ref, bf16[8192,256]{1,0:T(8,128)(2,1)} %own_ref.3), custom_call_target="tpu_custom_call" | custom-call | tf_op jit(solution)/shard_map/sum_and_cut/pallas_call | solution.py:307
  61.7 2.2 %collective-permute-start.5 = (bf16[5120,256]{1,0:T(8,128)(2,1)}, bf16[5120,256]{1,0:T(8,128)(2,1)}, u32[]{:S(2)}, u32[]{:S(2)}) collective-permute-start(bf16[5120,256]{1,0:T(8,128)(2,1)} %get-tuple-element.25), channel_id=1, source_target_pairs={{0,8},{1,17},{2,10},{3,19},{4,12},{5,21},{6,14},{7,23},{8,0},{9,25... | collective-permute-start | bytes 7864328 | tf_op jit(solution)/shard_map/ppermute | solution.py:262
  63.9 5.2 %all-to-all-start = ((bf16[8,32,1152]{2,1,0:T(8,128)(2,1)}), bf16[8,32,1152]{2,1,0:T(8,128)(2,1)S(1)}, u32[]{:S(2)}, u32[]{:S(2)}) async-start(bf16[8,32,1152]{2,1,0:T(8,128)(2,1)} %bitcast.7), calls=%async_computation | async-start | bytes 1179648 | tf_op jit(solution)/shard_map/all_to_all | solution.py:267
  69.1 24.7 %collective-permute-done.5.near_ref = bf16[5120,256]{1,0:T(8,128)(2,1)} collective-permute-done((bf16[5120,256]{1,0:T(8,128)(2,1)}, bf16[5120,256]{1,0:T(8,128)(2,1)}, u32[]{:S(2)}, u32[]{:S(2)}) %collective-permute-start.5) | collective-permute-done | bytes 2621472 | tf_op jit(solution)/shard_map/ppermute | solution.py:262
  93.8 2.5 %constant_dynamic-slice_fusion = bf16[2560,256]{1,0:T(8,128)(2,1)} fusion(bf16[5120,256]{1,0:T(8,128)(2,1)} %collective-permute-done.5.near_ref, s32[]{:T(128)S(6)} %select_n.11), kind=kLoop, calls=%fused_computation.2 | loop fusion | bytes 2621444 | tf_op jit(solution)/shard_map/dynamic_slice | solution.py:318
  96.3 1.0 collective-permute-start.7
  97.3 6.7 %rank_space.1 = (bf16[256,1024]{1,0:T(8,128)(2,1)S(1)}, bf16[256,32]{1,0:T(8,128)(2,1)S(1)}, bf16[32,8192]{1,0:T(8,128)(2,1)S(1)}, bf16[256,1024]{1,0:T(8,128)(2,1)S(1)}, bf16[8,32,1152]{2,1,0:T(8,128)(2,1)}) custom-call(s32[4]{0:T(128)S(1)} %pad_add_fusion.where_ref.refs_0_, s32[64]{0:T(128)S(1)} %copy-done.5, bf16[256,8192]{1,0:T(8,128)(2,1)} %tokens_ref.5, ...), custom_call_target="tpu_custom_call" | custom-call | tf_op jit(solution)/shard_map/rank_space/pallas_call | solution.py:321
  104.0 6.0 %all-to-all-start.1 = ((bf16[8,32,1152]{2,1,0:T(8,128)(2,1)}), bf16[8,32,1152]{2,1,0:T(8,128)(2,1)S(1)}, u32[]{:S(2)}, u32[]{:S(2)}) async-start(bf16[8,32,1152]{2,1,0:T(8,128)(2,1)} %get-tuple-element.35), calls=%async_computation.1 | async-start | bytes 1179648 | tf_op jit(solution)/shard_map/all_to_all | solution.py:267
  110.0 4.2 %collective-permute-done.7.mine_ref = bf16[2560,256]{1,0:T(8,128)(2,1)} collective-permute-done((bf16[2560,256]{1,0:T(8,128)(2,1)}, bf16[2560,256]{1,0:T(8,128)(2,1)}, u32[]{:S(2)}, u32[]{:S(2)}) %collective-permute-start.7) | collective-permute-done | bytes 1310752 | tf_op jit(solution)/shard_map/ppermute | solution.py:262
  114.2 9.9 %base_spread.1 = (bf16[256,8192]{1,0:T(8,128)(2,1)}, f32[256,1024]{1,0:T(8,128)S(1)}) custom-call(bf16[256,8192]{1,0:T(8,128)(2,1)} %tokens_ref.5, bf16[8192,256]{1,0:T(8,128)(2,1)} %own_ref.3, bf16[8,3,384,256]{3,2,1,0:T(8,128)(2,1)} %bitcast.11, bf16[32,8192]{1,0:T(8,128)(2,1)S(1)} %get-tuple-element.27.at_ref, ...), custom_call_target="tpu_custom_call" | custom-call | flops 3221225472 | bytes 11534336 | tf_op jit(solution)/shard_map/base_spread/pallas_call | solution.py:352
  124.1 2.6 %all-to-all-done.1 = bf16[8,32,1152]{2,1,0:T(8,128)(2,1)S(1)} async-done(((bf16[8,32,1152]{2,1,0:T(8,128)(2,1)}), bf16[8,32,1152]{2,1,0:T(8,128)(2,1)S(1)}, u32[]{:S(2)}, u32[]{:S(2)}) %all-to-all-start.1) | async-done | bytes 589856 | tf_op jit(solution)/shard_map/all_to_all | solution.py:267
  127.3 1.7 collective-permute-start.10
  129.1 13.0 %collective-permute-done.9.refs_4_ = bf16[256,1152]{1,0:T(8,128)(2,1)S(1)} collective-permute-done((bf16[256,1152]{1,0:T(8,128)(2,1)S(1)}, bf16[256,1152]{1,0:T(8,128)(2,1)S(1)}, u32[]{:S(2)}, u32[]{:S(2)}) %collective-permute-start.9) | collective-permute-done | bytes 589856 | tf_op jit(solution)/shard_map/ppermute | solution.py:262
  142.1 1.6 collective-permute-start.11
  143.7 13.5 %base_swapped.1 = (bf16[256,8192]{1,0:T(8,128)(2,1)}, bf16[256,1024]{1,0:T(8,128)(2,1)}) custom-call(s32[4]{0:T(128)S(1)} %pad_add_fusion.where_ref.refs_0_, s32[64]{0:T(128)S(1)} %copy-done.5, bf16[256,8192]{1,0:T(8,128)(2,1)} %tokens_ref.5, bf16[8192,256]{1,0:T(8,128)(2,1)} %own_ref.3, ...), custom_call_target="tpu_custom_call", output_to_operand_aliasing={{0}: (12, {})} | custom-call | flops 5368709120 | bytes 17825792 | tf_op jit(solution)/shard_map/base_swapped/pallas_call | solution.py:379
  157.2 1.0 copy-done.4
  158.3 6.4 %expand.1 = (f32[1024,1024]{1,0:T(8,128)}, f32[128,1024]{1,0:T(8,128)}) custom-call(s32[4]{0:T(128)S(1)} %pad_add_fusion.where_ref.refs_0_, s32[64]{0:T(128)S(1)} %copy-done.7, s32[64]{0:T(128)S(1)} %copy-done.5, bf16[256,1152]{1,0:T(8,128)(2,1)S(1)} %gate.1.refs_3_, bf16[256,1152]{1,0:T(8,128)(2,1)S(1)} %collective-permute-done.9.refs_4_, ...), custom_call_target="tpu_custom_call" | custom-call | tf_op jit(solution)/shard_map/expand/pallas_call | solution.py:404
  (27 shorter events, 1.6 us)
Async XLA Ops:
  7.2 107.0 %all-gather.3.cloned.1.call-start = ((), (), s32[]{:S(2)}) async-start(), calls=%async_computation.2 | async-start | bytes 5308416 | tf_op jit(solution)/shard_map/all_gather | solution.py:302
  7.3 1.6 copy-start
  8.9 0.9 copy-start.2
  9.8 0.7 copy-start.6
  15.5 8.2 %collective-permute-start.1 = (bf16[384,256]{1,0:T(8,128)(2,1)S(1)}, bf16[384,256]{1,0:T(8,128)(2,1)S(1)}, u32[]{:S(2)}, u32[]{:S(2)}) collective-permute-start(bf16[384,256]{1,0:T(8,128)(2,1)S(1)} %get-tuple-element.22), channel_id=1, source_target_pairs={{0,8},{1,17},{2,10},{3,19},{4,12},{5,21},{6,14},{7,23},{8,0},{9,25... | collective-permute-start | bytes 589832 | tf_op jit(solution)/shard_map/ppermute | solution.py:262
  18.5 6.8 %collective-permute-start.2 = (bf16[384,256]{1,0:T(8,128)(2,1)S(1)}, bf16[384,256]{1,0:T(8,128)(2,1)S(1)}, u32[]{:S(2)}, u32[]{:S(2)}) collective-permute-start(bf16[384,256]{1,0:T(8,128)(2,1)S(1)} %get-tuple-element.22), channel_id=1, source_target_pairs={{0,16},{1,9},{2,18},{3,11},{4,20},{5,13},{6,22},{7,15},{8,24},{9,1... | collective-permute-start | bytes 589832 | tf_op jit(solution)/shard_map/ppermute | solution.py:262
  23.7 5.7 %collective-permute-start.3 = (bf16[384,256]{1,0:T(8,128)(2,1)S(1)}, bf16[384,256]{1,0:T(8,128)(2,1)S(1)}, u32[]{:S(2)}, u32[]{:S(2)}) collective-permute-start(bf16[384,256]{1,0:T(8,128)(2,1)S(1)} %collective-permute-done.1), channel_id=1, source_target_pairs={{0,16},{1,9},{2,18},{3,11},{4,20},{5,13},{6,22},{7,15},{8,24},{9,1... | collective-permute-start | bytes 589832 | tf_op jit(solution)/shard_map/ppermute | solution.py:262
  30.3 16.7 %collective-permute-start = (bf16[512,1152]{1,0:T(8,128)(2,1)S(1)}, bf16[512,1152]{1,0:T(8,128)(2,1)S(1)}, u32[]{:S(2)}, u32[]{:S(2)}) collective-permute-start(bf16[512,1152]{1,0:T(8,128)(2,1)S(1)} %select_sent.1.refs_5_), channel_id=1, source_target_pairs={{0,8},{1,17},{2,10},{3,19},{4,12},{5,21},{6,14},{7,23},{8,0},{9,25... | collective-permute-start | bytes 3538952 | tf_op jit(solution)/shard_map/ppermute | solution.py:262
  47.0 1.1 copy-start.1
  48.2 9.9 %collective-permute-start.4 = (bf16[256,1152]{1,0:T(8,128)(2,1)S(1)}, bf16[256,1152]{1,0:T(8,128)(2,1)S(1)}, u32[]{:S(2)}, u32[]{:S(2)}) collective-permute-start(bf16[256,1152]{1,0:T(8,128)(2,1)S(1)} %get-tuple-element.24), channel_id=1, source_target_pairs={{0,16},{1,9},{2,18},{3,11},{4,20},{5,13},{6,22},{7,15},{8,24},{9,1... | collective-permute-start | bytes 1769480 | tf_op jit(solution)/shard_map/ppermute | solution.py:262
  61.6 35.7 %copy-start.3 = (bf16[256,1024]{1,0:T(8,128)(2,1)S(1)}, bf16[256,1024]{1,0:T(8,128)(2,1)}, u32[]{:S(2)}) copy-start(bf16[256,1024]{1,0:T(8,128)(2,1)} %cot_ref.1) | copy-start | bytes 1572868
  61.6 35.7 %copy-start.5 = (s32[64]{0:T(128)S(1)}, s32[64]{0:T(128)}, u32[]{:S(2)}) copy-start(s32[64]{0:T(128)} %refs_2_.3) | copy-start | bytes 772
  61.7 32.2 %collective-permute-start.5 = (bf16[5120,256]{1,0:T(8,128)(2,1)}, bf16[5120,256]{1,0:T(8,128)(2,1)}, u32[]{:S(2)}, u32[]{:S(2)}) collective-permute-start(bf16[5120,256]{1,0:T(8,128)(2,1)} %get-tuple-element.25), channel_id=1, source_target_pairs={{0,8},{1,17},{2,10},{3,19},{4,12},{5,21},{6,14},{7,23},{8,0},{9,25... | collective-permute-start | bytes 7864328 | tf_op jit(solution)/shard_map/ppermute | solution.py:262
  63.9 33.4 %all-to-all-start = ((bf16[8,32,1152]{2,1,0:T(8,128)(2,1)}), bf16[8,32,1152]{2,1,0:T(8,128)(2,1)S(1)}, u32[]{:S(2)}, u32[]{:S(2)}) async-start(bf16[8,32,1152]{2,1,0:T(8,128)(2,1)} %bitcast.7), calls=%async_computation | async-start | bytes 1179648 | tf_op jit(solution)/shard_map/all_to_all | solution.py:267
  93.8 49.9 %collective-permute-start.6 = (bf16[5120,256]{1,0:T(8,128)(2,1)}, bf16[5120,256]{1,0:T(8,128)(2,1)}, u32[]{:S(2)}, u32[]{:S(2)}) collective-permute-start(bf16[5120,256]{1,0:T(8,128)(2,1)} %collective-permute-done.5.near_ref), channel_id=1, source_target_pairs={{0,1},{1,0},{2,3},{3,2},{4,5},{5,4},{6,7},{7,6},{8,9},{9,8},{10,11... | collective-permute-start | bytes 7864328 | tf_op jit(solution)/shard_map/ppermute | solution.py:254
  96.3 17.9 %collective-permute-start.7 = (bf16[2560,256]{1,0:T(8,128)(2,1)}, bf16[2560,256]{1,0:T(8,128)(2,1)}, u32[]{:S(2)}, u32[]{:S(2)}) collective-permute-start(bf16[2560,256]{1,0:T(8,128)(2,1)} %constant_dynamic-slice_fusion), channel_id=1, source_target_pairs={{0,16},{1,9},{2,18},{3,11},{4,20},{5,13},{6,22},{7,15},{8,24},{9,1... | collective-permute-start | bytes 3932168 | tf_op jit(solution)/shard_map/ppermute | solution.py:262
  104.0 22.8 %all-to-all-start.1 = ((bf16[8,32,1152]{2,1,0:T(8,128)(2,1)}), bf16[8,32,1152]{2,1,0:T(8,128)(2,1)S(1)}, u32[]{:S(2)}, u32[]{:S(2)}) async-start(bf16[8,32,1152]{2,1,0:T(8,128)(2,1)} %get-tuple-element.35), calls=%async_computation.1 | async-start | bytes 1179648 | tf_op jit(solution)/shard_map/all_to_all | solution.py:267
  114.2 29.5 %collective-permute-start.8 = (bf16[2560,256]{1,0:T(8,128)(2,1)}, bf16[2560,256]{1,0:T(8,128)(2,1)}, u32[]{:S(2)}, u32[]{:S(2)}) collective-permute-start(bf16[2560,256]{1,0:T(8,128)(2,1)} %collective-permute-done.7.mine_ref), channel_id=1, source_target_pairs={{0,1},{1,0},{2,3},{3,2},{4,5},{5,4},{6,7},{7,6},{8,9},{9,8},{10,11... | collective-permute-start | bytes 3932168 | tf_op jit(solution)/shard_map/ppermute | solution.py:254
  126.8 15.3 %collective-permute-start.9 = (bf16[256,1152]{1,0:T(8,128)(2,1)S(1)}, bf16[256,1152]{1,0:T(8,128)(2,1)S(1)}, u32[]{:S(2)}, u32[]{:S(2)}) collective-permute-start(bf16[256,1152]{1,0:T(8,128)(2,1)S(1)} %gate.1.refs_3_), channel_id=1, source_target_pairs={{0,8},{1,17},{2,10},{3,19},{4,12},{5,21},{6,14},{7,23},{8,0},{9,25... | collective-permute-start | bytes 1769480 | tf_op jit(solution)/shard_map/ppermute | solution.py:262
  127.3 29.9 %collective-permute-start.10 = (bf16[256,1152]{1,0:T(8,128)(2,1)S(1)}, bf16[256,1152]{1,0:T(8,128)(2,1)S(1)}, u32[]{:S(2)}, u32[]{:S(2)}) collective-permute-start(bf16[256,1152]{1,0:T(8,128)(2,1)S(1)} %gate.1.refs_3_), channel_id=1, source_target_pairs={{0,16},{1,9},{2,18},{3,11},{4,20},{5,13},{6,22},{7,15},{8,24},{9,1... | collective-permute-start | bytes 1769480 | tf_op jit(solution)/shard_map/ppermute | solution.py:262
  142.1 15.1 %collective-permute-start.11 = (bf16[256,1152]{1,0:T(8,128)(2,1)S(1)}, bf16[256,1152]{1,0:T(8,128)(2,1)S(1)}, u32[]{:S(2)}, u32[]{:S(2)}) collective-permute-start(bf16[256,1152]{1,0:T(8,128)(2,1)S(1)} %collective-permute-done.9.refs_4_), channel_id=1, source_target_pairs={{0,16},{1,9},{2,18},{3,11},{4,20},{5,13},{6,22},{7,15},{8,24},{9,1... | collective-permute-start | bytes 1769480 | tf_op jit(solution)/shard_map/ppermute | solution.py:262
  143.7 13.5 %copy-start.7 = (s32[64]{0:T(128)S(1)}, s32[64]{0:T(128)}, u32[]{:S(2)}) copy-start(s32[64]{0:T(128)} %refs_1_.3) | copy-start | bytes 772
  157.2 1.0 copy-start.4
Sparse Core Ops, SparseCore 0:
  30.4 63.8 all-gather.2

commit v9 on v7

--- a/solution.py
+++ b/solution.py
@@ -10,7 +10,7 @@
 ADAPTER_RANK = 16
 BLOCK = 128
 ADAPTER_SCALE = 2.0
-CHUNKS = (3, 3, 2)
+CHUNKS = (5, 3)
 VMEM_LIMIT = 48 * 1024 * 1024
 
 F32 = jnp.float32
@@ -60,23 +60,19 @@
     picked(pick_ref, down_ref, up_ref, out_ref)
 
 
-def keep_select_kernel(group, where_ref, tenant_ref, down_ref, up_ref, weight_ref, out_ref, piece_ref, pick_ref, sem):
-    copy = pltpu.make_async_copy(weight_ref.at[pl.ds(0, piece_ref.shape[0]), :], piece_ref, sem)
-    copy.start()
+def keep_select_kernel(group, where_ref, tenant_ref, down_ref, up_ref, out_ref, pick_ref):
     here, core = where_ref[0], where_ref[1]
     pick_two(group, tenant_ref, pick_ref, here, (0, 2 - core))
     picked(pick_ref, down_ref, up_ref, out_ref)
-    copy.wait()
-
-
-def sum_two_kernel(kept_ref, came_ref, keep_ref, send_ref):
+
+
+def sum_two_kernel(kept_ref, came_ref, weight_ref, keep_ref, send_ref, piece_ref, sem):
+    copy = pltpu.make_async_copy(weight_ref.at[pl.ds(0, piece_ref.shape[0]), :], piece_ref, sem)
+    copy.start()
     rows = keep_ref.shape[0]
     send_ref[...] = kept_ref[rows:, :] + came_ref[rows:, :]
     keep_ref[...] = kept_ref[:rows, :] + came_ref[:rows, :]
-
-
-def sum_kernel(keep_ref, came_ref, out_ref):
-    out_ref[...] = keep_ref[...] + came_ref[...]
+    copy.wait()
 
 
 def cut_kernel(start, where_ref, near_ref, weight_ref, half_ref, *refs):
@@ -286,16 +282,33 @@
         [pick],
     )(where, tenants, down_maps, up_maps)
     came = first_way(sent)
-    kept, piece = call(
-        after(functools.partial(keep_select_kernel, group), 5, sent),
-        [shape(2 * group_rank, both), shape(parts[0][1], wide)],
-        [SMEM, SMEM, VMEM, VMEM, ANY, ANY],
+    kept = call(
+        after(functools.partial(keep_select_kernel, group), 4, sent),
+        shape(2 * group_rank, both),
+        [SMEM, SMEM, VMEM, VMEM, ANY],
         "select_kept",
-        [pick, pltpu.SemaphoreType.DMA],
-    )(where, tenants, down_maps, up_maps, weight, sent)
-    keep, sent = call(sum_two_kernel, [shape(group_rank, both)] * 2, [VMEM] * 2, "sum_two")(kept, came)
+        [pick],
+    )(where, tenants, down_maps, up_maps, sent)
+    keep, sent, piece = call(
+        sum_two_kernel,
+        [shape(group_rank, both)] * 2 + [shape(parts[0][1], wide)],
+        [VMEM, VMEM, ANY],
+        "sum_and_cut",
+        [pltpu.SemaphoreType.DMA],
+    )(kept, came, weight)
+    maps = along_tok((keep + second_way(sent)).reshape(shards, rank, both))
 
     arrived = []
+
+    def pass_after(a, *earlier):
+        return call(
+            lambda *refs: None,
+            shape(*a.shape),
+            [ANY] * (1 + len(earlier)),
+            "pass_after",
+            out_specs=ANY,
+            input_output_aliases={0: 0},
+        )(a, *earlier)
 
     def cut_chunk(*earlier):
         k = len(arrived)
@@ -308,20 +321,16 @@
             "cut_chunk",
             [pltpu.SemaphoreType.DMA((2,))],
         )(where, near, weight, *earlier)
-        mine = second_way(part)
-        arrived.append((near, on_core(near), mine, on_core(mine)))
+        near = pass_after(near, part)
+        arrived.append((near, on_core(near), second_way(part)))
         pieces.extend(cuts)
         return part
 
     pieces = [piece]
-    part = cut_chunk(sent)
-    maps = call(after(sum_kernel, 2, part), shape(group_rank, both), [VMEM, VMEM, ANY], "sum")(
-        keep, second_way(sent), part
-    )
-    maps = along_tok(maps.reshape(shards, rank, both))
+    part = cut_chunk(maps)
 
     grad, rank_grad, at, lora, terms = call(
-        rank_kernel,
+        after(rank_kernel, 5, part),
         [
             shape(rows, value),
             shape(rows, rank),
@@ -329,10 +338,10 @@
             shape(rows, value),
             shape(shards, rank, both),
         ],
-        [SMEM, SMEM, VMEM, VMEM, VMEM],
+        [SMEM, SMEM, VMEM, VMEM, VMEM, ANY],
         "rank_space",
         [pltpu.VMEM((rank, value), BF16)] * 2,
-    )(where, fills, tokens, cotangent, maps)
+    )(where, fills, tokens, cotangent, maps, part)
     r0 = along_tok(terms).reshape(group_rank, both)
     r1, r2 = first_way(r0), second_way(r0)
     r3 = second_way(r1)
@@ -354,16 +363,18 @@
         )
 
     tile = 512
-    total, token_gradient, early = lora, None, rank_grad
+    total, token_gradient = lora, None
     for k, (start, size) in enumerate(parts):
         final = k == len(parts) - 1
         steps = size // tile
         half = steps // 2
-        part = None if final else cut_chunk(early, arrived[k][1], arrived[k][3])
-        near, far, mine, theirs = arrived[k]
+        part = None if final else cut_chunk(r0, arrived[k][1])
+        near, far, mine = arrived[k]
+        mine = pass_after(mine, *((r1, r2, total) if final else (r0,)))
+        theirs = on_core(mine)
         turned = lambda i, w, f, half=half, steps=steps: (i + w[1] * half) % steps
         spot = lambda i, w, f, start=start, turned=turned: start // tile + turned(i, w, f)
-        extra = [a for a in (token_gradient, part, r0 if k == 0 else None) if a is not None]
+        extra = [a for a in (token_gradient, part) if a is not None]
         token_gradient, total = pl.pallas_call(
             functools.partial(base_kernel, steps, final),
             out_shape=[shape(rows, model), shape(rows, value, dtype=BF16 if final else F32)],
@@ -389,7 +400,6 @@
             cost_estimate=cost(size),
             name="base_chunk",
         )(where, fills, tokens, weight, near, far, mine, theirs, at, grad, rank_grad, total, *extra)
-        early = total
 
     grad_down, grad_up = call(
         after(functools.partial(expand_kernel, group), 7, total),

time: 170 us -> 149 us (0.88)
  waiting for transfers between devices: 79.7 us -> 56.9 us
  blocking collectives: 0 us -> 21.4 us
  starting transfers between devices: 24.4 us -> 16.2 us
  Pallas kernels: 51.7 us -> 44 us
  local copies, waits for them, and re-layouts: 11.9 us -> 8.92 us
    ppermute x11 -> x9, waiting for transfers between devices: 66 us -> 39.5 us  [split(): return lambda a: lax.ppermute(a, ('fsdp', 'tok'), pairs)]
    all_to_all x0 -> x1, blocking collectives: none -> 21.4 us  [along_tok(): return lax.all_to_all(a, 'tok', split_axis=0, concat_axis=0)]
    all_to_all x2 -> x1, starting transfers between devices: 9.89 us -> 3.54 us  [along_tok(): return lax.all_to_all(a, 'tok', split_axis=0, concat_axis=0)]
    pallas_call x3 -> x2, Pallas kernels: 9.09 us -> 2.99 us  [cut_chunk(): call(after(functools.partial(cut_kernel, nexts[0][0] if nexts else 0), 3,...]
    unnamed x42 -> x30, local copies, waits for them, and re-layouts: 11.9 us -> 8.92 us
    all_to_all x2 -> x1, waiting for transfers between devices: 13.6 us -> 16.1 us  [along_tok(): return lax.all_to_all(a, 'tok', split_axis=0, concat_axis=0)]
    pallas_call x3 -> x2, Pallas kernels: 23.6 us -> 21.2 us  [local(): pl.pallas_call(functools.partial(base_kernel, steps, final), out_shape=[s...]
    ppermute x11 -> x9, starting transfers between devices: 14.4 us -> 12.7 us  [split(): return lambda a: lax.ppermute(a, ('fsdp', 'tok'), pairs)]
  transfers between devices with their start and end apart: 19 -> 14, of which waited for: 7 -> 7; matrix products, arithmetic and copies ran while one was open for 0% -> 0% of each run, Pallas kernels for 21% -> 21%
where the time goes in v9:
time: 149 us; the launch traced here: 148 us
  waiting for transfers between devices  56.9 us (38%)
  Pallas kernels  44 us (30%)
  blocking collectives  21.4 us (14%)
  starting transfers between devices  16.2 us (11%)
  local copies, waits for them, and re-layouts  8.92 us (6%)
    ppermute x9, waiting for transfers between devices, split(): return lambda a: lax.ppermute(a, ('fsdp', 'tok'), pairs)  39.5 us
    all_to_all x1, blocking collectives, along_tok(): return lax.all_to_all(a, 'tok', split_axis=0, concat_axis=0)  21.4 us
    pallas_call x2, Pallas kernels, local(): pl.pallas_call(functools.partial(base_kernel, steps, final), out_shape=[s...  21.2 us
    all_to_all x1, waiting for transfers between devices, along_tok(): return lax.all_to_all(a, 'tok', split_axis=0, concat_axis=0)  16.1 us
    ppermute x9, starting transfers between devices, split(): return lambda a: lax.ppermute(a, ('fsdp', 'tok'), pairs)  12.7 us
    unnamed x30, local copies, waits for them, and re-layouts  8.92 us
    pallas_call x1, Pallas kernels, local(): call(after(rank_kernel, 5, part), [shape(rows, value), shape(rows, rank),...  6.61 us
    pallas_call x1, Pallas kernels, local(): call(after(functools.partial(expand_kernel, group), 7, total), [shape(cut...  6.38 us
  transfers between devices with their start and end apart: 14, of which 7 were waited for; matrix products, arithmetic and copies ran while one was open for 0% of the time, Pallas kernels for 21%

profile of v9, /device:TPU:0, one launch (start us, length us, event | category | flops | bytes accessed | tf_op | source)
XLA Modules:
  0.0 148.5 jit_solution(17834929746308365086)
XLA Ops:
  0.7 1.6 %copy-done = bf16[1024,1024]{1,0:T(8,128)(2,1)S(1)} copy-done((bf16[1024,1024]{1,0:T(8,128)(2,1)S(1)}, bf16[1024,1024]{1,0:T(8,128)(2,1)}, u32[]{:S(2)}) %copy-start) | copy-done | bytes 2097176
  2.3 0.9 copy-done.1
  3.9 2.5 %select_sent.1.refs_4_ = bf16[512,1152]{1,0:T(8,128)(2,1)S(1)} custom-call(s32[4]{0:T(128)S(1)} %pad_add_fusion.where_ref.refs_0_, s32[64]{0:T(128)S(1)} %copy-done.9, bf16[1024,1024]{1,0:T(8,128)(2,1)S(1)} %copy-done, bf16[128,1024]{1,0:T(8,128)(2,1)S(1)} %copy-done.1), custom_call_target="tpu_custom_call" | custom-call | tf_op jit(solution)/shard_map/select_sent/pallas_call | solution.py:277
  6.4 3.0 %collective-permute-start = (bf16[512,1152]{1,0:T(8,128)(2,1)S(1)}, bf16[512,1152]{1,0:T(8,128)(2,1)S(1)}, u32[]{:S(2)}, u32[]{:S(2)}) collective-permute-start(bf16[512,1152]{1,0:T(8,128)(2,1)S(1)} %select_sent.1.refs_4_), channel_id=1, source_target_pairs={{0,8},{1,17},{2,10},{3,19},{4,12},{5,21},{6,14},{7,23},{8,0},{9,25... | collective-permute-start | bytes 3538952 | tf_op jit(solution)/shard_map/ppermute | solution.py:255
  9.4 2.5 %select_kept.1.kept_ref = bf16[512,1152]{1,0:T(8,128)(2,1)S(1)} custom-call(s32[4]{0:T(128)S(1)} %pad_add_fusion.where_ref.refs_0_, s32[64]{0:T(128)S(1)} %copy-done.9, bf16[1024,1024]{1,0:T(8,128)(2,1)S(1)} %copy-done, bf16[128,1024]{1,0:T(8,128)(2,1)S(1)} %copy-done.1, bf16[512,1152]{1,0:T(8,128)(2,1)S(1)} %select_sent.1.refs_4_), custom_call_target="tpu_custom_call" | custom-call | tf_op jit(solution)/shard_map/select_kept/pallas_call | solution.py:285
  11.9 11.7 %collective-permute-done.came_ref = bf16[512,1152]{1,0:T(8,128)(2,1)S(1)} collective-permute-done((bf16[512,1152]{1,0:T(8,128)(2,1)S(1)}, bf16[512,1152]{1,0:T(8,128)(2,1)S(1)}, u32[]{:S(2)}, u32[]{:S(2)}) %collective-permute-start) | collective-permute-done | bytes 1179680 | tf_op jit(solution)/shard_map/ppermute | solution.py:255
  23.6 1.7 %sum_and_cut.1 = (bf16[256,1152]{1,0:T(8,128)(2,1)S(1)}, bf16[256,1152]{1,0:T(8,128)(2,1)S(1)}, bf16[5120,256]{1,0:T(8,128)(2,1)S(1)}) custom-call(bf16[512,1152]{1,0:T(8,128)(2,1)S(1)} %select_kept.1.kept_ref, bf16[512,1152]{1,0:T(8,128)(2,1)S(1)} %collective-permute-done.came_ref, bf16[8192,256]{1,0:T(8,128)(2,1)} %own_ref.3), custom_call_target="tpu_custom_call" | custom-call | tf_op jit(solution)/shard_map/sum_and_cut/pallas_call | solution.py:292
  25.4 2.1 %collective-permute-start.1 = (bf16[5120,256]{1,0:T(8,128)(2,1)S(1)}, bf16[5120,256]{1,0:T(8,128)(2,1)}, u32[]{:S(2)}, u32[]{:S(2)}) collective-permute-start(bf16[5120,256]{1,0:T(8,128)(2,1)S(1)} %get-tuple-element.20), channel_id=1, source_target_pairs={{0,8},{1,17},{2,10},{3,19},{4,12},{5,21},{6,14},{7,23},{8,0},{9,25... | collective-permute-start | bytes 7864328 | tf_op jit(solution)/shard_map/ppermute | solution.py:255
  27.5 1.5 %collective-permute-start.2 = (bf16[256,1152]{1,0:T(8,128)(2,1)S(1)}, bf16[256,1152]{1,0:T(8,128)(2,1)S(1)}, u32[]{:S(2)}, u32[]{:S(2)}) collective-permute-start(bf16[256,1152]{1,0:T(8,128)(2,1)S(1)} %get-tuple-element.22), channel_id=1, source_target_pairs={{0,16},{1,9},{2,18},{3,11},{4,20},{5,13},{6,22},{7,15},{8,24},{9,1... | collective-permute-start | bytes 1769480 | tf_op jit(solution)/shard_map/ppermute | solution.py:255
  29.0 14.7 %collective-permute-done.2 = bf16[256,1152]{1,0:T(8,128)(2,1)S(1)} collective-permute-done((bf16[256,1152]{1,0:T(8,128)(2,1)S(1)}, bf16[256,1152]{1,0:T(8,128)(2,1)S(1)}, u32[]{:S(2)}, u32[]{:S(2)}) %collective-permute-start.2) | collective-permute-done | bytes 589856 | tf_op jit(solution)/shard_map/ppermute | solution.py:255
  43.9 21.4 %all_to_all.10.refs_3_.refs_4_ = bf16[8,32,1152]{2,1,0:T(8,128)(2,1)S(1)} all-to-all(bf16[8,32,1152]{2,1,0:T(8,128)(2,1)S(1)} %bitcast.11), channel_id=1, replica_groups=mesh['fsdp'=4,'tok'=8] {'tok'}, dimensions={0} | all-to-all | bytes 1179648 | tf_op jit(solution)/shard_map/all_to_all | solution.py:260
  65.3 2.4 %cut_chunk.2 = (bf16[2560,256]{1,0:T(8,128)(2,1)S(1)}, bf16[3072,256]{1,0:T(8,128)(2,1)S(1)}) custom-call(s32[4]{0:T(128)S(1)} %pad_add_fusion.where_ref.refs_0_, bf16[5120,256]{1,0:T(8,128)(2,1)} %collective-permute-done.1.refs_1_.refs_0_, bf16[8192,256]{1,0:T(8,128)(2,1)} %own_ref.3, bf16[8,32,1152]{2,1,0:T(8,128)(2,1)S(1)} %all_to_all.10.refs_3_.refs_4_), custom_call_target="tpu_custom_call" | custom-call | tf_op jit(solution)/shard_map/cut_chunk/pallas_call | solution.py:317
  67.7 1.1 copy-done.11
  68.9 1.6 %collective-permute-start.9 = (bf16[2560,256]{1,0:T(8,128)(2,1)S(1)}, bf16[2560,256]{1,0:T(8,128)(2,1)}, u32[]{:S(2)}, u32[]{:S(2)}) collective-permute-start(bf16[2560,256]{1,0:T(8,128)(2,1)S(1)} %get-tuple-element.24.refs_5_.refs_1_), channel_id=1, source_target_pairs={{0,16},{1,9},{2,18},{3,11},{4,20},{5,13},{6,22},{7,15},{8,24},{9,1... | collective-permute-start | bytes 3932168 | tf_op jit(solution)/shard_map/ppermute | solution.py:255
  70.4 6.6 %rank_space.1 = (bf16[256,1024]{1,0:T(8,128)(2,1)S(1)}, bf16[256,32]{1,0:T(8,128)(2,1)S(1)}, bf16[32,8192]{1,0:T(8,128)(2,1)S(1)}, bf16[256,1024]{1,0:T(8,128)(2,1)S(1)}, bf16[8,32,1152]{2,1,0:T(8,128)(2,1)}) custom-call(s32[4]{0:T(128)S(1)} %pad_add_fusion.where_ref.refs_0_, s32[64]{0:T(128)S(1)} %copy-done.8, bf16[256,8192]{1,0:T(8,128)(2,1)} %tokens_ref.3, ...), custom_call_target="tpu_custom_call" | custom-call | tf_op jit(solution)/shard_map/rank_space/pallas_call | solution.py:332
  77.1 0.8 copy-done.2
  77.8 0.8 copy-done.4
  78.6 0.8 copy-done.12
  79.4 3.5 %all-to-all-start.1 = ((bf16[8,32,1152]{2,1,0:T(8,128)(2,1)}), bf16[8,32,1152]{2,1,0:T(8,128)(2,1)S(1)}, u32[]{:S(2)}, u32[]{:S(2)}) async-start(bf16[8,32,1152]{2,1,0:T(8,128)(2,1)} %get-tuple-element.25), calls=%async_computation.1 | async-start | bytes 1179648 | tf_op jit(solution)/shard_map/all_to_all | solution.py:260
  83.6 16.1 %all-to-all-done.1 = bf16[8,32,1152]{2,1,0:T(8,128)(2,1)S(1)} async-done(((bf16[8,32,1152]{2,1,0:T(8,128)(2,1)}), bf16[8,32,1152]{2,1,0:T(8,128)(2,1)S(1)}, u32[]{:S(2)}, u32[]{:S(2)}) %all-to-all-start.1) | async-done | bytes 589856 | tf_op jit(solution)/shard_map/all_to_all | solution.py:260
  99.7 4.0 %collective-permute-done.3.refs_1_.refs_0_ = bf16[3072,256]{1,0:T(8,128)(2,1)S(1)} collective-permute-done((bf16[3072,256]{1,0:T(8,128)(2,1)}, bf16[3072,256]{1,0:T(8,128)(2,1)S(1)}, u32[]{:S(2)}, u32[]{:S(2)}) %collective-permute-start.3) | collective-permute-done | bytes 1572896 | tf_op jit(solution)/shard_map/ppermute | solution.py:255
  104.3 1.0 collective-permute-start.6
  106.0 1.3 collective-permute-start.8
  107.2 12.7 %base_chunk.2 = (bf16[256,8192]{1,0:T(8,128)(2,1)}, f32[256,1024]{1,0:T(8,128)S(1)}) custom-call(s32[4]{0:T(128)S(1)} %pad_add_fusion.where_ref.refs_0_, s32[64]{0:T(128)S(1)} %copy-done.8, bf16[256,8192]{1,0:T(8,128)(2,1)} %tokens_ref.3, bf16[8192,256]{1,0:T(8,128)(2,1)} %own_ref.3, bf16[5120,256]{1,0:T(8,128)(2,1)} %pass_after.4.near_ref, ...), custom_call_target="tpu_custom_call" | custom-call | flops 5368709120 | bytes 17825792 | tf_op jit(solution)/shard_map/base_chunk/pallas_call | solution.py:378
  119.9 1.7 %collective-permute-done.7.refs_1_.refs_4_ = bf16[256,1152]{1,0:T(8,128)(2,1)S(1)} collective-permute-done((bf16[256,1152]{1,0:T(8,128)(2,1)S(1)}, bf16[256,1152]{1,0:T(8,128)(2,1)S(1)}, u32[]{:S(2)}, u32[]{:S(2)}) %collective-permute-start.7) | collective-permute-done | bytes 589856 | tf_op jit(solution)/shard_map/ppermute | solution.py:255
  121.6 7.4 %collective-permute-done.8.refs_2_.refs_5_ = bf16[256,1152]{1,0:T(8,128)(2,1)S(1)} collective-permute-done((bf16[256,1152]{1,0:T(8,128)(2,1)S(1)}, bf16[256,1152]{1,0:T(8,128)(2,1)S(1)}, u32[]{:S(2)}, u32[]{:S(2)}) %collective-permute-start.8) | collective-permute-done | bytes 589856 | tf_op jit(solution)/shard_map/ppermute | solution.py:255
  129.0 1.0 collective-permute-start.12
  130.1 1.3 collective-permute-done.11.theirs_ref
  131.3 1.1 copy-done.14
  132.5 8.6 %base_chunk.3 = (bf16[256,8192]{1,0:T(8,128)(2,1)}, bf16[256,1024]{1,0:T(8,128)(2,1)}) custom-call(s32[4]{0:T(128)S(1)} %pad_add_fusion.where_ref.refs_0_, s32[64]{0:T(128)S(1)} %copy-done.8, bf16[256,8192]{1,0:T(8,128)(2,1)} %tokens_ref.3, bf16[8192,256]{1,0:T(8,128)(2,1)} %own_ref.3, ...), custom_call_target="tpu_custom_call", output_to_operand_aliasing={{0}: (12, {})} | custom-call | flops 3221225472 | bytes 11534336 | tf_op jit(solution)/shard_map/base_chunk/pallas_call | solution.py:378
  141.1 1.0 copy-done.6
  142.1 6.4 %expand.1 = (f32[1024,1024]{1,0:T(8,128)}, f32[128,1024]{1,0:T(8,128)}) custom-call(s32[4]{0:T(128)S(1)} %pad_add_fusion.where_ref.refs_0_, s32[64]{0:T(128)S(1)} %copy-done.10, s32[64]{0:T(128)S(1)} %copy-done.8, bf16[256,1152]{1,0:T(8,128)(2,1)S(1)} %bitcast.10, bf16[256,1152]{1,0:T(8,128)(2,1)S(1)} %collective-permute-done.7.refs_1_.refs_4_, ...), custom_call_target="tpu_custom_call" | custom-call | tf_op jit(solution)/shard_map/expand/pallas_call | solution.py:404
  (42 shorter events, 2.8 us)
Async XLA Ops:
  0.7 1.6 %copy-start = (bf16[1024,1024]{1,0:T(8,128)(2,1)S(1)}, bf16[1024,1024]{1,0:T(8,128)(2,1)}, u32[]{:S(2)}) copy-start(bf16[1024,1024]{1,0:T(8,128)(2,1)} %refs_2_.5) | copy-start | bytes 6291460
  2.3 0.9 copy-start.1
  3.3 0.7 copy-start.9
  6.4 17.2 %collective-permute-start = (bf16[512,1152]{1,0:T(8,128)(2,1)S(1)}, bf16[512,1152]{1,0:T(8,128)(2,1)S(1)}, u32[]{:S(2)}, u32[]{:S(2)}) collective-permute-start(bf16[512,1152]{1,0:T(8,128)(2,1)S(1)} %select_sent.1.refs_4_), channel_id=1, source_target_pairs={{0,8},{1,17},{2,10},{3,19},{4,12},{5,21},{6,14},{7,23},{8,0},{9,25... | collective-permute-start | bytes 3538952 | tf_op jit(solution)/shard_map/ppermute | solution.py:255
  25.4 39.9 %collective-permute-start.1 = (bf16[5120,256]{1,0:T(8,128)(2,1)S(1)}, bf16[5120,256]{1,0:T(8,128)(2,1)}, u32[]{:S(2)}, u32[]{:S(2)}) collective-permute-start(bf16[5120,256]{1,0:T(8,128)(2,1)S(1)} %get-tuple-element.20), channel_id=1, source_target_pairs={{0,8},{1,17},{2,10},{3,19},{4,12},{5,21},{6,14},{7,23},{8,0},{9,25... | collective-permute-start | bytes 7864328 | tf_op jit(solution)/shard_map/ppermute | solution.py:255
  27.5 16.3 %collective-permute-start.2 = (bf16[256,1152]{1,0:T(8,128)(2,1)S(1)}, bf16[256,1152]{1,0:T(8,128)(2,1)S(1)}, u32[]{:S(2)}, u32[]{:S(2)}) collective-permute-start(bf16[256,1152]{1,0:T(8,128)(2,1)S(1)} %get-tuple-element.22), channel_id=1, source_target_pairs={{0,16},{1,9},{2,18},{3,11},{4,20},{5,13},{6,22},{7,15},{8,24},{9,1... | collective-permute-start | bytes 1769480 | tf_op jit(solution)/shard_map/ppermute | solution.py:255
  67.7 1.1 copy-start.11
  68.8 1.6 %copy-start.7 = (bf16[256,1024]{1,0:T(8,128)(2,1)S(1)}, bf16[256,1024]{1,0:T(8,128)(2,1)}, u32[]{:S(2)}) copy-start(bf16[256,1024]{1,0:T(8,128)(2,1)} %refs_3_.3) | copy-start | bytes 1572868
  68.8 1.6 %copy-start.8 = (s32[64]{0:T(128)S(1)}, s32[64]{0:T(128)}, u32[]{:S(2)}) copy-start(s32[64]{0:T(128)} %refs_2_.9) | copy-start | bytes 772
  68.8 34.8 %collective-permute-start.4 = (bf16[5120,256]{1,0:T(8,128)(2,1)}, bf16[5120,256]{1,0:T(8,128)(2,1)}, u32[]{:S(2)}, u32[]{:S(2)}) collective-permute-start(bf16[5120,256]{1,0:T(8,128)(2,1)} %pass_after.4.near_ref), channel_id=1, source_target_pairs={{0,1},{1,0},{2,3},{3,2},{4,5},{5,4},{6,7},{7,6},{8,9},{9,8},{10,11... | collective-permute-start | bytes 7864328 | tf_op jit(solution)/shard_map/ppermute | solution.py:247
  68.9 30.8 %collective-permute-start.9 = (bf16[2560,256]{1,0:T(8,128)(2,1)S(1)}, bf16[2560,256]{1,0:T(8,128)(2,1)}, u32[]{:S(2)}, u32[]{:S(2)}) collective-permute-start(bf16[2560,256]{1,0:T(8,128)(2,1)S(1)} %get-tuple-element.24.refs_5_.refs_1_), channel_id=1, source_target_pairs={{0,16},{1,9},{2,18},{3,11},{4,20},{5,13},{6,22},{7,15},{8,24},{9,1... | collective-permute-start | bytes 3932168 | tf_op jit(solution)/shard_map/ppermute | solution.py:255
  77.1 0.8 copy-start.2
  77.8 0.8 copy-start.4
  78.6 0.8 copy-start.12
  79.4 20.2 %all-to-all-start.1 = ((bf16[8,32,1152]{2,1,0:T(8,128)(2,1)}), bf16[8,32,1152]{2,1,0:T(8,128)(2,1)S(1)}, u32[]{:S(2)}, u32[]{:S(2)}) async-start(bf16[8,32,1152]{2,1,0:T(8,128)(2,1)} %get-tuple-element.25), calls=%async_computation.1 | async-start | bytes 1179648 | tf_op jit(solution)/shard_map/all_to_all | solution.py:260
  83.0 20.7 %collective-permute-start.3 = (bf16[3072,256]{1,0:T(8,128)(2,1)}, bf16[3072,256]{1,0:T(8,128)(2,1)S(1)}, u32[]{:S(2)}, u32[]{:S(2)}) collective-permute-start(bf16[3072,256]{1,0:T(8,128)(2,1)} %copy-done.11), channel_id=1, source_target_pairs={{0,8},{1,17},{2,10},{3,19},{4,12},{5,21},{6,14},{7,23},{8,0},{9,25... | collective-permute-start | bytes 4718600 | tf_op jit(solution)/shard_map/ppermute | solution.py:255
  99.7 7.6 %collective-permute-start.10 = (bf16[2560,256]{1,0:T(8,128)(2,1)}, bf16[2560,256]{1,0:T(8,128)(2,1)S(1)}, u32[]{:S(2)}, u32[]{:S(2)}) collective-permute-start(bf16[2560,256]{1,0:T(8,128)(2,1)} %pass_after.6.mine_ref), channel_id=1, source_target_pairs={{0,1},{1,0},{2,3},{3,2},{4,5},{5,4},{6,7},{7,6},{8,9},{9,8},{10,11... | collective-permute-start | bytes 3932168 | tf_op jit(solution)/shard_map/ppermute | solution.py:247
  104.3 2.9 %copy-start.3 = (bf16[256,1024]{1,0:T(8,128)(2,1)S(1)}, bf16[256,1024]{1,0:T(8,128)(2,1)}, u32[]{:S(2)}) copy-start(bf16[256,1024]{1,0:T(8,128)(2,1)} %copy-done.2) | copy-start | bytes 1572868
  104.3 2.9 %copy-start.5 = (bf16[32,8192]{1,0:T(8,128)(2,1)S(1)}, bf16[32,8192]{1,0:T(8,128)(2,1)}, u32[]{:S(2)}) copy-start(bf16[32,8192]{1,0:T(8,128)(2,1)} %copy-done.4) | copy-start | bytes 1572868
  104.3 2.9 %copy-start.13 = (bf16[256,1024]{1,0:T(8,128)(2,1)S(1)}, bf16[256,1024]{1,0:T(8,128)(2,1)}, u32[]{:S(2)}) copy-start(bf16[256,1024]{1,0:T(8,128)(2,1)} %copy-done.12) | copy-start | bytes 1572868
  104.3 24.7 %collective-permute-start.6 = (bf16[1536,256]{1,0:T(8,128)(2,1)S(1)}, bf16[1536,256]{1,0:T(8,128)(2,1)S(1)}, u32[]{:S(2)}, u32[]{:S(2)}) collective-permute-start(bf16[1536,256]{1,0:T(8,128)(2,1)S(1)} %cut_chunk.3.refs_1_.refs_0_), channel_id=1, source_target_pairs={{0,16},{1,9},{2,18},{3,11},{4,20},{5,13},{6,22},{7,15},{8,24},{9,1... | collective-permute-start | bytes 2359304 | tf_op jit(solution)/shard_map/ppermute | solution.py:255
  105.4 26.0 %collective-permute-start.5 = (bf16[3072,256]{1,0:T(8,128)(2,1)S(1)}, bf16[3072,256]{1,0:T(8,128)(2,1)S(1)}, u32[]{:S(2)}, u32[]{:S(2)}) collective-permute-start(bf16[3072,256]{1,0:T(8,128)(2,1)S(1)} %pass_after.5.near_ref), channel_id=1, source_target_pairs={{0,1},{1,0},{2,3},{3,2},{4,5},{5,4},{6,7},{7,6},{8,9},{9,8},{10,11... | collective-permute-start | bytes 4718600 | tf_op jit(solution)/shard_map/ppermute | solution.py:247
  105.4 16.3 %collective-permute-start.7 = (bf16[256,1152]{1,0:T(8,128)(2,1)S(1)}, bf16[256,1152]{1,0:T(8,128)(2,1)S(1)}, u32[]{:S(2)}, u32[]{:S(2)}) collective-permute-start(bf16[256,1152]{1,0:T(8,128)(2,1)S(1)} %bitcast.8), channel_id=1, source_target_pairs={{0,8},{1,17},{2,10},{3,19},{4,12},{5,21},{6,14},{7,23},{8,0},{9,25... | collective-permute-start | bytes 1769480 | tf_op jit(solution)/shard_map/ppermute | solution.py:255
  106.0 23.1 %collective-permute-start.8 = (bf16[256,1152]{1,0:T(8,128)(2,1)S(1)}, bf16[256,1152]{1,0:T(8,128)(2,1)S(1)}, u32[]{:S(2)}, u32[]{:S(2)}) collective-permute-start(bf16[256,1152]{1,0:T(8,128)(2,1)S(1)} %bitcast.9), channel_id=1, source_target_pairs={{0,16},{1,9},{2,18},{3,11},{4,20},{5,13},{6,22},{7,15},{8,24},{9,1... | collective-permute-start | bytes 1769480 | tf_op jit(solution)/shard_map/ppermute | solution.py:255
  129.0 2.3 %collective-permute-start.11 = (bf16[1536,256]{1,0:T(8,128)(2,1)S(1)}, bf16[1536,256]{1,0:T(8,128)(2,1)S(1)}, u32[]{:S(2)}, u32[]{:S(2)}) collective-permute-start(bf16[1536,256]{1,0:T(8,128)(2,1)S(1)} %pass_after.7.mine_ref), channel_id=1, source_target_pairs={{0,1},{1,0},{2,3},{3,2},{4,5},{5,4},{6,7},{7,6},{8,9},{9,8},{10,11... | collective-permute-start | bytes 2359304 | tf_op jit(solution)/shard_map/ppermute | solution.py:247
  129.0 12.0 %collective-permute-start.12 = (bf16[256,1152]{1,0:T(8,128)(2,1)S(1)}, bf16[256,1152]{1,0:T(8,128)(2,1)S(1)}, u32[]{:S(2)}, u32[]{:S(2)}) collective-permute-start(bf16[256,1152]{1,0:T(8,128)(2,1)S(1)} %collective-permute-done.7.refs_1_.refs_4_), channel_id=1, source_target_pairs={{0,16},{1,9},{2,18},{3,11},{4,20},{5,13},{6,22},{7,15},{8,24},{9,1... | collective-permute-start | bytes 1769480 | tf_op jit(solution)/shard_map/ppermute | solution.py:255
  131.3 1.1 copy-start.14
  132.5 8.6 %copy-start.10 = (s32[64]{0:T(128)S(1)}, s32[64]{0:T(128)}, u32[]{:S(2)}) copy-start(s32[64]{0:T(128)} %refs_1_.5) | copy-start | bytes 772
  141.1 1.0 copy-start.6

commit v10 on v9

--- a/solution.py
+++ b/solution.py
@@ -10,7 +10,7 @@
 ADAPTER_RANK = 16
 BLOCK = 128
 ADAPTER_SCALE = 2.0
-CHUNKS = (5, 3)
+CHUNKS = (4, 4)
 VMEM_LIMIT = 48 * 1024 * 1024
 
 F32 = jnp.float32
@@ -75,19 +75,19 @@
     copy.wait()
 
 
-def cut_kernel(start, where_ref, near_ref, weight_ref, half_ref, *refs):
-    *piece_refs, sems = refs
+def sum_kernel(start, keep_ref, came_ref, weight_ref, out_ref, piece_ref, sem):
+    copy = pltpu.make_async_copy(weight_ref.at[pl.ds(start, piece_ref.shape[0]), :], piece_ref, sem)
+    copy.start()
+    out_ref[...] = keep_ref[...] + came_ref[...]
+    copy.wait()
+
+
+def cut_kernel(where_ref, near_ref, half_ref, sem):
     half = half_ref.shape[0]
     at = pl.multiple_of(where_ref[1] * half, half)
-    copies = [pltpu.make_async_copy(near_ref.at[pl.ds(at, half), :], half_ref, sems.at[0])]
-    for piece_ref in piece_refs:
-        copies.append(
-            pltpu.make_async_copy(weight_ref.at[pl.ds(start, piece_ref.shape[0]), :], piece_ref, sems.at[1])
-        )
-    for copy in copies:
-        copy.start()
-    for copy in copies:
-        copy.wait()
+    copy = pltpu.make_async_copy(near_ref.at[pl.ds(at, half), :], half_ref, sem)
+    copy.start()
+    copy.wait()
 
 
 def block_diagonal(a):
@@ -296,7 +296,14 @@
         "sum_and_cut",
         [pltpu.SemaphoreType.DMA],
     )(kept, came, weight)
-    maps = along_tok((keep + second_way(sent)).reshape(shards, rank, both))
+    maps, later = call(
+        functools.partial(sum_kernel, parts[1][0]),
+        [shape(group_rank, both), shape(parts[1][1], wide)],
+        [VMEM, VMEM, ANY],
+        "sum_and_cut",
+        [pltpu.SemaphoreType.DMA],
+    )(keep, second_way(sent), weight)
+    maps = along_tok(maps.reshape(shards, rank, both))
 
     arrived = []
 
@@ -310,24 +317,20 @@
             input_output_aliases={0: 0},
         )(a, *earlier)
 
-    def cut_chunk(*earlier):
-        k = len(arrived)
-        nexts = parts[k + 1 : k + 2]
-        near = first_way(pieces[k])
-        part, *cuts = call(
-            after(functools.partial(cut_kernel, nexts[0][0] if nexts else 0), 3, *earlier),
-            [shape(parts[k][1] // 2, wide)] + [shape(n, wide) for _, n in nexts],
-            [SMEM, ANY, ANY] + [ANY] * len(earlier),
+    def cut_chunk(piece, *earlier):
+        near = first_way(piece)
+        part = call(
+            after(cut_kernel, 2, *earlier),
+            shape(piece.shape[0] // 2, wide),
+            [SMEM, ANY] + [ANY] * len(earlier),
             "cut_chunk",
-            [pltpu.SemaphoreType.DMA((2,))],
-        )(where, near, weight, *earlier)
+            [pltpu.SemaphoreType.DMA],
+        )(where, near, *earlier)
         near = pass_after(near, part)
         arrived.append((near, on_core(near), second_way(part)))
-        pieces.extend(cuts)
         return part
 
-    pieces = [piece]
-    part = cut_chunk(maps)
+    part = cut_chunk(piece, maps)
 
     grad, rank_grad, at, lora, terms = call(
         after(rank_kernel, 5, part),
@@ -344,7 +347,6 @@
     )(where, fills, tokens, cotangent, maps, part)
     r0 = along_tok(terms).reshape(group_rank, both)
     r1, r2 = first_way(r0), second_way(r0)
-    r3 = second_way(r1)
 
     whole = lambda i, *refs: (0, 0)
     along = lambda spot, tile: pl.BlockSpec((rows, tile), lambda i, *refs: (0, spot(i, *refs)))
@@ -368,13 +370,16 @@
         final = k == len(parts) - 1
         steps = size // tile
         half = steps // 2
-        part = None if final else cut_chunk(r0, arrived[k][1])
+        part = None if final else cut_chunk(later, rank_grad, arrived[k][1])
         near, far, mine = arrived[k]
-        mine = pass_after(mine, *((r1, r2, total) if final else (r0,)))
+        mine = pass_after(mine, r0)
         theirs = on_core(mine)
+        if final:
+            r1 = pass_after(r1, total)
+            r3 = second_way(r1)
         turned = lambda i, w, f, half=half, steps=steps: (i + w[1] * half) % steps
         spot = lambda i, w, f, start=start, turned=turned: start // tile + turned(i, w, f)
-        extra = [a for a in (token_gradient, part) if a is not None]
+        extra = [a for a in (token_gradient, part, *((r1, r2) if final else ())) if a is not None]
         token_gradient, total = pl.pallas_call(
             functools.partial(base_kernel, steps, final),
             out_shape=[shape(rows, model), shape(rows, value, dtype=BF16 if final else F32)],

time: 149 us -> 143 us (0.960)
  blocking collectives: 21.4 us -> 0 us
  starting transfers between devices: 16.2 us -> 22.2 us
  waiting for transfers between devices: 56.9 us -> 60.8 us
  Pallas kernels: 44 us -> 46.8 us
  local copies, waits for them, and re-layouts: 8.92 us -> 10.8 us
    all_to_all x1 -> x0, blocking collectives: 21.4 us -> none  [along_tok(): return lax.all_to_all(a, 'tok', split_axis=0, concat_axis=0)]
    all_to_all x1 -> x2, waiting for transfers between devices: 16.1 us -> 30 us  [along_tok(): return lax.all_to_all(a, 'tok', split_axis=0, concat_axis=0)]
    ppermute x9, waiting for transfers between devices: 39.5 us -> 29.6 us  [split(): return lambda a: lax.ppermute(a, ('fsdp', 'tok'), pairs)]
    all_to_all x1 -> x2, starting transfers between devices: 3.54 us -> 9.08 us  [along_tok(): return lax.all_to_all(a, 'tok', split_axis=0, concat_axis=0)]
    pallas_call x2 -> x3, Pallas kernels: 2.99 us -> 4.84 us  [the longest x1 2.43 us: local(): call(functools.partial(sum_kernel, parts[1][0]), [shape(group_rank, both)...]
    unnamed x30 -> x36, local copies, waits for them, and re-layouts: 8.92 us -> 10.8 us
  transfers between devices with their start and end apart: 14 -> 15, of which waited for: 7 -> 6; matrix products, arithmetic and copies ran while one was open for 0% -> 0% of each run, Pallas kernels for 21% -> 24%
where the time goes in v10:
time: 143 us; the launch traced here: 141 us
  waiting for transfers between devices  60.8 us (43%)
  Pallas kernels  46.8 us (33%)
  starting transfers between devices  22.2 us (16%)
  local copies, waits for them, and re-layouts  10.8 us (8%)
    all_to_all x2, waiting for transfers between devices, along_tok(): return lax.all_to_all(a, 'tok', split_axis=0, concat_axis=0)  30 us
    ppermute x9, waiting for transfers between devices, split(): return lambda a: lax.ppermute(a, ('fsdp', 'tok'), pairs)  29.6 us
    pallas_call x2, Pallas kernels, local(): pl.pallas_call(functools.partial(base_kernel, steps, final), out_shape=[s...  21.3 us
    ppermute x9, starting transfers between devices, split(): return lambda a: lax.ppermute(a, ('fsdp', 'tok'), pairs)  12.5 us
    unnamed x36, local copies, waits for them, and re-layouts  10.8 us
    all_to_all x2, starting transfers between devices, along_tok(): return lax.all_to_all(a, 'tok', split_axis=0, concat_axis=0)  9.08 us
    pallas_call x1, Pallas kernels, local(): call(after(functools.partial(expand_kernel, group), 7, total), [shape(cut...  6.91 us
    pallas_call x1, Pallas kernels, local(): call(after(rank_kernel, 5, part), [shape(rows, value), shape(rows, rank),...  5.78 us
  transfers between devices with their start and end apart: 15, of which 6 were waited for; matrix products, arithmetic and copies ran while one was open for 0% of the time, Pallas kernels for 24%

profile of v10, /device:TPU:0, one launch (start us, length us, event | category | flops | bytes accessed | tf_op | source)
XLA Modules:
  0.0 141.4 jit_solution(16836083338038171306)
XLA Ops:
  0.7 1.6 %copy-done.1 = bf16[1024,1024]{1,0:T(8,128)(2,1)S(1)} copy-done((bf16[1024,1024]{1,0:T(8,128)(2,1)S(1)}, bf16[1024,1024]{1,0:T(8,128)(2,1)}, u32[]{:S(2)}) %copy-start.1) | copy-done | bytes 2097176
  2.3 0.9 copy-done.8
  3.9 2.5 %select_sent.1.refs_4_ = bf16[512,1152]{1,0:T(8,128)(2,1)S(1)} custom-call(s32[4]{0:T(128)S(1)} %pad_add_fusion.where_ref.refs_0_, s32[64]{0:T(128)S(1)} %copy-done.15, bf16[1024,1024]{1,0:T(8,128)(2,1)S(1)} %copy-done.1, bf16[128,1024]{1,0:T(8,128)(2,1)S(1)} %copy-done.8), custom_call_target="tpu_custom_call" | custom-call | tf_op jit(solution)/shard_map/select_sent/pallas_call | solution.py:277
  6.4 3.0 %collective-permute-start = (bf16[512,1152]{1,0:T(8,128)(2,1)S(1)}, bf16[512,1152]{1,0:T(8,128)(2,1)S(1)}, u32[]{:S(2)}, u32[]{:S(2)}) collective-permute-start(bf16[512,1152]{1,0:T(8,128)(2,1)S(1)} %select_sent.1.refs_4_), channel_id=1, source_target_pairs={{0,8},{1,17},{2,10},{3,19},{4,12},{5,21},{6,14},{7,23},{8,0},{9,25... | collective-permute-start | bytes 3538952 | tf_op jit(solution)/shard_map/ppermute | solution.py:255
  9.4 2.5 %select_kept.1.kept_ref = bf16[512,1152]{1,0:T(8,128)(2,1)S(1)} custom-call(s32[4]{0:T(128)S(1)} %pad_add_fusion.where_ref.refs_0_, s32[64]{0:T(128)S(1)} %copy-done.16, bf16[1024,1024]{1,0:T(8,128)(2,1)S(1)} %copy-done.1, bf16[128,1024]{1,0:T(8,128)(2,1)S(1)} %copy-done.8, bf16[512,1152]{1,0:T(8,128)(2,1)S(1)} %select_sent.1.refs_4_), custom_call_target="tpu_custom_call" | custom-call | tf_op jit(solution)/shard_map/select_kept/pallas_call | solution.py:285
  12.0 11.7 %collective-permute-done.came_ref = bf16[512,1152]{1,0:T(8,128)(2,1)S(1)} collective-permute-done((bf16[512,1152]{1,0:T(8,128)(2,1)S(1)}, bf16[512,1152]{1,0:T(8,128)(2,1)S(1)}, u32[]{:S(2)}, u32[]{:S(2)}) %collective-permute-start) | collective-permute-done | bytes 1179680 | tf_op jit(solution)/shard_map/ppermute | solution.py:255
  23.6 2.9 %sum_and_cut.2 = (bf16[256,1152]{1,0:T(8,128)(2,1)S(1)}, bf16[256,1152]{1,0:T(8,128)(2,1)S(1)}, bf16[4096,256]{1,0:T(8,128)(2,1)}) custom-call(bf16[512,1152]{1,0:T(8,128)(2,1)S(1)} %select_kept.1.kept_ref, bf16[512,1152]{1,0:T(8,128)(2,1)S(1)} %collective-permute-done.came_ref, bf16[8192,256]{1,0:T(8,128)(2,1)} %own_ref.3), custom_call_target="tpu_custom_call" | custom-call | tf_op jit(solution)/shard_map/sum_and_cut/pallas_call | solution.py:292
  26.5 2.1 %collective-permute-start.3 = (bf16[4096,256]{1,0:T(8,128)(2,1)}, bf16[4096,256]{1,0:T(8,128)(2,1)S(1)}, u32[]{:S(2)}, u32[]{:S(2)}) collective-permute-start(bf16[4096,256]{1,0:T(8,128)(2,1)} %get-tuple-element.24), channel_id=1, source_target_pairs={{0,8},{1,17},{2,10},{3,19},{4,12},{5,21},{6,14},{7,23},{8,0},{9,25... | collective-permute-start | bytes 6291464 | tf_op jit(solution)/shard_map/ppermute | solution.py:255
  28.6 1.5 %collective-permute-start.1 = (bf16[256,1152]{1,0:T(8,128)(2,1)S(1)}, bf16[256,1152]{1,0:T(8,128)(2,1)S(1)}, u32[]{:S(2)}, u32[]{:S(2)}) collective-permute-start(bf16[256,1152]{1,0:T(8,128)(2,1)S(1)} %get-tuple-element.21), channel_id=1, source_target_pairs={{0,16},{1,9},{2,18},{3,11},{4,20},{5,13},{6,22},{7,15},{8,24},{9,1... | collective-permute-start | bytes 1769480 | tf_op jit(solution)/shard_map/ppermute | solution.py:255
  30.2 14.7 %collective-permute-done.1.came_ref = bf16[256,1152]{1,0:T(8,128)(2,1)S(1)} collective-permute-done((bf16[256,1152]{1,0:T(8,128)(2,1)S(1)}, bf16[256,1152]{1,0:T(8,128)(2,1)S(1)}, u32[]{:S(2)}, u32[]{:S(2)}) %collective-permute-start.1) | collective-permute-done | bytes 589856 | tf_op jit(solution)/shard_map/ppermute | solution.py:255
  44.9 2.4 %sum_and_cut.3 = (bf16[256,1152]{1,0:T(8,128)(2,1)}, bf16[4096,256]{1,0:T(8,128)(2,1)S(1)}) custom-call(bf16[256,1152]{1,0:T(8,128)(2,1)S(1)} %get-tuple-element.20.keep_ref, bf16[256,1152]{1,0:T(8,128)(2,1)S(1)} %collective-permute-done.1.came_ref, bf16[8192,256]{1,0:T(8,128)(2,1)} %own_ref.3), custom_call_target="tpu_custom_call" | custom-call | tf_op jit(solution)/shard_map/sum_and_cut/pallas_call | solution.py:299
  47.4 1.3 copy-done.17
  48.7 4.9 %all-to-all-start = ((bf16[8,32,1152]{2,1,0:T(8,128)(2,1)}), bf16[8,32,1152]{2,1,0:T(8,128)(2,1)S(1)}, u32[]{:S(2)}, u32[]{:S(2)}) async-start(bf16[8,32,1152]{2,1,0:T(8,128)(2,1)} %bitcast.4), calls=%async_computation | async-start | bytes 1179648 | tf_op jit(solution)/shard_map/all_to_all | solution.py:260
  54.1 16.2 %all-to-all-done.refs_2_.refs_4_ = bf16[8,32,1152]{2,1,0:T(8,128)(2,1)S(1)} async-done(((bf16[8,32,1152]{2,1,0:T(8,128)(2,1)}), bf16[8,32,1152]{2,1,0:T(8,128)(2,1)S(1)}, u32[]{:S(2)}, u32[]{:S(2)}) %all-to-all-start) | async-done | bytes 589856 | tf_op jit(solution)/shard_map/all_to_all | solution.py:260
  70.3 0.8 copy-done.2
  71.2 1.1 copy-done.3
  73.0 1.6 %collective-permute-start.8 = (bf16[2048,256]{1,0:T(8,128)(2,1)S(1)}, bf16[2048,256]{1,0:T(8,128)(2,1)}, u32[]{:S(2)}, u32[]{:S(2)}) collective-permute-start(bf16[2048,256]{1,0:T(8,128)(2,1)S(1)} %cut_chunk.2.refs_5_.refs_1_), channel_id=1, source_target_pairs={{0,16},{1,9},{2,18},{3,11},{4,20},{5,13},{6,22},{7,15},{8,24},{9,1... | collective-permute-start | bytes 3145736 | tf_op jit(solution)/shard_map/ppermute | solution.py:255
  74.6 5.8 %rank_space.1 = (bf16[256,1024]{1,0:T(8,128)(2,1)S(1)}, bf16[256,32]{1,0:T(8,128)(2,1)S(1)}, bf16[32,8192]{1,0:T(8,128)(2,1)S(1)}, bf16[256,1024]{1,0:T(8,128)(2,1)S(1)}, bf16[8,32,1152]{2,1,0:T(8,128)(2,1)S(1)}) custom-call(s32[4]{0:T(128)S(1)} %pad_add_fusion.where_ref.refs_0_, s32[64]{0:T(128)S(1)} %copy-done.14, bf16[256,8192]{1,0:T(8,128)(2,1)} %tokens_ref.3, ...), custom_call_target="tpu_custom_call" | custom-call | tf_op jit(solution)/shard_map/rank_space/pallas_call | solution.py:335
  82.0 0.9 copy-done.9
  82.8 0.8 copy-done.10
  83.6 4.2 %all-to-all-start.1 = ((bf16[8,32,1152]{2,1,0:T(8,128)(2,1)}), bf16[8,32,1152]{2,1,0:T(8,128)(2,1)}, u32[]{:S(2)}, u32[]{:S(2)}) async-start(bf16[8,32,1152]{2,1,0:T(8,128)(2,1)} %copy-done.9), calls=%async_computation.1 | async-start | bytes 1179648 | tf_op jit(solution)/shard_map/all_to_all | solution.py:260
  87.9 1.8 %cut_chunk.3.refs_1_.refs_0_ = bf16[2048,256]{1,0:T(8,128)(2,1)S(1)} custom-call(s32[4]{0:T(128)S(1)} %pad_add_fusion.where_ref.refs_0_, bf16[4096,256]{1,0:T(8,128)(2,1)} %collective-permute-done.2.refs_1_.refs_0_, bf16[256,32]{1,0:T(8,128)(2,1)S(1)} %get-tuple-element.25.refs_2_.rg_ref, bf16[4096,256]{1,0:T(8,128)(2,1)} %collective-permute-done.4.refs_3_.far_ref), custom_call_target="tpu_custom_call" | custom-call | tf_op jit(solution)/shard_map/cut_chunk/pallas_call | solution.py:322
  89.6 1.2 collective-permute-start.6
  90.8 13.8 %all-to-all-done.1 = bf16[8,32,1152]{2,1,0:T(8,128)(2,1)} async-done(((bf16[8,32,1152]{2,1,0:T(8,128)(2,1)}), bf16[8,32,1152]{2,1,0:T(8,128)(2,1)}, u32[]{:S(2)}, u32[]{:S(2)}) %all-to-all-start.1) | async-done | bytes 589856 | tf_op jit(solution)/shard_map/all_to_all | solution.py:260
  105.7 1.1 collective-permute-start.11
  106.9 1.2 collective-permute-done.9.theirs_ref
  108.1 10.3 %base_chunk.2 = (bf16[256,8192]{1,0:T(8,128)(2,1)}, f32[256,1024]{1,0:T(8,128)S(1)}) custom-call(s32[4]{0:T(128)S(1)} %pad_add_fusion.where_ref.refs_0_, s32[64]{0:T(128)S(1)} %copy-done.14, bf16[256,8192]{1,0:T(8,128)(2,1)} %tokens_ref.3, bf16[8192,256]{1,0:T(8,128)(2,1)} %own_ref.3, bf16[4096,256]{1,0:T(8,128)(2,1)} %copy-done, ...), custom_call_target="tpu_custom_call" | custom-call | flops 4294967296 | bytes 14680064 | tf_op jit(solution)/shard_map/base_chunk/pallas_call | solution.py:383
  118.4 3.1 %collective-permute-done.10.refs_0_ = bf16[256,1152]{1,0:T(8,128)(2,1)S(1)} collective-permute-done((bf16[256,1152]{1,0:T(8,128)(2,1)}, bf16[256,1152]{1,0:T(8,128)(2,1)S(1)}, u32[]{:S(2)}, u32[]{:S(2)}) %collective-permute-start.10) | collective-permute-done | bytes 589856 | tf_op jit(solution)/shard_map/ppermute | solution.py:255
  121.6 0.9 collective-permute-start.12
  122.5 11.0 %base_chunk.3 = (bf16[256,8192]{1,0:T(8,128)(2,1)}, bf16[256,1024]{1,0:T(8,128)(2,1)}) custom-call(s32[4]{0:T(128)S(1)} %pad_add_fusion.where_ref.refs_0_, s32[64]{0:T(128)S(1)} %copy-done.14, bf16[256,8192]{1,0:T(8,128)(2,1)} %tokens_ref.3, bf16[8192,256]{1,0:T(8,128)(2,1)} %own_ref.3, ...), custom_call_target="tpu_custom_call", output_to_operand_aliasing={{0}: (12, {})} | custom-call | flops 4294967296 | bytes 14680064 | tf_op jit(solution)/shard_map/base_chunk/pallas_call | solution.py:383
  133.5 1.0 copy-done.12
  134.5 6.9 %expand.1 = (f32[1024,1024]{1,0:T(8,128)}, f32[128,1024]{1,0:T(8,128)}) custom-call(s32[4]{0:T(128)S(1)} %pad_add_fusion.where_ref.refs_0_, s32[64]{0:T(128)S(1)} %copy-done.16, s32[64]{0:T(128)S(1)} %copy-done.14, bf16[256,1152]{1,0:T(8,128)(2,1)} %bitcast.5.refs_1_.refs_3_, bf16[256,1152]{1,0:T(8,128)(2,1)S(1)} %pass_after.9.refs_1_.refs_4_, ...), custom_call_target="tpu_custom_call" | custom-call | tf_op jit(solution)/shard_map/expand/pallas_call | solution.py:409
  (50 shorter events, 4.7 us)
Async XLA Ops:
  0.6 8.8 %copy-start.16 = (s32[64]{0:T(128)S(1)}, s32[64]{0:T(128)}, u32[]{:S(2)}) copy-start(s32[64]{0:T(128)} %refs_1_.5) | copy-start | bytes 772
  0.7 1.6 %copy-start.1 = (bf16[1024,1024]{1,0:T(8,128)(2,1)S(1)}, bf16[1024,1024]{1,0:T(8,128)(2,1)}, u32[]{:S(2)}) copy-start(bf16[1024,1024]{1,0:T(8,128)(2,1)} %refs_2_.3) | copy-start | bytes 6291460
  2.3 0.9 copy-start.8
  6.4 17.2 %collective-permute-start = (bf16[512,1152]{1,0:T(8,128)(2,1)S(1)}, bf16[512,1152]{1,0:T(8,128)(2,1)S(1)}, u32[]{:S(2)}, u32[]{:S(2)}) collective-permute-start(bf16[512,1152]{1,0:T(8,128)(2,1)S(1)} %select_sent.1.refs_4_), channel_id=1, source_target_pairs={{0,8},{1,17},{2,10},{3,19},{4,12},{5,21},{6,14},{7,23},{8,0},{9,25... | collective-permute-start | bytes 3538952 | tf_op jit(solution)/shard_map/ppermute | solution.py:255
  26.5 44.6 %collective-permute-start.3 = (bf16[4096,256]{1,0:T(8,128)(2,1)}, bf16[4096,256]{1,0:T(8,128)(2,1)S(1)}, u32[]{:S(2)}, u32[]{:S(2)}) collective-permute-start(bf16[4096,256]{1,0:T(8,128)(2,1)} %get-tuple-element.24), channel_id=1, source_target_pairs={{0,8},{1,17},{2,10},{3,19},{4,12},{5,21},{6,14},{7,23},{8,0},{9,25... | collective-permute-start | bytes 6291464 | tf_op jit(solution)/shard_map/ppermute | solution.py:255
  28.6 16.3 %collective-permute-start.1 = (bf16[256,1152]{1,0:T(8,128)(2,1)S(1)}, bf16[256,1152]{1,0:T(8,128)(2,1)S(1)}, u32[]{:S(2)}, u32[]{:S(2)}) collective-permute-start(bf16[256,1152]{1,0:T(8,128)(2,1)S(1)} %get-tuple-element.21), channel_id=1, source_target_pairs={{0,16},{1,9},{2,18},{3,11},{4,20},{5,13},{6,22},{7,15},{8,24},{9,1... | collective-permute-start | bytes 1769480 | tf_op jit(solution)/shard_map/ppermute | solution.py:255
  47.3 1.3 copy-start.17
  48.7 21.6 %all-to-all-start = ((bf16[8,32,1152]{2,1,0:T(8,128)(2,1)}), bf16[8,32,1152]{2,1,0:T(8,128)(2,1)S(1)}, u32[]{:S(2)}, u32[]{:S(2)}) async-start(bf16[8,32,1152]{2,1,0:T(8,128)(2,1)} %bitcast.4), calls=%async_computation | async-start | bytes 1179648 | tf_op jit(solution)/shard_map/all_to_all | solution.py:260
  53.5 34.3 %collective-permute-start.2 = (bf16[4096,256]{1,0:T(8,128)(2,1)}, bf16[4096,256]{1,0:T(8,128)(2,1)}, u32[]{:S(2)}, u32[]{:S(2)}) collective-permute-start(bf16[4096,256]{1,0:T(8,128)(2,1)} %copy-done.17), channel_id=1, source_target_pairs={{0,8},{1,17},{2,10},{3,19},{4,12},{5,21},{6,14},{7,23},{8,0},{9,25... | collective-permute-start | bytes 6291464 | tf_op jit(solution)/shard_map/ppermute | solution.py:255
  70.3 0.8 copy-start.2
  71.2 1.1 copy-start.3
  72.9 1.7 %copy-start.13 = (bf16[256,1024]{1,0:T(8,128)(2,1)S(1)}, bf16[256,1024]{1,0:T(8,128)(2,1)}, u32[]{:S(2)}) copy-start(bf16[256,1024]{1,0:T(8,128)(2,1)} %refs_3_.3) | copy-start | bytes 1572868
  72.9 1.7 %copy-start.14 = (s32[64]{0:T(128)S(1)}, s32[64]{0:T(128)}, u32[]{:S(2)}) copy-start(s32[64]{0:T(128)} %refs_2_.5) | copy-start | bytes 772
  72.9 7.5 %copy-start = (bf16[4096,256]{1,0:T(8,128)(2,1)}, bf16[4096,256]{1,0:T(8,128)(2,1)S(1)}, u32[]{:S(2)}) copy-start(bf16[4096,256]{1,0:T(8,128)(2,1)S(1)} %pass_after.5.near_ref) | copy-start | bytes 6291460
  72.9 15.0 %collective-permute-start.4 = (bf16[4096,256]{1,0:T(8,128)(2,1)S(1)}, bf16[4096,256]{1,0:T(8,128)(2,1)}, u32[]{:S(2)}, u32[]{:S(2)}) collective-permute-start(bf16[4096,256]{1,0:T(8,128)(2,1)S(1)} %pass_after.5.near_ref), channel_id=1, source_target_pairs={{0,1},{1,0},{2,3},{3,2},{4,5},{5,4},{6,7},{7,6},{8,9},{9,8},{10,11... | collective-permute-start | bytes 6291464 | tf_op jit(solution)/shard_map/ppermute | solution.py:247
  73.0 31.6 %collective-permute-start.8 = (bf16[2048,256]{1,0:T(8,128)(2,1)S(1)}, bf16[2048,256]{1,0:T(8,128)(2,1)}, u32[]{:S(2)}, u32[]{:S(2)}) collective-permute-start(bf16[2048,256]{1,0:T(8,128)(2,1)S(1)} %cut_chunk.2.refs_5_.refs_1_), channel_id=1, source_target_pairs={{0,16},{1,9},{2,18},{3,11},{4,20},{5,13},{6,22},{7,15},{8,24},{9,1... | collective-permute-start | bytes 3145736 | tf_op jit(solution)/shard_map/ppermute | solution.py:255
  80.4 0.8 copy-start.4
  81.2 0.8 copy-start.6
  82.0 0.9 copy-start.9
  82.8 0.8 copy-start.10
  83.6 21.0 %all-to-all-start.1 = ((bf16[8,32,1152]{2,1,0:T(8,128)(2,1)}), bf16[8,32,1152]{2,1,0:T(8,128)(2,1)}, u32[]{:S(2)}, u32[]{:S(2)}) async-start(bf16[8,32,1152]{2,1,0:T(8,128)(2,1)} %copy-done.9), calls=%async_computation.1 | async-start | bytes 1179648 | tf_op jit(solution)/shard_map/all_to_all | solution.py:260
  89.6 15.1 %collective-permute-start.6 = (bf16[2048,256]{1,0:T(8,128)(2,1)S(1)}, bf16[2048,256]{1,0:T(8,128)(2,1)S(1)}, u32[]{:S(2)}, u32[]{:S(2)}) collective-permute-start(bf16[2048,256]{1,0:T(8,128)(2,1)S(1)} %cut_chunk.3.refs_1_.refs_0_), channel_id=1, source_target_pairs={{0,16},{1,9},{2,18},{3,11},{4,20},{5,13},{6,22},{7,15},{8,24},{9,1... | collective-permute-start | bytes 3145736 | tf_op jit(solution)/shard_map/ppermute | solution.py:255
  90.8 31.7 %collective-permute-start.5 = (bf16[4096,256]{1,0:T(8,128)(2,1)}, bf16[4096,256]{1,0:T(8,128)(2,1)}, u32[]{:S(2)}, u32[]{:S(2)}) collective-permute-start(bf16[4096,256]{1,0:T(8,128)(2,1)} %pass_after.6.near_ref), channel_id=1, source_target_pairs={{0,1},{1,0},{2,3},{3,2},{4,5},{5,4},{6,7},{7,6},{8,9},{9,8},{10,11... | collective-permute-start | bytes 6291464 | tf_op jit(solution)/shard_map/ppermute | solution.py:247
  104.6 3.5 %copy-start.5 = (bf16[256,1024]{1,0:T(8,128)(2,1)S(1)}, bf16[256,1024]{1,0:T(8,128)(2,1)}, u32[]{:S(2)}) copy-start(bf16[256,1024]{1,0:T(8,128)(2,1)} %copy-done.4) | copy-start | bytes 1572868
  104.6 3.5 %copy-start.7 = (bf16[32,8192]{1,0:T(8,128)(2,1)S(1)}, bf16[32,8192]{1,0:T(8,128)(2,1)}, u32[]{:S(2)}) copy-start(bf16[32,8192]{1,0:T(8,128)(2,1)} %copy-done.6) | copy-start | bytes 1572868
  104.6 3.5 %copy-start.11 = (bf16[256,1024]{1,0:T(8,128)(2,1)S(1)}, bf16[256,1024]{1,0:T(8,128)(2,1)}, u32[]{:S(2)}) copy-start(bf16[256,1024]{1,0:T(8,128)(2,1)} %copy-done.10) | copy-start | bytes 1572868
  104.6 3.4 %collective-permute-start.9 = (bf16[2048,256]{1,0:T(8,128)(2,1)}, bf16[2048,256]{1,0:T(8,128)(2,1)S(1)}, u32[]{:S(2)}, u32[]{:S(2)}) collective-permute-start(bf16[2048,256]{1,0:T(8,128)(2,1)} %pass_after.8.mine_ref), channel_id=1, source_target_pairs={{0,1},{1,0},{2,3},{3,2},{4,5},{5,4},{6,7},{7,6},{8,9},{9,8},{10,11... | collective-permute-start | bytes 3145736 | tf_op jit(solution)/shard_map/ppermute | solution.py:247
  104.7 17.8 %collective-permute-start.7 = (bf16[2048,256]{1,0:T(8,128)(2,1)S(1)}, bf16[2048,256]{1,0:T(8,128)(2,1)S(1)}, u32[]{:S(2)}, u32[]{:S(2)}) collective-permute-start(bf16[2048,256]{1,0:T(8,128)(2,1)S(1)} %pass_after.7.mine_ref), channel_id=1, source_target_pairs={{0,1},{1,0},{2,3},{3,2},{4,5},{5,4},{6,7},{7,6},{8,9},{9,8},{10,11... | collective-permute-start | bytes 3145736 | tf_op jit(solution)/shard_map/ppermute | solution.py:247
  105.2 16.4 %collective-permute-start.10 = (bf16[256,1152]{1,0:T(8,128)(2,1)}, bf16[256,1152]{1,0:T(8,128)(2,1)S(1)}, u32[]{:S(2)}, u32[]{:S(2)}) collective-permute-start(bf16[256,1152]{1,0:T(8,128)(2,1)} %bitcast.5.refs_1_.refs_3_), channel_id=1, source_target_pairs={{0,8},{1,17},{2,10},{3,19},{4,12},{5,21},{6,14},{7,23},{8,0},{9,25... | collective-permute-start | bytes 1769480 | tf_op jit(solution)/shard_map/ppermute | solution.py:255
  105.7 16.8 %collective-permute-start.11 = (bf16[256,1152]{1,0:T(8,128)(2,1)}, bf16[256,1152]{1,0:T(8,128)(2,1)S(1)}, u32[]{:S(2)}, u32[]{:S(2)}) collective-permute-start(bf16[256,1152]{1,0:T(8,128)(2,1)} %bitcast.5.refs_1_.refs_3_), channel_id=1, source_target_pairs={{0,16},{1,9},{2,18},{3,11},{4,20},{5,13},{6,22},{7,15},{8,24},{9,1... | collective-permute-start | bytes 1769480 | tf_op jit(solution)/shard_map/ppermute | solution.py:255
  121.6 11.9 %collective-permute-start.12 = (bf16[256,1152]{1,0:T(8,128)(2,1)S(1)}, bf16[256,1152]{1,0:T(8,128)(2,1)S(1)}, u32[]{:S(2)}, u32[]{:S(2)}) collective-permute-start(bf16[256,1152]{1,0:T(8,128)(2,1)S(1)} %pass_after.9.refs_1_.refs_4_), channel_id=1, source_target_pairs={{0,16},{1,9},{2,18},{3,11},{4,20},{5,13},{6,22},{7,15},{8,24},{9,1... | collective-permute-start | bytes 1769480 | tf_op jit(solution)/shard_map/ppermute | solution.py:255
  133.5 1.0 copy-start.12
  (1 other events, 0.7 us)

commit v11 on v10

--- a/solution.py
+++ b/solution.py
@@ -11,7 +11,7 @@
 BLOCK = 128
 ADAPTER_SCALE = 2.0
 CHUNKS = (4, 4)
-VMEM_LIMIT = 48 * 1024 * 1024
+VMEM_LIMIT = 24 * 1024 * 1024
 
 F32 = jnp.float32
 BF16 = jnp.bfloat16
@@ -346,7 +346,6 @@
         [pltpu.VMEM((rank, value), BF16)] * 2,
     )(where, fills, tokens, cotangent, maps, part)
     r0 = along_tok(terms).reshape(group_rank, both)
-    r1, r2 = first_way(r0), second_way(r0)
 
     whole = lambda i, *refs: (0, 0)
     along = lambda spot, tile: pl.BlockSpec((rows, tile), lambda i, *refs: (0, spot(i, *refs)))
@@ -372,14 +371,11 @@
         half = steps // 2
         part = None if final else cut_chunk(later, rank_grad, arrived[k][1])
         near, far, mine = arrived[k]
-        mine = pass_after(mine, r0)
+        mine = pass_after(mine, r0 if final else part)
         theirs = on_core(mine)
-        if final:
-            r1 = pass_after(r1, total)
-            r3 = second_way(r1)
         turned = lambda i, w, f, half=half, steps=steps: (i + w[1] * half) % steps
         spot = lambda i, w, f, start=start, turned=turned: start // tile + turned(i, w, f)
-        extra = [a for a in (token_gradient, part, *((r1, r2) if final else ())) if a is not None]
+        extra = [a for a in (token_gradient, part) if a is not None]
         token_gradient, total = pl.pallas_call(
             functools.partial(base_kernel, steps, final),
             out_shape=[shape(rows, model), shape(rows, value, dtype=BF16 if final else F32)],
@@ -405,6 +401,12 @@
             cost_estimate=cost(size),
             name="base_chunk",
         )(where, fills, tokens, weight, near, far, mine, theirs, at, grad, rank_grad, total, *extra)
+        if final:
+            r1 = pass_after(r1, total)
+            r3 = second_way(r1)
+        else:
+            r0 = pass_after(r0, total)
+            r1, r2 = first_way(r0), second_way(r0)
 
     grad_down, grad_up = call(
         after(functools.partial(expand_kernel, group), 7, total),

time: 143 us -> 159 us (1.11)
  local copies, waits for them, and re-layouts: 10.8 us -> 23 us
  waiting for transfers between devices: 60.8 us -> 66.7 us
  Pallas kernels: 46.8 us -> 40.9 us
  starting transfers between devices: 22.2 us -> 25.7 us
    ppermute x9, waiting for transfers between devices: 29.6 us -> 50 us  [split(): return lambda a: lax.ppermute(a, ('fsdp', 'tok'), pairs)]
    all_to_all x2, waiting for transfers between devices: 30 us -> 16.2 us  [along_tok(): return lax.all_to_all(a, 'tok', split_axis=0, concat_axis=0)]
    unnamed x36 -> x58, local copies, waits for them, and re-layouts: 10.8 us -> 23 us
    all_to_all x2, starting transfers between devices: 9.08 us -> 11.7 us  [along_tok(): return lax.all_to_all(a, 'tok', split_axis=0, concat_axis=0)]
    ppermute x4, starting transfers between devices: 0.63 us -> 2.71 us  [on_core(): return lax.ppermute(a, 'tok', [(t, t ^ 1) for t in range(shards)])]
    pallas_call x1, Pallas kernels: 5.78 us -> 4.12 us  [local(): call(after(rank_kernel, 5, part), [shape(rows, value), shape(rows, rank),...]
    pallas_call x2, Pallas kernels: 21.3 us -> 19.7 us  [local(): pl.pallas_call(functools.partial(base_kernel, steps, final), out_shape=[s...]
  transfers between devices with their start and end apart: 15 -> 15, of which waited for: 6 -> 6; matrix products, arithmetic and copies ran while one was open for 0% -> 0% of each run, Pallas kernels for 24% -> 19%
where the time goes in v11:
time: 159 us; the launch traced here: 157 us
  waiting for transfers between devices  66.7 us (42%)
  Pallas kernels  40.9 us (26%)
  starting transfers between devices  25.7 us (16%)
  local copies, waits for them, and re-layouts  23 us (14%)
    ppermute x9, waiting for transfers between devices, split(): return lambda a: lax.ppermute(a, ('fsdp', 'tok'), pairs)  50 us
    unnamed x58, local copies, waits for them, and re-layouts  23 us
    pallas_call x2, Pallas kernels, local(): pl.pallas_call(functools.partial(base_kernel, steps, final), out_shape=[s...  19.7 us
    all_to_all x2, waiting for transfers between devices, along_tok(): return lax.all_to_all(a, 'tok', split_axis=0, concat_axis=0)  16.2 us
    all_to_all x2, starting transfers between devices, along_tok(): return lax.all_to_all(a, 'tok', split_axis=0, concat_axis=0)  11.7 us
    ppermute x9, starting transfers between devices, split(): return lambda a: lax.ppermute(a, ('fsdp', 'tok'), pairs)  11.4 us
    pallas_call x1, Pallas kernels, local(): call(after(functools.partial(expand_kernel, group), 7, total), [shape(cut...  6.89 us
    pallas_call x1, Pallas kernels, local(): call(after(rank_kernel, 5, part), [shape(rows, value), shape(rows, rank),...  4.12 us
  transfers between devices with their start and end apart: 15, of which 6 were waited for; matrix products, arithmetic and copies ran while one was open for 0% of the time, Pallas kernels for 19%

profile of v11, /device:TPU:0, one launch (start us, length us, event | category | flops | bytes accessed | tf_op | source)
XLA Modules:
  0.0 157.4 jit_solution(3895387245441544816)
XLA Ops:
  0.7 1.6 %copy-done.8 = bf16[1024,1024]{1,0:T(8,128)(2,1)S(1)} copy-done((bf16[1024,1024]{1,0:T(8,128)(2,1)S(1)}, bf16[1024,1024]{1,0:T(8,128)(2,1)}, u32[]{:S(2)}) %copy-start.8) | copy-done | bytes 2097176
  3.9 2.5 %select_sent.1.refs_4_ = bf16[512,1152]{1,0:T(8,128)(2,1)S(1)} custom-call(s32[4]{0:T(128)S(1)} %pad_add_fusion.where_ref.refs_0_, s32[64]{0:T(128)S(1)} %copy-done.26, bf16[1024,1024]{1,0:T(8,128)(2,1)S(1)} %copy-done.8, bf16[128,1024]{1,0:T(8,128)(2,1)S(1)} %copy-done.20), custom_call_target="tpu_custom_call" | custom-call | tf_op jit(solution)/shard_map/select_sent/pallas_call | solution.py:277
  6.4 3.0 %collective-permute-start = (bf16[512,1152]{1,0:T(8,128)(2,1)S(1)}, bf16[512,1152]{1,0:T(8,128)(2,1)S(1)}, u32[]{:S(2)}, u32[]{:S(2)}) collective-permute-start(bf16[512,1152]{1,0:T(8,128)(2,1)S(1)} %select_sent.1.refs_4_), channel_id=1, source_target_pairs={{0,8},{1,17},{2,10},{3,19},{4,12},{5,21},{6,14},{7,23},{8,0},{9,25... | collective-permute-start | bytes 3538952 | tf_op jit(solution)/shard_map/ppermute | solution.py:255
  9.5 2.5 %select_kept.1.kept_ref = bf16[512,1152]{1,0:T(8,128)(2,1)S(1)} custom-call(s32[4]{0:T(128)S(1)} %pad_add_fusion.where_ref.refs_0_, s32[64]{0:T(128)S(1)} %copy-done.27, bf16[1024,1024]{1,0:T(8,128)(2,1)S(1)} %copy-done.8, bf16[128,1024]{1,0:T(8,128)(2,1)S(1)} %copy-done.20, bf16[512,1152]{1,0:T(8,128)(2,1)S(1)} %select_sent.1.refs_4_), custom_call_target="tpu_custom_call" | custom-call | tf_op jit(solution)/shard_map/select_kept/pallas_call | solution.py:285
  12.0 11.7 %collective-permute-done.came_ref = bf16[512,1152]{1,0:T(8,128)(2,1)S(1)} collective-permute-done((bf16[512,1152]{1,0:T(8,128)(2,1)S(1)}, bf16[512,1152]{1,0:T(8,128)(2,1)S(1)}, u32[]{:S(2)}, u32[]{:S(2)}) %collective-permute-start) | collective-permute-done | bytes 1179680 | tf_op jit(solution)/shard_map/ppermute | solution.py:255
  23.6 1.6 %sum_and_cut.2 = (bf16[256,1152]{1,0:T(8,128)(2,1)S(1)}, bf16[256,1152]{1,0:T(8,128)(2,1)S(1)}, bf16[4096,256]{1,0:T(8,128)(2,1)}) custom-call(bf16[512,1152]{1,0:T(8,128)(2,1)S(1)} %select_kept.1.kept_ref, bf16[512,1152]{1,0:T(8,128)(2,1)S(1)} %collective-permute-done.came_ref, bf16[8192,256]{1,0:T(8,128)(2,1)S(1)} %copy-done), custom_call_target="tpu_custom_call" | custom-call | tf_op jit(solution)/shard_map/sum_and_cut/pallas_call | solution.py:292
  25.2 2.1 %collective-permute-start.3 = (bf16[4096,256]{1,0:T(8,128)(2,1)}, bf16[4096,256]{1,0:T(8,128)(2,1)S(1)}, u32[]{:S(2)}, u32[]{:S(2)}) collective-permute-start(bf16[4096,256]{1,0:T(8,128)(2,1)} %get-tuple-element.24), channel_id=1, source_target_pairs={{0,8},{1,17},{2,10},{3,19},{4,12},{5,21},{6,14},{7,23},{8,0},{9,25... | collective-permute-start | bytes 6291464 | tf_op jit(solution)/shard_map/ppermute | solution.py:255
  27.3 1.5 collective-permute-start.1
  28.9 14.7 %collective-permute-done.1.came_ref = bf16[256,1152]{1,0:T(8,128)(2,1)S(1)} collective-permute-done((bf16[256,1152]{1,0:T(8,128)(2,1)S(1)}, bf16[256,1152]{1,0:T(8,128)(2,1)S(1)}, u32[]{:S(2)}, u32[]{:S(2)}) %collective-permute-start.1) | collective-permute-done | bytes 589856 | tf_op jit(solution)/shard_map/ppermute | solution.py:255
  44.6 1.3 copy-done.28
  46.0 4.9 %all-to-all-start = ((bf16[8,32,1152]{2,1,0:T(8,128)(2,1)}), bf16[8,32,1152]{2,1,0:T(8,128)(2,1)S(1)}, u32[]{:S(2)}, u32[]{:S(2)}) async-start(bf16[8,32,1152]{2,1,0:T(8,128)(2,1)} %bitcast.4), calls=%async_computation | async-start | bytes 1179648 | tf_op jit(solution)/shard_map/all_to_all | solution.py:260
  51.4 16.2 %all-to-all-done.refs_2_.refs_4_ = bf16[8,32,1152]{2,1,0:T(8,128)(2,1)S(1)} async-done(((bf16[8,32,1152]{2,1,0:T(8,128)(2,1)}), bf16[8,32,1152]{2,1,0:T(8,128)(2,1)S(1)}, u32[]{:S(2)}, u32[]{:S(2)}) %all-to-all-start) | async-done | bytes 589856 | tf_op jit(solution)/shard_map/all_to_all | solution.py:260
  68.4 1.6 %collective-permute-start.7 = (bf16[2048,256]{1,0:T(8,128)(2,1)S(1)}, bf16[2048,256]{1,0:T(8,128)(2,1)}, u32[]{:S(2)}, u32[]{:S(2)}) collective-permute-start(bf16[2048,256]{1,0:T(8,128)(2,1)S(1)} %cut_chunk.2.refs_5_.refs_1_), channel_id=1, source_target_pairs={{0,16},{1,9},{2,18},{3,11},{4,20},{5,13},{6,22},{7,15},{8,24},{9,1... | collective-permute-start | bytes 3145736 | tf_op jit(solution)/shard_map/ppermute | solution.py:255
  70.6 4.1 %rank_space.1 = (bf16[256,1024]{1,0:T(8,128)(2,1)S(1)}, bf16[256,32]{1,0:T(8,128)(2,1)S(1)}, bf16[32,8192]{1,0:T(8,128)(2,1)S(1)}, bf16[256,1024]{1,0:T(8,128)(2,1)S(1)}, bf16[8,32,1152]{2,1,0:T(8,128)(2,1)S(1)}) custom-call(s32[4]{0:T(128)S(1)} %pad_add_fusion.where_ref.refs_0_, s32[64]{0:T(128)S(1)} %copy-done.25, bf16[256,8192]{1,0:T(8,128)(2,1)S(1)} %copy-done.3, ...), custom_call_target="tpu_custom_call" | custom-call | tf_op jit(solution)/shard_map/rank_space/pallas_call | solution.py:335
  74.7 13.7 %collective-permute-done.2.refs_1_.refs_0_ = bf16[4096,256]{1,0:T(8,128)(2,1)} collective-permute-done((bf16[4096,256]{1,0:T(8,128)(2,1)}, bf16[4096,256]{1,0:T(8,128)(2,1)}, u32[]{:S(2)}, u32[]{:S(2)}) %collective-permute-start.2) | collective-permute-done | bytes 2097184 | tf_op jit(solution)/shard_map/ppermute | solution.py:255
  88.4 2.0 %cut_chunk.3.refs_1_.refs_0_ = bf16[2048,256]{1,0:T(8,128)(2,1)S(1)} custom-call(s32[4]{0:T(128)S(1)} %pad_add_fusion.where_ref.refs_0_, bf16[4096,256]{1,0:T(8,128)(2,1)} %collective-permute-done.2.refs_1_.refs_0_, bf16[256,32]{1,0:T(8,128)(2,1)S(1)} %get-tuple-element.25.refs_2_.rg_ref, bf16[4096,256]{1,0:T(8,128)(2,1)S(1)} %collective-permute-done.4.refs_3_.far_ref), custom_call_target="tpu_custom_call" | custom-call | tf_op jit(solution)/shard_map/cut_chunk/pallas_call | solution.py:322
  91.8 1.4 collective-permute-start.5
  93.2 6.8 %all-to-all-start.1 = ((bf16[8,32,1152]{2,1,0:T(8,128)(2,1)}), bf16[8,32,1152]{2,1,0:T(8,128)(2,1)}, u32[]{:S(2)}, u32[]{:S(2)}) async-start(bf16[8,32,1152]{2,1,0:T(8,128)(2,1)} %copy-done.21), calls=%async_computation.1 | async-start | bytes 1179648 | tf_op jit(solution)/shard_map/all_to_all | solution.py:260
  100.0 2.2 %copy-done.1 = bf16[8192,256]{1,0:T(8,128)(2,1)S(1)} copy-done((bf16[8192,256]{1,0:T(8,128)(2,1)S(1)}, bf16[8192,256]{1,0:T(8,128)(2,1)}, u32[]{:S(2)}) %copy-start.1) | copy-done | bytes 4194328
  102.2 2.2 %copy-done.4 = bf16[256,8192]{1,0:T(8,128)(2,1)S(1)} copy-done((bf16[256,8192]{1,0:T(8,128)(2,1)S(1)}, bf16[256,8192]{1,0:T(8,128)(2,1)}, u32[]{:S(2)}) %copy-start.4) | copy-done | bytes 4194328
  104.4 1.6 %copy-done.7 = bf16[4096,256]{1,0:T(8,128)(2,1)S(1)} copy-done((bf16[4096,256]{1,0:T(8,128)(2,1)S(1)}, bf16[4096,256]{1,0:T(8,128)(2,1)}, u32[]{:S(2)}) %copy-start.7) | copy-done | bytes 2097176
  106.0 1.0 copy-done.15
  107.0 1.0 copy-done.18
  109.1 9.3 %base_chunk.2 = (bf16[256,8192]{1,0:T(8,128)(2,1)}, f32[256,1024]{1,0:T(8,128)S(1)}) custom-call(s32[4]{0:T(128)S(1)} %pad_add_fusion.where_ref.refs_0_, s32[64]{0:T(128)S(1)} %copy-done.25, bf16[256,8192]{1,0:T(8,128)(2,1)S(1)} %copy-done.4, bf16[8192,256]{1,0:T(8,128)(2,1)S(1)} %copy-done.1, bf16[4096,256]{1,0:T(8,128)(2,1)S(1)} %pass_after.6.near_ref, ...), custom_call_target="tpu_custom_call" | custom-call | flops 4294967296 | bytes 14680064 | tf_op jit(solution)/shard_map/base_chunk/pallas_call | solution.py:379
  119.3 1.2 copy-done.10
  121.4 1.7 %collective-permute-start.11 = (bf16[256,1152]{1,0:T(8,128)(2,1)}, bf16[256,1152]{1,0:T(8,128)(2,1)S(1)}, u32[]{:S(2)}, u32[]{:S(2)}) collective-permute-start(bf16[256,1152]{1,0:T(8,128)(2,1)} %pass_after.9.refs_1_.refs_3_), channel_id=1, source_target_pairs={{0,16},{1,9},{2,18},{3,11},{4,20},{5,13},{6,22},{7,15},{8,24},{9,1... | collective-permute-start | bytes 1769480 | tf_op jit(solution)/shard_map/ppermute | solution.py:255
  123.7 2.2 %copy-done.5 = bf16[256,8192]{1,0:T(8,128)(2,1)S(1)} copy-done((bf16[256,8192]{1,0:T(8,128)(2,1)S(1)}, bf16[256,8192]{1,0:T(8,128)(2,1)}, u32[]{:S(2)}) %copy-start.5) | copy-done | bytes 4194328
  125.9 1.2 copy-done.11
  128.1 10.4 %base_chunk.3 = (bf16[256,8192]{1,0:T(8,128)(2,1)}, bf16[256,1024]{1,0:T(8,128)(2,1)}) custom-call(s32[4]{0:T(128)S(1)} %pad_add_fusion.where_ref.refs_0_, s32[64]{0:T(128)S(1)} %copy-done.25, bf16[256,8192]{1,0:T(8,128)(2,1)S(1)} %copy-done.5, bf16[8192,256]{1,0:T(8,128)(2,1)S(1)} %copy-done.2, ...), custom_call_target="tpu_custom_call", output_to_operand_aliasing={{0}: (12, {})} | custom-call | flops 4294967296 | bytes 14680064 | tf_op jit(solution)/shard_map/base_chunk/pallas_call | solution.py:379
  139.6 9.9 %collective-permute-done.12.refs_6_ = bf16[256,1152]{1,0:T(8,128)(2,1)S(1)} collective-permute-done((bf16[256,1152]{1,0:T(8,128)(2,1)S(1)}, bf16[256,1152]{1,0:T(8,128)(2,1)S(1)}, u32[]{:S(2)}, u32[]{:S(2)}) %collective-permute-start.12) | collective-permute-done | bytes 589856 | tf_op jit(solution)/shard_map/ppermute | solution.py:255
  149.5 1.0 copy-done.13
  150.5 6.9 %expand.1 = (f32[1024,1024]{1,0:T(8,128)}, f32[128,1024]{1,0:T(8,128)}) custom-call(s32[4]{0:T(128)S(1)} %pad_add_fusion.where_ref.refs_0_, s32[64]{0:T(128)S(1)} %copy-done.27, s32[64]{0:T(128)S(1)} %copy-done.25, bf16[256,1152]{1,0:T(8,128)(2,1)} %pass_after.9.refs_1_.refs_3_, bf16[256,1152]{1,0:T(8,128)(2,1)S(1)} %pass_after.11.refs_4_, ...), custom_call_target="tpu_custom_call" | custom-call | tf_op jit(solution)/shard_map/expand/pallas_call | solution.py:411
  (73 shorter events, 11.4 us)
Async XLA Ops:
  0.6 8.8 %copy-start.27 = (s32[64]{0:T(128)S(1)}, s32[64]{0:T(128)}, u32[]{:S(2)}) copy-start(s32[64]{0:T(128)} %refs_1_.5) | copy-start | bytes 772
  0.7 1.6 %copy-start.8 = (bf16[1024,1024]{1,0:T(8,128)(2,1)S(1)}, bf16[1024,1024]{1,0:T(8,128)(2,1)}, u32[]{:S(2)}) copy-start(bf16[1024,1024]{1,0:T(8,128)(2,1)} %refs_2_.3) | copy-start | bytes 6291460
  6.4 17.2 %copy-start = (bf16[8192,256]{1,0:T(8,128)(2,1)S(1)}, bf16[8192,256]{1,0:T(8,128)(2,1)}, u32[]{:S(2)}) copy-start(bf16[8192,256]{1,0:T(8,128)(2,1)} %own_ref.3) | copy-start | bytes 12582916
  6.4 17.2 %collective-permute-start = (bf16[512,1152]{1,0:T(8,128)(2,1)S(1)}, bf16[512,1152]{1,0:T(8,128)(2,1)S(1)}, u32[]{:S(2)}, u32[]{:S(2)}) collective-permute-start(bf16[512,1152]{1,0:T(8,128)(2,1)S(1)} %select_sent.1.refs_4_), channel_id=1, source_target_pairs={{0,8},{1,17},{2,10},{3,19},{4,12},{5,21},{6,14},{7,23},{8,0},{9,25... | collective-permute-start | bytes 3538952 | tf_op jit(solution)/shard_map/ppermute | solution.py:255
  25.2 42.4 %collective-permute-start.3 = (bf16[4096,256]{1,0:T(8,128)(2,1)}, bf16[4096,256]{1,0:T(8,128)(2,1)S(1)}, u32[]{:S(2)}, u32[]{:S(2)}) collective-permute-start(bf16[4096,256]{1,0:T(8,128)(2,1)} %get-tuple-element.24), channel_id=1, source_target_pairs={{0,8},{1,17},{2,10},{3,19},{4,12},{5,21},{6,14},{7,23},{8,0},{9,25... | collective-permute-start | bytes 6291464 | tf_op jit(solution)/shard_map/ppermute | solution.py:255
  27.3 16.3 %collective-permute-start.1 = (bf16[256,1152]{1,0:T(8,128)(2,1)S(1)}, bf16[256,1152]{1,0:T(8,128)(2,1)S(1)}, u32[]{:S(2)}, u32[]{:S(2)}) collective-permute-start(bf16[256,1152]{1,0:T(8,128)(2,1)S(1)} %get-tuple-element.21), channel_id=1, source_target_pairs={{0,16},{1,9},{2,18},{3,11},{4,20},{5,13},{6,22},{7,15},{8,24},{9,1... | collective-permute-start | bytes 1769480 | tf_op jit(solution)/shard_map/ppermute | solution.py:255
  46.0 21.6 %all-to-all-start = ((bf16[8,32,1152]{2,1,0:T(8,128)(2,1)}), bf16[8,32,1152]{2,1,0:T(8,128)(2,1)S(1)}, u32[]{:S(2)}, u32[]{:S(2)}) async-start(bf16[8,32,1152]{2,1,0:T(8,128)(2,1)} %bitcast.4), calls=%async_computation | async-start | bytes 1179648 | tf_op jit(solution)/shard_map/all_to_all | solution.py:260
  50.8 37.6 %collective-permute-start.2 = (bf16[4096,256]{1,0:T(8,128)(2,1)}, bf16[4096,256]{1,0:T(8,128)(2,1)}, u32[]{:S(2)}, u32[]{:S(2)}) collective-permute-start(bf16[4096,256]{1,0:T(8,128)(2,1)} %copy-done.28), channel_id=1, source_target_pairs={{0,8},{1,17},{2,10},{3,19},{4,12},{5,21},{6,14},{7,23},{8,0},{9,25... | collective-permute-start | bytes 6291464 | tf_op jit(solution)/shard_map/ppermute | solution.py:255
  68.2 2.2 %copy-start.3 = (bf16[256,8192]{1,0:T(8,128)(2,1)S(1)}, bf16[256,8192]{1,0:T(8,128)(2,1)}, u32[]{:S(2)}) copy-start(bf16[256,8192]{1,0:T(8,128)(2,1)} %tokens_ref.3) | copy-start | bytes 12582916
  68.3 2.3 %copy-start.24 = (bf16[256,1024]{1,0:T(8,128)(2,1)S(1)}, bf16[256,1024]{1,0:T(8,128)(2,1)}, u32[]{:S(2)}) copy-start(bf16[256,1024]{1,0:T(8,128)(2,1)} %refs_3_.3) | copy-start | bytes 1572868
  68.3 2.3 %copy-start.25 = (s32[64]{0:T(128)S(1)}, s32[64]{0:T(128)}, u32[]{:S(2)}) copy-start(s32[64]{0:T(128)} %refs_2_.5) | copy-start | bytes 772
  68.3 20.1 %collective-permute-start.4 = (bf16[4096,256]{1,0:T(8,128)(2,1)S(1)}, bf16[4096,256]{1,0:T(8,128)(2,1)S(1)}, u32[]{:S(2)}, u32[]{:S(2)}) collective-permute-start(bf16[4096,256]{1,0:T(8,128)(2,1)S(1)} %pass_after.6.near_ref), channel_id=1, source_target_pairs={{0,1},{1,0},{2,3},{3,2},{4,5},{5,4},{6,7},{7,6},{8,9},{9,8},{10,11... | collective-permute-start | bytes 6291464 | tf_op jit(solution)/shard_map/ppermute | solution.py:247
  68.4 22.1 %collective-permute-start.7 = (bf16[2048,256]{1,0:T(8,128)(2,1)S(1)}, bf16[2048,256]{1,0:T(8,128)(2,1)}, u32[]{:S(2)}, u32[]{:S(2)}) collective-permute-start(bf16[2048,256]{1,0:T(8,128)(2,1)S(1)} %cut_chunk.2.refs_5_.refs_1_), channel_id=1, source_target_pairs={{0,16},{1,9},{2,18},{3,11},{4,20},{5,13},{6,22},{7,15},{8,24},{9,1... | collective-permute-start | bytes 3145736 | tf_op jit(solution)/shard_map/ppermute | solution.py:255
  74.7 15.7 %copy-start.14 = (bf16[256,1024]{1,0:T(8,128)(2,1)}, bf16[256,1024]{1,0:T(8,128)(2,1)S(1)}, u32[]{:S(2)}) copy-start(bf16[256,1024]{1,0:T(8,128)(2,1)S(1)} %get-tuple-element.28.grad_ref) | copy-start | bytes 1572868
  74.7 15.7 %copy-start.17 = (bf16[32,8192]{1,0:T(8,128)(2,1)}, bf16[32,8192]{1,0:T(8,128)(2,1)S(1)}, u32[]{:S(2)}) copy-start(bf16[32,8192]{1,0:T(8,128)(2,1)S(1)} %get-tuple-element.27.at_ref) | copy-start | bytes 1572868
  74.7 15.7 %copy-start.21 = (bf16[8,32,1152]{2,1,0:T(8,128)(2,1)}, bf16[8,32,1152]{2,1,0:T(8,128)(2,1)S(1)}, u32[]{:S(2)}) copy-start(bf16[8,32,1152]{2,1,0:T(8,128)(2,1)S(1)} %get-tuple-element.26) | copy-start | bytes 1769476
  74.7 15.7 %copy-start.22 = (bf16[256,1024]{1,0:T(8,128)(2,1)}, bf16[256,1024]{1,0:T(8,128)(2,1)S(1)}, u32[]{:S(2)}) copy-start(bf16[256,1024]{1,0:T(8,128)(2,1)S(1)} %get-tuple-element.29.sum_ref) | copy-start | bytes 1572868
  88.4 2.0 %copy-start.6 = (bf16[4096,256]{1,0:T(8,128)(2,1)}, bf16[4096,256]{1,0:T(8,128)(2,1)S(1)}, u32[]{:S(2)}) copy-start(bf16[4096,256]{1,0:T(8,128)(2,1)S(1)} %collective-permute-done.4.refs_3_.far_ref) | copy-start | bytes 6291460
  90.5 9.5 %collective-permute-start.8 = (bf16[2048,256]{1,0:T(8,128)(2,1)}, bf16[2048,256]{1,0:T(8,128)(2,1)}, u32[]{:S(2)}, u32[]{:S(2)}) collective-permute-start(bf16[2048,256]{1,0:T(8,128)(2,1)} %pass_after.8.mine_ref), channel_id=1, source_target_pairs={{0,1},{1,0},{2,3},{3,2},{4,5},{5,4},{6,7},{7,6},{8,9},{9,8},{10,11... | collective-permute-start | bytes 3145736 | tf_op jit(solution)/shard_map/ppermute | solution.py:247
  91.1 29.5 %collective-permute-start.6 = (bf16[2048,256]{1,0:T(8,128)(2,1)S(1)}, bf16[2048,256]{1,0:T(8,128)(2,1)}, u32[]{:S(2)}, u32[]{:S(2)}) collective-permute-start(bf16[2048,256]{1,0:T(8,128)(2,1)S(1)} %cut_chunk.3.refs_1_.refs_0_), channel_id=1, source_target_pairs={{0,16},{1,9},{2,18},{3,11},{4,20},{5,13},{6,22},{7,15},{8,24},{9,1... | collective-permute-start | bytes 3145736 | tf_op jit(solution)/shard_map/ppermute | solution.py:255
  91.8 31.9 %collective-permute-start.5 = (bf16[4096,256]{1,0:T(8,128)(2,1)}, bf16[4096,256]{1,0:T(8,128)(2,1)}, u32[]{:S(2)}, u32[]{:S(2)}) collective-permute-start(bf16[4096,256]{1,0:T(8,128)(2,1)} %pass_after.7.near_ref), channel_id=1, source_target_pairs={{0,1},{1,0},{2,3},{3,2},{4,5},{5,4},{6,7},{7,6},{8,9},{9,8},{10,11... | collective-permute-start | bytes 6291464 | tf_op jit(solution)/shard_map/ppermute | solution.py:247
  93.2 26.1 %all-to-all-start.1 = ((bf16[8,32,1152]{2,1,0:T(8,128)(2,1)}), bf16[8,32,1152]{2,1,0:T(8,128)(2,1)}, u32[]{:S(2)}, u32[]{:S(2)}) async-start(bf16[8,32,1152]{2,1,0:T(8,128)(2,1)} %copy-done.21), calls=%async_computation.1 | async-start | bytes 1179648 | tf_op jit(solution)/shard_map/all_to_all | solution.py:260
  100.0 2.2 %copy-start.1 = (bf16[8192,256]{1,0:T(8,128)(2,1)S(1)}, bf16[8192,256]{1,0:T(8,128)(2,1)}, u32[]{:S(2)}) copy-start(bf16[8192,256]{1,0:T(8,128)(2,1)} %own_ref.3) | copy-start | bytes 12582916
  102.2 2.2 %copy-start.4 = (bf16[256,8192]{1,0:T(8,128)(2,1)S(1)}, bf16[256,8192]{1,0:T(8,128)(2,1)}, u32[]{:S(2)}) copy-start(bf16[256,8192]{1,0:T(8,128)(2,1)} %tokens_ref.3) | copy-start | bytes 12582916
  104.4 1.6 %copy-start.7 = (bf16[4096,256]{1,0:T(8,128)(2,1)S(1)}, bf16[4096,256]{1,0:T(8,128)(2,1)}, u32[]{:S(2)}) copy-start(bf16[4096,256]{1,0:T(8,128)(2,1)} %copy-done.6) | copy-start | bytes 6291460
  120.6 3.1 %copy-start.2 = (bf16[8192,256]{1,0:T(8,128)(2,1)S(1)}, bf16[8192,256]{1,0:T(8,128)(2,1)}, u32[]{:S(2)}) copy-start(bf16[8192,256]{1,0:T(8,128)(2,1)} %own_ref.3) | copy-start | bytes 12582916
  120.6 3.1 %copy-start.16 = (bf16[256,1024]{1,0:T(8,128)(2,1)S(1)}, bf16[256,1024]{1,0:T(8,128)(2,1)}, u32[]{:S(2)}) copy-start(bf16[256,1024]{1,0:T(8,128)(2,1)} %copy-done.14) | copy-start | bytes 1572868
  120.6 3.1 %collective-permute-start.9 = (bf16[2048,256]{1,0:T(8,128)(2,1)}, bf16[2048,256]{1,0:T(8,128)(2,1)S(1)}, u32[]{:S(2)}, u32[]{:S(2)}) collective-permute-start(bf16[2048,256]{1,0:T(8,128)(2,1)} %pass_after.10.mine_ref), channel_id=1, source_target_pairs={{0,1},{1,0},{2,3},{3,2},{4,5},{5,4},{6,7},{7,6},{8,9},{9,8},{10,11... | collective-permute-start | bytes 3145736 | tf_op jit(solution)/shard_map/ppermute | solution.py:247
  121.2 17.4 %collective-permute-start.10 = (bf16[256,1152]{1,0:T(8,128)(2,1)}, bf16[256,1152]{1,0:T(8,128)(2,1)S(1)}, u32[]{:S(2)}, u32[]{:S(2)}) collective-permute-start(bf16[256,1152]{1,0:T(8,128)(2,1)} %pass_after.9.refs_1_.refs_3_), channel_id=1, source_target_pairs={{0,8},{1,17},{2,10},{3,19},{4,12},{5,21},{6,14},{7,23},{8,0},{9,25... | collective-permute-start | bytes 1769480 | tf_op jit(solution)/shard_map/ppermute | solution.py:255
  121.4 18.1 %collective-permute-start.11 = (bf16[256,1152]{1,0:T(8,128)(2,1)}, bf16[256,1152]{1,0:T(8,128)(2,1)S(1)}, u32[]{:S(2)}, u32[]{:S(2)}) collective-permute-start(bf16[256,1152]{1,0:T(8,128)(2,1)} %pass_after.9.refs_1_.refs_3_), channel_id=1, source_target_pairs={{0,16},{1,9},{2,18},{3,11},{4,20},{5,13},{6,22},{7,15},{8,24},{9,1... | collective-permute-start | bytes 1769480 | tf_op jit(solution)/shard_map/ppermute | solution.py:255
  123.7 2.2 %copy-start.5 = (bf16[256,8192]{1,0:T(8,128)(2,1)S(1)}, bf16[256,8192]{1,0:T(8,128)(2,1)}, u32[]{:S(2)}) copy-start(bf16[256,8192]{1,0:T(8,128)(2,1)} %tokens_ref.3) | copy-start | bytes 12582916
  139.6 9.9 %collective-permute-start.12 = (bf16[256,1152]{1,0:T(8,128)(2,1)S(1)}, bf16[256,1152]{1,0:T(8,128)(2,1)S(1)}, u32[]{:S(2)}, u32[]{:S(2)}) collective-permute-start(bf16[256,1152]{1,0:T(8,128)(2,1)S(1)} %pass_after.11.refs_4_), channel_id=1, source_target_pairs={{0,16},{1,9},{2,18},{3,11},{4,20},{5,13},{6,22},{7,15},{8,24},{9,1... | collective-permute-start | bytes 1769480 | tf_op jit(solution)/shard_map/ppermute | solution.py:255
  (12 other events, 12.6 us)

commit v12 on v10

--- a/solution.py
+++ b/solution.py
@@ -11,7 +11,8 @@
 BLOCK = 128
 ADAPTER_SCALE = 2.0
 CHUNKS = (4, 4)
-VMEM_LIMIT = 48 * 1024 * 1024
+BASE_MIB = 40
+MIB = 1024 * 1024
 
 F32 = jnp.float32
 BF16 = jnp.bfloat16
@@ -217,8 +218,8 @@
     return lambda *refs: body(*refs[:place], *refs[place + len(tokens) :])
 
 
-def params(**extra):
-    return pltpu.CompilerParams(vmem_limit_bytes=VMEM_LIMIT, **extra)
+def params(mib, **extra):
+    return pltpu.CompilerParams(vmem_limit_bytes=mib * MIB, **extra)
 
 
 def shape(*dims, dtype=BF16):
@@ -259,14 +260,14 @@
     def along_tok(a):
         return lax.all_to_all(a, "tok", split_axis=0, concat_axis=0)
 
-    def call(body, out_shape, in_specs, name, scratch=(), out_specs=None, **extra):
+    def call(body, out_shape, in_specs, name, scratch=(), out_specs=None, mib=24, **extra):
         return pl.pallas_call(
             body,
             out_shape=out_shape,
             in_specs=in_specs,
             out_specs=out_specs or jax.tree.map(lambda _: VMEM, out_shape),
             scratch_shapes=list(scratch),
-            compiler_params=params(),
+            compiler_params=params(mib),
             name=name,
             **extra,
         )
@@ -295,6 +296,7 @@
         [VMEM, VMEM, ANY],
         "sum_and_cut",
         [pltpu.SemaphoreType.DMA],
+        mib=12,
     )(kept, came, weight)
     maps, later = call(
         functools.partial(sum_kernel, parts[1][0]),
@@ -302,6 +304,7 @@
         [VMEM, VMEM, ANY],
         "sum_and_cut",
         [pltpu.SemaphoreType.DMA],
+        mib=12,
     )(keep, second_way(sent), weight)
     maps = along_tok(maps.reshape(shards, rank, both))
 
@@ -315,6 +318,7 @@
             "pass_after",
             out_specs=ANY,
             input_output_aliases={0: 0},
+            mib=8,
         )(a, *earlier)
 
     def cut_chunk(piece, *earlier):
@@ -325,6 +329,7 @@
             [SMEM, ANY] + [ANY] * len(earlier),
             "cut_chunk",
             [pltpu.SemaphoreType.DMA],
+            mib=8,
         )(where, near, *earlier)
         near = pass_after(near, part)
         arrived.append((near, on_core(near), second_way(part)))
@@ -343,7 +348,8 @@
         ],
         [SMEM, SMEM, VMEM, VMEM, VMEM, ANY],
         "rank_space",
-        [pltpu.VMEM((rank, value), BF16)] * 2,
+        mib=24,
+        scratch=[pltpu.VMEM((rank, value), BF16)] * 2,
     )(where, fills, tokens, cotangent, maps, part)
     r0 = along_tok(terms).reshape(group_rank, both)
     r1, r2 = first_way(r0), second_way(r0)
@@ -401,7 +407,7 @@
                 scratch_shapes=[pltpu.VMEM((rows, value), F32)] if final else [],
             ),
             input_output_aliases={12: 0} if k else {},
-            compiler_params=params(dimension_semantics=("arbitrary",)),
+            compiler_params=params(BASE_MIB, dimension_semantics=("arbitrary",)),
             cost_estimate=cost(size),
             name="base_chunk",
         )(where, fills, tokens, weight, near, far, mine, theirs, at, grad, rank_grad, total, *extra)

time: 143 us -> 143 us (level)
  the two profiles are of different devices: /device:TPU:0 before, /device:TPU:9 now
where the time goes in v12:
time: 143 us; the launch traced here: 142 us
  waiting for transfers between devices  52 us (36%)
  Pallas kernels  43.5 us (30%)
  starting transfers between devices  35.3 us (25%)
  local copies, waits for them, and re-layouts  10.5 us (7%)
    ppermute x9, waiting for transfers between devices, split(): return lambda a: lax.ppermute(a, ('fsdp', 'tok'), pairs)  36 us
    pallas_call x2, Pallas kernels, local(): pl.pallas_call(functools.partial(base_kernel, steps, final), out_shape=[s...  20.6 us
    all_to_all x2, starting transfers between devices, along_tok(): return lax.all_to_all(a, 'tok', split_axis=0, concat_axis=0)  16.3 us
    all_to_all x2, waiting for transfers between devices, along_tok(): return lax.all_to_all(a, 'tok', split_axis=0, concat_axis=0)  16 us
    ppermute x9, starting transfers between devices, split(): return lambda a: lax.ppermute(a, ('fsdp', 'tok'), pairs)  13.9 us
    unnamed x34, local copies, waits for them, and re-layouts  10.5 us
    pallas_call x1, Pallas kernels, local(): call(after(functools.partial(expand_kernel, group), 7, total), [shape(cut...  6.91 us
    ppermute x4, starting transfers between devices, on_core(): return lax.ppermute(a, 'tok', [(t, t ^ 1) for t in range(shards)])  5.16 us
  transfers between devices with their start and end apart: 15, of which 6 were waited for; matrix products, arithmetic and copies ran while one was open for 0% of the time, Pallas kernels for 23%

profile of v12, /device:TPU:9, one launch (start us, length us, event | category | flops | bytes accessed | tf_op | source)
XLA Modules:
  0.0 142.3 jit_solution(16035182375779475947)
XLA Ops:
  0.7 1.6 %copy-done.3 = bf16[1024,1024]{1,0:T(8,128)(2,1)S(1)} copy-done((bf16[1024,1024]{1,0:T(8,128)(2,1)S(1)}, bf16[1024,1024]{1,0:T(8,128)(2,1)}, u32[]{:S(2)}) %copy-start.3) | copy-done | bytes 2097176
  2.3 0.9 copy-done.8
  3.9 2.5 %select_sent.1.refs_4_ = bf16[512,1152]{1,0:T(8,128)(2,1)S(1)} custom-call(s32[4]{0:T(128)S(1)} %pad_add_fusion.where_ref.refs_0_, s32[64]{0:T(128)S(1)} %copy-done.14, bf16[1024,1024]{1,0:T(8,128)(2,1)S(1)} %copy-done.3, bf16[128,1024]{1,0:T(8,128)(2,1)S(1)} %copy-done.8), custom_call_target="tpu_custom_call" | custom-call | tf_op jit(solution)/shard_map/select_sent/pallas_call | solution.py:278
  6.5 1.3 collective-permute-start
  7.8 2.5 %select_kept.1.kept_ref = bf16[512,1152]{1,0:T(8,128)(2,1)S(1)} custom-call(s32[4]{0:T(128)S(1)} %pad_add_fusion.where_ref.refs_0_, s32[64]{0:T(128)S(1)} %copy-done.15, bf16[1024,1024]{1,0:T(8,128)(2,1)S(1)} %copy-done.3, bf16[128,1024]{1,0:T(8,128)(2,1)S(1)} %copy-done.8, bf16[512,1152]{1,0:T(8,128)(2,1)S(1)} %select_sent.1.refs_4_), custom_call_target="tpu_custom_call" | custom-call | tf_op jit(solution)/shard_map/select_kept/pallas_call | solution.py:286
  10.3 11.6 %collective-permute-done.came_ref = bf16[512,1152]{1,0:T(8,128)(2,1)S(1)} collective-permute-done((bf16[512,1152]{1,0:T(8,128)(2,1)S(1)}, bf16[512,1152]{1,0:T(8,128)(2,1)S(1)}, u32[]{:S(2)}, u32[]{:S(2)}) %collective-permute-start) | collective-permute-done | bytes 1179680 | tf_op jit(solution)/shard_map/ppermute | solution.py:256
  21.9 1.6 %sum_and_cut.2 = (bf16[256,1152]{1,0:T(8,128)(2,1)S(1)}, bf16[256,1152]{1,0:T(8,128)(2,1)S(1)}, bf16[4096,256]{1,0:T(8,128)(2,1)}) custom-call(bf16[512,1152]{1,0:T(8,128)(2,1)S(1)} %select_kept.1.kept_ref, bf16[512,1152]{1,0:T(8,128)(2,1)S(1)} %collective-permute-done.came_ref, bf16[8192,256]{1,0:T(8,128)(2,1)S(1)} %copy-done), custom_call_target="tpu_custom_call" | custom-call | tf_op jit(solution)/shard_map/sum_and_cut/pallas_call | solution.py:293
  23.5 1.3 collective-permute-start.3
  24.8 1.2 collective-permute-start.1
  26.0 13.2 %collective-permute-done.1.came_ref = bf16[256,1152]{1,0:T(8,128)(2,1)S(1)} collective-permute-done((bf16[256,1152]{1,0:T(8,128)(2,1)S(1)}, bf16[256,1152]{1,0:T(8,128)(2,1)S(1)}, u32[]{:S(2)}, u32[]{:S(2)}) %collective-permute-start.1) | collective-permute-done | bytes 589856 | tf_op jit(solution)/shard_map/ppermute | solution.py:256
  39.2 1.0 sum_and_cut.3
  40.2 1.3 copy-done.16
  41.5 8.6 %all-to-all-start = ((bf16[8,32,1152]{2,1,0:T(8,128)(2,1)}), bf16[8,32,1152]{2,1,0:T(8,128)(2,1)S(1)}, u32[]{:S(2)}, u32[]{:S(2)}) async-start(bf16[8,32,1152]{2,1,0:T(8,128)(2,1)} %bitcast.4), calls=%async_computation | async-start | bytes 1179648 | tf_op jit(solution)/shard_map/all_to_all | solution.py:261
  50.2 1.2 collective-permute-start.2
  51.4 12.0 %all-to-all-done.refs_2_.refs_4_ = bf16[8,32,1152]{2,1,0:T(8,128)(2,1)S(1)} async-done(((bf16[8,32,1152]{2,1,0:T(8,128)(2,1)}), bf16[8,32,1152]{2,1,0:T(8,128)(2,1)S(1)}, u32[]{:S(2)}, u32[]{:S(2)}) %all-to-all-start) | async-done | bytes 589856 | tf_op jit(solution)/shard_map/all_to_all | solution.py:261
  63.4 1.6 %cut_chunk.2.refs_5_.refs_1_ = bf16[2048,256]{1,0:T(8,128)(2,1)} custom-call(s32[4]{0:T(128)S(1)} %pad_add_fusion.where_ref.refs_0_, bf16[4096,256]{1,0:T(8,128)(2,1)S(1)} %collective-permute-done.3.refs_1_.refs_0_, bf16[8,32,1152]{2,1,0:T(8,128)(2,1)S(1)} %all-to-all-done.refs_2_.refs_4_), custom_call_target="tpu_custom_call" | custom-call | tf_op jit(solution)/shard_map/cut_chunk/pallas_call | solution.py:326
  65.8 1.4 copy-done.1
  67.3 5.0 %rank_space.1 = (bf16[256,1024]{1,0:T(8,128)(2,1)S(1)}, bf16[256,32]{1,0:T(8,128)(2,1)S(1)}, bf16[32,8192]{1,0:T(8,128)(2,1)S(1)}, bf16[256,1024]{1,0:T(8,128)(2,1)S(1)}, bf16[8,32,1152]{2,1,0:T(8,128)(2,1)}) custom-call(s32[4]{0:T(128)S(1)} %pad_add_fusion.where_ref.refs_0_, s32[64]{0:T(128)S(1)} %copy-done.13, bf16[256,8192]{1,0:T(8,128)(2,1)S(1)} %copy-done.1, ...), custom_call_target="tpu_custom_call" | custom-call | tf_op jit(solution)/shard_map/rank_space/pallas_call | solution.py:340
  74.7 7.6 %all-to-all-start.1 = ((bf16[8,32,1152]{2,1,0:T(8,128)(2,1)}), bf16[8,32,1152]{2,1,0:T(8,128)(2,1)}, u32[]{:S(2)}, u32[]{:S(2)}) async-start(bf16[8,32,1152]{2,1,0:T(8,128)(2,1)} %get-tuple-element.26), calls=%async_computation.1 | async-start | bytes 1179648 | tf_op jit(solution)/shard_map/all_to_all | solution.py:261
  82.3 4.2 %collective-permute-done.2.refs_1_.refs_0_ = bf16[4096,256]{1,0:T(8,128)(2,1)} collective-permute-done((bf16[4096,256]{1,0:T(8,128)(2,1)}, bf16[4096,256]{1,0:T(8,128)(2,1)}, u32[]{:S(2)}, u32[]{:S(2)}) %collective-permute-start.2) | collective-permute-done | bytes 2097184 | tf_op jit(solution)/shard_map/ppermute | solution.py:256
  86.5 1.8 %cut_chunk.3.refs_1_.refs_0_ = bf16[2048,256]{1,0:T(8,128)(2,1)S(1)} custom-call(s32[4]{0:T(128)S(1)} %pad_add_fusion.where_ref.refs_0_, bf16[4096,256]{1,0:T(8,128)(2,1)} %collective-permute-done.2.refs_1_.refs_0_, bf16[256,32]{1,0:T(8,128)(2,1)S(1)} %get-tuple-element.25.refs_2_.rg_ref, bf16[4096,256]{1,0:T(8,128)(2,1)} %collective-permute-done.4.refs_3_.far_ref), custom_call_target="tpu_custom_call" | custom-call | tf_op jit(solution)/shard_map/cut_chunk/pallas_call | solution.py:326
  88.3 2.2 %collective-permute-start.6 = (bf16[2048,256]{1,0:T(8,128)(2,1)S(1)}, bf16[2048,256]{1,0:T(8,128)(2,1)}, u32[]{:S(2)}, u32[]{:S(2)}) collective-permute-start(bf16[2048,256]{1,0:T(8,128)(2,1)S(1)} %cut_chunk.3.refs_1_.refs_0_), channel_id=1, source_target_pairs={{0,16},{1,9},{2,18},{3,11},{4,20},{5,13},{6,22},{7,15},{8,24},{9,1... | collective-permute-start | bytes 3145736 | tf_op jit(solution)/shard_map/ppermute | solution.py:256
  91.4 4.1 %all-to-all-done.1 = bf16[8,32,1152]{2,1,0:T(8,128)(2,1)} async-done(((bf16[8,32,1152]{2,1,0:T(8,128)(2,1)}), bf16[8,32,1152]{2,1,0:T(8,128)(2,1)}, u32[]{:S(2)}, u32[]{:S(2)}) %all-to-all-start.1) | async-done | bytes 589856 | tf_op jit(solution)/shard_map/all_to_all | solution.py:261
  96.1 7.0 %collective-permute-done.6.refs_0_ = bf16[2048,256]{1,0:T(8,128)(2,1)} collective-permute-done((bf16[2048,256]{1,0:T(8,128)(2,1)S(1)}, bf16[2048,256]{1,0:T(8,128)(2,1)}, u32[]{:S(2)}, u32[]{:S(2)}) %collective-permute-start.6) | collective-permute-done | bytes 1048608 | tf_op jit(solution)/shard_map/ppermute | solution.py:256
  103.1 3.1 %collective-permute-start.7 = (bf16[2048,256]{1,0:T(8,128)(2,1)}, bf16[2048,256]{1,0:T(8,128)(2,1)S(1)}, u32[]{:S(2)}, u32[]{:S(2)}) collective-permute-start(bf16[2048,256]{1,0:T(8,128)(2,1)} %pass_after.7.mine_ref), channel_id=1, source_target_pairs={{0,1},{1,0},{2,3},{3,2},{4,5},{5,4},{6,7},{7,6},{8,9},{9,8},{10,11... | collective-permute-start | bytes 3145736 | tf_op jit(solution)/shard_map/ppermute | solution.py:248
  106.3 2.2 %collective-permute-start.11 = (bf16[256,1152]{1,0:T(8,128)(2,1)}, bf16[256,1152]{1,0:T(8,128)(2,1)S(1)}, u32[]{:S(2)}, u32[]{:S(2)}) collective-permute-start(bf16[256,1152]{1,0:T(8,128)(2,1)} %bitcast.5.refs_1_.refs_3_), channel_id=1, source_target_pairs={{0,16},{1,9},{2,18},{3,11},{4,20},{5,13},{6,22},{7,15},{8,24},{9,1... | collective-permute-start | bytes 1769480 | tf_op jit(solution)/shard_map/ppermute | solution.py:256
  108.5 1.0 copy-done.10
  109.5 9.8 %base_chunk.2 = (bf16[256,8192]{1,0:T(8,128)(2,1)}, f32[256,1024]{1,0:T(8,128)S(1)}) custom-call(s32[4]{0:T(128)S(1)} %pad_add_fusion.where_ref.refs_0_, s32[64]{0:T(128)S(1)} %copy-done.13, bf16[256,8192]{1,0:T(8,128)(2,1)S(1)} %copy-done.2, bf16[8192,256]{1,0:T(8,128)(2,1)} %own_ref.3, bf16[4096,256]{1,0:T(8,128)(2,1)S(1)} %pass_after.5.near_ref, ...), custom_call_target="tpu_custom_call" | custom-call | flops 4294967296 | bytes 14680064 | tf_op jit(solution)/shard_map/base_chunk/pallas_call | solution.py:389
  119.3 4.2 %collective-permute-start.12 = (bf16[256,1152]{1,0:T(8,128)(2,1)S(1)}, bf16[256,1152]{1,0:T(8,128)(2,1)S(1)}, u32[]{:S(2)}, u32[]{:S(2)}) collective-permute-start(bf16[256,1152]{1,0:T(8,128)(2,1)S(1)} %pass_after.9.refs_1_.refs_4_), channel_id=1, source_target_pairs={{0,16},{1,9},{2,18},{3,11},{4,20},{5,13},{6,22},{7,15},{8,24},{9,1... | collective-permute-start | bytes 1769480 | tf_op jit(solution)/shard_map/ppermute | solution.py:256
  123.5 10.8 %base_chunk.3 = (bf16[256,8192]{1,0:T(8,128)(2,1)}, bf16[256,1024]{1,0:T(8,128)(2,1)}) custom-call(s32[4]{0:T(128)S(1)} %pad_add_fusion.where_ref.refs_0_, s32[64]{0:T(128)S(1)} %copy-done.13, bf16[256,8192]{1,0:T(8,128)(2,1)S(1)} %copy-done.2, bf16[8192,256]{1,0:T(8,128)(2,1)} %own_ref.3, ...), custom_call_target="tpu_custom_call", output_to_operand_aliasing={{0}: (12, {})} | custom-call | flops 4294967296 | bytes 14680064 | tf_op jit(solution)/shard_map/base_chunk/pallas_call | solution.py:389
  134.3 1.0 copy-done.11
  135.3 6.9 %expand.1 = (f32[1024,1024]{1,0:T(8,128)}, f32[128,1024]{1,0:T(8,128)}) custom-call(s32[4]{0:T(128)S(1)} %pad_add_fusion.where_ref.refs_0_, s32[64]{0:T(128)S(1)} %copy-done.15, s32[64]{0:T(128)S(1)} %copy-done.13, bf16[256,1152]{1,0:T(8,128)(2,1)} %bitcast.5.refs_1_.refs_3_, bf16[256,1152]{1,0:T(8,128)(2,1)S(1)} %pass_after.9.refs_1_.refs_4_, ...), custom_call_target="tpu_custom_call" | custom-call | tf_op jit(solution)/shard_map/expand/pallas_call | solution.py:415
  (48 shorter events, 5.6 us)
Async XLA Ops:
  0.6 7.1 %copy-start.15 = (s32[64]{0:T(128)S(1)}, s32[64]{0:T(128)}, u32[]{:S(2)}) copy-start(s32[64]{0:T(128)} %refs_1_.5) | copy-start | bytes 772
  0.7 1.6 %copy-start.3 = (bf16[1024,1024]{1,0:T(8,128)(2,1)S(1)}, bf16[1024,1024]{1,0:T(8,128)(2,1)}, u32[]{:S(2)}) copy-start(bf16[1024,1024]{1,0:T(8,128)(2,1)} %refs_2_.3) | copy-start | bytes 6291460
  2.3 0.9 copy-start.8
  3.3 0.7 copy-start.14
  6.4 15.4 %copy-start = (bf16[8192,256]{1,0:T(8,128)(2,1)S(1)}, bf16[8192,256]{1,0:T(8,128)(2,1)}, u32[]{:S(2)}) copy-start(bf16[8192,256]{1,0:T(8,128)(2,1)} %own_ref.3) | copy-start | bytes 12582916
  6.5 15.4 %collective-permute-start = (bf16[512,1152]{1,0:T(8,128)(2,1)S(1)}, bf16[512,1152]{1,0:T(8,128)(2,1)S(1)}, u32[]{:S(2)}, u32[]{:S(2)}) collective-permute-start(bf16[512,1152]{1,0:T(8,128)(2,1)S(1)} %select_sent.1.refs_4_), channel_id=1, source_target_pairs={{0,8},{1,17},{2,10},{3,19},{4,12},{5,21},{6,14},{7,23},{8,0},{9,25... | collective-permute-start | bytes 3538952 | tf_op jit(solution)/shard_map/ppermute | solution.py:256
  23.5 39.9 %collective-permute-start.3 = (bf16[4096,256]{1,0:T(8,128)(2,1)}, bf16[4096,256]{1,0:T(8,128)(2,1)S(1)}, u32[]{:S(2)}, u32[]{:S(2)}) collective-permute-start(bf16[4096,256]{1,0:T(8,128)(2,1)} %get-tuple-element.24), channel_id=1, source_target_pairs={{0,8},{1,17},{2,10},{3,19},{4,12},{5,21},{6,14},{7,23},{8,0},{9,25... | collective-permute-start | bytes 6291464 | tf_op jit(solution)/shard_map/ppermute | solution.py:256
  24.8 14.4 %collective-permute-start.1 = (bf16[256,1152]{1,0:T(8,128)(2,1)S(1)}, bf16[256,1152]{1,0:T(8,128)(2,1)S(1)}, u32[]{:S(2)}, u32[]{:S(2)}) collective-permute-start(bf16[256,1152]{1,0:T(8,128)(2,1)S(1)} %get-tuple-element.21), channel_id=1, source_target_pairs={{0,16},{1,9},{2,18},{3,11},{4,20},{5,13},{6,22},{7,15},{8,24},{9,1... | collective-permute-start | bytes 1769480 | tf_op jit(solution)/shard_map/ppermute | solution.py:256
  40.2 1.3 copy-start.16
  41.5 21.8 %all-to-all-start = ((bf16[8,32,1152]{2,1,0:T(8,128)(2,1)}), bf16[8,32,1152]{2,1,0:T(8,128)(2,1)S(1)}, u32[]{:S(2)}, u32[]{:S(2)}) async-start(bf16[8,32,1152]{2,1,0:T(8,128)(2,1)} %bitcast.4), calls=%async_computation | async-start | bytes 1179648 | tf_op jit(solution)/shard_map/all_to_all | solution.py:261
  50.2 36.3 %collective-permute-start.2 = (bf16[4096,256]{1,0:T(8,128)(2,1)}, bf16[4096,256]{1,0:T(8,128)(2,1)}, u32[]{:S(2)}, u32[]{:S(2)}) collective-permute-start(bf16[4096,256]{1,0:T(8,128)(2,1)} %copy-done.16), channel_id=1, source_target_pairs={{0,8},{1,17},{2,10},{3,19},{4,12},{5,21},{6,14},{7,23},{8,0},{9,25... | collective-permute-start | bytes 6291464 | tf_op jit(solution)/shard_map/ppermute | solution.py:256
  65.0 2.2 %copy-start.1 = (bf16[256,8192]{1,0:T(8,128)(2,1)S(1)}, bf16[256,8192]{1,0:T(8,128)(2,1)}, u32[]{:S(2)}) copy-start(bf16[256,8192]{1,0:T(8,128)(2,1)} %tokens_ref.3) | copy-start | bytes 12582916
  65.0 2.3 %copy-start.12 = (bf16[256,1024]{1,0:T(8,128)(2,1)S(1)}, bf16[256,1024]{1,0:T(8,128)(2,1)}, u32[]{:S(2)}) copy-start(bf16[256,1024]{1,0:T(8,128)(2,1)} %refs_3_.3) | copy-start | bytes 1572868
  65.0 2.3 %copy-start.13 = (s32[64]{0:T(128)S(1)}, s32[64]{0:T(128)}, u32[]{:S(2)}) copy-start(s32[64]{0:T(128)} %refs_2_.5) | copy-start | bytes 772
  65.0 21.5 %collective-permute-start.4 = (bf16[4096,256]{1,0:T(8,128)(2,1)S(1)}, bf16[4096,256]{1,0:T(8,128)(2,1)}, u32[]{:S(2)}, u32[]{:S(2)}) collective-permute-start(bf16[4096,256]{1,0:T(8,128)(2,1)S(1)} %pass_after.5.near_ref), channel_id=1, source_target_pairs={{0,1},{1,0},{2,3},{3,2},{4,5},{5,4},{6,7},{7,6},{8,9},{9,8},{10,11... | collective-permute-start | bytes 6291464 | tf_op jit(solution)/shard_map/ppermute | solution.py:248
  65.5 30.0 %collective-permute-start.8 = (bf16[2048,256]{1,0:T(8,128)(2,1)}, bf16[2048,256]{1,0:T(8,128)(2,1)}, u32[]{:S(2)}, u32[]{:S(2)}) collective-permute-start(bf16[2048,256]{1,0:T(8,128)(2,1)} %cut_chunk.2.refs_5_.refs_1_), channel_id=1, source_target_pairs={{0,16},{1,9},{2,18},{3,11},{4,20},{5,13},{6,22},{7,15},{8,24},{9,1... | collective-permute-start | bytes 3145736 | tf_op jit(solution)/shard_map/ppermute | solution.py:256
  72.3 0.8 copy-start.4
  73.0 0.8 copy-start.6
  73.8 0.8 copy-start.9
  74.7 20.8 %all-to-all-start.1 = ((bf16[8,32,1152]{2,1,0:T(8,128)(2,1)}), bf16[8,32,1152]{2,1,0:T(8,128)(2,1)}, u32[]{:S(2)}, u32[]{:S(2)}) async-start(bf16[8,32,1152]{2,1,0:T(8,128)(2,1)} %get-tuple-element.26), calls=%async_computation.1 | async-start | bytes 1179648 | tf_op jit(solution)/shard_map/all_to_all | solution.py:261
  88.3 14.8 %collective-permute-start.6 = (bf16[2048,256]{1,0:T(8,128)(2,1)S(1)}, bf16[2048,256]{1,0:T(8,128)(2,1)}, u32[]{:S(2)}, u32[]{:S(2)}) collective-permute-start(bf16[2048,256]{1,0:T(8,128)(2,1)S(1)} %cut_chunk.3.refs_1_.refs_0_), channel_id=1, source_target_pairs={{0,16},{1,9},{2,18},{3,11},{4,20},{5,13},{6,22},{7,15},{8,24},{9,1... | collective-permute-start | bytes 3145736 | tf_op jit(solution)/shard_map/ppermute | solution.py:256
  90.5 33.0 %collective-permute-start.5 = (bf16[4096,256]{1,0:T(8,128)(2,1)}, bf16[4096,256]{1,0:T(8,128)(2,1)}, u32[]{:S(2)}, u32[]{:S(2)}) collective-permute-start(bf16[4096,256]{1,0:T(8,128)(2,1)} %pass_after.6.near_ref), channel_id=1, source_target_pairs={{0,1},{1,0},{2,3},{3,2},{4,5},{5,4},{6,7},{7,6},{8,9},{9,8},{10,11... | collective-permute-start | bytes 6291464 | tf_op jit(solution)/shard_map/ppermute | solution.py:248
  95.5 12.9 %copy-start.2 = (bf16[256,8192]{1,0:T(8,128)(2,1)S(1)}, bf16[256,8192]{1,0:T(8,128)(2,1)}, u32[]{:S(2)}) copy-start(bf16[256,8192]{1,0:T(8,128)(2,1)} %tokens_ref.3) | copy-start | bytes 12582916
  95.5 12.9 %copy-start.5 = (bf16[256,1024]{1,0:T(8,128)(2,1)S(1)}, bf16[256,1024]{1,0:T(8,128)(2,1)}, u32[]{:S(2)}) copy-start(bf16[256,1024]{1,0:T(8,128)(2,1)} %copy-done.4) | copy-start | bytes 1572868
  95.5 12.9 %copy-start.7 = (bf16[32,8192]{1,0:T(8,128)(2,1)S(1)}, bf16[32,8192]{1,0:T(8,128)(2,1)}, u32[]{:S(2)}) copy-start(bf16[32,8192]{1,0:T(8,128)(2,1)} %copy-done.6) | copy-start | bytes 1572868
  95.5 12.9 %collective-permute-start.9 = (bf16[2048,256]{1,0:T(8,128)(2,1)}, bf16[2048,256]{1,0:T(8,128)(2,1)S(1)}, u32[]{:S(2)}, u32[]{:S(2)}) collective-permute-start(bf16[2048,256]{1,0:T(8,128)(2,1)} %pass_after.8.mine_ref), channel_id=1, source_target_pairs={{0,1},{1,0},{2,3},{3,2},{4,5},{5,4},{6,7},{7,6},{8,9},{9,8},{10,11... | collective-permute-start | bytes 3145736 | tf_op jit(solution)/shard_map/ppermute | solution.py:248
  103.1 20.4 %collective-permute-start.7 = (bf16[2048,256]{1,0:T(8,128)(2,1)}, bf16[2048,256]{1,0:T(8,128)(2,1)S(1)}, u32[]{:S(2)}, u32[]{:S(2)}) collective-permute-start(bf16[2048,256]{1,0:T(8,128)(2,1)} %pass_after.7.mine_ref), channel_id=1, source_target_pairs={{0,1},{1,0},{2,3},{3,2},{4,5},{5,4},{6,7},{7,6},{8,9},{9,8},{10,11... | collective-permute-start | bytes 3145736 | tf_op jit(solution)/shard_map/ppermute | solution.py:248
  106.3 13.0 %collective-permute-start.10 = (bf16[256,1152]{1,0:T(8,128)(2,1)}, bf16[256,1152]{1,0:T(8,128)(2,1)S(1)}, u32[]{:S(2)}, u32[]{:S(2)}) collective-permute-start(bf16[256,1152]{1,0:T(8,128)(2,1)} %bitcast.5.refs_1_.refs_3_), channel_id=1, source_target_pairs={{0,8},{1,17},{2,10},{3,19},{4,12},{5,21},{6,14},{7,23},{8,0},{9,25... | collective-permute-start | bytes 1769480 | tf_op jit(solution)/shard_map/ppermute | solution.py:256
  106.3 17.3 %collective-permute-start.11 = (bf16[256,1152]{1,0:T(8,128)(2,1)}, bf16[256,1152]{1,0:T(8,128)(2,1)S(1)}, u32[]{:S(2)}, u32[]{:S(2)}) collective-permute-start(bf16[256,1152]{1,0:T(8,128)(2,1)} %bitcast.5.refs_1_.refs_3_), channel_id=1, source_target_pairs={{0,16},{1,9},{2,18},{3,11},{4,20},{5,13},{6,22},{7,15},{8,24},{9,1... | collective-permute-start | bytes 1769480 | tf_op jit(solution)/shard_map/ppermute | solution.py:256
  108.4 1.0 copy-start.10
  119.3 15.0 %collective-permute-start.12 = (bf16[256,1152]{1,0:T(8,128)(2,1)S(1)}, bf16[256,1152]{1,0:T(8,128)(2,1)S(1)}, u32[]{:S(2)}, u32[]{:S(2)}) collective-permute-start(bf16[256,1152]{1,0:T(8,128)(2,1)S(1)} %pass_after.9.refs_1_.refs_4_), channel_id=1, source_target_pairs={{0,16},{1,9},{2,18},{3,11},{4,20},{5,13},{6,22},{7,15},{8,24},{9,1... | collective-permute-start | bytes 1769480 | tf_op jit(solution)/shard_map/ppermute | solution.py:256
  134.3 1.0 copy-start.11
